TPU v7x, 32 devices: a whole 2x2x4 slice. The times are simulated.
32 devices in a mesh: seq: 4 (over x, core), wshard: 8 (over z, y).
Axes of the slice: x: 2, y: 2, z: 4, core: 2. Of those that a mesh axis runs over, the one named last changes fastest.
Arguments:
- block_in: bfloat16 [8, 1024, 1024], P('wshard', 'seq'), may hold values from -6 to 6
- cotangent: bfloat16 [8, 1024, 1024], P('wshard', 'seq'), may hold values from -6 to 6
- in_weight: float32 [1024, 4384], P('wshard'), may hold values from -0.1875 to 0.1875
- in_first: float32 [1024, 4384], P('wshard'), may hold values from -32 to 32
- in_second: float32 [1024, 4384], P('wshard'), may hold values from 106.496 to 434.176
- out_weight: float32 [2048, 1024], P('wshard'), may hold values from -0.125 to 0.125
- out_first: float32 [2048, 1024], P('wshard'), may hold values from -64 to 64
- out_second: float32 [2048, 1024], P('wshard'), may hold values from 434.176 to 1720.32
- vec_weight: float32 [14688], replicated, may hold values from -7 to 3, as said below
- vec_first: float32 [14688], replicated, may hold values from -325.8348 to 325.8348, as said below
- vec_second: float32 [14688], replicated, may hold values from 32.768 to 114688, as said below
Outputs:
- block_out: float32 [8, 1024, 1024], P('wshard', 'seq')
- block_in_grad: float32 [8, 1024, 1024], P('wshard', 'seq')
- in_first_new: float32 [1024, 4384], P('wshard')
- in_second_new: float32 [1024, 4384], P('wshard')
- in_weight_new: float32 [1024, 4384], P('wshard')
- out_first_new: float32 [2048, 1024], P('wshard')
- out_second_new: float32 [2048, 1024], P('wshard')
- out_weight_new: float32 [2048, 1024], P('wshard')
- vec_first_new: float32 [14688], replicated
- vec_second_new: float32 [14688], replicated
- vec_weight_new: float32 [14688], replicated
Inputs may be any that keep to these rules, and one draw needn't show every extreme that they name: `vec_weight`: gains near one, a_log the logarithm of a positive rate, dt_bias an inverse softplus of a small step. `vec_first`: both signs. `vec_second`: entries are positive.
All inputs are finite; a program needn't handle non-finite values.
Results may differ from a plain program's by a relative error of at most 0.018.
Values may be sent and summed in bfloat16 or wider, within the bound.
No kernel may reach another device: no remote copies, remote signals or barrier semaphores. Data moves between devices by JAX's collectives and lax.ppermute only.
A program may use at most 192 MiB of HBM per device.

v0:
```python
import jax
import jax.numpy as jnp
from jax import lax
from jax.sharding import PartitionSpec as P

D = 1024
HEADS = 32
HEADDIM = 64
STATE = 128
WIDTH = 4
BLOCK = 256
STEP = 10
DI = 2048
CONVCH = 2304


precise = lax.Precision.HIGHEST
norm_eps = 1e-05
beta_one = 0.9
beta_two = 0.95
adam_eps = 1e-08
matrix_rate = 0.05
matrix_decay = 0.1
vector_rate = 0.5


def from_behind(block, axis, distance):
    devices = range(lax.axis_size(axis))
    route = [(i - distance, i) for i in devices if i - distance in devices]
    return lax.ppermute(block, axis, route)


def rms_scale(values):
    return values * lax.rsqrt(jnp.mean(values * values, axis=-1, keepdims=True) + norm_eps)


def split_vector(vector):
    extents = [D, DI, WIDTH * CONVCH, CONVCH, HEADS, HEADS, HEADS]
    pieces = []
    offset = 0
    for extent in extents:
        pieces.append(vector[offset : offset + extent])
        offset = offset + extent
    pieces[2] = pieces[2].reshape(WIDTH, CONVCH)
    return pieces


def convolve(extended, kernel, conv_bias):
    rows_out = extended.shape[0] - kernel.shape[0] + 1
    summed = jnp.broadcast_to(conv_bias[None, :], (rows_out, kernel.shape[1]))
    for offset in range(kernel.shape[0]):
        summed = summed + kernel[offset][None, :] * extended[offset : offset + rows_out]
    return jax.nn.silu(summed)


def state_scan(inputs_x, step_size, a_log, b_rows, c_rows, d_skip):
    length, head_count, head_width = inputs_x.shape
    blocks = length // BLOCK
    log_decay = step_size * (-jnp.exp(a_log))[None, :]
    weighted = inputs_x * step_size[:, :, None]
    causal = jnp.tril(jnp.ones((BLOCK, BLOCK), jnp.float32))
    lower = causal > 0.5

    def advance(carry_state, pieces):
        x_block, r_block, b_block, c_block = pieces
        cumulative = jnp.cumsum(r_block.T, axis=1)
        differ = (cumulative[:, :, None] - cumulative[:, None, :]) * causal[None]
        scores = jnp.dot(c_block, b_block.T, precision=precise)
        decay_mat = jnp.where(lower[None], jnp.exp(differ), 0.0) * scores[None]
        within = jnp.einsum("hij,jhp->ihp", decay_mat, x_block, precision=precise)
        carried = jnp.einsum("in,hpn->ihp", c_block, carry_state, precision=precise)
        carried = carried * jnp.exp(cumulative.T)[:, :, None]
        to_end = jnp.exp(cumulative[:, -1:] - cumulative)
        fresh = jnp.einsum(
            "jn,jhp->hpn", b_block, x_block * to_end.T[:, :, None], precision=precise
        )
        carry_state = carry_state * jnp.exp(cumulative[:, -1])[:, None, None] + fresh
        return (carry_state, within + carried)

    initial = jnp.zeros((head_count, head_width, b_rows.shape[1]), jnp.float32)
    pieces = (
        weighted.reshape(blocks, BLOCK, head_count, head_width),
        log_decay.reshape(blocks, BLOCK, head_count),
        b_rows.reshape(blocks, BLOCK, b_rows.shape[1]),
        c_rows.reshape(blocks, BLOCK, c_rows.shape[1]),
    )
    last_state, outputs = lax.scan(jax.checkpoint(advance), initial, pieces)
    return outputs.reshape(length, head_count, head_width) + d_skip[None, :, None] * inputs_x


def pre_norm(hidden, gain):
    return rms_scale(hidden) * gain[None, :]


def gated_norm(mixed, gating, gain):
    return rms_scale(mixed * jax.nn.silu(gating)) * gain[None, :]


def head_mixer(inputs_x, dt_part, both_rows, decay_part, bias_part, skip_part):
    step_size = jax.nn.softplus(dt_part + bias_part[None, :])
    return state_scan(
        inputs_x, step_size, decay_part, both_rows[:, :STATE], both_rows[:, STATE:], skip_part
    )


def adamw_step(weight, first, second, grad, rate, decay):
    first_new = beta_one * first + (1.0 - beta_one) * grad
    second_new = beta_two * second + (1.0 - beta_two) * grad * grad
    fix_one = 1.0 - beta_one**STEP
    fix_two = 1.0 - beta_two**STEP
    normalized = first_new / fix_one / (jnp.sqrt(second_new / fix_two) + adam_eps)
    return (first_new, second_new, weight - rate * (normalized + decay * weight))


def rows_sum(grad_pair):
    return (
        lax.psum_scatter(grad_pair[0], "wshard", scatter_dimension=0, tiled=True),
        lax.psum_scatter(grad_pair[1], "wshard", scatter_dimension=0, tiled=True),
    )


def cols_sum(grad_pair):
    return (
        lax.psum_scatter(
            grad_pair[0].astype(jnp.bfloat16), "seq", scatter_dimension=1, tiled=True
        ).astype(jnp.float32),
        lax.psum_scatter(
            grad_pair[1].astype(jnp.bfloat16), "seq", scatter_dimension=1, tiled=True
        ).astype(jnp.float32),
    )


def shards(
    block_in,
    cotangent,
    in_weight,
    in_first,
    in_second,
    out_weight,
    out_first,
    out_second,
    vec_weight,
    vec_first,
    vec_second,
):
    rows_here = block_in.shape[1]
    hidden = block_in.reshape(rows_here, D).astype(jnp.float32)
    seq_count = lax.axis_size("seq")
    seq_index = lax.axis_index("seq")
    local_heads = HEADS // seq_count
    first_head = seq_index * local_heads
    in_low, out_low = (
        lax.all_gather(in_weight.astype(jnp.bfloat16), "wshard", axis=0, tiled=True),
        lax.all_gather(out_weight.astype(jnp.bfloat16), "wshard", axis=0, tiled=True),
    )
    gain_one, gain_two, kernel, conv_bias, a_log, dt_bias, d_skip = split_vector(vec_weight)
    normed, norm_pullback = jax.vjp(pre_norm, hidden, gain_one)
    normed_low = normed.astype(jnp.bfloat16)
    projected = jnp.dot(normed_low, in_low, preferred_element_type=jnp.float32)
    gating = projected[:, :DI]
    conv_in = projected[:, DI : DI + CONVCH]
    dt_raw = projected[:, DI + CONVCH :]
    border = from_behind(conv_in[rows_here - WIDTH + 1 :], "seq", 1)
    conv_out, conv_pullback = jax.vjp(
        convolve, jnp.concatenate([border, conv_in], 0), kernel, conv_bias
    )
    inner_low = conv_out[:, :DI].astype(jnp.bfloat16).reshape(rows_here, HEADS, HEADDIM)
    dt_low = dt_raw.astype(jnp.bfloat16)
    inner_heads, dt_heads = (
        lax.all_to_all(inner_low, "seq", split_axis=1, concat_axis=0, tiled=True),
        lax.all_to_all(dt_low, "seq", split_axis=1, concat_axis=0, tiled=True),
    )
    both_rows = lax.all_gather(conv_out[:, DI:].astype(jnp.bfloat16), "seq", axis=0, tiled=True)

    def head_part(values):
        return lax.dynamic_slice_in_dim(values, first_head, local_heads, 0)

    def spread_heads(values):
        return lax.dynamic_update_slice_in_dim(
            jnp.zeros((HEADS,), jnp.float32), values, first_head, 0
        )

    scanned, scan_pullback = jax.vjp(
        head_mixer,
        inner_heads.astype(jnp.float32),
        dt_heads.astype(jnp.float32),
        both_rows.astype(jnp.float32),
        head_part(a_log),
        head_part(dt_bias),
        head_part(d_skip),
    )
    back_rows = lax.all_to_all(
        scanned.astype(jnp.bfloat16), "seq", split_axis=0, concat_axis=1, tiled=True
    )
    mixed = back_rows.reshape(rows_here, DI).astype(jnp.float32)
    normed_out, gated_pullback = jax.vjp(gated_norm, mixed, gating, gain_two)
    normed_out_low = normed_out.astype(jnp.bfloat16)
    block_out = hidden + jnp.dot(normed_out_low, out_low, preferred_element_type=jnp.float32)
    cot_rows = cotangent.reshape(rows_here, D)
    d_normed_out = jnp.dot(cot_rows, out_low.T, preferred_element_type=jnp.float32)
    grad_out = jnp.dot(normed_out_low.T, cot_rows, preferred_element_type=jnp.float32)
    d_mixed, d_gating, d_gain_two = gated_pullback(d_normed_out)
    d_heads = lax.all_to_all(
        d_mixed.astype(jnp.bfloat16).reshape(rows_here, HEADS, HEADDIM),
        "seq",
        split_axis=1,
        concat_axis=0,
        tiled=True,
    )
    d_inner_heads, d_dt_heads, d_both, d_a_log, d_dt_bias, d_skip_part = scan_pullback(
        d_heads.astype(jnp.float32)
    )
    d_inner_rows, d_dt_rows = (
        lax.all_to_all(
            d_inner_heads.astype(jnp.bfloat16), "seq", split_axis=0, concat_axis=1, tiled=True
        ),
        lax.all_to_all(
            d_dt_heads.astype(jnp.bfloat16), "seq", split_axis=0, concat_axis=1, tiled=True
        ),
    )
    d_both_rows = lax.psum_scatter(
        d_both.astype(jnp.bfloat16), "seq", scatter_dimension=0, tiled=True
    ).astype(jnp.float32)
    d_conv_out = jnp.concatenate(
        [d_inner_rows.reshape(rows_here, DI).astype(jnp.float32), d_both_rows], 1
    )
    d_extended, d_kernel, d_conv_bias = conv_pullback(d_conv_out)
    returned = from_behind(d_extended[: WIDTH - 1], "seq", -1)
    d_conv_in = d_extended[WIDTH - 1 :].at[rows_here - WIDTH + 1 :].add(returned)
    d_projected = jnp.concatenate([d_gating, d_conv_in, d_dt_rows.astype(jnp.float32)], 1).astype(
        jnp.bfloat16
    )
    d_normed = jnp.dot(d_projected, in_low.T, preferred_element_type=jnp.float32)
    grad_in = jnp.dot(normed_low.T, d_projected, preferred_element_type=jnp.float32)
    d_hidden, d_gain_one = norm_pullback(d_normed)
    block_grad = cot_rows.astype(jnp.float32) + d_hidden
    vec_grad = jnp.concatenate(
        [
            d_gain_one,
            d_gain_two,
            d_kernel.reshape(-1),
            d_conv_bias,
            spread_heads(d_a_log),
            spread_heads(d_dt_bias),
            spread_heads(d_skip_part),
        ]
    )
    vec_total = lax.psum(vec_grad, ("seq", "wshard"))
    vec_first_new, vec_second_new, vec_weight_new = adamw_step(
        vec_weight, vec_first, vec_second, vec_total, vector_rate, 0.0
    )
    in_part, out_part = cols_sum(rows_sum((grad_in, grad_out)))

    def quarter(values):
        extent = values.shape[1] // seq_count
        return lax.dynamic_slice_in_dim(values, seq_index * extent, extent, 1)

    in_first_new, in_second_new, in_weight_new = adamw_step(
        quarter(in_weight),
        quarter(in_first),
        quarter(in_second),
        in_part,
        matrix_rate,
        matrix_decay,
    )
    out_first_new, out_second_new, out_weight_new = adamw_step(
        quarter(out_weight),
        quarter(out_first),
        quarter(out_second),
        out_part,
        matrix_rate,
        matrix_decay,
    )
    gathered = (
        lax.all_gather(in_first_new.astype(jnp.bfloat16), "seq", axis=1, tiled=True).astype(
            in_first_new.dtype
        ),
        lax.all_gather(in_second_new.astype(jnp.bfloat16), "seq", axis=1, tiled=True).astype(
            in_second_new.dtype
        ),
        lax.all_gather(in_weight_new.astype(jnp.bfloat16), "seq", axis=1, tiled=True).astype(
            in_weight_new.dtype
        ),
        lax.all_gather(out_first_new.astype(jnp.bfloat16), "seq", axis=1, tiled=True).astype(
            out_first_new.dtype
        ),
        lax.all_gather(out_second_new.astype(jnp.bfloat16), "seq", axis=1, tiled=True).astype(
            out_second_new.dtype
        ),
        lax.all_gather(out_weight_new.astype(jnp.bfloat16), "seq", axis=1, tiled=True).astype(
            out_weight_new.dtype
        ),
    )
    return (
        block_out.reshape(1, rows_here, D),
        block_grad.reshape(1, rows_here, D),
        gathered[0],
        gathered[1],
        gathered[2],
        gathered[3],
        gathered[4],
        gathered[5],
        vec_first_new,
        vec_second_new,
        vec_weight_new,
    )


def solution(mesh):
    return jax.shard_map(
        shards,
        mesh=mesh,
        in_specs=(
            P("wshard", "seq", None),
            P("wshard", "seq", None),
            P("wshard", None),
            P("wshard", None),
            P("wshard", None),
            P("wshard", None),
            P("wshard", None),
            P("wshard", None),
            P(),
            P(),
            P(),
        ),
        out_specs=(
            P("wshard", "seq", None),
            P("wshard", "seq", None),
            P("wshard", None),
            P("wshard", None),
            P("wshard", None),
            P("wshard", None),
            P("wshard", None),
            P("wshard", None),
            P(),
            P(),
            P(),
        ),
        check_vma=False,
    )
```

profile of v0, /device:TPU:0, one launch (start us, length us, event | category | flops | bytes accessed | tf_op | source)
XLA Modules:
  0.0 1139.9 jit_solution(9492582755534624455)
XLA Ops:
  12.2 133.7 %all-gather.6.cloned.1.call-done = bf16[1024,4384]{0,1:T(8,128)(2,1)} async-done(((bf16[128,4384]{0,1:T(8,128)(2,1)}), bf16[1024,4384]{0,1:T(8,128)(2,1)}) %all-gather.6.cloned.1.call-update) | async-done | bytes 8978448 | tf_op jit(solution)/shard_map/all_gather | solution.py:153
  146.0 6.4 fusion.134
  164.6 7.6 multiply_convert_fusion
  179.5 16.4 %all_gather.28 = bf16[1024,256]{0,1:T(8,128)(2,1)S(1)} all-gather(bf16[256,256]{0,1:T(8,128)(2,1)S(1)} %slice.209), channel_id=1, replica_groups=mesh['seq'=4,'wshard'=8] {'seq'}, dimensions={0}, use_global_device_ids=true | all-gather | bytes 655360 | tf_op jit(solution)/shard_map/all_gather | solution.py:173
  199.0 90.2 %while.40 = (s32[]{:T(128)}, f32[8,64,128]{2,1,0:T(8,128)S(1)}, f32[4,256,8,64]{1,0,3,2:T(4,128)}, f32[4,8,64,128]{3,2,1,0:T(8,128)}, f32[4,256,8]{1,2,0:T(8,128...) while((s32[]{:T(128)}, f32[8,64,128]{2,1,0:T(8,128)S(1)}, ...), condition=%wide.region_4.5_spmd.clone, body=%wide.region_1.4_spmd.clone.sunk | while | flops 909182976 | bytes 7778084 | solution.py:87
  209.2 12.3 %dynamic_update_slice.81 = f32[4,256,8,64]{1,0,3,2:T(4,128)} dynamic-update-slice(f32[4,256,8,64]{1,0,3,2:T(4,128)} %get-tuple-element.901, f32[1,256,8,64]{1,0,3,2:T(1,128)S(1)} %copy.158, s32[]{:T(128)S(6)} %copy.171, s32[]{:T(128)} %constant.182.clone.1..sunk, s32[]{:T(128)} %constant.182.clone.1..sunk, s32[]{:T(128)} %constant.182.clone.1..sunk) | dynamic-update-slice | bytes 1048580 | tf_op jit(solution)/shard_map/jvp()/while/body/jit(dynamic_update_index_in_dim)/dynamic_update_slice | solution.py:87
  231.8 12.3 %dynamic_update_slice.81 = f32[4,256,8,64]{1,0,3,2:T(4,128)} dynamic-update-slice(f32[4,256,8,64]{1,0,3,2:T(4,128)} %get-tuple-element.901, f32[1,256,8,64]{1,0,3,2:T(1,128)S(1)} %copy.158, s32[]{:T(128)S(6)} %copy.171, s32[]{:T(128)} %constant.182.clone.1..sunk, s32[]{:T(128)} %constant.182.clone.1..sunk, s32[]{:T(128)} %constant.182.clone.1..sunk) | dynamic-update-slice | bytes 1048580 | tf_op jit(solution)/shard_map/jvp()/while/body/jit(dynamic_update_index_in_dim)/dynamic_update_slice | solution.py:87
  254.3 12.3 %dynamic_update_slice.81 = f32[4,256,8,64]{1,0,3,2:T(4,128)} dynamic-update-slice(f32[4,256,8,64]{1,0,3,2:T(4,128)} %get-tuple-element.901, f32[1,256,8,64]{1,0,3,2:T(1,128)S(1)} %copy.158, s32[]{:T(128)S(6)} %copy.171, s32[]{:T(128)} %constant.182.clone.1..sunk, s32[]{:T(128)} %constant.182.clone.1..sunk, s32[]{:T(128)} %constant.182.clone.1..sunk) | dynamic-update-slice | bytes 1048580 | tf_op jit(solution)/shard_map/jvp()/while/body/jit(dynamic_update_index_in_dim)/dynamic_update_slice | solution.py:87
  276.8 12.3 %dynamic_update_slice.81 = f32[4,256,8,64]{1,0,3,2:T(4,128)} dynamic-update-slice(f32[4,256,8,64]{1,0,3,2:T(4,128)} %get-tuple-element.901, f32[1,256,8,64]{1,0,3,2:T(1,128)S(1)} %copy.158, s32[]{:T(128)S(6)} %copy.171, s32[]{:T(128)} %constant.182.clone.1..sunk, s32[]{:T(128)} %constant.182.clone.1..sunk, s32[]{:T(128)} %constant.182.clone.1..sunk) | dynamic-update-slice | bytes 1048580 | tf_op jit(solution)/shard_map/jvp()/while/body/jit(dynamic_update_index_in_dim)/dynamic_update_slice | solution.py:87
  289.2 4.1 reshape.513
  301.9 4.5 all-to-all-start.2
  306.4 14.5 %all-to-all-done.2 = bf16[4,2,65536]{2,1,0:T(2,128)(2,1)} async-done(((bf16[4,2,65536]{2,1,0:T(2,128)(2,1)}), bf16[4,2,65536]{2,1,0:T(2,128)(2,1)}, u32[]{:S(2)}, u32[]{:S(2)}) %all-to-all-start.2) | async-done | bytes 1048608 | tf_op jit(solution)/shard_map/all_to_all | solution.py:192
  331.9 5.3 multiply_reduce_fusion.7
  345.3 13.6 %all-to-all-done.3 = bf16[256,32,64]{0,2,1:T(8,128)(2,1)S(1)} async-done(((bf16[256,32,64]{0,2,1:T(8,128)(2,1)}), bf16[256,32,64]{0,2,1:T(8,128)(2,1)S(1)}, u32[]{:S(2)}, u32[]{:S(2)}) %all-to-all-start.3) | async-done | bytes 1048608 | tf_op jit(solution)/shard_map/all_to_all | solution.py:203
  366.1 95.7 %while.41 = (s32[]{:T(128)}, f32[8,64,128]{2,1,0:T(8,128)S(1)}, f32[4,256,8,64]{1,3,2,0:T(8,128)}, f32[4,256,8]{1,2,0:T(8,128)}, f32[4,256,128]{2,1,0:T(8,128)},...) while((s32[]{:T(128)}, f32[8,64,128]{2,1,0:T(8,128)S(1)}, ...), condition=%wide.region_19.20_spmd.clone, body=%wide.region_7.19_spmd.clone.sunk | while | flops 2124171264 | bytes 19195672 | solution.py:87
  474.7 4.4 reshape.557
  479.1 4.3 all-to-all-start.4
  485.9 12.2 %all-to-all-done.4 = bf16[4,2,65536]{2,1,0:T(2,128)(2,1)} async-done(((bf16[4,2,65536]{2,1,0:T(2,128)(2,1)}), bf16[4,2,65536]{2,1,0:T(2,128)(2,1)}, u32[]{:S(2)}, u32[]{:S(2)}) %all-to-all-start.4) | async-done | bytes 1048608 | tf_op jit(solution)/shard_map/all_to_all | solution.py:214
  498.1 4.3 reshape.558
  508.5 7.4 multiply_reduce_fusion.5
  536.4 7.5 scatter-add.4
  544.0 10.5 fusion.121
  556.2 4.6 fusion.125
  560.8 298.0 %reduce-scatter.10.cloned.1.call-done = f32[128,4384]{0,1:T(8,128)} async-done(((f32[1024,4384]{0,1:T(8,128)}), f32[128,4384]{0,1:T(8,128)}) %reduce-scatter.10.cloned.1.call-update) | async-done | bytes 2244624 | tf_op jit(solution)/shard_map/reduce_scatter | solution.py:117
  861.6 149.3 %reduce-scatter.12.cloned.1.call-done = f32[256,1024]{1,0:T(8,128)} async-done(((f32[2048,1024]{1,0:T(8,128)}), f32[256,1024]{1,0:T(8,128)}) %reduce-scatter.12.cloned.1.call-update) | async-done | bytes 1048592 | tf_op jit(solution)/shard_map/reduce_scatter | solution.py:118
  1013.1 25.2 %reduce-scatter.16.cloned.1.call-done = bf16[128,1096]{0,1:T(8,128)(2,1)} async-done(((bf16[128,4384]{0,1:T(8,128)(2,1)}), bf16[128,1096]{0,1:T(8,128)(2,1)}) %reduce-scatter.16.cloned.1.call-update) | async-done | bytes 280592
  1042.1 4.7 fusion.112
  1047.7 7.0 fusion.116
  1054.8 40.0 %psum.7 = f32[14688]{0:T(1024)S(1)} all-reduce(f32[14688]{0:T(1024)S(1)} %concatenate.22), channel_id=1, replica_groups=mesh['seq'=4,'wshard'=8] {'seq','wshard'}, use_global_device_ids=true, to_apply=%region_37.38 | all-reduce | flops 14688 | bytes 117504 | tf_op jit(solution)/shard_map/psum | solution.py:248
  1098.3 8.0 all_gather.35
  1107.4 7.4 all_gather.34
  1115.8 7.6 all_gather.33
  (477 shorter events, 265.7 us)
Async XLA Ops:
  7.2 138.8 %all-gather.6.cloned.1.call-start = ((), (), s32[]{:S(2)}) async-start(), calls=%async_computation.11 | async-start | bytes 10100736 | tf_op jit(solution)/shard_map/all_gather | solution.py:153
  10.1 321.8 %all-gather.8.cloned.1.call-start = ((), (), s32[]{:S(2)}) async-start(), calls=%async_computation.12 | async-start | bytes 4718592 | tf_op jit(solution)/shard_map/all_gather | solution.py:154
  11.1 166.6 %copy-start.58 = (f32[32]{0:T(128)}, f32[32]{0:T(128)S(1)}, u32[]{:S(2)}) copy-start(f32[32]{0:T(128)S(1)} %get-tuple-element.692) | copy-start | bytes 388
  11.1 141.2 %copy-start.47 = (f32[1024]{0:T(1024)}, f32[1024]{0:T(1024)S(1)}, u32[]{:S(2)}) copy-start(f32[1024]{0:T(1024)S(1)} %slice.164) | copy-start | bytes 12292
  11.1 153.4 %copy-start.32 = (f32[2304]{0:T(1024)}, f32[2304]{0:T(1024)S(1)}, u32[]{:S(2)}) copy-start(f32[2304]{0:T(1024)S(1)} %get-tuple-element.695) | copy-start | bytes 27652
  11.1 153.4 %copy-start.34 = (f32[2304]{0:T(1024)}, f32[2304]{0:T(1024)S(1)}, u32[]{:S(2)}) copy-start(f32[2304]{0:T(1024)S(1)} %get-tuple-element.696) | copy-start | bytes 27652
  11.2 153.4 %copy-start.36 = (f32[2304]{0:T(1024)}, f32[2304]{0:T(1024)S(1)}, u32[]{:S(2)}) copy-start(f32[2304]{0:T(1024)S(1)} %get-tuple-element.697) | copy-start | bytes 27652
  11.2 153.4 %copy-start.38 = (f32[2304]{0:T(1024)}, f32[2304]{0:T(1024)S(1)}, u32[]{:S(2)}) copy-start(f32[2304]{0:T(1024)S(1)} %get-tuple-element.698) | copy-start | bytes 27652
  12.0 140.3 %copy-start.53 = (f32[256]{0:T(256)}, f32[256]{0:T(256)S(1)}, u32[]{:S(2)}) copy-start(f32[256]{0:T(256)S(1)} %fusion.119) | copy-start | bytes 3076
  12.1 140.3 %copy-start.51 = (f32[256]{0:T(256)}, f32[256]{0:T(256)S(1)}, u32[]{:S(2)}) copy-start(f32[256]{0:T(256)S(1)} %fusion.147) | copy-start | bytes 3076
  12.1 281.6 %copy-start.61 = (f32[8]{0:T(128)}, f32[8]{0:T(128)S(1)}, u32[]{:S(2)}) copy-start(f32[8]{0:T(128)S(1)} %dynamic_slice.107) | copy-start | bytes 100
  12.2 332.4 %copy-start.56 = (f32[8]{0:T(128)}, f32[8]{0:T(128)S(1)}, u32[]{:S(2)}) copy-start(f32[8]{0:T(128)S(1)} %dynamic_slice.105) | copy-start | bytes 100
  155.2 8.0 collective-permute-start
  159.7 14.5 %all-to-all-start = ((bf16[256,4,8]{0,2,1:T(8,128)(2,1)}), bf16[256,4,8]{0,2,1:T(8,128)(2,1)S(1)}, u32[]{:S(2)}, u32[]{:S(2)}) async-start(bf16[256,4,8]{0,2,1:T(8,128)(2,1)} %fusion.146), calls=%async_computation | async-start | bytes 32768 | tf_op jit(solution)/shard_map/all_to_all | solution.py:171
  174.2 170.4 %copy-start.27 = (bf16[256,4,8]{0,2,1:T(8,128)(2,1)}, bf16[256,4,8]{0,2,1:T(8,128)(2,1)S(1)}, u32[]{:S(2)}) copy-start(bf16[256,4,8]{0,2,1:T(8,128)(2,1)S(1)} %all-to-all-done) | copy-start | bytes 49156
  174.2 23.7 %all-to-all-start.1 = ((bf16[256,32,64]{0,2,1:T(8,128)(2,1)}), bf16[256,32,64]{0,2,1:T(8,128)(2,1)S(1)}, u32[]{:S(2)}, u32[]{:S(2)}) async-start(bf16[256,32,64]{0,2,1:T(8,128)(2,1)} %bitcast.4), calls=%async_computation.1 | async-start | bytes 2097152 | tf_op jit(solution)/shard_map/all_to_all | solution.py:170
  301.9 19.0 %all-to-all-start.2 = ((bf16[4,2,65536]{2,1,0:T(2,128)(2,1)}), bf16[4,2,65536]{2,1,0:T(2,128)(2,1)}, u32[]{:S(2)}, u32[]{:S(2)}) async-start(bf16[4,2,65536]{2,1,0:T(2,128)(2,1)} %reshape.555), calls=%async_computation.2 | async-start | bytes 2097152 | tf_op jit(solution)/shard_map/all_to_all | solution.py:192
  341.0 18.0 %all-to-all-start.3 = ((bf16[256,32,64]{0,2,1:T(8,128)(2,1)}), bf16[256,32,64]{0,2,1:T(8,128)(2,1)S(1)}, u32[]{:S(2)}, u32[]{:S(2)}) async-start(bf16[256,32,64]{0,2,1:T(8,128)(2,1)} %bitcast.355), calls=%async_computation.3 | async-start | bytes 2097152 | tf_op jit(solution)/shard_map/all_to_all | solution.py:203
  344.5 164.0 %reduce-scatter.8.cloned.1.call-start = ((), (), s32[]{:S(2)}) async-start(), calls=%async_computation.13 | async-start | bytes 655360 | tf_op jit(solution)/shard_map/reduce_scatter | solution.py:221
  479.1 19.0 %all-to-all-start.4 = ((bf16[4,2,65536]{2,1,0:T(2,128)(2,1)}), bf16[4,2,65536]{2,1,0:T(2,128)(2,1)}, u32[]{:S(2)}, u32[]{:S(2)}) async-start(bf16[4,2,65536]{2,1,0:T(2,128)(2,1)} %reshape.557), calls=%async_computation.4 | async-start | bytes 2097152 | tf_op jit(solution)/shard_map/all_to_all | solution.py:214
  523.8 8.2 collective-permute-start.1
  527.3 16.7 %all-to-all-start.5 = ((bf16[4,256,8]{1,2,0:T(8,128)(2,1)}), bf16[4,256,8]{1,2,0:T(8,128)(2,1)S(1)}, u32[]{:S(2)}, u32[]{:S(2)}) async-start(bf16[4,256,8]{1,2,0:T(8,128)(2,1)} %get-tuple-element.659), calls=%async_computation.6 | async-start | bytes 32768 | tf_op jit(solution)/shard_map/all_to_all | solution.py:217
  530.6 328.2 %reduce-scatter.10.cloned.1.call-start = ((), (), s32[]{:S(2)}) async-start(), calls=%async_computation.14 | async-start | bytes 20201472 | tf_op jit(solution)/shard_map/reduce_scatter | solution.py:117
  554.5 456.4 %reduce-scatter.12.cloned.1.call-start = ((), (), s32[]{:S(2)}) async-start(), calls=%async_computation.18 | async-start | bytes 9437184 | tf_op jit(solution)/shard_map/reduce_scatter | solution.py:118
  560.8 477.6 %reduce-scatter.16.cloned.1.call-start = ((), (), s32[]{:S(2)}) async-start(), calls=%async_computation.20 | async-start | bytes 1402880
  861.6 235.3 %reduce-scatter.14.cloned.1.call-start = ((), (), s32[]{:S(2)}) async-start(), calls=%async_computation.19 | async-start | bytes 655360 | tf_op jit(solution)/shard_map/reduce_scatter | solution.py:127
  1013.1 111.5 %all-gather.10.cloned.1.call-start = ((), (), s32[]{:S(2)}) async-start(), calls=%async_computation.15 | async-start | bytes 1402880 | tf_op jit(solution)/shard_map/all_gather | solution.py:275
  1041.2 86.2 %all-gather.12.cloned.1.call-start = ((), (), s32[]{:S(2)}) async-start(), calls=%async_computation.16 | async-start | bytes 1402880 | tf_op jit(solution)/shard_map/all_gather | solution.py:278
  1042.0 88.1 %all-gather.14.cloned.1.call-start = ((), (), s32[]{:S(2)}) async-start(), calls=%async_computation.17 | async-start | bytes 1402880 | tf_op jit(solution)/shard_map/all_gather | solution.py:281
  1047.6 47.2 %copy-start.20 = (bf16[1,256,1024]{2,1,0:T(8,128)(2,1)S(1)}, bf16[1,256,1024]{2,1,0:T(8,128)(2,1)}, u32[]{:S(2)}) copy-start(bf16[1,256,1024]{2,1,0:T(8,128)(2,1)} %param.17) | copy-start | bytes 1572868
  1047.6 47.2 %copy-start.23 = (bf16[1,256,1024]{2,1,0:T(8,128)(2,1)S(1)}, bf16[1,256,1024]{2,1,0:T(8,128)(2,1)}, u32[]{:S(2)}) copy-start(bf16[1,256,1024]{2,1,0:T(8,128)(2,1)} %param.18) | copy-start | bytes 1572868
  1054.6 41.6 %copy-start.26 = (f32[14688]{0:T(1024)S(1)}, f32[14688]{0:T(1024)}, u32[]{:S(2)}) copy-start(f32[14688]{0:T(1024)} %param.25) | copy-start | bytes 176260
  (60 other events, 397.8 us)
Sparse Core Ops, SparseCore 0:
  10.6 135.2 all-gather.5
  148.7 71.5 all-gather.7
  468.2 19.6 reduce-scatter.7
  554.7 304.1 reduce-scatter.9
  862.7 148.1 reduce-scatter.11
  1014.0 24.3 reduce-scatter.15
  1041.6 21.8 reduce-scatter.13
  1065.6 17.3 all-gather.9
  1084.5 17.2 all-gather.11
  1103.8 17.5 all-gather.13
where the time goes:
time: 1150 us; the launch traced here: 1140 us
  waiting for transfers between devices  647 us (56%)
  local copies, waits for them, and re-layouts  146 us (13%)
  matrix products  128 us (11%)
  other arithmetic  97.5 us (8%)
  blocking collectives  79.4 us (7%)
  starting transfers between devices  25.5 us (2%)
  between operations  15.3 us (1%)
    reduce_scatter x1, waiting for transfers between devices, rows_sum(): lax.psum_scatter(grad_pair[0], 'wshard', scatter_dimension=0, tiled=True)  298 us
    reduce_scatter x1, waiting for transfers between devices, rows_sum(): lax.psum_scatter(grad_pair[1], 'wshard', scatter_dimension=0, tiled=True)  149 us
    all_gather x1, waiting for transfers between devices, shards(): lax.all_gather(in_weight.astype(jnp.bfloat16), 'wshard', axis=0, tiled=True)  134 us
    dynamic_update_slice x8, local copies, waits for them, and re-layouts, state_scan(): last_state, outputs = lax.scan(jax.checkpoint(advance), initial, pieces)  51.4 us
    dot_general x12, matrix products, advance(): within = jnp.einsum('hij,jhp->ihp', decay_mat, x_block, precision=precise)  43.3 us
    psum x1, blocking collectives, shards(): vec_total = lax.psum(vec_grad, ('seq', 'wshard'))  40 us
    another operation x31, other arithmetic  29.6 us
    unnamed x11, waiting for transfers between devices  26 us
  transfers between devices with their start and end apart: 18, of which 7 were waited for; matrix products, arithmetic and copies ran while one was open for 19% of the time, Pallas kernels for 0%

commit v1 on v0

v1 whole, which is shorter than its diff:
```python
import jax
import jax.numpy as jnp
from jax import lax
from jax.sharding import PartitionSpec as P

D = 1024
HEADS = 32
HEADDIM = 64
STATE = 128
WIDTH = 4
BLOCK = 256
STEP = 10
DI = 2048
CONVCH = 2304


precise = lax.Precision.HIGHEST
norm_eps = 1e-05
beta_one = 0.9
beta_two = 0.95
adam_eps = 1e-08
matrix_rate = 0.05
matrix_decay = 0.1
vector_rate = 0.5


def rms_scale(values):
    return values * lax.rsqrt(jnp.mean(values * values, axis=-1, keepdims=True) + norm_eps)


def split_vector(vector):
    extents = [D, DI, WIDTH * CONVCH, CONVCH, HEADS, HEADS, HEADS]
    pieces = []
    offset = 0
    for extent in extents:
        pieces.append(vector[offset : offset + extent])
        offset = offset + extent
    pieces[2] = pieces[2].reshape(WIDTH, CONVCH)
    return pieces


def convolve(extended, kernel, conv_bias):
    rows_out = extended.shape[0] - kernel.shape[0] + 1
    summed = jnp.broadcast_to(conv_bias[None, :], (rows_out, kernel.shape[1]))
    for offset in range(kernel.shape[0]):
        summed = summed + kernel[offset][None, :] * extended[offset : offset + rows_out]
    return jax.nn.silu(summed)


def state_scan(inputs_x, step_size, a_log, b_rows, c_rows, d_skip):
    length, head_count, head_width = inputs_x.shape
    blocks = length // BLOCK
    log_decay = step_size * (-jnp.exp(a_log))[None, :]
    weighted = inputs_x * step_size[:, :, None]
    causal = jnp.tril(jnp.ones((BLOCK, BLOCK), jnp.float32))
    lower = causal > 0.5

    def advance(carry_state, pieces):
        x_block, r_block, b_block, c_block = pieces
        cumulative = jnp.cumsum(r_block.T, axis=1)
        differ = (cumulative[:, :, None] - cumulative[:, None, :]) * causal[None]
        scores = jnp.dot(c_block, b_block.T, precision=precise)
        decay_mat = jnp.where(lower[None], jnp.exp(differ), 0.0) * scores[None]
        within = jnp.einsum("hij,jhp->ihp", decay_mat, x_block, precision=precise)
        carried = jnp.einsum("in,hpn->ihp", c_block, carry_state, precision=precise)
        carried = carried * jnp.exp(cumulative.T)[:, :, None]
        to_end = jnp.exp(cumulative[:, -1:] - cumulative)
        fresh = jnp.einsum(
            "jn,jhp->hpn", b_block, x_block * to_end.T[:, :, None], precision=precise
        )
        carry_state = carry_state * jnp.exp(cumulative[:, -1])[:, None, None] + fresh
        return (carry_state, within + carried)

    initial = jnp.zeros((head_count, head_width, b_rows.shape[1]), jnp.float32)
    pieces = (
        weighted.reshape(blocks, BLOCK, head_count, head_width),
        log_decay.reshape(blocks, BLOCK, head_count),
        b_rows.reshape(blocks, BLOCK, b_rows.shape[1]),
        c_rows.reshape(blocks, BLOCK, c_rows.shape[1]),
    )
    last_state, outputs = lax.scan(jax.checkpoint(advance), initial, pieces)
    return outputs.reshape(length, head_count, head_width) + d_skip[None, :, None] * inputs_x


def head_mixer(inputs_x, dt_part, both_rows, decay_part, bias_part, skip_part):
    step_size = jax.nn.softplus(dt_part + bias_part[None, :])
    return state_scan(
        inputs_x, step_size, decay_part, both_rows[:, :STATE], both_rows[:, STATE:], skip_part
    )


def adamw_step(weight, first, second, grad, rate, decay):
    first_new = beta_one * first + (1.0 - beta_one) * grad
    second_new = beta_two * second + (1.0 - beta_two) * grad * grad
    fix_one = 1.0 - beta_one**STEP
    fix_two = 1.0 - beta_two**STEP
    normalized = first_new / fix_one / (jnp.sqrt(second_new / fix_two) + adam_eps)
    return (first_new, second_new, weight - rate * (normalized + decay * weight))


def pick_heads(values, axis, width, index, groups):
    shape = values.shape
    split = shape[:axis] + (HEADS // groups, groups, width) + shape[axis + 1 :]
    taken = lax.dynamic_index_in_dim(values.reshape(split), index, axis + 1, keepdims=False)
    return taken.reshape(shape[:axis] + (HEADS // groups * width,) + shape[axis + 1 :])


def merge_heads(stacked, axis, width):
    groups = stacked.shape[0]
    shape = stacked.shape[1:]
    split = (groups,) + shape[:axis] + (HEADS // groups, width) + shape[axis + 1 :]
    moved = jnp.moveaxis(stacked.reshape(split), 0, axis + 1)
    return moved.reshape(shape[:axis] + (HEADS * width,) + shape[axis + 1 :])


def seq_sum_rows(partial):
    return lax.psum_scatter(
        partial.astype(jnp.bfloat16), "seq", scatter_dimension=0, tiled=True
    ).astype(jnp.float32)


def gather_out(out_low, seq_index, groups):
    rows = out_low.shape[0]
    if rows % (groups * HEADDIM) == 0:
        mine = pick_rows(out_low, seq_index, groups)
        return lax.all_gather(mine, "wshard", axis=0, tiled=True)
    whole = lax.all_gather(out_low, "wshard", axis=0, tiled=True)
    return pick_heads(whole, 0, HEADDIM, seq_index, groups)


def pick_rows(values, seq_index, groups):
    rows = values.shape[0]
    split = values.reshape(rows // (groups * HEADDIM), groups, HEADDIM, values.shape[1])
    return lax.dynamic_index_in_dim(split, seq_index, 1, keepdims=False).reshape(
        rows // groups, values.shape[1]
    )


def sum_out_grad(grad, rows, seq_index, groups):
    grad = grad.astype(jnp.bfloat16)
    if rows % (groups * HEADDIM) == 0:
        mine = lax.psum_scatter(grad, "wshard", scatter_dimension=0, tiled=True)
        every = lax.all_gather(mine, "seq", axis=0, tiled=False)
        split = every.reshape(groups, rows // (groups * HEADDIM), HEADDIM, grad.shape[1])
        return jnp.moveaxis(split, 0, 1).reshape(rows, grad.shape[1]).astype(jnp.float32)
    blocks = grad.reshape(HEADS // groups, 1, HEADDIM, grad.shape[1])
    here = (jnp.arange(groups) == seq_index)[None, :, None, None]
    spread = jnp.where(here, blocks, jnp.zeros((), jnp.bfloat16)).reshape(DI, grad.shape[1])
    mine = lax.psum_scatter(spread, "wshard", scatter_dimension=0, tiled=True)
    return lax.psum(mine.astype(jnp.float32), "seq")


def shards(
    block_in,
    cotangent,
    in_weight,
    in_first,
    in_second,
    out_weight,
    out_first,
    out_second,
    vec_weight,
    vec_first,
    vec_second,
):
    rows_here = block_in.shape[1]
    groups = lax.axis_size("seq")
    seq_index = lax.axis_index("seq")
    local_heads = HEADS // groups
    local_di = DI // groups
    hidden_rows = block_in.reshape(rows_here, D)
    cot_rows = cotangent.reshape(rows_here, D)
    gain_one, gain_two, kernel, conv_bias, a_log, dt_bias, d_skip = split_vector(vec_weight)

    def heads_of(values, axis, width):
        return pick_heads(values, axis, width, seq_index, groups)

    in_low = in_weight.astype(jnp.bfloat16)
    in_mine = jnp.concatenate(
        [
            heads_of(in_low[:, :DI], 1, HEADDIM),
            heads_of(in_low[:, DI : 2 * DI], 1, HEADDIM),
            in_low[:, 2 * DI : 2 * DI + 2 * STATE],
            heads_of(in_low[:, DI + CONVCH :], 1, 1),
        ],
        1,
    )
    hidden_low = lax.all_gather(hidden_rows, "seq", axis=0, tiled=True)
    in_mine = lax.all_gather(in_mine, "wshard", axis=0, tiled=True)
    cot = lax.all_gather(cot_rows, "seq", axis=0, tiled=True)
    out_mine = gather_out(out_weight.astype(jnp.bfloat16), seq_index, groups)
    length = hidden_low.shape[0]
    my_gain_two = heads_of(gain_two, 0, HEADDIM)
    my_kernel = jnp.concatenate([heads_of(kernel[:, :DI], 1, HEADDIM), kernel[:, DI:]], 1)
    my_bias = jnp.concatenate([heads_of(conv_bias[:DI], 0, HEADDIM), conv_bias[DI:]], 0)

    hidden = hidden_low.astype(jnp.float32)
    unit = rms_scale(hidden)
    normed_low = (unit * gain_one[None, :]).astype(jnp.bfloat16)
    projected = jnp.dot(normed_low, in_mine, preferred_element_type=jnp.float32)
    gating = projected[:, :local_di]
    conv_in = projected[:, local_di : 2 * local_di + 2 * STATE]
    dt_low = projected[:, 2 * local_di + 2 * STATE :].astype(jnp.bfloat16)
    padding = jnp.zeros((WIDTH - 1, conv_in.shape[1]), jnp.float32)
    conv_out, conv_pullback = jax.vjp(
        convolve, jnp.concatenate([padding, conv_in], 0), my_kernel, my_bias
    )
    conv_low = conv_out.astype(jnp.bfloat16).astype(jnp.float32)
    scanned, scan_pullback = jax.vjp(
        head_mixer,
        conv_low[:, :local_di].reshape(length, local_heads, HEADDIM),
        dt_low.astype(jnp.float32),
        conv_low[:, local_di:],
        heads_of(a_log, 0, 1),
        heads_of(dt_bias, 0, 1),
        heads_of(d_skip, 0, 1),
    )
    mixed = scanned.astype(jnp.bfloat16).reshape(length, local_di).astype(jnp.float32)
    gate, gate_pullback = jax.vjp(jax.nn.silu, gating)
    gated = mixed * gate
    d_gnorm = jnp.dot(cot, out_mine.T, preferred_element_type=jnp.float32)
    d_unit = d_gnorm * my_gain_two[None, :]
    sums = jnp.stack([jnp.sum(gated * gated, axis=1), jnp.sum(d_unit * gated, axis=1)])
    sums = jnp.sum(lax.all_gather(sums, "seq", axis=0, tiled=False), axis=0) / DI
    scale = lax.rsqrt(sums[0] + norm_eps)[:, None]
    unit_two = gated * scale
    gnorm_low = (unit_two * my_gain_two[None, :]).astype(jnp.bfloat16)
    block_part = jnp.dot(gnorm_low, out_mine, preferred_element_type=jnp.float32)
    block_out = hidden_rows.astype(jnp.float32) + seq_sum_rows(block_part)
    grad_out = jnp.dot(gnorm_low.T, cot, preferred_element_type=jnp.float32)
    d_gain_two = jnp.sum(d_gnorm * unit_two, axis=0)
    d_gated = scale * d_unit - unit_two * (scale * scale * sums[1][:, None])
    (d_gating,) = gate_pullback(d_gated * mixed)
    d_scanned = (d_gated * gate).astype(jnp.bfloat16).astype(jnp.float32)
    d_inner, d_dt, d_both, d_a_log, d_dt_bias, d_skip_part = scan_pullback(
        d_scanned.reshape(length, local_heads, HEADDIM)
    )
    d_conv_out = jnp.concatenate([d_inner.reshape(length, local_di), d_both], 1)
    d_extended, d_kernel, d_conv_bias = conv_pullback(d_conv_out)
    d_projected = jnp.concatenate([d_gating, d_extended[WIDTH - 1 :], d_dt], 1).astype(
        jnp.bfloat16
    )
    d_normed_part = jnp.dot(d_projected, in_mine.T, preferred_element_type=jnp.float32)
    grad_in = jnp.dot(normed_low.T, d_projected, preferred_element_type=jnp.float32)
    d_gain_one = jnp.sum(d_normed_part * unit, axis=0)
    d_normed = seq_sum_rows(d_normed_part)
    own_hidden = hidden_rows.astype(jnp.float32)
    own_scale = lax.rsqrt(jnp.mean(own_hidden * own_hidden, axis=-1, keepdims=True) + norm_eps)
    own_unit = own_hidden * own_scale
    d_own = d_normed * gain_one[None, :]
    d_hidden = own_scale * (
        d_own - own_unit * jnp.mean(d_own * own_unit, axis=-1, keepdims=True)
    )
    block_grad = cot_rows.astype(jnp.float32) + d_hidden

    def spread_heads(values, axis, width):
        here = (jnp.arange(groups) == seq_index).reshape((groups,) + (1,) * values.ndim)
        return merge_heads(jnp.where(here, values[None], 0.0), axis, width)

    vec_grad = jnp.concatenate(
        [
            d_gain_one,
            spread_heads(d_gain_two, 0, HEADDIM),
            jnp.concatenate(
                [spread_heads(d_kernel[:, :local_di], 1, HEADDIM), d_kernel[:, local_di:]], 1
            ).reshape(-1),
            spread_heads(d_conv_bias[:local_di], 0, HEADDIM),
            d_conv_bias[local_di:],
            spread_heads(d_a_log, 0, 1),
            spread_heads(d_dt_bias, 0, 1),
            spread_heads(d_skip_part, 0, 1),
        ]
    )
    vec_total = lax.psum(vec_grad, ("seq", "wshard"))
    vec_first_new, vec_second_new, vec_weight_new = adamw_step(
        vec_weight, vec_first, vec_second, vec_total, vector_rate, 0.0
    )
    out_total = sum_out_grad(grad_out, out_weight.shape[0], seq_index, groups)
    in_part = lax.psum_scatter(
        grad_in.astype(jnp.bfloat16), "wshard", scatter_dimension=0, tiled=True
    )
    in_every = lax.all_gather(in_part, "seq", axis=0, tiled=False)
    both_end = 2 * local_di + 2 * STATE
    in_total = jnp.concatenate(
        [
            merge_heads(in_every[:, :, :local_di], 1, HEADDIM),
            merge_heads(in_every[:, :, local_di : 2 * local_di], 1, HEADDIM),
            jnp.sum(in_every[:, :, 2 * local_di : both_end].astype(jnp.float32), axis=0).astype(
                jnp.bfloat16
            ),
            merge_heads(in_every[:, :, both_end:], 1, 1),
        ],
        1,
    ).astype(jnp.float32)
    in_first_new, in_second_new, in_weight_new = adamw_step(
        in_weight, in_first, in_second, in_total, matrix_rate, matrix_decay
    )
    out_first_new, out_second_new, out_weight_new = adamw_step(
        out_weight, out_first, out_second, out_total, matrix_rate, matrix_decay
    )
    return (
        block_out.reshape(1, rows_here, D),
        block_grad.reshape(1, rows_here, D),
        in_first_new,
        in_second_new,
        in_weight_new,
        out_first_new,
        out_second_new,
        out_weight_new,
        vec_first_new,
        vec_second_new,
        vec_weight_new,
    )


def solution(mesh):
    return jax.shard_map(
        shards,
        mesh=mesh,
        in_specs=(
            P("wshard", "seq", None),
            P("wshard", "seq", None),
            P("wshard", None),
            P("wshard", None),
            P("wshard", None),
            P("wshard", None),
            P("wshard", None),
            P("wshard", None),
            P(),
            P(),
            P(),
        ),
        out_specs=(
            P("wshard", "seq", None),
            P("wshard", "seq", None),
            P("wshard", None),
            P("wshard", None),
            P("wshard", None),
            P("wshard", None),
            P("wshard", None),
            P("wshard", None),
            P(),
            P(),
            P(),
        ),
        check_vma=False,
    )
```

time: 1150 us -> 670 us (0.58)
  waiting for transfers between devices: 647 us -> 226 us
  local copies, waits for them, and re-layouts: 146 us -> 177 us
  blocking collectives: 79.4 us -> 53.1 us
  starting transfers between devices: 25.5 us -> 0.58 us
  other arithmetic: 97.5 us -> 76.4 us
  matrix products: 128 us -> 112 us
    reduce_scatter x4 -> x3, waiting for transfers between devices: 447 us -> 79.3 us  [the longest x2 55.7 us: seq_sum_rows(): lax.psum_scatter(partial.astype(jnp.bfloat16), 'seq', scatter_dimension=0...]
    dynamic_update_slice x8 -> x16, local copies, waits for them, and re-layouts: 51.4 us -> 103 us  [state_scan(): last_state, outputs = lax.scan(jax.checkpoint(advance), initial, pieces)]
    all_to_all x6 -> x0, waiting for transfers between devices: 40.3 us -> none  [the longest x1 14.5 us: shards(): lax.all_to_all(scanned.astype(jnp.bfloat16), 'seq', split_axis=0, concat_...]
    all_gather x5, waiting for transfers between devices: 134 us -> 94.3 us  [the longest x1 57.6 us: shards(): in_mine = lax.all_gather(in_mine, 'wshard', axis=0, tiled=True)]
    unnamed x11 -> x10, waiting for transfers between devices: 26 us -> 52.7 us
    all_gather x4 -> x2, blocking collectives: 39.4 us -> 12.8 us  [the longest x1 7.59 us: sum_out_grad(): every = lax.all_gather(mine, 'seq', axis=0, tiled=False)]
    convert_element_type x16 -> x3, other arithmetic: 29.4 us -> 6.58 us  [the longest x1 4.76 us: shards(): conv_low = conv_out.astype(jnp.bfloat16).astype(jnp.float32)]
    all_to_all x6 -> x0, starting transfers between devices: 22.6 us -> none  [the longest x1 4.47 us: shards(): lax.all_to_all(scanned.astype(jnp.bfloat16), 'seq', split_axis=0, concat_...]
  transfers between devices with their start and end apart: 18 -> 9, of which waited for: 7 -> 7; matrix products, arithmetic and copies ran while one was open for 19% -> 23% of each run, Pallas kernels for 0% -> 0%
where the time goes in v1:
time: 670 us; the launch traced here: 662 us
  waiting for transfers between devices  226 us (34%)
  local copies, waits for them, and re-layouts  177 us (26%)
  matrix products  112 us (17%)
  other arithmetic  76.4 us (11%)
  blocking collectives  53.1 us (8%)
  between operations  14.9 us (2%)
    dynamic_update_slice x16, local copies, waits for them, and re-layouts, state_scan(): last_state, outputs = lax.scan(jax.checkpoint(advance), initial, pieces)  103 us
    all_gather x1, waiting for transfers between devices, shards(): in_mine = lax.all_gather(in_mine, 'wshard', axis=0, tiled=True)  57.6 us
    reduce_scatter x2, waiting for transfers between devices, seq_sum_rows(): lax.psum_scatter(partial.astype(jnp.bfloat16), 'seq', scatter_dimension=0...  55.7 us
    unnamed x10, waiting for transfers between devices  52.7 us
    psum x1, blocking collectives, shards(): vec_total = lax.psum(vec_grad, ('seq', 'wshard'))  40.3 us
    dot_general x12, matrix products, advance(): within = jnp.einsum('hij,jhp->ihp', decay_mat, x_block, precision=precise)  37.6 us
    unnamed x99, local copies, waits for them, and re-layouts  25.5 us
    reduce_scatter x1, waiting for transfers between devices, sum_out_grad(): mine = lax.psum_scatter(grad, 'wshard', scatter_dimension=0, tiled=True)  23.5 us
  transfers between devices with their start and end apart: 9, of which 7 were waited for; matrix products, arithmetic and copies ran while one was open for 23% of the time, Pallas kernels for 0%

profile of v1, /device:TPU:0, one launch (start us, length us, event | category | flops | bytes accessed | tf_op | source)
XLA Modules:
  0.0 661.9 jit_solution(3020382418029992963)
XLA Ops:
  15.9 19.0 %all-gather.15.cloned.1.call-done = bf16[1,1024,1024]{2,1,0:T(8,128)(2,1)} async-done(((bf16[1,256,1024]{2,1,0:T(8,128)(2,1)}), bf16[1,1024,1024]{2,1,0:T(8,128)(2,1)}) %all-gather.15.cloned.1.call-update) | async-done | bytes 2097168 | tf_op jit(solution)/shard_map/all_gather | solution.py:188
  37.0 57.6 %all-gather.13.cloned.1.call-done = bf16[1024,1288]{0,1:T(8,128)(2,1)} async-done(((bf16[128,1288]{0,1:T(8,128)(2,1)}), bf16[1024,1288]{0,1:T(8,128)(2,1)}) %all-gather.13.cloned.1.call-update) | async-done | bytes 2637840 | tf_op jit(solution)/shard_map/all_gather | solution.py:189
  94.6 5.4 fusion.136
  102.4 4.8 fusion.116
  120.0 91.6 %while.39 = (s32[]{:T(128)}, f32[8,64,128]{2,1,0:T(8,128)S(1)}, f32[4,256,8,64]{1,0,3,2:T(4,128)}, f32[4,8,64,128]{3,2,1,0:T(8,128)}, f32[4,256,8]{1,2,0:T(8,128...) while((s32[]{:T(128)}, f32[8,64,128]{2,1,0:T(8,128)S(1)}, ...), condition=%wide.region_4.5_spmd.clone, body=%wide.region_1.4_spmd.clone.sunk | while | flops 909182976 | bytes 7777604 | solution.py:81
  122.5 3.5 fusion.230
  130.6 12.3 %dynamic_update_slice.67 = f32[4,256,8,64]{1,0,3,2:T(4,128)} dynamic-update-slice(f32[4,256,8,64]{1,0,3,2:T(4,128)} %get-tuple-element.905, f32[1,256,8,64]{1,0,3,2:T(1,128)S(1)} %copy.155, s32[]{:T(128)S(6)} %copy.170, s32[]{:T(128)} %constant.184.clone.1..sunk, s32[]{:T(128)} %constant.184.clone.1..sunk, s32[]{:T(128)} %constant.184.clone.1..sunk) | dynamic-update-slice | bytes 1048580 | tf_op jit(solution)/shard_map/jvp()/while/body/jit(dynamic_update_index_in_dim)/dynamic_update_slice | solution.py:81
  153.5 12.3 %dynamic_update_slice.67 = f32[4,256,8,64]{1,0,3,2:T(4,128)} dynamic-update-slice(f32[4,256,8,64]{1,0,3,2:T(4,128)} %get-tuple-element.905, f32[1,256,8,64]{1,0,3,2:T(1,128)S(1)} %copy.155, s32[]{:T(128)S(6)} %copy.170, s32[]{:T(128)} %constant.184.clone.1..sunk, s32[]{:T(128)} %constant.184.clone.1..sunk, s32[]{:T(128)} %constant.184.clone.1..sunk) | dynamic-update-slice | bytes 1048580 | tf_op jit(solution)/shard_map/jvp()/while/body/jit(dynamic_update_index_in_dim)/dynamic_update_slice | solution.py:81
  168.3 3.5 fusion.230
  176.4 12.3 %dynamic_update_slice.67 = f32[4,256,8,64]{1,0,3,2:T(4,128)} dynamic-update-slice(f32[4,256,8,64]{1,0,3,2:T(4,128)} %get-tuple-element.905, f32[1,256,8,64]{1,0,3,2:T(1,128)S(1)} %copy.155, s32[]{:T(128)S(6)} %copy.170, s32[]{:T(128)} %constant.184.clone.1..sunk, s32[]{:T(128)} %constant.184.clone.1..sunk, s32[]{:T(128)} %constant.184.clone.1..sunk) | dynamic-update-slice | bytes 1048580 | tf_op jit(solution)/shard_map/jvp()/while/body/jit(dynamic_update_index_in_dim)/dynamic_update_slice | solution.py:81
  191.2 3.5 fusion.230
  199.2 12.3 %dynamic_update_slice.67 = f32[4,256,8,64]{1,0,3,2:T(4,128)} dynamic-update-slice(f32[4,256,8,64]{1,0,3,2:T(4,128)} %get-tuple-element.905, f32[1,256,8,64]{1,0,3,2:T(1,128)S(1)} %copy.155, s32[]{:T(128)S(6)} %copy.170, s32[]{:T(128)} %constant.184.clone.1..sunk, s32[]{:T(128)} %constant.184.clone.1..sunk, s32[]{:T(128)} %constant.184.clone.1..sunk) | dynamic-update-slice | bytes 1048580 | tf_op jit(solution)/shard_map/jvp()/while/body/jit(dynamic_update_index_in_dim)/dynamic_update_slice | solution.py:81
  215.1 6.6 multiply_reduce_fusion.10
  221.8 5.2 all-gather.6
  227.0 5.8 multiply_reduce_fusion.7
  239.9 142.5 %while.40 = (s32[]{:T(128)}, f32[8,64,128]{2,1,0:T(8,128)S(1)}, f32[4,256,8,64]{1,0,3,2:T(4,128)}, f32[4,256,8]{1,2,0:T(8,128)}, f32[4,256,128]{2,1,0:T(8,128)},...) while((s32[]{:T(128)}, f32[8,64,128]{2,1,0:T(8,128)S(1)}, ...), condition=%wide.region_22.23_spmd.clone, body=%wide.region_10.22_spmd.clone.sunk | while | flops 2124171264 | bytes 20236004 | solution.py:81
  263.5 12.3 %dynamic_update_slice.71 = f32[4,256,8,64]{1,0,3,2:T(4,128)} dynamic-update-slice(f32[4,256,8,64]{1,0,3,2:T(4,128)} %get-tuple-element.945, f32[1,256,8,64]{1,0,3,2:T(1,128)S(1)} %copy.159, s32[]{:T(128)S(6)} %sub.274, s32[]{:T(128)} %constant.184.clone.1..sunk.1, s32[]{:T(128)} %constant.184.clone.1..sunk.1, s32[]{:T(128)} %constant.184.clone.1..sunk.1) | dynamic-update-slice | bytes 1048580 | tf_op jit(solution)/shard_map/transpose(jvp())/while/body/jit(dynamic_update_index_in_dim)/dynamic_update_slice | solution.py:81
  299.0 12.3 %dynamic_update_slice.71 = f32[4,256,8,64]{1,0,3,2:T(4,128)} dynamic-update-slice(f32[4,256,8,64]{1,0,3,2:T(4,128)} %get-tuple-element.945, f32[1,256,8,64]{1,0,3,2:T(1,128)S(1)} %copy.159, s32[]{:T(128)S(6)} %sub.274, s32[]{:T(128)} %constant.184.clone.1..sunk.1, s32[]{:T(128)} %constant.184.clone.1..sunk.1, s32[]{:T(128)} %constant.184.clone.1..sunk.1) | dynamic-update-slice | bytes 1048580 | tf_op jit(solution)/shard_map/transpose(jvp())/while/body/jit(dynamic_update_index_in_dim)/dynamic_update_slice | solution.py:81
  334.5 12.3 %dynamic_update_slice.71 = f32[4,256,8,64]{1,0,3,2:T(4,128)} dynamic-update-slice(f32[4,256,8,64]{1,0,3,2:T(4,128)} %get-tuple-element.945, f32[1,256,8,64]{1,0,3,2:T(1,128)S(1)} %copy.159, s32[]{:T(128)S(6)} %sub.274, s32[]{:T(128)} %constant.184.clone.1..sunk.1, s32[]{:T(128)} %constant.184.clone.1..sunk.1, s32[]{:T(128)} %constant.184.clone.1..sunk.1) | dynamic-update-slice | bytes 1048580 | tf_op jit(solution)/shard_map/transpose(jvp())/while/body/jit(dynamic_update_index_in_dim)/dynamic_update_slice | solution.py:81
  370.0 12.3 %dynamic_update_slice.71 = f32[4,256,8,64]{1,0,3,2:T(4,128)} dynamic-update-slice(f32[4,256,8,64]{1,0,3,2:T(4,128)} %get-tuple-element.945, f32[1,256,8,64]{1,0,3,2:T(1,128)S(1)} %copy.159, s32[]{:T(128)S(6)} %sub.274, s32[]{:T(128)} %constant.184.clone.1..sunk.1, s32[]{:T(128)} %constant.184.clone.1..sunk.1, s32[]{:T(128)} %constant.184.clone.1..sunk.1) | dynamic-update-slice | bytes 1048580 | tf_op jit(solution)/shard_map/transpose(jvp())/while/body/jit(dynamic_update_index_in_dim)/dynamic_update_slice | solution.py:81
  394.2 5.5 multiply_reduce_fusion.5
  412.7 4.0 fusion.117
  417.0 7.6 %fusion.99 = (f32[1024]{0:T(1024)S(1)}, bf16[1024,1024]{1,0:T(8,128)(2,1)}) fusion(bf16[1,1024,1024]{2,1,0:T(8,128)(2,1)S(1)} %copy-done.18, f32[1024]{0:T(1024)S(1)} %copy-done.42, bf16[1024,1288]{0,1:T(8,128)(2,1)} %all-gather.13.cloned.1.call-done, bf16[1024,8]{0,1:T(8,128)(2,1)S(1)} %get-tuple-element.649, bf16[1024,768]{0,1:T(8,128)(2,1)} %copy-done.19, ...), kind=kOutput, calls=%fused_computation.131 | convolution fusion | flops 2714287104 | bytes 9478144 | tf_op jit(solution)/shard_map/dot_general | solution.py:243
  424.6 3.8 convolution_convert_fusion.1
  431.0 51.4 %reduce-scatter.13.cloned.1.call-done = bf16[128,1288]{1,0:T(8,128)(2,1)} async-done(((bf16[1024,1288]{1,0:T(8,128)(2,1)}), bf16[128,1288]{1,0:T(8,128)(2,1)}) %reduce-scatter.13.cloned.1.call-update) | async-done | bytes 329744
  484.4 40.3 %psum.7 = f32[14688]{0:T(1024)S(1)} all-reduce(f32[14688]{0:T(1024)S(1)} %concatenate.36), channel_id=1, replica_groups=mesh['seq'=4,'wshard'=8] {'seq','wshard'}, use_global_device_ids=true, to_apply=%region_40.41 | all-reduce | flops 14688 | bytes 117504 | tf_op jit(solution)/shard_map/psum | solution.py:274
  525.4 23.5 %reduce-scatter.11.cloned.1.call-done = bf16[64,1024]{1,0:T(8,128)(2,1)} async-done(((bf16[512,1024]{1,0:T(8,128)(2,1)}), bf16[64,1024]{1,0:T(8,128)(2,1)}) %reduce-scatter.11.cloned.1.call-update) | async-done | bytes 131088 | tf_op jit(solution)/shard_map/reduce_scatter | solution.py:142
  548.9 7.6 %all-gather.5 = bf16[256,1024]{1,0:T(8,128)(2,1)S(1)} all-gather(bf16[64,1024]{1,0:T(8,128)(2,1)} %reduce-scatter.11.cloned.1.call-done), channel_id=7, replica_groups=mesh['seq'=4,'wshard'=8] {'seq'}, dimensions={0}, use_global_device_ids=true | all-gather | bytes 655360 | tf_op jit(solution)/shard_map/all_gather | solution.py:143
  560.1 22.6 %reduce-scatter.9.cloned.1.call-done = bf16[256,1024]{1,0:T(8,128)(2,1)} async-done(((bf16[1024,1024]{1,0:T(8,128)(2,1)}), bf16[256,1024]{1,0:T(8,128)(2,1)}) %reduce-scatter.9.cloned.1.call-update) | async-done | bytes 524304 | tf_op jit(solution)/shard_map/reduce_scatter | solution.py:117
  584.1 33.1 %reduce-scatter.7.cloned.1.call-done = bf16[256,1024]{1,0:T(8,128)(2,1)} async-done(((bf16[1024,1024]{1,0:T(8,128)(2,1)}), bf16[256,1024]{1,0:T(8,128)(2,1)}) %reduce-scatter.7.cloned.1.call-update) | async-done | bytes 524304 | tf_op jit(solution)/shard_map/reduce_scatter | solution.py:117
  620.1 17.7 %all-gather.21.cloned.1.call-done = bf16[512,1288]{0,1:T(8,128)(2,1)} async-done(((bf16[128,1288]{0,1:T(8,128)(2,1)}), bf16[512,1288]{0,1:T(8,128)(2,1)}) %all-gather.21.cloned.1.call-update) | async-done | bytes 1318928 | tf_op jit(solution)/shard_map/all_gather | solution.py:282
  642.9 12.2 %multiply_subtract_fusion = (f32[128,4384]{0,1:T(8,128)}, f32[128,4384]{0,1:T(8,128)}, f32[128,4384]{0,1:T(8,128)}) fusion(f32[128,4384]{0,1:T(8,128)S(1)} %copy-done.9, bf16[128,32]{0,1:T(8,128)(2,1)S(1)} %bitcast.378, bf16[128,256]{0,1:T(8,128)(2,1)S(1)} %slice_reduce_fusion.5, bf16[128,2048]{0,1:T(8,128)(2,1)S(1)} %bitcast.360, ...), kind=kLoop, calls=%fused_computation.159 | loop fusion | flops 12906496 | bytes 14589952 | tf_op jit(solution)/shard_map/sub | solution.py:98
  (450 shorter events, 202.8 us)
Async XLA Ops:
  7.2 27.7 %all-gather.15.cloned.1.call-start = ((), (), s32[]{:S(2)}) async-start(), calls=%async_computation.8 | async-start | bytes 2621440 | tf_op jit(solution)/shard_map/all_gather | solution.py:188
  7.9 86.7 %all-gather.13.cloned.1.call-start = ((), (), s32[]{:S(2)}) async-start(), calls=%async_computation.4 | async-start | bytes 2967552 | tf_op jit(solution)/shard_map/all_gather | solution.py:189
  9.9 5.9 slice-start
  10.7 204.4 %all-gather.17.cloned.1.call-start = ((), (), s32[]{:S(2)}) async-start(), calls=%async_computation.9 | async-start | bytes 1179648 | tf_op jit(solution)/shard_map/all_gather | solution.py:126
  11.8 203.3 %all-gather.19.cloned.1.call-start = ((), (), s32[]{:S(2)}) async-start(), calls=%async_computation.10 | async-start | bytes 2621440 | tf_op jit(solution)/shard_map/all_gather | solution.py:190
  12.4 469.9 %reduce-scatter.13.cloned.1.call-start = ((), (), s32[]{:S(2)}) async-start(), calls=%async_computation.12 | async-start | bytes 3244032
  12.5 87.5 %copy-start.32 = (f32[1024]{0:T(1024)}, f32[1024]{0:T(1024)S(1)}, u32[]{:S(2)}) copy-start(f32[1024]{0:T(1024)S(1)} %slice.210) | copy-start | bytes 12292
  14.1 100.1 %copy-start.39 = (f32[8]{0:T(128)}, f32[8]{0:T(128)S(1)}, u32[]{:S(2)}) copy-start(f32[8]{0:T(128)S(1)} %get-tuple-element.705) | copy-start | bytes 100
  14.6 99.6 %copy-start.43 = (f32[8]{0:T(128)}, f32[8]{0:T(128)S(1)}, u32[]{:S(2)}) copy-start(f32[8]{0:T(128)S(1)} %neg.39) | copy-start | bytes 100
  15.8 86.5 %copy-start.28 = (f32[768]{0:T(1024)}, f32[768]{0:T(1024)S(1)}, u32[]{:S(2)}) copy-start(f32[768]{0:T(1024)S(1)} %get-tuple-element.595) | copy-start | bytes 9220
  15.9 86.5 %copy-start.30 = (f32[768]{0:T(1024)}, f32[768]{0:T(1024)S(1)}, u32[]{:S(2)}) copy-start(f32[768]{0:T(1024)S(1)} %get-tuple-element.596) | copy-start | bytes 9220
  37.0 63.1 %copy-start.41 = (f32[1024]{0:T(1024)}, f32[1024]{0:T(1024)S(1)}, u32[]{:S(2)}) copy-start(f32[1024]{0:T(1024)S(1)} %add_rsqrt_fusion) | copy-start | bytes 12292
  102.4 4.8 copy-start.3
  211.6 3.6 copy-start.34
  211.6 3.6 copy-start.38
  394.2 5.5 copy-start.29
  394.2 5.5 copy-start.31
  401.8 3.7 copy-start.17
  401.8 3.7 copy-start.21
  401.8 3.7 copy-start.33
  401.8 3.7 copy-start.42
  411.5 137.4 %reduce-scatter.11.cloned.1.call-start = ((), (), s32[]{:S(2)}) async-start(), calls=%async_computation.7 | async-start | bytes 1179648 | tf_op jit(solution)/shard_map/reduce_scatter | solution.py:142
  412.7 4.3 copy-start.18
  416.7 165.9 %reduce-scatter.9.cloned.1.call-start = ((), (), s32[]{:S(2)}) async-start(), calls=%async_computation.6 | async-start | bytes 2621440 | tf_op jit(solution)/shard_map/reduce_scatter | solution.py:117
  424.6 192.6 %reduce-scatter.7.cloned.1.call-start = ((), (), s32[]{:S(2)}) async-start(), calls=%async_computation.5 | async-start | bytes 2621440 | tf_op jit(solution)/shard_map/reduce_scatter | solution.py:117
  428.5 96.2 %copy-start.24 = (f32[14688]{0:T(1024)S(1)}, f32[14688]{0:T(1024)}, u32[]{:S(2)}) copy-start(f32[14688]{0:T(1024)} %param.23) | copy-start | bytes 176260
  428.5 96.2 %copy-start.26 = (f32[14688]{0:T(1024)S(1)}, f32[14688]{0:T(1024)}, u32[]{:S(2)}) copy-start(f32[14688]{0:T(1024)} %param.25) | copy-start | bytes 176260
  428.5 96.2 %copy-start.27 = (f32[14688]{0:T(1024)S(1)}, f32[14688]{0:T(1024)}, u32[]{:S(2)}) copy-start(f32[14688]{0:T(1024)} %param.24) | copy-start | bytes 176260
  428.6 128.0 %copy-start.14 = (f32[256,1024]{1,0:T(8,128)S(1)}, f32[256,1024]{1,0:T(8,128)}, u32[]{:S(2)}) copy-start(f32[256,1024]{1,0:T(8,128)} %param.20) | copy-start | bytes 3145732
  428.6 128.0 %copy-start.22 = (f32[256,1024]{1,0:T(8,128)S(1)}, f32[256,1024]{1,0:T(8,128)}, u32[]{:S(2)}) copy-start(f32[256,1024]{1,0:T(8,128)} %param.22) | copy-start | bytes 3145732
  428.6 209.2 %all-gather.21.cloned.1.call-start = ((), (), s32[]{:S(2)}) async-start(), calls=%async_computation.11 | async-start | bytes 1648640 | tf_op jit(solution)/shard_map/all_gather | solution.py:282
  556.5 60.7 %copy-start.16 = (bf16[1,256,1024]{2,1,0:T(8,128)(2,1)S(1)}, bf16[1,256,1024]{2,1,0:T(8,128)(2,1)}, u32[]{:S(2)}) copy-start(bf16[1,256,1024]{2,1,0:T(8,128)(2,1)} %param.16) | copy-start | bytes 1572868
  (29 other events, 57.2 us)
Sparse Core Ops, SparseCore 0:
  9.6 25.2 all-gather.14
  37.5 57.0 all-gather.12
  97.3 38.3 all-gather.16
  137.1 21.3 all-gather.18
  411.7 70.6 reduce-scatter.12
  486.2 62.7 reduce-scatter.10
  552.2 30.4 reduce-scatter.8
  585.8 31.3 reduce-scatter.6
  619.4 18.3 all-gather.20

commit v2 on v1

--- a/solution.py
+++ b/solution.py
@@ -1,6 +1,8 @@
 import jax
 import jax.numpy as jnp
 from jax import lax
+from jax.experimental import pallas as pl
+from jax.experimental.pallas import tpu as pltpu
 from jax.sharding import PartitionSpec as P
 
 D = 1024
@@ -39,53 +41,560 @@
     return pieces
 
 
-def convolve(extended, kernel, conv_bias):
-    rows_out = extended.shape[0] - kernel.shape[0] + 1
-    summed = jnp.broadcast_to(conv_bias[None, :], (rows_out, kernel.shape[1]))
-    for offset in range(kernel.shape[0]):
-        summed = summed + kernel[offset][None, :] * extended[offset : offset + rows_out]
-    return jax.nn.silu(summed)
-
-
-def state_scan(inputs_x, step_size, a_log, b_rows, c_rows, d_skip):
-    length, head_count, head_width = inputs_x.shape
-    blocks = length // BLOCK
-    log_decay = step_size * (-jnp.exp(a_log))[None, :]
-    weighted = inputs_x * step_size[:, :, None]
-    causal = jnp.tril(jnp.ones((BLOCK, BLOCK), jnp.float32))
-    lower = causal > 0.5
-
-    def advance(carry_state, pieces):
-        x_block, r_block, b_block, c_block = pieces
-        cumulative = jnp.cumsum(r_block.T, axis=1)
-        differ = (cumulative[:, :, None] - cumulative[:, None, :]) * causal[None]
-        scores = jnp.dot(c_block, b_block.T, precision=precise)
-        decay_mat = jnp.where(lower[None], jnp.exp(differ), 0.0) * scores[None]
-        within = jnp.einsum("hij,jhp->ihp", decay_mat, x_block, precision=precise)
-        carried = jnp.einsum("in,hpn->ihp", c_block, carry_state, precision=precise)
-        carried = carried * jnp.exp(cumulative.T)[:, :, None]
-        to_end = jnp.exp(cumulative[:, -1:] - cumulative)
-        fresh = jnp.einsum(
-            "jn,jhp->hpn", b_block, x_block * to_end.T[:, :, None], precision=precise
-        )
-        carry_state = carry_state * jnp.exp(cumulative[:, -1])[:, None, None] + fresh
-        return (carry_state, within + carried)
-
-    initial = jnp.zeros((head_count, head_width, b_rows.shape[1]), jnp.float32)
-    pieces = (
-        weighted.reshape(blocks, BLOCK, head_count, head_width),
-        log_decay.reshape(blocks, BLOCK, head_count),
-        b_rows.reshape(blocks, BLOCK, b_rows.shape[1]),
-        c_rows.reshape(blocks, BLOCK, c_rows.shape[1]),
-    )
-    last_state, outputs = lax.scan(jax.checkpoint(advance), initial, pieces)
-    return outputs.reshape(length, head_count, head_width) + d_skip[None, :, None] * inputs_x
-
-
-def head_mixer(inputs_x, dt_part, both_rows, decay_part, bias_part, skip_part):
-    step_size = jax.nn.softplus(dt_part + bias_part[None, :])
-    return state_scan(
-        inputs_x, step_size, decay_part, both_rows[:, :STATE], both_rows[:, STATE:], skip_part
+def wide(extent):
+    return pl.BlockSpec((BLOCK, extent), lambda q: (q, 0))
+
+
+def wide_back(extent, count):
+    return pl.BlockSpec((BLOCK, extent), lambda q: (count - 1 - q, 0))
+
+
+def whole(*shape):
+    return pl.BlockSpec(shape, lambda q: (0,) * len(shape))
+
+
+def dot_nt(left, right, precision=None):
+    return lax.dot_general(
+        left,
+        right,
+        (((1,), (1,)), ((), ())),
+        precision=precision,
+        preferred_element_type=jnp.float32,
+    )
+
+
+def dot_tn(left, right):
+    return lax.dot_general(
+        left, right, (((0,), (0,)), ((), ())), preferred_element_type=jnp.float32
+    )
+
+
+def dot_nn(left, right, precision=None):
+    return jnp.dot(left, right, precision=precision, preferred_element_type=jnp.float32)
+
+
+def sigmoid(values):
+    return 1.0 / (1.0 + jnp.exp(-values))
+
+
+def low(values):
+    return values.astype(jnp.bfloat16)
+
+
+def lower_mask():
+    rows = lax.broadcasted_iota(jnp.int32, (BLOCK, BLOCK), 0)
+    return rows >= lax.broadcasted_iota(jnp.int32, (BLOCK, BLOCK), 1)
+
+
+def decay_sums(dt_raw, dt_bias, a_log, expand):
+    shifted = dt_raw + dt_bias
+    step = jnp.maximum(shifted, 0.0) + jnp.log1p(jnp.exp(-jnp.abs(shifted)))
+    log_decay = -jnp.exp(a_log) * step
+    ones = jnp.where(lower_mask(), 1.0, 0.0)
+    running = dot_nn(ones, log_decay, precise)
+    step_wide = dot_nn(step, expand, precise)
+    running_wide = dot_nn(running, expand, precise)
+    return shifted, step, log_decay, running, step_wide, running_wide
+
+
+def forward_kernel(
+    hidden_ref,
+    cot_ref,
+    in_ref,
+    dt_weight_ref,
+    out_ref,
+    gain_one_ref,
+    gain_two_ref,
+    conv_ref,
+    bias_ref,
+    a_log_ref,
+    dt_bias_ref,
+    skip_ref,
+    expand_ref,
+    normed_ref,
+    gating_ref,
+    conv_in_ref,
+    conv_pre_ref,
+    dt_ref,
+    y_ref,
+    scanned_ref,
+    state_ref,
+    d_gnorm_ref,
+    sums_ref,
+    ext,
+    state,
+):
+    local_di = gating_ref.shape[1]
+    heads = local_di // HEADDIM
+
+    @pl.when(pl.program_id(0) == 0)
+    def _():
+        ext[0:8, :] = jnp.zeros((8, ext.shape[1]), jnp.float32)
+        state[...] = jnp.zeros_like(state)
+
+    hidden = hidden_ref[...].astype(jnp.float32)
+    normed = low(rms_scale(hidden) * gain_one_ref[...])
+    normed_ref[...] = normed
+    projected = dot_nn(normed, in_ref[...])
+    gating = projected[:, :local_di]
+    gating_ref[...] = gating
+    conv_in = projected[:, local_di:]
+    conv_in_ref[...] = conv_in
+    ext[8 : 8 + BLOCK, :] = conv_in
+    conv_pre = bias_ref[...] + conv_ref[WIDTH - 1 : WIDTH, :] * conv_in
+    for tap in range(WIDTH - 1):
+        first = 8 - WIDTH + 1 + tap
+        conv_pre = conv_pre + conv_ref[tap : tap + 1, :] * ext[first : first + BLOCK, :]
+    conv_pre_ref[...] = conv_pre
+    ext[8 - WIDTH + 1 : 8, :] = ext[8 + BLOCK - WIDTH + 1 : 8 + BLOCK, :]
+    conv_low = low(conv_pre * sigmoid(conv_pre))
+    inner = conv_low[:, :local_di]
+    b_rows = conv_low[:, local_di : local_di + STATE]
+    c_rows = conv_low[:, local_di + STATE :]
+    dt_raw = low(dot_nn(normed, dt_weight_ref[...])).astype(jnp.float32)
+    dt_ref[...] = dt_raw
+
+    _, _, _, running, step_wide, running_wide = decay_sums(
+        dt_raw, dt_bias_ref[...], a_log_ref[...], expand_ref[...]
+    )
+    running_t = running.T
+    b_t = low(b_rows.astype(jnp.float32).T)
+    scores = dot_nn(c_rows, b_t)
+    mask = lower_mask()
+    inner_wide = inner.astype(jnp.float32)
+    stepped = step_wide * inner_wide
+    stepped_low = low(stepped)
+    first_half = lax.broadcasted_iota(jnp.int32, (BLOCK, 2 * HEADDIM), 1) < HEADDIM
+    zero = jnp.zeros((), jnp.bfloat16)
+    state_ref[...] = state[...].reshape(state_ref.shape)
+    held = state[...]
+    carried = jnp.exp(running_wide) * dot_nn(c_rows, low(held))
+    for pair in range(heads // 2):
+        span = slice(pair * 2 * HEADDIM, (pair + 1) * 2 * HEADDIM)
+        both = stepped_low[:, span]
+        total = carried[:, span]
+        for half in range(2):
+            head = 2 * pair + half
+            differ = running[:, head : head + 1] - running_t[head : head + 1, :]
+            mixed = low(jnp.exp(jnp.where(mask, differ, -jnp.inf)) * scores)
+            mine = jnp.where(first_half if half == 0 else ~first_half, both, zero)
+            total = total + dot_nn(mixed, mine)
+        y_ref[:, span] = total
+    last = running_wide[BLOCK - 1 : BLOCK, :]
+    to_end = jnp.exp(last - running_wide)
+    state[...] = jnp.exp(last) * held + dot_nn(b_t, low(to_end * stepped))
+    scanned = low(y_ref[...] + skip_ref[...] * inner_wide)
+    scanned_ref[...] = scanned
+    gated = scanned.astype(jnp.float32) * (gating * sigmoid(gating))
+    d_gnorm = dot_nt(cot_ref[...], out_ref[...])
+    d_gnorm_ref[...] = d_gnorm
+    ones = jnp.ones((8, local_di), jnp.float32)
+    squares = dot_nt(ones, gated * gated, precise)
+    products = dot_nt(ones, d_gnorm * gain_two_ref[...] * gated, precise)
+    sums_ref[...] = jnp.where(
+        lax.broadcasted_iota(jnp.int32, squares.shape, 0) == 0, squares, products
+    )
+
+
+def middle_kernel(
+    scanned_ref,
+    gating_ref,
+    d_gnorm_ref,
+    cot_ref,
+    normed_ref,
+    scale_ref,
+    slope_ref,
+    out_ref,
+    gain_two_ref,
+    block_ref,
+    d_gating_ref,
+    d_scanned_ref,
+    grad_out_ref,
+    grad_gate_ref,
+    d_gain_two_ref,
+    out_sum,
+    gate_sum,
+):
+    chunk = pl.program_id(0)
+
+    @pl.when(chunk == 0)
+    def _():
+        out_sum[...] = jnp.zeros_like(out_sum)
+        gate_sum[...] = jnp.zeros_like(gate_sum)
+        d_gain_two_ref[...] = jnp.zeros_like(d_gain_two_ref)
+
+    gating = gating_ref[...]
+    open_part = sigmoid(gating)
+    gate = gating * open_part
+    scanned = scanned_ref[...].astype(jnp.float32)
+    scale = scale_ref[:, :1]
+    unit = scanned * gate * scale
+    d_gnorm = d_gnorm_ref[...]
+    gain_two = gain_two_ref[...]
+    gnorm = low(unit * gain_two)
+    block_ref[...] = low(dot_nn(gnorm, out_ref[...]))
+    out_sum[...] += dot_tn(gnorm, cot_ref[...])
+    d_gain_two_ref[...] += jnp.sum(d_gnorm * unit, axis=0, keepdims=True)
+    d_gated = scale * (d_gnorm * gain_two) - unit * slope_ref[:, :1]
+    d_gating = low(d_gated * scanned * (open_part * (1.0 + gating * (1.0 - open_part))))
+    d_gating_ref[...] = d_gating
+    d_scanned_ref[...] = low(d_gated * gate)
+    gate_sum[...] += dot_tn(normed_ref[...], d_gating)
+
+    @pl.when(chunk == pl.num_programs(0) - 1)
+    def _():
+        grad_out_ref[...] = low(out_sum[...])
+        grad_gate_ref[...] = low(gate_sum[...])
+
+
+def backward_kernel(
+    hidden_ref,
+    normed_ref,
+    conv_in_ref,
+    conv_pre_ref,
+    dt_ref,
+    y_ref,
+    state_ref,
+    d_scanned_ref,
+    d_gating_ref,
+    in_ref,
+    dt_weight_ref,
+    conv_ref,
+    a_log_ref,
+    dt_bias_ref,
+    skip_ref,
+    expand_ref,
+    d_normed_ref,
+    grad_conv_ref,
+    grad_dt_ref,
+    d_gain_one_ref,
+    d_kernel_ref,
+    d_conv_bias_ref,
+    d_skip_ref,
+    d_head_ref,
+    ext,
+    d_state,
+    later_state,
+    conv_sum,
+    dt_sum,
+):
+    local_di = y_ref.shape[1]
+    heads = local_di // HEADDIM
+    chunk = pl.program_id(0)
+
+    @pl.when(chunk == 0)
+    def _():
+        ext[BLOCK : BLOCK + 8, :] = jnp.zeros((8, ext.shape[1]), jnp.float32)
+        d_state[...] = jnp.zeros_like(d_state)
+        later_state[...] = jnp.zeros_like(later_state)
+        conv_sum[...] = jnp.zeros_like(conv_sum)
+        dt_sum[...] = jnp.zeros_like(dt_sum)
+        d_gain_one_ref[...] = jnp.zeros_like(d_gain_one_ref)
+        d_kernel_ref[...] = jnp.zeros_like(d_kernel_ref)
+        d_conv_bias_ref[...] = jnp.zeros_like(d_conv_bias_ref)
+        d_skip_ref[...] = jnp.zeros_like(d_skip_ref)
+        d_head_ref[...] = jnp.zeros_like(d_head_ref)
+
+    expand = expand_ref[...]
+    conv_pre = conv_pre_ref[...]
+    open_part = sigmoid(conv_pre)
+    conv_low = low(conv_pre * open_part)
+    inner = conv_low[:, :local_di].astype(jnp.float32)
+    b_rows = conv_low[:, local_di : local_di + STATE]
+    c_rows = conv_low[:, local_di + STATE :]
+    a_log = a_log_ref[...]
+    shifted, _, log_decay, running, step_wide, running_wide = decay_sums(
+        dt_ref[...], dt_bias_ref[...], a_log, expand
+    )
+    running_t = running.T
+    b_t = low(b_rows.astype(jnp.float32).T)
+    c_t = low(c_rows.astype(jnp.float32).T)
+    scores = dot_nn(c_rows, b_t)
+    scores_t = dot_nn(b_rows, c_t)
+    mask = lower_mask()
+    rows = lax.broadcasted_iota(jnp.int32, (BLOCK, BLOCK), 0)
+    mask_t = rows <= lax.broadcasted_iota(jnp.int32, (BLOCK, BLOCK), 1)
+    d_y_low = d_scanned_ref[...]
+    d_y = d_y_low.astype(jnp.float32)
+    stepped_low = low(step_wide * inner)
+    stepped = stepped_low.astype(jnp.float32)
+    last = running_wide[BLOCK - 1 : BLOCK, :]
+    to_end = jnp.exp(last - running_wide)
+    d_later = d_state[...]
+    d_later_low = low(d_later)
+    held = state_ref[...].reshape(d_state.shape)
+    decayed_dy = low(jnp.exp(running_wide) * d_y)
+    d_c = dot_nt(decayed_dy, low(held))
+    d_b = dot_nt(low(to_end * stepped), d_later_low)
+    d_stepped = to_end * dot_nn(b_rows, d_later_low)
+    cross = jnp.sum(later_state[...] * d_later, axis=0, keepdims=True)
+    d_state[...] = jnp.exp(last) * d_later + dot_nn(c_t, decayed_dy)
+    later_state[...] = held
+    first_half = lax.broadcasted_iota(jnp.int32, (BLOCK, 2 * HEADDIM), 1) < HEADDIM
+    zero = jnp.zeros((), jnp.bfloat16)
+    d_scores = jnp.zeros((BLOCK, BLOCK), jnp.float32)
+    pieces = []
+    for pair in range(heads // 2):
+        span = slice(pair * 2 * HEADDIM, (pair + 1) * 2 * HEADDIM)
+        total = d_stepped[:, span]
+        for half in range(2):
+            head = 2 * pair + half
+            mine = jnp.where(first_half if half == 0 else ~first_half, d_y_low[:, span], zero)
+            column = running[:, head : head + 1]
+            row = running_t[head : head + 1, :]
+            decay = jnp.exp(jnp.where(mask, column - row, -jnp.inf))
+            decay_t = jnp.exp(jnp.where(mask_t, row - column, -jnp.inf))
+            d_scores = d_scores + dot_nt(mine, stepped_low[:, span]) * decay
+            total = total + dot_nn(low(decay_t * scores_t), mine)
+        pieces.append(total)
+    d_stepped = jnp.concatenate(pieces, 1)
+    d_scores_low = low(d_scores)
+    d_c = d_c + dot_nn(d_scores_low, b_rows)
+    d_b = d_b + dot_nn(low(d_scores.T), c_rows)
+    d_inner = step_wide * d_stepped + skip_ref[...] * d_y
+    d_running = dot_nt(d_y * y_ref[...] - d_stepped * stepped, expand, precise)
+    upper = jnp.where(mask_t, 1.0, 0.0)
+    d_log = dot_nn(upper, d_running, precise) + dot_nt(cross, expand, precise)
+    d_step = dot_nt(d_stepped * inner, expand, precise) - jnp.exp(a_log) * d_log
+    d_dt = d_step * sigmoid(shifted)
+    d_head_ref[0:1, :] += jnp.sum(d_log * log_decay, axis=0, keepdims=True)
+    d_head_ref[1:2, :] += jnp.sum(d_dt, axis=0, keepdims=True)
+    d_skip_ref[...] += jnp.sum(d_y * inner, axis=0, keepdims=True)
+
+    d_conv_out = jnp.concatenate([d_inner, d_b, d_c], 1)
+    d_pre = d_conv_out * (open_part * (1.0 + conv_pre * (1.0 - open_part)))
+    ext[0:BLOCK, :] = d_pre
+    d_conv_bias_ref[...] += jnp.sum(d_pre, axis=0, keepdims=True)
+    conv_in = conv_in_ref[...]
+    d_conv_in = jnp.zeros_like(conv_in)
+    for tap in range(WIDTH):
+        moved = ext[WIDTH - 1 - tap : WIDTH - 1 - tap + BLOCK, :]
+        d_conv_in = d_conv_in + conv_ref[tap : tap + 1, :] * moved
+        d_kernel_ref[tap : tap + 1, :] += jnp.sum(moved * conv_in, axis=0, keepdims=True)
+    ext[BLOCK : BLOCK + 8, :] = ext[0:8, :]
+    d_conv_low = low(d_conv_in)
+    d_dt_low = low(d_dt)
+    normed = normed_ref[...]
+    conv_sum[...] += dot_tn(normed, d_conv_low)
+    dt_sum[...] += dot_tn(normed, d_dt_low)
+    d_normed = dot_nt(d_gating_ref[...], in_ref[:, :local_di])
+    d_normed = d_normed + dot_nt(d_conv_low, in_ref[:, local_di:])
+    d_normed = d_normed + dot_nt(d_dt_low, dt_weight_ref[...])
+    d_normed_ref[...] = low(d_normed)
+    unit = rms_scale(hidden_ref[...].astype(jnp.float32))
+    d_gain_one_ref[...] += jnp.sum(d_normed * unit, axis=0, keepdims=True)
+
+    @pl.when(chunk == pl.num_programs(0) - 1)
+    def _():
+        grad_conv_ref[...] = low(conv_sum[...])
+        grad_dt_ref[...] = low(dt_sum[...])
+
+
+def kernel_params():
+    return pltpu.CompilerParams(
+        dimension_semantics=("arbitrary",), vmem_limit_bytes=50 * 1024 * 1024
+    )
+
+
+def run_forward(hidden, cot, in_low, dt_weight, out_low, gains, conv, heads_vectors, expand):
+    length = hidden.shape[0]
+    chunks = length // BLOCK
+    local_di = out_low.shape[0]
+    channels = in_low.shape[1] - local_di
+    lanes = dt_weight.shape[1]
+    shape = jax.ShapeDtypeStruct
+    f32, bf16 = jnp.float32, jnp.bfloat16
+    return pl.pallas_call(
+        forward_kernel,
+        grid=(chunks,),
+        in_specs=[
+            wide(D),
+            wide(D),
+            whole(D, local_di + channels),
+            whole(D, lanes),
+            whole(local_di, D),
+            whole(1, D),
+            whole(1, local_di),
+            whole(WIDTH, channels),
+            whole(1, channels),
+            whole(1, lanes),
+            whole(1, lanes),
+            whole(1, local_di),
+            whole(lanes, local_di),
+        ],
+        out_specs=[
+            wide(D),
+            wide(local_di),
+            wide(channels),
+            wide(channels),
+            wide(lanes),
+            wide(local_di),
+            wide(local_di),
+            pl.BlockSpec((1, STATE, local_di), lambda q: (q, 0, 0)),
+            wide(local_di),
+            pl.BlockSpec((8, BLOCK), lambda q: (0, q)),
+        ],
+        out_shape=[
+            shape((length, D), bf16),
+            shape((length, local_di), f32),
+            shape((length, channels), f32),
+            shape((length, channels), f32),
+            shape((length, lanes), f32),
+            shape((length, local_di), f32),
+            shape((length, local_di), bf16),
+            shape((chunks, STATE, local_di), f32),
+            shape((length, local_di), f32),
+            shape((8, length), f32),
+        ],
+        scratch_shapes=[
+            pltpu.VMEM((8 + BLOCK, channels), f32),
+            pltpu.VMEM((STATE, local_di), f32),
+        ],
+        compiler_params=kernel_params(),
+        cost_estimate=pl.CostEstimate(
+            flops=8_000_000_000, bytes_accessed=25_000_000, transcendentals=8_000_000
+        ),
+        name="forward",
+    )(hidden, cot, in_low, dt_weight, out_low, *gains, *conv, *heads_vectors, expand)
+
+
+def run_middle(scanned, gating, d_gnorm, cot, normed, scale, slope, out_low, gain_two):
+    length, local_di = scanned.shape
+    shape = jax.ShapeDtypeStruct
+    f32, bf16 = jnp.float32, jnp.bfloat16
+    return pl.pallas_call(
+        middle_kernel,
+        grid=(length // BLOCK,),
+        in_specs=[
+            wide(local_di),
+            wide(local_di),
+            wide(local_di),
+            wide(D),
+            wide(D),
+            wide(1),
+            wide(1),
+            whole(local_di, D),
+            whole(1, local_di),
+        ],
+        out_specs=[
+            wide(D),
+            wide(local_di),
+            wide(local_di),
+            whole(local_di, D),
+            whole(D, local_di),
+            whole(1, local_di),
+        ],
+        out_shape=[
+            shape((length, D), bf16),
+            shape((length, local_di), bf16),
+            shape((length, local_di), bf16),
+            shape((local_di, D), bf16),
+            shape((D, local_di), bf16),
+            shape((1, local_di), f32),
+        ],
+        scratch_shapes=[pltpu.VMEM((local_di, D), f32), pltpu.VMEM((D, local_di), f32)],
+        compiler_params=kernel_params(),
+        cost_estimate=pl.CostEstimate(
+            flops=4_000_000_000, bytes_accessed=15_000_000, transcendentals=500_000
+        ),
+        name="middle",
+    )(scanned, gating, d_gnorm, cot, normed, scale, slope, out_low, gain_two)
+
+
+def run_backward(
+    hidden,
+    normed,
+    conv_in,
+    conv_pre,
+    dt_raw,
+    y,
+    states,
+    d_scanned,
+    d_gating,
+    in_low,
+    dt_weight,
+    kernel,
+    heads_vectors,
+    expand,
+):
+    length, local_di = y.shape
+    chunks = length // BLOCK
+    channels = conv_in.shape[1]
+    lanes = dt_weight.shape[1]
+    shape = jax.ShapeDtypeStruct
+    f32, bf16 = jnp.float32, jnp.bfloat16
+
+    def back(extent):
+        return wide_back(extent, chunks)
+
+    return pl.pallas_call(
+        backward_kernel,
+        grid=(chunks,),
+        in_specs=[
+            back(D),
+            back(D),
+            back(channels),
+            back(channels),
+            back(lanes),
+            back(local_di),
+            pl.BlockSpec((1, STATE, local_di), lambda q: (chunks - 1 - q, 0, 0)),
+            back(local_di),
+            back(local_di),
+            whole(D, local_di + channels),
+            whole(D, lanes),
+            whole(WIDTH, channels),
+            whole(1, lanes),
+            whole(1, lanes),
+            whole(1, local_di),
+            whole(lanes, local_di),
+        ],
+        out_specs=[
+            back(D),
+            whole(D, channels),
+            whole(D, lanes),
+            whole(1, D),
+            whole(WIDTH, channels),
+            whole(1, channels),
+            whole(1, local_di),
+            whole(2, lanes),
+        ],
+        out_shape=[
+            shape((length, D), bf16),
+            shape((D, channels), bf16),
+            shape((D, lanes), bf16),
+            shape((1, D), f32),
+            shape((WIDTH, channels), f32),
+            shape((1, channels), f32),
+            shape((1, local_di), f32),
+            shape((2, lanes), f32),
+        ],
+        scratch_shapes=[
+            pltpu.VMEM((BLOCK + 8, channels), f32),
+            pltpu.VMEM((STATE, local_di), f32),
+            pltpu.VMEM((STATE, local_di), f32),
+            pltpu.VMEM((D, channels), f32),
+            pltpu.VMEM((D, lanes), f32),
+        ],
+        compiler_params=kernel_params(),
+        cost_estimate=pl.CostEstimate(
+            flops=16_000_000_000, bytes_accessed=25_000_000, transcendentals=10_000_000
+        ),
+        name="backward",
+    )(
+        hidden,
+        normed,
+        conv_in,
+        conv_pre,
+        dt_raw,
+        y,
+        states,
+        d_scanned,
+        d_gating,
+        in_low,
+        dt_weight,
+        kernel,
+        *heads_vectors,
+        expand,
     )
 
 
@@ -189,60 +698,95 @@
     in_mine = lax.all_gather(in_mine, "wshard", axis=0, tiled=True)
     cot = lax.all_gather(cot_rows, "seq", axis=0, tiled=True)
     out_mine = gather_out(out_weight.astype(jnp.bfloat16), seq_index, groups)
-    length = hidden_low.shape[0]
     my_gain_two = heads_of(gain_two, 0, HEADDIM)
     my_kernel = jnp.concatenate([heads_of(kernel[:, :DI], 1, HEADDIM), kernel[:, DI:]], 1)
     my_bias = jnp.concatenate([heads_of(conv_bias[:DI], 0, HEADDIM), conv_bias[DI:]], 0)
 
-    hidden = hidden_low.astype(jnp.float32)
-    unit = rms_scale(hidden)
-    normed_low = (unit * gain_one[None, :]).astype(jnp.bfloat16)
-    projected = jnp.dot(normed_low, in_mine, preferred_element_type=jnp.float32)
-    gating = projected[:, :local_di]
-    conv_in = projected[:, local_di : 2 * local_di + 2 * STATE]
-    dt_low = projected[:, 2 * local_di + 2 * STATE :].astype(jnp.bfloat16)
-    padding = jnp.zeros((WIDTH - 1, conv_in.shape[1]), jnp.float32)
-    conv_out, conv_pullback = jax.vjp(
-        convolve, jnp.concatenate([padding, conv_in], 0), my_kernel, my_bias
-    )
-    conv_low = conv_out.astype(jnp.bfloat16).astype(jnp.float32)
-    scanned, scan_pullback = jax.vjp(
-        head_mixer,
-        conv_low[:, :local_di].reshape(length, local_heads, HEADDIM),
-        dt_low.astype(jnp.float32),
-        conv_low[:, local_di:],
-        heads_of(a_log, 0, 1),
-        heads_of(dt_bias, 0, 1),
-        heads_of(d_skip, 0, 1),
-    )
-    mixed = scanned.astype(jnp.bfloat16).reshape(length, local_di).astype(jnp.float32)
-    gate, gate_pullback = jax.vjp(jax.nn.silu, gating)
-    gated = mixed * gate
-    d_gnorm = jnp.dot(cot, out_mine.T, preferred_element_type=jnp.float32)
-    d_unit = d_gnorm * my_gain_two[None, :]
-    sums = jnp.stack([jnp.sum(gated * gated, axis=1), jnp.sum(d_unit * gated, axis=1)])
-    sums = jnp.sum(lax.all_gather(sums, "seq", axis=0, tiled=False), axis=0) / DI
-    scale = lax.rsqrt(sums[0] + norm_eps)[:, None]
-    unit_two = gated * scale
-    gnorm_low = (unit_two * my_gain_two[None, :]).astype(jnp.bfloat16)
-    block_part = jnp.dot(gnorm_low, out_mine, preferred_element_type=jnp.float32)
+    lanes = 128
+    in_main = in_mine[:, : 2 * local_di + 2 * STATE]
+    dt_weight = jnp.pad(in_mine[:, 2 * local_di + 2 * STATE :], ((0, 0), (0, lanes - local_heads)))
+    my_skip = heads_of(d_skip, 0, 1)
+
+    def on_lanes(values):
+        return jnp.pad(values, (0, lanes - local_heads))[None, :]
+
+    heads_vectors = (
+        on_lanes(heads_of(a_log, 0, 1)),
+        on_lanes(heads_of(dt_bias, 0, 1)),
+        jnp.repeat(my_skip, HEADDIM)[None, :],
+    )
+    expand = (
+        jnp.arange(lanes)[:, None] == jnp.arange(local_di)[None, :] // HEADDIM
+    ).astype(jnp.float32)
+    (
+        normed_low,
+        gating,
+        conv_in,
+        conv_pre,
+        dt_raw,
+        y,
+        scanned,
+        states,
+        d_gnorm,
+        sums,
+    ) = run_forward(
+        hidden_low,
+        cot,
+        in_main,
+        dt_weight,
+        out_mine,
+        (gain_one[None, :], my_gain_two[None, :]),
+        (my_kernel, my_bias[None, :]),
+        heads_vectors,
+        expand,
+    )
+    sums = jnp.sum(lax.all_gather(sums[:2], "seq", axis=0, tiled=False), axis=0) / DI
+    scale = lax.rsqrt(sums[0] + norm_eps)
+    slope = scale * scale * sums[1]
+    block_part, d_gating, d_scanned, grad_out, grad_gate, d_gain_two = run_middle(
+        scanned,
+        gating,
+        d_gnorm,
+        cot,
+        normed_low,
+        scale[:, None],
+        slope[:, None],
+        out_mine,
+        my_gain_two[None, :],
+    )
     block_out = hidden_rows.astype(jnp.float32) + seq_sum_rows(block_part)
-    grad_out = jnp.dot(gnorm_low.T, cot, preferred_element_type=jnp.float32)
-    d_gain_two = jnp.sum(d_gnorm * unit_two, axis=0)
-    d_gated = scale * d_unit - unit_two * (scale * scale * sums[1][:, None])
-    (d_gating,) = gate_pullback(d_gated * mixed)
-    d_scanned = (d_gated * gate).astype(jnp.bfloat16).astype(jnp.float32)
-    d_inner, d_dt, d_both, d_a_log, d_dt_bias, d_skip_part = scan_pullback(
-        d_scanned.reshape(length, local_heads, HEADDIM)
-    )
-    d_conv_out = jnp.concatenate([d_inner.reshape(length, local_di), d_both], 1)
-    d_extended, d_kernel, d_conv_bias = conv_pullback(d_conv_out)
-    d_projected = jnp.concatenate([d_gating, d_extended[WIDTH - 1 :], d_dt], 1).astype(
-        jnp.bfloat16
-    )
-    d_normed_part = jnp.dot(d_projected, in_mine.T, preferred_element_type=jnp.float32)
-    grad_in = jnp.dot(normed_low.T, d_projected, preferred_element_type=jnp.float32)
-    d_gain_one = jnp.sum(d_normed_part * unit, axis=0)
+    (
+        d_normed_part,
+        grad_conv,
+        grad_dt,
+        d_gain_one,
+        d_kernel,
+        d_conv_bias,
+        d_skip_wide,
+        d_head,
+    ) = run_backward(
+        hidden_low,
+        normed_low,
+        conv_in,
+        conv_pre,
+        dt_raw,
+        y,
+        states,
+        d_scanned,
+        d_gating,
+        in_main,
+        dt_weight,
+        my_kernel,
+        heads_vectors,
+        expand,
+    )
+    d_gain_one = d_gain_one[0]
+    d_gain_two = d_gain_two[0]
+    d_conv_bias = d_conv_bias[0]
+    d_a_log = d_head[0, :local_heads]
+    d_dt_bias = d_head[1, :local_heads]
+    d_skip_part = jnp.sum(d_skip_wide.reshape(local_heads, HEADDIM), axis=1)
+    grad_in = jnp.concatenate([grad_gate, grad_conv, grad_dt[:, :local_heads]], 1)
     d_normed = seq_sum_rows(d_normed_part)
     own_hidden = hidden_rows.astype(jnp.float32)
     own_scale = lax.rsqrt(jnp.mean(own_hidden * own_hidden, axis=-1, keepdims=True) + norm_eps)
@@ -279,19 +823,17 @@
     in_part = lax.psum_scatter(
         grad_in.astype(jnp.bfloat16), "wshard", scatter_dimension=0, tiled=True
     )
-    in_every = lax.all_gather(in_part, "seq", axis=0, tiled=False)
+    in_every = lax.all_gather(in_part, "seq", axis=0, tiled=False).astype(jnp.float32)
     both_end = 2 * local_di + 2 * STATE
     in_total = jnp.concatenate(
         [
             merge_heads(in_every[:, :, :local_di], 1, HEADDIM),
             merge_heads(in_every[:, :, local_di : 2 * local_di], 1, HEADDIM),
-            jnp.sum(in_every[:, :, 2 * local_di : both_end].astype(jnp.float32), axis=0).astype(
-                jnp.bfloat16
-            ),
+            jnp.sum(in_every[:, :, 2 * local_di : both_end], axis=0),
             merge_heads(in_every[:, :, both_end:], 1, 1),
         ],
         1,
-    ).astype(jnp.float32)
+    )
     in_first_new, in_second_new, in_weight_new = adamw_step(
         in_weight, in_first, in_second, in_total, matrix_rate, matrix_decay
     )

time: 670 us -> 484 us (0.72); the launches traced: 662 us -> 484 us
  local copies, waits for them, and re-layouts: 177 us -> 21.5 us
  matrix products: 112 us -> 0 us
  waiting for transfers between devices: 226 us -> 308 us
  Pallas kernels: 0 us -> 61.1 us
  other arithmetic: 76.4 us -> 24.7 us
    dot_general x62 -> x0, matrix products: 112 us -> none  [the longest x12 37.6 us: advance(): within = jnp.einsum('hij,jhp->ihp', decay_mat, x_block, precision=precise)]
    dynamic_update_slice x16 -> x0, local copies, waits for them, and re-layouts: 103 us -> none  [state_scan(): last_state, outputs = lax.scan(jax.checkpoint(advance), initial, pieces)]
    reduce_scatter x0 -> x1, waiting for transfers between devices: none -> 66.5 us  [shards(): lax.psum_scatter(grad_in.astype(jnp.bfloat16), 'wshard', scatter_dimensio...]
    pallas_call x0 -> x3, Pallas kernels: none -> 61.1 us  [the longest x1 30.2 us: run_backward(): pl.pallas_call(backward_kernel, grid=(chunks,), in_specs=[back(D), back(D...]
    unnamed x10 -> x9, waiting for transfers between devices: 52.7 us -> 3.16 us
    all_gather x1, waiting for transfers between devices: 0.01 us -> 37 us  [gather_out(): return lax.all_gather(mine, 'wshard', axis=0, tiled=True)]
    all_gather x1, waiting for transfers between devices: 0.01 us -> 24 us  [shards(): cot = lax.all_gather(cot_rows, 'seq', axis=0, tiled=True)]
    unnamed x99 -> x28, local copies, waits for them, and re-layouts: 25.5 us -> 6.92 us
  transfers between devices with their start and end apart: 9 -> 9, of which waited for: 7 -> 9; matrix products, arithmetic and copies ran while one was open for 23% -> 4% of each run, Pallas kernels for 0% -> 0%
where the time goes in v2:
time: 484 us
  waiting for transfers between devices  308 us (64%)
  Pallas kernels  61.1 us (13%)
  blocking collectives  53.2 us (11%)
  other arithmetic  24.7 us (5%)
  local copies, waits for them, and re-layouts  21.5 us (4%)
  between operations  14.4 us (3%)
    reduce_scatter x1, waiting for transfers between devices, shards(): lax.psum_scatter(grad_in.astype(jnp.bfloat16), 'wshard', scatter_dimensio...  66.5 us
    all_gather x1, waiting for transfers between devices, shards(): in_mine = lax.all_gather(in_mine, 'wshard', axis=0, tiled=True)  56.7 us
    reduce_scatter x2, waiting for transfers between devices, seq_sum_rows(): lax.psum_scatter(partial.astype(jnp.bfloat16), 'seq', scatter_dimension=0...  55.2 us
    psum x1, blocking collectives, shards(): vec_total = lax.psum(vec_grad, ('seq', 'wshard'))  40.2 us
    all_gather x1, waiting for transfers between devices, gather_out(): return lax.all_gather(mine, 'wshard', axis=0, tiled=True)  37 us
    pallas_call x1, Pallas kernels, run_backward(): pl.pallas_call(backward_kernel, grid=(chunks,), in_specs=[back(D), back(D...  30.2 us
    reduce_scatter x1, waiting for transfers between devices, sum_out_grad(): mine = lax.psum_scatter(grad, 'wshard', scatter_dimension=0, tiled=True)  25.3 us
    all_gather x1, waiting for transfers between devices, shards(): cot = lax.all_gather(cot_rows, 'seq', axis=0, tiled=True)  24 us
  transfers between devices with their start and end apart: 9, of which 9 were waited for; matrix products, arithmetic and copies ran while one was open for 4% of the time, Pallas kernels for 0%

profile of v2, /device:TPU:0, one launch (start us, length us, event | category | flops | bytes accessed | tf_op | source)
XLA Modules:
  0.0 483.6 jit_solution(624073582481057836)
XLA Ops:
  7.2 1.9 copy.74
  15.1 56.7 %all-gather.13.cloned.1.call-done = bf16[1024,1288]{1,0:T(8,128)(2,1)} async-done(((bf16[128,1288]{1,0:T(8,128)(2,1)}), bf16[1024,1288]{1,0:T(8,128)(2,1)}) %all-gather.13.cloned.1.call-update) | async-done | bytes 2637840 | tf_op jit(solution)/shard_map/all_gather | solution.py:698
  71.7 1.0 slice.157
  72.8 3.5 slice.156.in_ref
  76.2 37.0 %all-gather.19.cloned.1.call-done = bf16[1,1,512,1024]{3,2,1,0:T(8,128)(2,1)} async-done(((bf16[1,1,64,1024]{3,2,1,0:T(8,128)(2,1)}), bf16[1,1,512,1024]{3,2,1,0:T(8,128)(2,1)}) %all-gather.19.cloned.1.call-update) | async-done | bytes 1048592 | tf_op jit(solution)/shard_map/all_gather | solution.py:635
  113.2 22.9 %all-gather.15.cloned.1.call-done = bf16[1,1024,1024]{2,1,0:T(8,128)(2,1)} async-done(((bf16[1,256,1024]{2,1,0:T(8,128)(2,1)}), bf16[1,1024,1024]{2,1,0:T(8,128)(2,1)}) %all-gather.15.cloned.1.call-update) | async-done | bytes 2097168 | tf_op jit(solution)/shard_map/all_gather | solution.py:697
  136.2 24.0 %all-gather.17.cloned.1.call-done = bf16[1,1024,1024]{2,1,0:T(8,128)(2,1)} async-done(((bf16[1,256,1024]{2,1,0:T(8,128)(2,1)}), bf16[1,1024,1024]{2,1,0:T(8,128)(2,1)}) %all-gather.17.cloned.1.call-update) | async-done | bytes 2097168 | tf_op jit(solution)/shard_map/all_gather | solution.py:699
  160.2 20.9 %forward.1 = (bf16[1024,1024]{1,0:T(8,128)(2,1)}, f32[1024,512]{1,0:T(8,128)}, f32[1024,768]{1,0:T(8,128)}, f32[1024,768]{1,0:T(8,128)}, f32[1024,128]{1,0:T(8,1...) custom-call(bf16[1024,1024]{1,0:T(8,128)(2,1)} %bitcast.87, ...), custom_call_target="tpu_custom_call" | custom-call | flops 8000000000 | bytes 25000000 | tf_op jit(solution)/shard_map/forward/pallas_call | solution.py:407
  181.2 1.0 copy-done
  182.1 5.4 %all-gather.6 = f32[4,2,1024]{2,1,0:T(2,128)S(1)} all-gather(f32[1,2,1024]{2,1,0:T(2,128)S(1)} %slice_bitcast_fusion.1), channel_id=5, replica_groups=mesh['seq'=4,'wshard'=8] {'seq'}, dimensions={0}, use_global_device_ids=true | all-gather | bytes 40960 | tf_op jit(solution)/shard_map/all_gather | solution.py:743
  187.8 1.0 copy.81
  188.8 1.0 copy.82
  189.9 1.3 mul.150.slope_ref
  191.1 10.0 %middle.1 = (bf16[1024,1024]{1,0:T(8,128)(2,1)}, bf16[1024,512]{1,0:T(8,128)(2,1)S(1)}, bf16[1024,512]{1,0:T(8,128)(2,1)S(1)}, bf16[512,1024]{1,0:T(8,128)(2,1)}...) custom-call(bf16[1024,512]{1,0:T(8,128)(2,1)} %copy-done, f32[1024,512]{1,0:T(8,128)} %get-tuple-element.36.gating_ref, ...), custom_call_target="tpu_custom_call" | custom-call | flops 4000000000 | bytes 15000000 | tf_op jit(solution)/shard_map/middle/pallas_call | solution.py:465
  201.1 1.0 copy-done.1
  202.1 30.2 %backward.1 = (bf16[1024,1024]{1,0:T(8,128)(2,1)}, bf16[1024,768]{1,0:T(8,128)(2,1)}, bf16[1024,128]{1,0:T(8,128)(2,1)S(1)}, f32[1,1024]{1,0:T(1,128)S(1)}, f32[...) custom-call(bf16[1024,1024]{1,0:T(8,128)(2,1)} %bitcast.88, ...), custom_call_target="tpu_custom_call" | custom-call | flops 16000000000 | bytes 25000000 | tf_op jit(solution)/shard_map/backward/pallas_call | solution.py:530
  232.3 3.2 pad_maximum_fusion
  241.0 66.5 %reduce-scatter.9.cloned.1.call-done = bf16[128,1288]{1,0:T(8,128)(2,1)} async-done(((bf16[1024,1288]{1,0:T(8,128)(2,1)}), bf16[128,1288]{1,0:T(8,128)(2,1)}) %reduce-scatter.9.cloned.1.call-update) | async-done | bytes 329744 | tf_op jit(solution)/shard_map/reduce_scatter | solution.py:823
  307.6 40.2 %psum.7 = f32[14688]{0:T(1024)S(1)} all-reduce(f32[14688]{0:T(1024)S(1)} %concatenate.27), channel_id=1, replica_groups=mesh['seq'=4,'wshard'=8] {'seq','wshard'}, use_global_device_ids=true, to_apply=%region_9.10 | all-reduce | flops 14688 | bytes 117504 | tf_op jit(solution)/shard_map/psum | solution.py:818
  348.6 25.3 %reduce-scatter.11.cloned.1.call-done = bf16[64,1024]{1,0:T(8,128)(2,1)} async-done(((bf16[512,1024]{1,0:T(8,128)(2,1)}), bf16[64,1024]{1,0:T(8,128)(2,1)}) %reduce-scatter.11.cloned.1.call-update) | async-done | bytes 131088 | tf_op jit(solution)/shard_map/reduce_scatter | solution.py:651
  373.9 7.6 %all-gather.5 = bf16[256,1024]{1,0:T(8,128)(2,1)S(1)} all-gather(bf16[64,1024]{1,0:T(8,128)(2,1)} %reduce-scatter.11.cloned.1.call-done), channel_id=7, replica_groups=mesh['seq'=4,'wshard'=8] {'seq'}, dimensions={0}, use_global_device_ids=true | all-gather | bytes 655360 | tf_op jit(solution)/shard_map/all_gather | solution.py:652
  381.4 3.5 multiply_subtract_fusion.1
  385.0 22.6 %reduce-scatter.7.cloned.1.call-done = bf16[256,1024]{1,0:T(8,128)(2,1)} async-done(((bf16[1024,1024]{1,0:T(8,128)(2,1)}), bf16[256,1024]{1,0:T(8,128)(2,1)}) %reduce-scatter.7.cloned.1.call-update) | async-done | bytes 524304 | tf_op jit(solution)/shard_map/reduce_scatter | solution.py:626
  407.6 1.4 fusion.3
  409.0 32.6 %reduce-scatter.5.cloned.1.call-done = bf16[256,1024]{1,0:T(8,128)(2,1)} async-done(((bf16[1024,1024]{1,0:T(8,128)(2,1)}), bf16[256,1024]{1,0:T(8,128)(2,1)}) %reduce-scatter.5.cloned.1.call-update) | async-done | bytes 524304 | tf_op jit(solution)/shard_map/reduce_scatter | solution.py:626
  441.6 3.0 fusion.7
  444.5 17.7 %all-gather.21.cloned.1.call-done = bf16[512,1288]{1,0:T(8,128)(2,1)} async-done(((bf16[128,1288]{1,0:T(8,128)(2,1)}), bf16[512,1288]{1,0:T(8,128)(2,1)}) %all-gather.21.cloned.1.call-update) | async-done | bytes 1318928 | tf_op jit(solution)/shard_map/all_gather | solution.py:826
  462.2 1.6 bitcast_convert_fusion
  463.8 1.3 fusion.24
  465.8 2.7 copy.90
  468.4 1.3 copy.85
  469.8 7.4 %multiply_subtract_fusion = (f32[128,4384]{0,1:T(8,128)}, f32[128,4384]{0,1:T(8,128)}, f32[128,4384]{0,1:T(8,128)}) fusion(f32[128,4384]{0,1:T(8,128)S(1)} %copy-done.2, f32[128,32]{0,1:T(8,128)S(1)} %bitcast.84, f32[128,256]{0,1:T(8,128)S(1)} %copy.89, f32[128,2048]{0,1:T(8,128)S(1)} %bitcast.74, f32[128,2048]{0,1:T(8,128)S(1)} %bitcast.75, ...), kind=kLoop, calls=%fused_computation.4 | loop fusion | flops 10100736 | bytes 15712256 | tf_op jit(solution)/shard_map/sub | solution.py:607
  (135 shorter events, 12.9 us)
Async XLA Ops:
  7.2 64.6 %all-gather.13.cloned.1.call-start = ((), (), s32[]{:S(2)}) async-start(), calls=%async_computation.4 | async-start | bytes 3244032 | tf_op jit(solution)/shard_map/all_gather | solution.py:698
  9.3 2.0 copy-start.4
  10.3 3.1 copy-start.9
  10.3 3.2 slice-start
  10.4 3.7 slice-start.1
  11.2 102.0 %all-gather.19.cloned.1.call-start = ((), (), s32[]{:S(2)}) async-start(), calls=%async_computation.11 | async-start | bytes 1179648 | tf_op jit(solution)/shard_map/all_gather | solution.py:635
  12.0 124.1 %all-gather.15.cloned.1.call-start = ((), (), s32[]{:S(2)}) async-start(), calls=%async_computation.9 | async-start | bytes 2621440 | tf_op jit(solution)/shard_map/all_gather | solution.py:697
  12.8 147.4 %all-gather.17.cloned.1.call-start = ((), (), s32[]{:S(2)}) async-start(), calls=%async_computation.10 | async-start | bytes 2621440 | tf_op jit(solution)/shard_map/all_gather | solution.py:699
  13.4 294.1 %reduce-scatter.9.cloned.1.call-start = ((), (), s32[]{:S(2)}) async-start(), calls=%async_computation.7 | async-start | bytes 3244032 | tf_op jit(solution)/shard_map/reduce_scatter | solution.py:823
  181.2 1.0 copy-start
  201.1 1.0 copy-start.1
  202.1 30.2 %copy-start.8 = (bf16[1024,512]{1,0:T(8,128)(2,1)S(1)}, bf16[1024,512]{1,0:T(8,128)(2,1)}, u32[]{:S(2)}) copy-start(bf16[1024,512]{1,0:T(8,128)(2,1)} %get-tuple-element.49) | copy-start | bytes 3145732
  235.5 138.4 %reduce-scatter.11.cloned.1.call-start = ((), (), s32[]{:S(2)}) async-start(), calls=%async_computation.8 | async-start | bytes 1179648 | tf_op jit(solution)/shard_map/reduce_scatter | solution.py:651
  236.1 1.8 copy-start.3
  236.1 171.5 %reduce-scatter.7.cloned.1.call-start = ((), (), s32[]{:S(2)}) async-start(), calls=%async_computation.6 | async-start | bytes 2621440 | tf_op jit(solution)/shard_map/reduce_scatter | solution.py:626
  236.8 111.0 %copy-start.10 = (f32[14688]{0:T(1024)S(1)}, f32[14688]{0:T(1024)}, u32[]{:S(2)}) copy-start(f32[14688]{0:T(1024)} %param.21) | copy-start | bytes 176260
  236.8 111.0 %copy-start.11 = (f32[14688]{0:T(1024)S(1)}, f32[14688]{0:T(1024)}, u32[]{:S(2)}) copy-start(f32[14688]{0:T(1024)} %param.20) | copy-start | bytes 176260
  236.8 204.7 %reduce-scatter.5.cloned.1.call-start = ((), (), s32[]{:S(2)}) async-start(), calls=%async_computation.5 | async-start | bytes 2621440 | tf_op jit(solution)/shard_map/reduce_scatter | solution.py:626
  236.9 144.5 %copy-start.5 = (f32[256,1024]{1,0:T(8,128)S(1)}, f32[256,1024]{1,0:T(8,128)}, u32[]{:S(2)}) copy-start(f32[256,1024]{1,0:T(8,128)} %param.16) | copy-start | bytes 3145732
  236.9 144.5 %copy-start.7 = (f32[256,1024]{1,0:T(8,128)S(1)}, f32[256,1024]{1,0:T(8,128)}, u32[]{:S(2)}) copy-start(f32[256,1024]{1,0:T(8,128)} %param.18) | copy-start | bytes 3145732
  237.6 224.6 %all-gather.21.cloned.1.call-start = ((), (), s32[]{:S(2)}) async-start(), calls=%async_computation.12 | async-start | bytes 1802240 | tf_op jit(solution)/shard_map/all_gather | solution.py:826
  381.4 60.2 %copy-start.6 = (bf16[1,256,1024]{2,1,0:T(8,128)(2,1)S(1)}, bf16[1,256,1024]{2,1,0:T(8,128)(2,1)}, u32[]{:S(2)}) copy-start(bf16[1,256,1024]{2,1,0:T(8,128)(2,1)} %param.12) | copy-start | bytes 1572868
  465.8 4.0 copy-start.2
Sparse Core Ops, SparseCore 0:
  11.3 60.3 all-gather.12
  74.4 38.7 all-gather.18
  114.8 21.3 all-gather.14
  137.6 22.5 all-gather.16
  235.6 71.8 reduce-scatter.8
  311.3 62.4 reduce-scatter.10
  377.1 30.4 reduce-scatter.6
  410.1 31.4 reduce-scatter.4
  443.2 18.9 all-gather.20

commit v3 on v2

--- a/solution.py
+++ b/solution.py
@@ -99,12 +99,9 @@
 
 def forward_kernel(
     hidden_ref,
-    cot_ref,
-    in_ref,
+    conv_weight_ref,
     dt_weight_ref,
-    out_ref,
     gain_one_ref,
-    gain_two_ref,
     conv_ref,
     bias_ref,
     a_log_ref,
@@ -112,19 +109,16 @@
     skip_ref,
     expand_ref,
     normed_ref,
-    gating_ref,
     conv_in_ref,
     conv_pre_ref,
     dt_ref,
     y_ref,
     scanned_ref,
     state_ref,
-    d_gnorm_ref,
-    sums_ref,
     ext,
     state,
 ):
-    local_di = gating_ref.shape[1]
+    local_di = y_ref.shape[1]
     heads = local_di // HEADDIM
 
     @pl.when(pl.program_id(0) == 0)
@@ -135,10 +129,7 @@
     hidden = hidden_ref[...].astype(jnp.float32)
     normed = low(rms_scale(hidden) * gain_one_ref[...])
     normed_ref[...] = normed
-    projected = dot_nn(normed, in_ref[...])
-    gating = projected[:, :local_di]
-    gating_ref[...] = gating
-    conv_in = projected[:, local_di:]
+    conv_in = dot_nn(normed, conv_weight_ref[...])
     conv_in_ref[...] = conv_in
     ext[8 : 8 + BLOCK, :] = conv_in
     conv_pre = bias_ref[...] + conv_ref[WIDTH - 1 : WIDTH, :] * conv_in
@@ -183,11 +174,37 @@
     last = running_wide[BLOCK - 1 : BLOCK, :]
     to_end = jnp.exp(last - running_wide)
     state[...] = jnp.exp(last) * held + dot_nn(b_t, low(to_end * stepped))
-    scanned = low(y_ref[...] + skip_ref[...] * inner_wide)
-    scanned_ref[...] = scanned
-    gated = scanned.astype(jnp.float32) * (gating * sigmoid(gating))
-    d_gnorm = dot_nt(cot_ref[...], out_ref[...])
+    scanned_ref[...] = low(y_ref[...] + skip_ref[...] * inner_wide)
+
+
+def out_halves(packed_ref):
+    packed = packed_ref[...].reshape(-1, 2, HEADDIM, packed_ref.shape[1])
+    extent = packed_ref.shape[0] // 2
+    return (
+        packed[:, 0].reshape(extent, packed_ref.shape[1]),
+        packed[:, 1].reshape(extent, packed_ref.shape[1]),
+    )
+
+
+def gate_kernel(
+    normed_ref,
+    scanned_ref,
+    cot_ref,
+    gate_weight_ref,
+    out_ref,
+    gain_two_ref,
+    gating_ref,
+    d_gnorm_ref,
+    sums_ref,
+):
+    local_di = gating_ref.shape[1]
+    gating = dot_nn(normed_ref[...], gate_weight_ref[...])
+    gating_ref[...] = gating
+    out_left, out_right = out_halves(out_ref)
+    half = out_left.shape[1]
+    d_gnorm = dot_nt(cot_ref[:, :half], out_left) + dot_nt(cot_ref[:, half:], out_right)
     d_gnorm_ref[...] = d_gnorm
+    gated = scanned_ref[...].astype(jnp.float32) * (gating * sigmoid(gating))
     ones = jnp.ones((8, local_di), jnp.float32)
     squares = dot_nt(ones, gated * gated, precise)
     products = dot_nt(ones, d_gnorm * gain_two_ref[...] * gated, precise)
@@ -209,17 +226,18 @@
     block_ref,
     d_gating_ref,
     d_scanned_ref,
-    grad_out_ref,
-    grad_gate_ref,
+    grad_ref,
     d_gain_two_ref,
-    out_sum,
+    left_sum,
+    right_sum,
     gate_sum,
 ):
     chunk = pl.program_id(0)
 
     @pl.when(chunk == 0)
     def _():
-        out_sum[...] = jnp.zeros_like(out_sum)
+        left_sum[...] = jnp.zeros_like(left_sum)
+        right_sum[...] = jnp.zeros_like(right_sum)
         gate_sum[...] = jnp.zeros_like(gate_sum)
         d_gain_two_ref[...] = jnp.zeros_like(d_gain_two_ref)
 
@@ -232,8 +250,12 @@
     d_gnorm = d_gnorm_ref[...]
     gain_two = gain_two_ref[...]
     gnorm = low(unit * gain_two)
-    block_ref[...] = low(dot_nn(gnorm, out_ref[...]))
-    out_sum[...] += dot_tn(gnorm, cot_ref[...])
+    out_left, out_right = out_halves(out_ref)
+    half = out_left.shape[1]
+    block_ref[:, :half] = low(dot_nn(gnorm, out_left))
+    block_ref[:, half:] = low(dot_nn(gnorm, out_right))
+    left_sum[...] += dot_tn(gnorm, cot_ref[:, :half])
+    right_sum[...] += dot_tn(gnorm, cot_ref[:, half:])
     d_gain_two_ref[...] += jnp.sum(d_gnorm * unit, axis=0, keepdims=True)
     d_gated = scale * (d_gnorm * gain_two) - unit * slope_ref[:, :1]
     d_gating = low(d_gated * scanned * (open_part * (1.0 + gating * (1.0 - open_part))))
@@ -243,12 +265,16 @@
 
     @pl.when(chunk == pl.num_programs(0) - 1)
     def _():
-        grad_out_ref[...] = low(out_sum[...])
-        grad_gate_ref[...] = low(gate_sum[...])
+        local_di = gating_ref.shape[1]
+        grad_ref[:, :local_di] = low(gate_sum[...])
+        for head in range(local_di // HEADDIM):
+            rows = slice(head * HEADDIM, (head + 1) * HEADDIM)
+            base = 2 * head * HEADDIM
+            grad_ref[base : base + HEADDIM, local_di:] = low(left_sum[rows, :])
+            grad_ref[base + HEADDIM : base + 2 * HEADDIM, local_di:] = low(right_sum[rows, :])
 
 
 def backward_kernel(
-    hidden_ref,
     normed_ref,
     conv_in_ref,
     conv_pre_ref,
@@ -256,18 +282,13 @@
     y_ref,
     state_ref,
     d_scanned_ref,
-    d_gating_ref,
-    in_ref,
-    dt_weight_ref,
     conv_ref,
     a_log_ref,
     dt_bias_ref,
     skip_ref,
     expand_ref,
-    d_normed_ref,
-    grad_conv_ref,
-    grad_dt_ref,
-    d_gain_one_ref,
+    d_rest_ref,
+    grad_ref,
     d_kernel_ref,
     d_conv_bias_ref,
     d_skip_ref,
@@ -275,8 +296,7 @@
     ext,
     d_state,
     later_state,
-    conv_sum,
-    dt_sum,
+    rest_sum,
 ):
     local_di = y_ref.shape[1]
     heads = local_di // HEADDIM
@@ -287,9 +307,7 @@
         ext[BLOCK : BLOCK + 8, :] = jnp.zeros((8, ext.shape[1]), jnp.float32)
         d_state[...] = jnp.zeros_like(d_state)
         later_state[...] = jnp.zeros_like(later_state)
-        conv_sum[...] = jnp.zeros_like(conv_sum)
-        dt_sum[...] = jnp.zeros_like(dt_sum)
-        d_gain_one_ref[...] = jnp.zeros_like(d_gain_one_ref)
+        rest_sum[...] = jnp.zeros_like(rest_sum)
         d_kernel_ref[...] = jnp.zeros_like(d_kernel_ref)
         d_conv_bias_ref[...] = jnp.zeros_like(d_conv_bias_ref)
         d_skip_ref[...] = jnp.zeros_like(d_skip_ref)
@@ -372,23 +390,34 @@
         d_conv_in = d_conv_in + conv_ref[tap : tap + 1, :] * moved
         d_kernel_ref[tap : tap + 1, :] += jnp.sum(moved * conv_in, axis=0, keepdims=True)
     ext[BLOCK : BLOCK + 8, :] = ext[0:8, :]
-    d_conv_low = low(d_conv_in)
-    d_dt_low = low(d_dt)
-    normed = normed_ref[...]
-    conv_sum[...] += dot_tn(normed, d_conv_low)
-    dt_sum[...] += dot_tn(normed, d_dt_low)
-    d_normed = dot_nt(d_gating_ref[...], in_ref[:, :local_di])
-    d_normed = d_normed + dot_nt(d_conv_low, in_ref[:, local_di:])
-    d_normed = d_normed + dot_nt(d_dt_low, dt_weight_ref[...])
+    d_rest = jnp.concatenate([low(d_conv_in), low(d_dt)], 1)
+    d_rest_ref[...] = d_rest
+    rest_sum[...] += dot_tn(normed_ref[...], d_rest)
+
+    @pl.when(chunk == pl.num_programs(0) - 1)
+    def _():
+        grad_ref[...] = low(rest_sum[...])
+
+
+def normed_kernel(
+    hidden_ref,
+    d_gating_ref,
+    d_rest_ref,
+    gate_weight_ref,
+    rest_weight_ref,
+    d_normed_ref,
+    d_gain_one_ref,
+):
+    @pl.when(pl.program_id(0) == 0)
+    def _():
+        d_gain_one_ref[...] = jnp.zeros_like(d_gain_one_ref)
+
+    d_normed = dot_nt(d_gating_ref[...], gate_weight_ref[...])
+    d_normed = d_normed + dot_nt(d_rest_ref[...], rest_weight_ref[...])
     d_normed_ref[...] = low(d_normed)
     unit = rms_scale(hidden_ref[...].astype(jnp.float32))
     d_gain_one_ref[...] += jnp.sum(d_normed * unit, axis=0, keepdims=True)
 
-    @pl.when(chunk == pl.num_programs(0) - 1)
-    def _():
-        grad_conv_ref[...] = low(conv_sum[...])
-        grad_dt_ref[...] = low(dt_sum[...])
-
 
 def kernel_params():
     return pltpu.CompilerParams(
@@ -396,12 +425,15 @@
     )
 
 
-def run_forward(hidden, cot, in_low, dt_weight, out_low, gains, conv, heads_vectors, expand):
+def cost(flops, moved, transcendentals):
+    return pl.CostEstimate(flops=flops, bytes_accessed=moved, transcendentals=transcendentals)
+
+
+def run_forward(hidden, rest_weight, gain_one, conv, heads_vectors, expand):
     length = hidden.shape[0]
     chunks = length // BLOCK
-    local_di = out_low.shape[0]
-    channels = in_low.shape[1] - local_di
-    lanes = dt_weight.shape[1]
+    lanes, local_di = expand.shape
+    channels = rest_weight.shape[1] - lanes
     shape = jax.ShapeDtypeStruct
     f32, bf16 = jnp.float32, jnp.bfloat16
     return pl.pallas_call(
@@ -409,12 +441,9 @@
         grid=(chunks,),
         in_specs=[
             wide(D),
-            wide(D),
-            whole(D, local_di + channels),
-            whole(D, lanes),
-            whole(local_di, D),
+            whole(D, channels),
+            pl.BlockSpec((D, lanes), lambda q: (0, channels // lanes)),
             whole(1, D),
-            whole(1, local_di),
             whole(WIDTH, channels),
             whole(1, channels),
             whole(1, lanes),
@@ -424,42 +453,66 @@
         ],
         out_specs=[
             wide(D),
-            wide(local_di),
             wide(channels),
             wide(channels),
             wide(lanes),
             wide(local_di),
             wide(local_di),
             pl.BlockSpec((1, STATE, local_di), lambda q: (q, 0, 0)),
-            wide(local_di),
-            pl.BlockSpec((8, BLOCK), lambda q: (0, q)),
         ],
         out_shape=[
             shape((length, D), bf16),
-            shape((length, local_di), f32),
             shape((length, channels), f32),
             shape((length, channels), f32),
             shape((length, lanes), f32),
             shape((length, local_di), f32),
             shape((length, local_di), bf16),
             shape((chunks, STATE, local_di), f32),
-            shape((length, local_di), f32),
-            shape((8, length), f32),
         ],
         scratch_shapes=[
             pltpu.VMEM((8 + BLOCK, channels), f32),
             pltpu.VMEM((STATE, local_di), f32),
         ],
         compiler_params=kernel_params(),
-        cost_estimate=pl.CostEstimate(
-            flops=8_000_000_000, bytes_accessed=25_000_000, transcendentals=8_000_000
-        ),
+        cost_estimate=cost(6_000_000_000, 30_000_000, 8_000_000),
         name="forward",
-    )(hidden, cot, in_low, dt_weight, out_low, *gains, *conv, *heads_vectors, expand)
-
-
-def run_middle(scanned, gating, d_gnorm, cot, normed, scale, slope, out_low, gain_two):
+    )(hidden, rest_weight, rest_weight, gain_one, *conv, *heads_vectors, expand)
+
+
+def run_gate(normed, scanned, cot, gate_out, gain_two):
     length, local_di = scanned.shape
+    half = D // 2
+    shape = jax.ShapeDtypeStruct
+    return pl.pallas_call(
+        gate_kernel,
+        grid=(length // BLOCK,),
+        in_specs=[
+            wide(D),
+            wide(local_di),
+            wide(D),
+            pl.BlockSpec((D, local_di), lambda q: (0, 0)),
+            pl.BlockSpec((2 * local_di, half), lambda q: (0, local_di // half)),
+            whole(1, local_di),
+        ],
+        out_specs=[
+            wide(local_di),
+            wide(local_di),
+            pl.BlockSpec((8, BLOCK), lambda q: (0, q)),
+        ],
+        out_shape=[
+            shape((length, local_di), jnp.float32),
+            shape((length, local_di), jnp.float32),
+            shape((8, length), jnp.float32),
+        ],
+        compiler_params=kernel_params(),
+        cost_estimate=cost(2_500_000_000, 12_000_000, 1_000_000),
+        name="gate",
+    )(normed, scanned, cot, gate_out, gate_out, gain_two)
+
+
+def run_middle(scanned, gating, d_gnorm, cot, normed, scale, slope, gate_out, gain_two):
+    length, local_di = scanned.shape
+    half = D // 2
     shape = jax.ShapeDtypeStruct
     f32, bf16 = jnp.float32, jnp.bfloat16
     return pl.pallas_call(
@@ -473,54 +526,41 @@
             wide(D),
             wide(1),
             wide(1),
-            whole(local_di, D),
+            pl.BlockSpec((2 * local_di, half), lambda q: (0, local_di // half)),
             whole(1, local_di),
         ],
         out_specs=[
             wide(D),
             wide(local_di),
             wide(local_di),
-            whole(local_di, D),
-            whole(D, local_di),
+            whole(D, local_di + half),
             whole(1, local_di),
         ],
         out_shape=[
             shape((length, D), bf16),
             shape((length, local_di), bf16),
             shape((length, local_di), bf16),
-            shape((local_di, D), bf16),
-            shape((D, local_di), bf16),
+            shape((D, local_di + half), bf16),
             shape((1, local_di), f32),
         ],
-        scratch_shapes=[pltpu.VMEM((local_di, D), f32), pltpu.VMEM((D, local_di), f32)],
+        scratch_shapes=[
+            pltpu.VMEM((local_di, half), f32),
+            pltpu.VMEM((local_di, half), f32),
+            pltpu.VMEM((D, local_di), f32),
+        ],
         compiler_params=kernel_params(),
-        cost_estimate=pl.CostEstimate(
-            flops=4_000_000_000, bytes_accessed=15_000_000, transcendentals=500_000
-        ),
+        cost_estimate=cost(4_000_000_000, 15_000_000, 500_000),
         name="middle",
-    )(scanned, gating, d_gnorm, cot, normed, scale, slope, out_low, gain_two)
+    )(scanned, gating, d_gnorm, cot, normed, scale, slope, gate_out, gain_two)
 
 
 def run_backward(
-    hidden,
-    normed,
-    conv_in,
-    conv_pre,
-    dt_raw,
-    y,
-    states,
-    d_scanned,
-    d_gating,
-    in_low,
-    dt_weight,
-    kernel,
-    heads_vectors,
-    expand,
+    normed, conv_in, conv_pre, dt_raw, y, states, d_scanned, kernel, heads_vectors, expand
 ):
     length, local_di = y.shape
     chunks = length // BLOCK
     channels = conv_in.shape[1]
-    lanes = dt_weight.shape[1]
+    lanes = expand.shape[0]
     shape = jax.ShapeDtypeStruct
     f32, bf16 = jnp.float32, jnp.bfloat16
 
@@ -531,7 +571,6 @@
         backward_kernel,
         grid=(chunks,),
         in_specs=[
-            back(D),
             back(D),
             back(channels),
             back(channels),
@@ -539,9 +578,6 @@
             back(local_di),
             pl.BlockSpec((1, STATE, local_di), lambda q: (chunks - 1 - q, 0, 0)),
             back(local_di),
-            back(local_di),
-            whole(D, local_di + channels),
-            whole(D, lanes),
             whole(WIDTH, channels),
             whole(1, lanes),
             whole(1, lanes),
@@ -549,20 +585,16 @@
             whole(lanes, local_di),
         ],
         out_specs=[
-            back(D),
-            whole(D, channels),
-            whole(D, lanes),
-            whole(1, D),
+            back(channels + lanes),
+            whole(D, channels + lanes),
             whole(WIDTH, channels),
             whole(1, channels),
             whole(1, local_di),
             whole(2, lanes),
         ],
         out_shape=[
-            shape((length, D), bf16),
-            shape((D, channels), bf16),
-            shape((D, lanes), bf16),
-            shape((1, D), f32),
+            shape((length, channels + lanes), bf16),
+            shape((D, channels + lanes), bf16),
             shape((WIDTH, channels), f32),
             shape((1, channels), f32),
             shape((1, local_di), f32),
@@ -572,30 +604,30 @@
             pltpu.VMEM((BLOCK + 8, channels), f32),
             pltpu.VMEM((STATE, local_di), f32),
             pltpu.VMEM((STATE, local_di), f32),
-            pltpu.VMEM((D, channels), f32),
-            pltpu.VMEM((D, lanes), f32),
+            pltpu.VMEM((D, channels + lanes), f32),
         ],
         compiler_params=kernel_params(),
-        cost_estimate=pl.CostEstimate(
-            flops=16_000_000_000, bytes_accessed=25_000_000, transcendentals=10_000_000
-        ),
+        cost_estimate=cost(14_000_000_000, 40_000_000, 10_000_000),
         name="backward",
-    )(
-        hidden,
-        normed,
-        conv_in,
-        conv_pre,
-        dt_raw,
-        y,
-        states,
-        d_scanned,
-        d_gating,
-        in_low,
-        dt_weight,
-        kernel,
-        *heads_vectors,
-        expand,
-    )
+    )(normed, conv_in, conv_pre, dt_raw, y, states, d_scanned, kernel, *heads_vectors, expand)
+
+
+def run_normed(hidden, d_gating, d_rest, gate_out, rest_weight):
+    length, local_di = d_gating.shape
+    rest = d_rest.shape[1]
+    return pl.pallas_call(
+        normed_kernel,
+        grid=(length // BLOCK,),
+        in_specs=[wide(D), wide(local_di), wide(rest), whole(D, local_di), whole(D, rest)],
+        out_specs=[wide(D), whole(1, D)],
+        out_shape=[
+            jax.ShapeDtypeStruct((length, D), jnp.bfloat16),
+            jax.ShapeDtypeStruct((1, D), jnp.float32),
+        ],
+        compiler_params=kernel_params(),
+        cost_estimate=cost(3_000_000_000, 9_000_000, 1000),
+        name="normed",
+    )(hidden, d_gating, d_rest, gate_out, rest_weight)
 
 
 def adamw_step(weight, first, second, grad, rate, decay):
@@ -622,10 +654,118 @@
     return moved.reshape(shape[:axis] + (HEADS * width,) + shape[axis + 1 :])
 
 
-def seq_sum_rows(partial):
-    return lax.psum_scatter(
-        partial.astype(jnp.bfloat16), "seq", scatter_dimension=0, tiled=True
-    ).astype(jnp.float32)
+def swap(values, axis, mask):
+    route = [(i, i ^ mask) for i in range(lax.axis_size(axis))]
+    return lax.ppermute(values, axis, route)
+
+
+def put_block(buffer, block, index):
+    return lax.dynamic_update_slice_in_dim(buffer, block, index * block.shape[0], 0)
+
+
+def seq_gather(rows):
+    count = lax.axis_size("seq")
+    if count != 4:
+        return lax.all_gather(rows, "seq", axis=0, tiled=True)
+    index = lax.axis_index("seq")
+    far = swap(rows, "seq", 2)
+    blocks = [rows, swap(rows, "seq", 1), far, swap(far, "seq", 1)]
+    result = jnp.zeros((count * rows.shape[0],) + rows.shape[1:], rows.dtype)
+    for mask, block in enumerate(blocks):
+        result = put_block(result, block, index ^ mask)
+    return result
+
+
+def take_block(values, index, rows):
+    return lax.dynamic_slice_in_dim(values, index * rows, rows, 0)
+
+
+def seq_scatter(partial):
+    count = lax.axis_size("seq")
+    if count != 4:
+        return lax.psum_scatter(partial, "seq", scatter_dimension=0, tiled=True).astype(
+            jnp.float32
+        )
+    index = lax.axis_index("seq")
+    rows = partial.shape[0] // count
+    total = take_block(partial, index, rows).astype(jnp.float32)
+    for mask in range(1, count):
+        piece = swap(take_block(partial, index ^ mask, rows), "seq", mask)
+        total = total + piece.astype(jnp.float32)
+    return total
+
+
+def seq_scatter_near(partial):
+    count = lax.axis_size("seq")
+    if count != 4:
+        return seq_scatter(partial)
+    index = lax.axis_index("seq")
+    rows = partial.shape[0] // count
+
+    def near(mask):
+        arrived = swap(take_block(partial, index ^ 1 ^ mask, rows), "seq", 1)
+        mine = take_block(partial, index ^ mask, rows)
+        return arrived.astype(jnp.float32) + mine.astype(jnp.float32)
+
+    far = swap(low(near(2)), "seq", 2)
+    return near(0) + far.astype(jnp.float32)
+
+
+def ring_route(count):
+    return [(i, (i + 2) % count) for i in range(count)]
+
+
+def shard_gather(rows):
+    count = lax.axis_size("wshard")
+    if count != 8:
+        return lax.all_gather(rows, "wshard", axis=0, tiled=True)
+    index = lax.axis_index("wshard")
+    result = jnp.zeros((count * rows.shape[0],) + rows.shape[1:], rows.dtype)
+    held = rows
+    for step in range(count // 2):
+        source = (index + count - 2 * step) % count
+        result = put_block(result, held, source)
+        result = put_block(result, swap(held, "wshard", 1), source ^ 1)
+        if step < count // 2 - 1:
+            held = lax.ppermute(held, "wshard", ring_route(count))
+    return result
+
+
+def shard_scatter(partial):
+    count = lax.axis_size("wshard")
+    if count != 8:
+        return lax.psum_scatter(partial, "wshard", scatter_dimension=0, tiled=True)
+    index = lax.axis_index("wshard")
+    rows = partial.shape[0] // count
+    total = None
+    for step in range(1, count // 2 + 1):
+        target = (index + count - 2 * step) % count
+        arrived = swap(take_block(partial, target ^ 1, rows), "wshard", 1)
+        mine = take_block(partial, target, rows).astype(jnp.float32)
+        mine = mine + arrived.astype(jnp.float32)
+        if total is not None:
+            mine = mine + lax.ppermute(total, "wshard", ring_route(count)).astype(jnp.float32)
+        total = low(mine)
+    return total
+
+
+def shard_total(values):
+    count = lax.axis_size("wshard")
+    mask = 1
+    while mask < count:
+        values = values + swap(values, "wshard", mask)
+        mask = 2 * mask
+    return values
+
+
+def pack_out(rows):
+    split = rows.reshape(-1, HEADDIM, 2, rows.shape[1] // 2)
+    return jnp.swapaxes(split, 1, 2).reshape(2 * rows.shape[0], rows.shape[1] // 2)
+
+
+def unpack_out(packed):
+    split = packed.reshape(-1, 2, HEADDIM, packed.shape[1])
+    return jnp.swapaxes(split, 1, 2).reshape(packed.shape[0] // 2, 2 * packed.shape[1])
 
 
 def gather_out(out_low, seq_index, groups):
@@ -684,28 +824,38 @@
     def heads_of(values, axis, width):
         return pick_heads(values, axis, width, seq_index, groups)
 
-    in_low = in_weight.astype(jnp.bfloat16)
-    in_mine = jnp.concatenate(
+    lanes = 128
+    channels = local_di + 2 * STATE
+    packs = out_weight.shape[0] == groups * HEADDIM
+    in_low = low(in_weight)
+    rest_mine = jnp.concatenate(
         [
-            heads_of(in_low[:, :DI], 1, HEADDIM),
             heads_of(in_low[:, DI : 2 * DI], 1, HEADDIM),
             in_low[:, 2 * DI : 2 * DI + 2 * STATE],
-            heads_of(in_low[:, DI + CONVCH :], 1, 1),
+            jnp.pad(heads_of(in_low[:, DI + CONVCH :], 1, 1), ((0, 0), (0, lanes - local_heads))),
         ],
         1,
     )
-    hidden_low = lax.all_gather(hidden_rows, "seq", axis=0, tiled=True)
-    in_mine = lax.all_gather(in_mine, "wshard", axis=0, tiled=True)
-    cot = lax.all_gather(cot_rows, "seq", axis=0, tiled=True)
-    out_mine = gather_out(out_weight.astype(jnp.bfloat16), seq_index, groups)
-    my_gain_two = heads_of(gain_two, 0, HEADDIM)
+    gate_mine = heads_of(in_low[:, :DI], 1, HEADDIM)
+    rest_weight = shard_gather(rest_mine)
+    hidden_low = seq_gather(hidden_rows)
+    if packs:
+        out_mine = pack_out(pick_rows(low(out_weight), seq_index, groups))
+        gate_out = lax.all_gather(
+            jnp.concatenate([gate_mine, out_mine], 1), "wshard", axis=0, tiled=True
+        )
+    else:
+        gate_out = jnp.concatenate(
+            [
+                lax.all_gather(gate_mine, "wshard", axis=0, tiled=True),
+                pack_out(gather_out(low(out_weight), seq_index, groups)),
+            ],
+            1,
+        )
+    cot = seq_gather(cot_rows)
+    my_gain_two = heads_of(gain_two, 0, HEADDIM)[None, :]
     my_kernel = jnp.concatenate([heads_of(kernel[:, :DI], 1, HEADDIM), kernel[:, DI:]], 1)
     my_bias = jnp.concatenate([heads_of(conv_bias[:DI], 0, HEADDIM), conv_bias[DI:]], 0)
-
-    lanes = 128
-    in_main = in_mine[:, : 2 * local_di + 2 * STATE]
-    dt_weight = jnp.pad(in_mine[:, 2 * local_di + 2 * STATE :], ((0, 0), (0, lanes - local_heads)))
-    my_skip = heads_of(d_skip, 0, 1)
 
     def on_lanes(values):
         return jnp.pad(values, (0, lanes - local_heads))[None, :]
@@ -713,37 +863,29 @@
     heads_vectors = (
         on_lanes(heads_of(a_log, 0, 1)),
         on_lanes(heads_of(dt_bias, 0, 1)),
-        jnp.repeat(my_skip, HEADDIM)[None, :],
+        jnp.repeat(heads_of(d_skip, 0, 1), HEADDIM)[None, :],
     )
     expand = (
         jnp.arange(lanes)[:, None] == jnp.arange(local_di)[None, :] // HEADDIM
     ).astype(jnp.float32)
-    (
-        normed_low,
-        gating,
-        conv_in,
-        conv_pre,
-        dt_raw,
-        y,
-        scanned,
-        states,
-        d_gnorm,
-        sums,
-    ) = run_forward(
+    normed_low, conv_in, conv_pre, dt_raw, y, scanned, states = run_forward(
         hidden_low,
-        cot,
-        in_main,
-        dt_weight,
-        out_mine,
-        (gain_one[None, :], my_gain_two[None, :]),
+        rest_weight,
+        gain_one[None, :],
         (my_kernel, my_bias[None, :]),
         heads_vectors,
         expand,
     )
-    sums = jnp.sum(lax.all_gather(sums[:2], "seq", axis=0, tiled=False), axis=0) / DI
+    gating, d_gnorm, sums = run_gate(normed_low, scanned, cot, gate_out, my_gain_two)
+    sums = sums[:2]
+    for mask in (1, 2) if groups == 4 else ():
+        sums = sums + swap(sums, "seq", mask)
+    if groups != 4:
+        sums = lax.psum(sums, "seq")
+    sums = sums / DI
     scale = lax.rsqrt(sums[0] + norm_eps)
     slope = scale * scale * sums[1]
-    block_part, d_gating, d_scanned, grad_out, grad_gate, d_gain_two = run_middle(
+    block_part, d_gating, d_scanned, grad_gate_out, d_gain_two = run_middle(
         scanned,
         gating,
         d_gnorm,
@@ -751,21 +893,11 @@
         normed_low,
         scale[:, None],
         slope[:, None],
-        out_mine,
-        my_gain_two[None, :],
-    )
-    block_out = hidden_rows.astype(jnp.float32) + seq_sum_rows(block_part)
-    (
-        d_normed_part,
-        grad_conv,
-        grad_dt,
-        d_gain_one,
-        d_kernel,
-        d_conv_bias,
-        d_skip_wide,
-        d_head,
-    ) = run_backward(
-        hidden_low,
+        gate_out,
+        my_gain_two,
+    )
+    block_out = hidden_rows.astype(jnp.float32) + seq_scatter(block_part)
+    d_rest, grad_rest, d_kernel, d_conv_bias, d_skip_wide, d_head = run_backward(
         normed_low,
         conv_in,
         conv_pre,
@@ -773,21 +905,13 @@
         y,
         states,
         d_scanned,
-        d_gating,
-        in_main,
-        dt_weight,
         my_kernel,
         heads_vectors,
         expand,
     )
-    d_gain_one = d_gain_one[0]
-    d_gain_two = d_gain_two[0]
-    d_conv_bias = d_conv_bias[0]
-    d_a_log = d_head[0, :local_heads]
-    d_dt_bias = d_head[1, :local_heads]
-    d_skip_part = jnp.sum(d_skip_wide.reshape(local_heads, HEADDIM), axis=1)
-    grad_in = jnp.concatenate([grad_gate, grad_conv, grad_dt[:, :local_heads]], 1)
-    d_normed = seq_sum_rows(d_normed_part)
+    rest_part = shard_scatter(grad_rest)
+    d_normed_part, d_gain_one = run_normed(hidden_low, d_gating, d_rest, gate_out, rest_weight)
+    d_normed = seq_scatter_near(d_normed_part)
     own_hidden = hidden_rows.astype(jnp.float32)
     own_scale = lax.rsqrt(jnp.mean(own_hidden * own_hidden, axis=-1, keepdims=True) + norm_eps)
     own_unit = own_hidden * own_scale
@@ -797,40 +921,76 @@
     )
     block_grad = cot_rows.astype(jnp.float32) + d_hidden
 
-    def spread_heads(values, axis, width):
-        here = (jnp.arange(groups) == seq_index).reshape((groups,) + (1,) * values.ndim)
-        return merge_heads(jnp.where(here, values[None], 0.0), axis, width)
-
-    vec_grad = jnp.concatenate(
+    d_skip_part = jnp.sum(d_skip_wide.reshape(local_heads, HEADDIM), axis=1)
+    shared = jnp.concatenate(
+        [d_gain_one[0], d_kernel[:, local_di:].reshape(-1), d_conv_bias[0, local_di:]]
+    )
+    apart = jnp.concatenate(
         [
-            d_gain_one,
-            spread_heads(d_gain_two, 0, HEADDIM),
+            d_gain_two[0],
+            d_kernel[:, :local_di].reshape(-1),
+            d_conv_bias[0, :local_di],
+            d_head[:, :local_heads].reshape(-1),
+            d_skip_part,
+        ]
+    )
+    vec_part = shard_total(jnp.concatenate([shared, apart]))
+    shared = vec_part[: shared.shape[0]]
+    every = seq_gather(vec_part[None, shared.shape[0] :])
+    for mask in (1, 2) if groups == 4 else ():
+        shared = shared + swap(shared, "seq", mask)
+    if groups != 4:
+        shared = lax.psum(shared, "seq")
+    kernel_end = local_di * (1 + WIDTH)
+    heads_at = kernel_end + local_di
+    both_kernel = D + 2 * STATE * WIDTH
+    vec_total = jnp.concatenate(
+        [
+            shared[:D],
+            merge_heads(every[:, :local_di], 0, HEADDIM),
             jnp.concatenate(
-                [spread_heads(d_kernel[:, :local_di], 1, HEADDIM), d_kernel[:, local_di:]], 1
+                [
+                    merge_heads(
+                        every[:, local_di:kernel_end].reshape(groups, WIDTH, local_di), 1, HEADDIM
+                    ),
+                    shared[D:both_kernel].reshape(WIDTH, 2 * STATE),
+                ],
+                1,
             ).reshape(-1),
-            spread_heads(d_conv_bias[:local_di], 0, HEADDIM),
-            d_conv_bias[local_di:],
-            spread_heads(d_a_log, 0, 1),
-            spread_heads(d_dt_bias, 0, 1),
-            spread_heads(d_skip_part, 0, 1),
+            merge_heads(every[:, kernel_end:heads_at], 0, HEADDIM),
+            shared[both_kernel:],
+            merge_heads(every[:, heads_at : heads_at + local_heads], 0, 1),
+            merge_heads(every[:, heads_at + local_heads : heads_at + 2 * local_heads], 0, 1),
+            merge_heads(every[:, heads_at + 2 * local_heads :], 0, 1),
         ]
     )
-    vec_total = lax.psum(vec_grad, ("seq", "wshard"))
     vec_first_new, vec_second_new, vec_weight_new = adamw_step(
         vec_weight, vec_first, vec_second, vec_total, vector_rate, 0.0
     )
-    out_total = sum_out_grad(grad_out, out_weight.shape[0], seq_index, groups)
-    in_part = lax.psum_scatter(
-        grad_in.astype(jnp.bfloat16), "wshard", scatter_dimension=0, tiled=True
-    )
-    in_every = lax.all_gather(in_part, "seq", axis=0, tiled=False).astype(jnp.float32)
-    both_end = 2 * local_di + 2 * STATE
+    rows_in = in_weight.shape[0]
+    if packs:
+        gate_out_part = lax.psum_scatter(grad_gate_out, "wshard", scatter_dimension=0, tiled=True)
+        gate_out_every = seq_gather(gate_out_part).reshape(groups, rows_in, -1)
+        gate_every = gate_out_every[:, :, :local_di]
+        out_total = unpack_out(
+            gate_out_every[:, :, local_di:].reshape(groups * rows_in, -1)
+        ).astype(jnp.float32)
+    else:
+        gate_part = lax.psum_scatter(
+            grad_gate_out[:, :local_di], "wshard", scatter_dimension=0, tiled=True
+        )
+        gate_every = lax.all_gather(gate_part, "seq", axis=0, tiled=False)
+        out_total = sum_out_grad(
+            unpack_out(grad_gate_out[:, local_di:]), out_weight.shape[0], seq_index, groups
+        )
+    rest_every = seq_gather(rest_part).reshape(groups, rows_in, -1).astype(jnp.float32)
+    both_total = jnp.sum(rest_every, axis=0)
     in_total = jnp.concatenate(
         [
-            merge_heads(in_every[:, :, :local_di], 1, HEADDIM),
-            merge_heads(in_every[:, :, local_di : 2 * local_di], 1, HEADDIM),
-            jnp.sum(in_every[:, :, 2 * local_di : both_end], axis=0),
-            merge_heads(in_every[:, :, both_end:], 1, 1),
+            merge_heads(gate_every.astype(jnp.float32), 1, HEADDIM),
+            merge_heads(rest_every[:, :, :local_di], 1, HEADDIM),
+            both_total[:, local_di:channels],
+            merge_heads(rest_every[:, :, channels : channels + local_heads], 1, 1),
         ],
         1,
     )

time: 484 us -> 261 us (0.54)
  waiting for transfers between devices: 308 us -> 79.3 us
  blocking collectives: 53.2 us -> 0 us
  starting transfers between devices: 0.35 us -> 29.8 us
  local copies, waits for them, and re-layouts: 21.5 us -> 46.4 us
  Pallas kernels: 61.1 us -> 67 us
    all_gather x5 -> x1, waiting for transfers between devices: 158 us -> 0.02 us  [shards(): lax.all_gather(jnp.concatenate([gate_mine, out_mine], 1), 'wshard', axis=...]
    reduce_scatter x4 -> x1, waiting for transfers between devices: 147 us -> 0.02 us  [shards(): lax.psum_scatter(grad_gate_out, 'wshard', scatter_dimension=0, tiled=True)]
    ppermute x0 -> x42, waiting for transfers between devices: none -> 79.2 us  [the longest x36 47.2 us: swap(): return lax.ppermute(values, axis, route)]
    psum x1 -> x0, blocking collectives: 40.2 us -> none  [shards(): vec_total = lax.psum(vec_grad, ('seq', 'wshard'))]
    ppermute x0 -> x42, starting transfers between devices: none -> 29.7 us  [the longest x36 26.7 us: swap(): return lax.ppermute(values, axis, route)]
    dynamic_update_slice x0 -> x26, local copies, waits for them, and re-layouts: none -> 17.8 us  [put_block(): lax.dynamic_update_slice_in_dim(buffer, block, index * block.shape[0], 0)]
    all_gather x2 -> x0, blocking collectives: 12.9 us -> none  [the longest x1 7.56 us: sum_out_grad(): every = lax.all_gather(mine, 'seq', axis=0, tiled=False)]
    pallas_call x2 -> x4, Pallas kernels: 51.1 us -> 57.1 us  [the longest x1 25.9 us: run_backward(): pl.pallas_call(backward_kernel, grid=(chunks,), in_specs=[back(D), back(c...]
  transfers between devices with their start and end apart: 9 -> 44, of which waited for: 9 -> 19; matrix products, arithmetic and copies ran while one was open for 4% -> 16% of each run, Pallas kernels for 0% -> 6%
where the time goes in v3:
time: 261 us; the launch traced here: 260 us
  waiting for transfers between devices  79.3 us (30%)
  Pallas kernels  67 us (26%)
  local copies, waits for them, and re-layouts  46.4 us (18%)
  starting transfers between devices  29.8 us (11%)
  other arithmetic  22.6 us (9%)
  between operations  15.1 us (6%)
    ppermute x36, waiting for transfers between devices, swap(): return lax.ppermute(values, axis, route)  47.2 us
    ppermute x36, starting transfers between devices, swap(): return lax.ppermute(values, axis, route)  26.7 us
    ppermute x3, waiting for transfers between devices, shard_scatter(): lax.ppermute(total, 'wshard', ring_route(count)).astype(jnp.float32)  26.6 us
    pallas_call x1, Pallas kernels, run_backward(): pl.pallas_call(backward_kernel, grid=(chunks,), in_specs=[back(D), back(c...  25.9 us
    dynamic_update_slice x26, local copies, waits for them, and re-layouts, put_block(): lax.dynamic_update_slice_in_dim(buffer, block, index * block.shape[0], 0)  17.8 us
    pallas_call x1, Pallas kernels, run_forward(): pl.pallas_call(forward_kernel, grid=(chunks,), in_specs=[wide(D), whole(D...  14.4 us
    pallas_call x1, Pallas kernels, run_middle(): pl.pallas_call(middle_kernel, grid=(length // BLOCK,), in_specs=[wide(loc...  9.96 us
    unnamed x58, local copies, waits for them, and re-layouts  9.65 us
  transfers between devices with their start and end apart: 44, of which 19 were waited for; matrix products, arithmetic and copies ran while one was open for 16% of the time, Pallas kernels for 6%

profile of v3, /device:TPU:0, one launch (start us, length us, event | category | flops | bytes accessed | tf_op | source)
XLA Modules:
  0.0 260.2 jit_solution(15545862996611383417)
XLA Ops:
  7.2 1.9 copy.97
  12.9 3.0 %collective-permute-start.3 = (bf16[128,896]{1,0:T(8,128)(2,1)}, bf16[128,896]{1,0:T(8,128)(2,1)}, u32[]{:S(2)}, u32[]{:S(2)}) collective-permute-start(bf16[128,896]{1,0:T(8,128)(2,1)} %get-tuple-element.83), channel_id=1, source_target_pairs={{0,1},{1,0},{2,3},{3,2},{4,5},{5,4},{6,7},{7,6},{8,9},{9,8},{10,11... | collective-permute-start | bytes 688136 | tf_op jit(solution)/shard_map/ppermute | solution.py:659
  26.7 1.7 constant_dynamic-update-slice_fusion.18
  28.3 4.8 %collective-permute-done.5 = bf16[128,896]{1,0:T(8,128)(2,1)} collective-permute-done((bf16[128,896]{1,0:T(8,128)(2,1)}, bf16[128,896]{1,0:T(8,128)(2,1)}, u32[]{:S(2)}, u32[]{:S(2)}) %collective-permute-start.5) | collective-permute-done | bytes 229408 | tf_op jit(solution)/shard_map/ppermute | solution.py:659
  33.1 1.6 constant_dynamic-update-slice_fusion.17
  34.8 3.0 %collective-permute-done.6 = bf16[128,896]{1,0:T(8,128)(2,1)S(1)} collective-permute-done((bf16[128,896]{1,0:T(8,128)(2,1)}, bf16[128,896]{1,0:T(8,128)(2,1)S(1)}, u32[]{:S(2)}, u32[]{:S(2)}) %collective-permute-start.6) | collective-permute-done | bytes 229408 | tf_op jit(solution)/shard_map/ppermute | solution.py:730
  38.9 1.7 constant_dynamic-update-slice_fusion.16
  41.4 1.7 collective-permute-done.11
  43.1 1.9 constant_dynamic-update-slice_fusion.22
  45.0 1.9 constant_dynamic-update-slice_fusion.21
  51.4 10.1 %collective-permute-done.9 = bf16[128,896]{1,0:T(8,128)(2,1)S(1)} collective-permute-done((bf16[128,896]{1,0:T(8,128)(2,1)S(1)}, bf16[128,896]{1,0:T(8,128)(2,1)S(1)}, u32[]{:S(2)}, u32[]{:S(2)}) %collective-permute-start.9) | collective-permute-done | bytes 229408 | tf_op jit(solution)/shard_map/ppermute | solution.py:659
  64.5 14.4 %forward.1 = (bf16[1024,1024]{1,0:T(8,128)(2,1)}, f32[1024,768]{1,0:T(8,128)}, f32[1024,768]{1,0:T(8,128)}, f32[1024,128]{1,0:T(8,128)S(1)}, f32[1024,512]{1,0:T...) custom-call(bf16[1024,1024]{1,0:T(8,128)(2,1)} %constant_dynamic-update-slice_fusion.20.hidden_ref, ...), custom_call_target="tpu_custom_call" | custom-call | flops 6000000000 | bytes 30000000 | tf_op jit(solution)/shard_map/forward/pallas_call | solution.py:439
  78.9 9.6 %gate.1 = (f32[1024,512]{1,0:T(8,128)S(1)}, f32[1024,512]{1,0:T(8,128)}, f32[8,1024]{1,0:T(8,128)S(1)}) custom-call(bf16[1024,1024]{1,0:T(8,128)(2,1)} %get-tuple-element.35.normed_ref, bf16[1024,512]{1,0:T(8,128)(2,1)S(1)} %get-tuple-element.34.scanned_ref, bf16[1024,1024]{1,0:T(8,128)(2,1)} %copy-done.6, ...), custom_call_target="tpu_custom_call" | custom-call | flops 2500000000 | bytes 12000000 | tf_op jit(solution)/shard_map/gate/pallas_call | solution.py:486
  92.5 2.1 collective-permute-done.14
  95.5 10.0 %middle.1 = (bf16[1024,1024]{1,0:T(8,128)(2,1)}, bf16[1024,512]{1,0:T(8,128)(2,1)S(1)}, bf16[1024,512]{1,0:T(8,128)(2,1)S(1)}, bf16[1024,1024]{1,0:T(8,128)(2,1)}, f32[1,512]{1,0:T(1,128)S(1)}) custom-call(bf16[1024,512]{1,0:T(8,128)(2,1)} %copy-done, f32[1024,512]{1,0:T(8,128)} %copy-done.1, f32[1024,512]{1,0:T(8,128)} %get-tuple-element.37.d_gnorm_ref, ...), custom_call_target="tpu_custom_call" | custom-call | flops 4000000000 | bytes 15000000 | tf_op jit(solution)/shard_map/middle/pallas_call | solution.py:518
  105.5 25.9 %backward.1 = (bf16[1024,896]{1,0:T(8,128)(2,1)}, bf16[1024,896]{1,0:T(8,128)(2,1)}, f32[4,768]{1,0:T(4,128)S(1)}, f32[1,768]{1,0:T(1,128)S(1)}, f32[1,512]{1,0:T(1,128)S(1)}, /*index=5*/f32[2,128]{1,0:T(2,128)S(1)}) custom-call(bf16[1024,1024]{1,0:T(8,128)(2,1)} %get-tuple-element.35.normed_ref, f32[1024,768]{1,0:T(8,128)} %get-tuple-element.41.conv_in_ref, ...), custom_call_target="tpu_custom_call" | custom-call | flops 14000000000 | bytes 40000000 | tf_op jit(solution)/shard_map/backward/pallas_call | solution.py:570
  134.3 7.3 %normed.1 = (bf16[1024,1024]{1,0:T(8,128)(2,1)}, f32[1,1024]{1,0:T(1,128)S(1)}) custom-call(bf16[1024,1024]{1,0:T(8,128)(2,1)} %constant_dynamic-update-slice_fusion.20.hidden_ref, bf16[1024,512]{1,0:T(8,128)(2,1)S(1)} %get-tuple-element.40.d_gating_ref, bf16[1024,896]{1,0:T(8,128)(2,1)S(1)} %copy-done.2, ...), custom_call_target="tpu_custom_call" | custom-call | flops 3000000000 | bytes 9000000 | tf_op jit(solution)/shard_map/normed/pallas_call | solution.py:618
  142.9 2.6 %collective-permute-done.34 = f32[5400]{0:T(1024)S(1)} collective-permute-done((f32[5400]{0:T(1024)S(1)}, f32[5400]{0:T(1024)S(1)}, u32[]{:S(2)}, u32[]{:S(2)}) %collective-permute-start.34) | collective-permute-done | bytes 21632 | tf_op jit(solution)/shard_map/ppermute | solution.py:659
  146.6 2.8 %collective-permute-done.35 = f32[5400]{0:T(1024)S(1)} collective-permute-done((f32[5400]{0:T(1024)S(1)}, f32[5400]{0:T(1024)S(1)}, u32[]{:S(2)}, u32[]{:S(2)}) %collective-permute-start.35) | collective-permute-done | bytes 21632 | tf_op jit(solution)/shard_map/ppermute | solution.py:659
  149.3 2.0 collective-permute-start.36
  154.5 2.5 constant_dynamic-slice_fusion.8
  165.2 1.7 add_convert_fusion.4
  169.4 12.5 %collective-permute-done.28 = bf16[128,896]{1,0:T(8,128)(2,1)} collective-permute-done((bf16[128,896]{1,0:T(8,128)(2,1)}, bf16[128,896]{1,0:T(8,128)(2,1)}, u32[]{:S(2)}, u32[]{:S(2)}) %collective-permute-start.28) | collective-permute-done | bytes 229408 | tf_op jit(solution)/shard_map/ppermute | solution.py:747
  185.8 7.1 %collective-permute-done.29 = bf16[128,896]{1,0:T(8,128)(2,1)S(1)} collective-permute-done((bf16[128,896]{1,0:T(8,128)(2,1)S(1)}, bf16[128,896]{1,0:T(8,128)(2,1)S(1)}, u32[]{:S(2)}, u32[]{:S(2)}) %collective-permute-start.29) | collective-permute-done | bytes 229408 | tf_op jit(solution)/shard_map/ppermute | solution.py:747
  196.4 7.0 %collective-permute-done.30 = bf16[128,896]{1,0:T(8,128)(2,1)S(1)} collective-permute-done((bf16[128,896]{1,0:T(8,128)(2,1)S(1)}, bf16[128,896]{1,0:T(8,128)(2,1)S(1)}, u32[]{:S(2)}, u32[]{:S(2)}) %collective-permute-start.30) | collective-permute-done | bytes 229408 | tf_op jit(solution)/shard_map/ppermute | solution.py:747
  207.3 3.2 %collective-permute-done.16 = bf16[256,1024]{1,0:T(8,128)(2,1)S(1)} collective-permute-done((bf16[256,1024]{1,0:T(8,128)(2,1)}, bf16[256,1024]{1,0:T(8,128)(2,1)S(1)}, u32[]{:S(2)}, u32[]{:S(2)}) %collective-permute-start.16) | collective-permute-done | bytes 524320 | tf_op jit(solution)/shard_map/ppermute | solution.py:659
  210.5 10.4 %collective-permute-done.17 = bf16[256,1024]{1,0:T(8,128)(2,1)S(1)} collective-permute-done((bf16[256,1024]{1,0:T(8,128)(2,1)}, bf16[256,1024]{1,0:T(8,128)(2,1)S(1)}, u32[]{:S(2)}, u32[]{:S(2)}) %collective-permute-start.17) | collective-permute-done | bytes 524320 | tf_op jit(solution)/shard_map/ppermute | solution.py:659
  220.9 3.7 %fusion.7 = (f32[1,256,1024]{2,1,0:T(8,128)}, f32[1,256,1024]{2,1,0:T(8,128)}) fusion(bf16[256,1024]{1,0:T(8,128)(2,1)S(1)} %collective-permute-done.20, bf16[256,1024]{1,0:T(8,128)(2,1)S(1)} %collective-permute-done.18, f32[256]{0:T(256)S(1)} %broadcast_multiply_fusion, f32[1024]{0:T(1024)S(1)} %slice.154, f32[256]{0:T(256)S(1)} %add_rsqrt_fusion, ...), kind=kLoop, calls=%fused_computation.15 | loop fusion | flops 5505024 | bytes 6821892 | tf_op jit(solution)/shard_map/reshape | solution.py:1005
  224.6 1.7 collective-permute-done.32
  232.5 4.0 %collective-permute-done.22 = bf16[128,1024]{1,0:T(8,128)(2,1)} collective-permute-done((bf16[128,1024]{1,0:T(8,128)(2,1)}, bf16[128,1024]{1,0:T(8,128)(2,1)}, u32[]{:S(2)}, u32[]{:S(2)}) %collective-permute-start.22) | collective-permute-done | bytes 262176 | tf_op jit(solution)/shard_map/ppermute | solution.py:659
  243.5 2.3 multiply_subtract_fusion.1
  247.6 5.8 %multiply_subtract_fusion = (f32[128,4384]{0,1:T(8,128)}, f32[128,4384]{0,1:T(8,128)}, f32[128,4384]{0,1:T(8,128)}) fusion(f32[128,4384]{0,1:T(8,128)S(1)} %copy-done.5, f32[128,32]{0,1:T(8,128)S(1)} %bitcast.120, f32[128,256]{0,1:T(8,128)S(1)} %copy.113, f32[128,2048]{0,1:T(8,128)S(1)} %bitcast.103, f32[128,2048]{0,1:T(8,128)S(1)} %bitcast.104, ...), kind=kLoop, calls=%fused_computation.3 | loop fusion | flops 10100736 | bytes 15712256 | tf_op jit(solution)/shard_map/sub | solution.py:639
  (283 shorter events, 73.4 us)
Async XLA Ops:
  7.2 71.7 %all-gather.2.cloned.1.call-start = ((), (), s32[]{:S(2)}) async-start(), calls=%async_computation.1 | async-start | bytes 2359296 | tf_op jit(solution)/shard_map/all_gather | solution.py:844
  12.9 13.4 %collective-permute-start.3 = (bf16[128,896]{1,0:T(8,128)(2,1)}, bf16[128,896]{1,0:T(8,128)(2,1)}, u32[]{:S(2)}, u32[]{:S(2)}) collective-permute-start(bf16[128,896]{1,0:T(8,128)(2,1)} %get-tuple-element.83), channel_id=1, source_target_pairs={{0,1},{1,0},{2,3},{3,2},{4,5},{5,4},{6,7},{7,6},{8,9},{9,8},{10,11... | collective-permute-start | bytes 688136 | tf_op jit(solution)/shard_map/ppermute | solution.py:659
  15.9 9.3 %collective-permute-start.4 = (bf16[128,896]{1,0:T(8,128)(2,1)}, bf16[128,896]{1,0:T(8,128)(2,1)}, u32[]{:S(2)}, u32[]{:S(2)}) collective-permute-start(bf16[128,896]{1,0:T(8,128)(2,1)} %get-tuple-element.83), channel_id=1, source_target_pairs={{0,2},{1,3},{2,4},{3,5},{4,6},{5,7},{6,0},{7,1},{8,10},{9,11},{10,... | collective-permute-start | bytes 688136 | tf_op jit(solution)/shard_map/ppermute | solution.py:730
  17.4 23.9 %collective-permute-start = (bf16[256,1024]{1,0:T(8,128)(2,1)S(1)}, bf16[256,1024]{1,0:T(8,128)(2,1)}, u32[]{:S(2)}, u32[]{:S(2)}) collective-permute-start(bf16[256,1024]{1,0:T(8,128)(2,1)S(1)} %bitcast.101), channel_id=1, source_target_pairs={{0,8},{8,0},{16,24},{24,16},{1,9},{9,1},{17,25},{25,17},{2,10},{10... | collective-permute-start | bytes 1572872 | tf_op jit(solution)/shard_map/ppermute | solution.py:659
  17.4 23.9 %collective-permute-start.1 = (bf16[256,1024]{1,0:T(8,128)(2,1)S(1)}, bf16[256,1024]{1,0:T(8,128)(2,1)}, u32[]{:S(2)}, u32[]{:S(2)}) collective-permute-start(bf16[256,1024]{1,0:T(8,128)(2,1)S(1)} %bitcast.102), channel_id=1, source_target_pairs={{0,16},{8,24},{16,0},{24,8},{1,17},{9,25},{17,1},{25,9},{2,18},{10... | collective-permute-start | bytes 1572872 | tf_op jit(solution)/shard_map/ppermute | solution.py:659
  19.0 24.1 %collective-permute-start.11 = (bf16[256,1024]{1,0:T(8,128)(2,1)}, bf16[256,1024]{1,0:T(8,128)(2,1)}, u32[]{:S(2)}, u32[]{:S(2)}) collective-permute-start(bf16[256,1024]{1,0:T(8,128)(2,1)} %bitcast.8), channel_id=1, source_target_pairs={{0,16},{8,24},{16,0},{24,8},{1,17},{9,25},{17,1},{25,9},{2,18},{10... | collective-permute-start | bytes 1572872 | tf_op jit(solution)/shard_map/ppermute | solution.py:659
  20.6 207.1 %reduce-scatter.2.cloned.1.call-start = ((), (), s32[]{:S(2)}) async-start(), calls=%async_computation.2 | async-start | bytes 2359296 | tf_op jit(solution)/shard_map/reduce_scatter | solution.py:972
  25.1 8.0 %collective-permute-start.5 = (bf16[128,896]{1,0:T(8,128)(2,1)}, bf16[128,896]{1,0:T(8,128)(2,1)}, u32[]{:S(2)}, u32[]{:S(2)}) collective-permute-start(bf16[128,896]{1,0:T(8,128)(2,1)} %collective-permute-done.4), channel_id=1, source_target_pairs={{0,1},{1,0},{2,3},{3,2},{4,5},{5,4},{6,7},{7,6},{8,9},{9,8},{10,11... | collective-permute-start | bytes 688136 | tf_op jit(solution)/shard_map/ppermute | solution.py:659
  26.3 11.5 %collective-permute-start.6 = (bf16[128,896]{1,0:T(8,128)(2,1)}, bf16[128,896]{1,0:T(8,128)(2,1)S(1)}, u32[]{:S(2)}, u32[]{:S(2)}) collective-permute-start(bf16[128,896]{1,0:T(8,128)(2,1)} %collective-permute-done.4), channel_id=1, source_target_pairs={{0,2},{1,3},{2,4},{3,5},{4,6},{5,7},{6,0},{7,1},{8,10},{9,11},{10,... | collective-permute-start | bytes 688136 | tf_op jit(solution)/shard_map/ppermute | solution.py:730
  33.1 13.8 %collective-permute-start.10 = (bf16[256,1024]{1,0:T(8,128)(2,1)}, bf16[256,1024]{1,0:T(8,128)(2,1)S(1)}, u32[]{:S(2)}, u32[]{:S(2)}) collective-permute-start(bf16[256,1024]{1,0:T(8,128)(2,1)} %bitcast.8), channel_id=1, source_target_pairs={{0,8},{8,0},{16,24},{24,16},{1,9},{9,1},{17,25},{25,17},{2,10},{10... | collective-permute-start | bytes 1572872 | tf_op jit(solution)/shard_map/ppermute | solution.py:659
  37.8 12.2 %collective-permute-start.7 = (bf16[128,896]{1,0:T(8,128)(2,1)S(1)}, bf16[128,896]{1,0:T(8,128)(2,1)S(1)}, u32[]{:S(2)}, u32[]{:S(2)}) collective-permute-start(bf16[128,896]{1,0:T(8,128)(2,1)S(1)} %collective-permute-done.6), channel_id=1, source_target_pairs={{0,1},{1,0},{2,3},{3,2},{4,5},{5,4},{6,7},{7,6},{8,9},{9,8},{10,11... | collective-permute-start | bytes 688136 | tf_op jit(solution)/shard_map/ppermute | solution.py:659
  41.3 7.8 %collective-permute-start.8 = (bf16[128,896]{1,0:T(8,128)(2,1)S(1)}, bf16[128,896]{1,0:T(8,128)(2,1)S(1)}, u32[]{:S(2)}, u32[]{:S(2)}) collective-permute-start(bf16[128,896]{1,0:T(8,128)(2,1)S(1)} %collective-permute-done.6), channel_id=1, source_target_pairs={{0,2},{1,3},{2,4},{3,5},{4,6},{5,7},{6,0},{7,1},{8,10},{9,11},{10,... | collective-permute-start | bytes 688136 | tf_op jit(solution)/shard_map/ppermute | solution.py:730
  41.3 21.0 %collective-permute-start.2 = (bf16[256,1024]{1,0:T(8,128)(2,1)}, bf16[256,1024]{1,0:T(8,128)(2,1)S(1)}, u32[]{:S(2)}, u32[]{:S(2)}) collective-permute-start(bf16[256,1024]{1,0:T(8,128)(2,1)} %collective-permute-done.1), channel_id=1, source_target_pairs={{0,8},{8,0},{16,24},{24,16},{1,9},{9,1},{17,25},{25,17},{2,10},{10... | collective-permute-start | bytes 1572872 | tf_op jit(solution)/shard_map/ppermute | solution.py:659
  43.1 20.0 %collective-permute-start.12 = (bf16[256,1024]{1,0:T(8,128)(2,1)}, bf16[256,1024]{1,0:T(8,128)(2,1)S(1)}, u32[]{:S(2)}, u32[]{:S(2)}) collective-permute-start(bf16[256,1024]{1,0:T(8,128)(2,1)} %collective-permute-done.11), channel_id=1, source_target_pairs={{0,8},{8,0},{16,24},{24,16},{1,9},{9,1},{17,25},{25,17},{2,10},{10... | collective-permute-start | bytes 1572872 | tf_op jit(solution)/shard_map/ppermute | solution.py:659
  49.1 12.4 %collective-permute-start.9 = (bf16[128,896]{1,0:T(8,128)(2,1)S(1)}, bf16[128,896]{1,0:T(8,128)(2,1)S(1)}, u32[]{:S(2)}, u32[]{:S(2)}) collective-permute-start(bf16[128,896]{1,0:T(8,128)(2,1)S(1)} %collective-permute-done.8), channel_id=1, source_target_pairs={{0,1},{1,0},{2,3},{3,2},{4,5},{5,4},{6,7},{7,6},{8,9},{9,8},{10,11... | collective-permute-start | bytes 688136 | tf_op jit(solution)/shard_map/ppermute | solution.py:659
  152.4 12.9 %collective-permute-start.27 = (bf16[128,896]{1,0:T(8,128)(2,1)}, bf16[128,896]{1,0:T(8,128)(2,1)S(1)}, u32[]{:S(2)}, u32[]{:S(2)}) collective-permute-start(bf16[128,896]{1,0:T(8,128)(2,1)} %get-tuple-element.74), channel_id=1, source_target_pairs={{0,1},{1,0},{2,3},{3,2},{4,5},{5,4},{6,7},{7,6},{8,9},{9,8},{10,11... | collective-permute-start | bytes 688136 | tf_op jit(solution)/shard_map/ppermute | solution.py:659
  152.8 15.8 %collective-permute-start.26 = (bf16[128,896]{1,0:T(8,128)(2,1)}, bf16[128,896]{1,0:T(8,128)(2,1)S(1)}, u32[]{:S(2)}, u32[]{:S(2)}) collective-permute-start(bf16[128,896]{1,0:T(8,128)(2,1)} %get-tuple-element.75), channel_id=1, source_target_pairs={{0,1},{1,0},{2,3},{3,2},{4,5},{5,4},{6,7},{7,6},{8,9},{9,8},{10,11... | collective-permute-start | bytes 688136 | tf_op jit(solution)/shard_map/ppermute | solution.py:659
  160.9 23.6 %collective-permute-start.25 = (bf16[128,896]{1,0:T(8,128)(2,1)}, bf16[128,896]{1,0:T(8,128)(2,1)}, u32[]{:S(2)}, u32[]{:S(2)}) collective-permute-start(bf16[128,896]{1,0:T(8,128)(2,1)} %get-tuple-element.76), channel_id=1, source_target_pairs={{0,1},{1,0},{2,3},{3,2},{4,5},{5,4},{6,7},{7,6},{8,9},{9,8},{10,11... | collective-permute-start | bytes 688136 | tf_op jit(solution)/shard_map/ppermute | solution.py:659
  162.0 33.1 %collective-permute-start.24 = (bf16[128,896]{1,0:T(8,128)(2,1)}, bf16[128,896]{1,0:T(8,128)(2,1)}, u32[]{:S(2)}, u32[]{:S(2)}) collective-permute-start(bf16[128,896]{1,0:T(8,128)(2,1)} %get-tuple-element.73), channel_id=1, source_target_pairs={{0,1},{1,0},{2,3},{3,2},{4,5},{5,4},{6,7},{7,6},{8,9},{9,8},{10,11... | collective-permute-start | bytes 688136 | tf_op jit(solution)/shard_map/ppermute | solution.py:659
  164.6 18.5 %collective-permute-start.19 = (bf16[256,1024]{1,0:T(8,128)(2,1)}, bf16[256,1024]{1,0:T(8,128)(2,1)}, u32[]{:S(2)}, u32[]{:S(2)}) collective-permute-start(bf16[256,1024]{1,0:T(8,128)(2,1)} %get-tuple-element.69), channel_id=1, source_target_pairs={{0,8},{8,0},{16,24},{24,16},{1,9},{9,1},{17,25},{25,17},{2,10},{10... | collective-permute-start | bytes 1572872 | tf_op jit(solution)/shard_map/ppermute | solution.py:659
  166.9 14.9 %collective-permute-start.28 = (bf16[128,896]{1,0:T(8,128)(2,1)}, bf16[128,896]{1,0:T(8,128)(2,1)}, u32[]{:S(2)}, u32[]{:S(2)}) collective-permute-start(bf16[128,896]{1,0:T(8,128)(2,1)} %add_convert_fusion.4), channel_id=1, source_target_pairs={{0,2},{1,3},{2,4},{3,5},{4,6},{5,7},{6,0},{7,1},{8,10},{9,11},{10,... | collective-permute-start | bytes 688136 | tf_op jit(solution)/shard_map/ppermute | solution.py:747
  169.3 35.3 %collective-permute-start.18 = (bf16[256,1024]{1,0:T(8,128)(2,1)}, bf16[256,1024]{1,0:T(8,128)(2,1)S(1)}, u32[]{:S(2)}, u32[]{:S(2)}) collective-permute-start(bf16[256,1024]{1,0:T(8,128)(2,1)} %get-tuple-element.68), channel_id=1, source_target_pairs={{0,8},{8,0},{16,24},{24,16},{1,9},{9,1},{17,25},{25,17},{2,10},{10... | collective-permute-start | bytes 1572872 | tf_op jit(solution)/shard_map/ppermute | solution.py:659
  181.8 25.5 %collective-permute-start.15 = (bf16[256,1024]{1,0:T(8,128)(2,1)}, bf16[256,1024]{1,0:T(8,128)(2,1)S(1)}, u32[]{:S(2)}, u32[]{:S(2)}) collective-permute-start(bf16[256,1024]{1,0:T(8,128)(2,1)} %get-tuple-element.70), channel_id=1, source_target_pairs={{0,8},{8,0},{16,24},{24,16},{1,9},{9,1},{17,25},{25,17},{2,10},{10... | collective-permute-start | bytes 1572872 | tf_op jit(solution)/shard_map/ppermute | solution.py:659
  183.1 9.8 %collective-permute-start.29 = (bf16[128,896]{1,0:T(8,128)(2,1)S(1)}, bf16[128,896]{1,0:T(8,128)(2,1)S(1)}, u32[]{:S(2)}, u32[]{:S(2)}) collective-permute-start(bf16[128,896]{1,0:T(8,128)(2,1)S(1)} %add_convert_fusion.3), channel_id=1, source_target_pairs={{0,2},{1,3},{2,4},{3,5},{4,6},{5,7},{6,0},{7,1},{8,10},{9,11},{10,... | collective-permute-start | bytes 688136 | tf_op jit(solution)/shard_map/ppermute | solution.py:747
  184.5 21.7 %collective-permute-start.20 = (bf16[256,1024]{1,0:T(8,128)(2,1)S(1)}, bf16[256,1024]{1,0:T(8,128)(2,1)S(1)}, u32[]{:S(2)}, u32[]{:S(2)}) collective-permute-start(bf16[256,1024]{1,0:T(8,128)(2,1)S(1)} %add_convert_fusion), channel_id=1, source_target_pairs={{0,16},{8,24},{16,0},{24,8},{1,17},{9,25},{17,1},{25,9},{2,18},{10... | collective-permute-start | bytes 1572872 | tf_op jit(solution)/shard_map/ppermute | solution.py:659
  194.1 9.3 %collective-permute-start.30 = (bf16[128,896]{1,0:T(8,128)(2,1)S(1)}, bf16[128,896]{1,0:T(8,128)(2,1)S(1)}, u32[]{:S(2)}, u32[]{:S(2)}) collective-permute-start(bf16[128,896]{1,0:T(8,128)(2,1)S(1)} %add_convert_fusion.2), channel_id=1, source_target_pairs={{0,2},{1,3},{2,4},{3,5},{4,6},{5,7},{6,0},{7,1},{8,10},{9,11},{10,... | collective-permute-start | bytes 688136 | tf_op jit(solution)/shard_map/ppermute | solution.py:747
  195.1 15.4 %collective-permute-start.16 = (bf16[256,1024]{1,0:T(8,128)(2,1)}, bf16[256,1024]{1,0:T(8,128)(2,1)S(1)}, u32[]{:S(2)}, u32[]{:S(2)}) collective-permute-start(bf16[256,1024]{1,0:T(8,128)(2,1)} %get-tuple-element.72), channel_id=1, source_target_pairs={{0,16},{8,24},{16,0},{24,8},{1,17},{9,25},{17,1},{25,9},{2,18},{10... | collective-permute-start | bytes 1572872 | tf_op jit(solution)/shard_map/ppermute | solution.py:659
  203.4 17.5 %collective-permute-start.17 = (bf16[256,1024]{1,0:T(8,128)(2,1)}, bf16[256,1024]{1,0:T(8,128)(2,1)S(1)}, u32[]{:S(2)}, u32[]{:S(2)}) collective-permute-start(bf16[256,1024]{1,0:T(8,128)(2,1)} %get-tuple-element.71), channel_id=1, source_target_pairs={{0,24},{8,16},{16,8},{24,0},{1,25},{9,17},{17,9},{25,1},{2,26},{10... | collective-permute-start | bytes 1572872 | tf_op jit(solution)/shard_map/ppermute | solution.py:659
  204.7 21.6 %collective-permute-start.31 = (bf16[128,896]{1,0:T(8,128)(2,1)S(1)}, bf16[128,896]{1,0:T(8,128)(2,1)S(1)}, u32[]{:S(2)}, u32[]{:S(2)}) collective-permute-start(bf16[128,896]{1,0:T(8,128)(2,1)S(1)} %get-tuple-element.67), channel_id=1, source_target_pairs={{0,8},{8,0},{16,24},{24,16},{1,9},{9,1},{17,25},{25,17},{2,10},{10... | collective-permute-start | bytes 688136 | tf_op jit(solution)/shard_map/ppermute | solution.py:659
  206.2 20.1 %collective-permute-start.32 = (bf16[128,896]{1,0:T(8,128)(2,1)S(1)}, bf16[128,896]{1,0:T(8,128)(2,1)S(1)}, u32[]{:S(2)}, u32[]{:S(2)}) collective-permute-start(bf16[128,896]{1,0:T(8,128)(2,1)S(1)} %get-tuple-element.67), channel_id=1, source_target_pairs={{0,16},{8,24},{16,0},{24,8},{1,17},{9,25},{17,1},{25,9},{2,18},{10... | collective-permute-start | bytes 688136 | tf_op jit(solution)/shard_map/ppermute | solution.py:659
  227.8 8.7 %collective-permute-start.22 = (bf16[128,1024]{1,0:T(8,128)(2,1)}, bf16[128,1024]{1,0:T(8,128)(2,1)}, u32[]{:S(2)}, u32[]{:S(2)}) collective-permute-start(bf16[128,1024]{1,0:T(8,128)(2,1)} %reduce-scatter.2.cloned.1.call-done), channel_id=1, source_target_pairs={{0,16},{8,24},{16,0},{24,8},{1,17},{9,25},{17,1},{25,9},{2,18},{10... | collective-permute-start | bytes 786440 | tf_op jit(solution)/shard_map/ppermute | solution.py:659
  232.3 5.3 %collective-permute-start.21 = (bf16[128,1024]{1,0:T(8,128)(2,1)}, bf16[128,1024]{1,0:T(8,128)(2,1)S(1)}, u32[]{:S(2)}, u32[]{:S(2)}) collective-permute-start(bf16[128,1024]{1,0:T(8,128)(2,1)} %reduce-scatter.2.cloned.1.call-done), channel_id=1, source_target_pairs={{0,8},{8,0},{16,24},{24,16},{1,9},{9,1},{17,25},{25,17},{2,10},{10... | collective-permute-start | bytes 786440 | tf_op jit(solution)/shard_map/ppermute | solution.py:659
  (41 other events, 233.8 us)
Sparse Core Ops, SparseCore 0:
  20.8 56.2 all-gather.1
  146.7 70.0 reduce-scatter.1

commit v4 on v3

--- a/solution.py
+++ b/solution.py
@@ -275,7 +275,6 @@
 
 
 def backward_kernel(
-    normed_ref,
     conv_in_ref,
     conv_pre_ref,
     dt_ref,
@@ -288,7 +287,6 @@
     skip_ref,
     expand_ref,
     d_rest_ref,
-    grad_ref,
     d_kernel_ref,
     d_conv_bias_ref,
     d_skip_ref,
@@ -296,7 +294,6 @@
     ext,
     d_state,
     later_state,
-    rest_sum,
 ):
     local_di = y_ref.shape[1]
     heads = local_di // HEADDIM
@@ -307,7 +304,6 @@
         ext[BLOCK : BLOCK + 8, :] = jnp.zeros((8, ext.shape[1]), jnp.float32)
         d_state[...] = jnp.zeros_like(d_state)
         later_state[...] = jnp.zeros_like(later_state)
-        rest_sum[...] = jnp.zeros_like(rest_sum)
         d_kernel_ref[...] = jnp.zeros_like(d_kernel_ref)
         d_conv_bias_ref[...] = jnp.zeros_like(d_conv_bias_ref)
         d_skip_ref[...] = jnp.zeros_like(d_skip_ref)
@@ -390,16 +386,30 @@
         d_conv_in = d_conv_in + conv_ref[tap : tap + 1, :] * moved
         d_kernel_ref[tap : tap + 1, :] += jnp.sum(moved * conv_in, axis=0, keepdims=True)
     ext[BLOCK : BLOCK + 8, :] = ext[0:8, :]
-    d_rest = jnp.concatenate([low(d_conv_in), low(d_dt)], 1)
-    d_rest_ref[...] = d_rest
-    rest_sum[...] += dot_tn(normed_ref[...], d_rest)
-
-    @pl.when(chunk == pl.num_programs(0) - 1)
+    d_rest_ref[...] = jnp.concatenate([low(d_conv_in), low(d_dt)], 1)
+
+
+def rest_kernel(normed_ref, d_rest_ref, grad_ref):
+    grad_ref[...] = low(dot_tn(normed_ref[...], d_rest_ref[...]))
+
+
+def normed_first_kernel(*refs):
+    @pl.when(pl.program_id(0) == 0)
     def _():
-        grad_ref[...] = low(rest_sum[...])
-
-
-def normed_kernel(
+        refs[-1][...] = jnp.zeros_like(refs[-1])
+
+    normed_part(*refs)
+
+
+def normed_kernel(*refs):
+    @pl.when(pl.program_id(0) == 0)
+    def _():
+        refs[-1][...] = refs[6][...]
+
+    normed_part(*refs[:5], *refs[7:])
+
+
+def normed_part(
     hidden_ref,
     d_gating_ref,
     d_rest_ref,
@@ -408,10 +418,6 @@
     d_normed_ref,
     d_gain_one_ref,
 ):
-    @pl.when(pl.program_id(0) == 0)
-    def _():
-        d_gain_one_ref[...] = jnp.zeros_like(d_gain_one_ref)
-
     d_normed = dot_nt(d_gating_ref[...], gate_weight_ref[...])
     d_normed = d_normed + dot_nt(d_rest_ref[...], rest_weight_ref[...])
     d_normed_ref[...] = low(d_normed)
@@ -425,11 +431,22 @@
     )
 
 
+def after(kernel, inputs, arrived):
+    def run(*refs):
+        kernel(*refs[:inputs], *refs[inputs + arrived :])
+
+    return run
+
+
+def anywhere(arrived):
+    return [pl.BlockSpec(memory_space=pl.ANY)] * len(arrived)
+
+
 def cost(flops, moved, transcendentals):
     return pl.CostEstimate(flops=flops, bytes_accessed=moved, transcendentals=transcendentals)
 
 
-def run_forward(hidden, rest_weight, gain_one, conv, heads_vectors, expand):
+def run_forward(hidden, rest_weight, gain_one, conv, heads_vectors, expand, arrived):
     length = hidden.shape[0]
     chunks = length // BLOCK
     lanes, local_di = expand.shape
@@ -437,7 +454,7 @@
     shape = jax.ShapeDtypeStruct
     f32, bf16 = jnp.float32, jnp.bfloat16
     return pl.pallas_call(
-        forward_kernel,
+        after(forward_kernel, 10, len(arrived)),
         grid=(chunks,),
         in_specs=[
             wide(D),
@@ -450,7 +467,8 @@
             whole(1, lanes),
             whole(1, local_di),
             whole(lanes, local_di),
-        ],
+        ]
+        + anywhere(arrived),
         out_specs=[
             wide(D),
             wide(channels),
@@ -476,7 +494,7 @@
         compiler_params=kernel_params(),
         cost_estimate=cost(6_000_000_000, 30_000_000, 8_000_000),
         name="forward",
-    )(hidden, rest_weight, rest_weight, gain_one, *conv, *heads_vectors, expand)
+    )(hidden, rest_weight, rest_weight, gain_one, *conv, *heads_vectors, expand, *arrived)
 
 
 def run_gate(normed, scanned, cot, gate_out, gain_two):
@@ -555,7 +573,7 @@
 
 
 def run_backward(
-    normed, conv_in, conv_pre, dt_raw, y, states, d_scanned, kernel, heads_vectors, expand
+    conv_in, conv_pre, dt_raw, y, states, d_scanned, kernel, heads_vectors, expand
 ):
     length, local_di = y.shape
     chunks = length // BLOCK
@@ -571,7 +589,6 @@
         backward_kernel,
         grid=(chunks,),
         in_specs=[
-            back(D),
             back(channels),
             back(channels),
             back(lanes),
@@ -586,7 +603,6 @@
         ],
         out_specs=[
             back(channels + lanes),
-            whole(D, channels + lanes),
             whole(WIDTH, channels),
             whole(1, channels),
             whole(1, local_di),
@@ -594,7 +610,6 @@
         ],
         out_shape=[
             shape((length, channels + lanes), bf16),
-            shape((D, channels + lanes), bf16),
             shape((WIDTH, channels), f32),
             shape((1, channels), f32),
             shape((1, local_di), f32),
@@ -604,30 +619,55 @@
             pltpu.VMEM((BLOCK + 8, channels), f32),
             pltpu.VMEM((STATE, local_di), f32),
             pltpu.VMEM((STATE, local_di), f32),
-            pltpu.VMEM((D, channels + lanes), f32),
         ],
         compiler_params=kernel_params(),
         cost_estimate=cost(14_000_000_000, 40_000_000, 10_000_000),
         name="backward",
-    )(normed, conv_in, conv_pre, dt_raw, y, states, d_scanned, kernel, *heads_vectors, expand)
-
-
-def run_normed(hidden, d_gating, d_rest, gate_out, rest_weight):
+    )(conv_in, conv_pre, dt_raw, y, states, d_scanned, kernel, *heads_vectors, expand)
+
+
+def run_rest(normed, d_rest, arrived):
+    length, rest = d_rest.shape
+    rows = D // 4
+    return pl.pallas_call(
+        after(rest_kernel, 2, len(arrived)),
+        grid=(4,),
+        in_specs=[pl.BlockSpec((length, rows), lambda q: (0, q)), whole(length, rest)]
+        + anywhere(arrived),
+        out_specs=pl.BlockSpec((rows, rest), lambda q: (q, 0)),
+        out_shape=jax.ShapeDtypeStruct((D, rest), jnp.bfloat16),
+        compiler_params=kernel_params(),
+        cost_estimate=cost(2_000_000_000, 6_000_000, 0),
+        name="rest",
+    )(normed, d_rest, *arrived)
+
+
+def run_normed(hidden, d_gating, d_rest, gate_out, rest_weight, before, arrived):
     length, local_di = d_gating.shape
     rest = d_rest.shape[1]
+    chunks = length // BLOCK // 2
+    first = 0 if not before else chunks
+
+    def part(extent):
+        return pl.BlockSpec((BLOCK, extent), lambda q: (q + first, 0))
+
+    kernel = normed_kernel if before else normed_first_kernel
     return pl.pallas_call(
-        normed_kernel,
-        grid=(length // BLOCK,),
-        in_specs=[wide(D), wide(local_di), wide(rest), whole(D, local_di), whole(D, rest)],
-        out_specs=[wide(D), whole(1, D)],
+        after(kernel, 5 + len(before), len(arrived)),
+        grid=(chunks,),
+        in_specs=[part(D), part(local_di), part(rest), whole(D, local_di), whole(D, rest)]
+        + [pl.BlockSpec(memory_space=pl.ANY), whole(1, D)][: len(before)]
+        + anywhere(arrived),
+        out_specs=[part(D), whole(1, D)],
         out_shape=[
             jax.ShapeDtypeStruct((length, D), jnp.bfloat16),
             jax.ShapeDtypeStruct((1, D), jnp.float32),
         ],
+        input_output_aliases={5: 0} if before else {},
         compiler_params=kernel_params(),
-        cost_estimate=cost(3_000_000_000, 9_000_000, 1000),
+        cost_estimate=cost(1_500_000_000, 6_000_000, 1000),
         name="normed",
-    )(hidden, d_gating, d_rest, gate_out, rest_weight)
+    )(hidden, d_gating, d_rest, gate_out, rest_weight, *before, *arrived)
 
 
 def adamw_step(weight, first, second, grad, rate, decay):
@@ -663,12 +703,12 @@
     return lax.dynamic_update_slice_in_dim(buffer, block, index * block.shape[0], 0)
 
 
-def seq_gather(rows):
+def seq_gather(rows, far=None):
     count = lax.axis_size("seq")
     if count != 4:
         return lax.all_gather(rows, "seq", axis=0, tiled=True)
     index = lax.axis_index("seq")
-    far = swap(rows, "seq", 2)
+    far = swap(rows, "seq", 2) if far is None else far
     blocks = [rows, swap(rows, "seq", 1), far, swap(far, "seq", 1)]
     result = jnp.zeros((count * rows.shape[0],) + rows.shape[1:], rows.dtype)
     for mask, block in enumerate(blocks):
@@ -680,82 +720,184 @@
     return lax.dynamic_slice_in_dim(values, index * rows, rows, 0)
 
 
-def seq_scatter(partial):
+def seq_pieces(partial):
+    index = lax.axis_index("seq")
     count = lax.axis_size("seq")
-    if count != 4:
-        return lax.psum_scatter(partial, "seq", scatter_dimension=0, tiled=True).astype(
-            jnp.float32
-        )
-    index = lax.axis_index("seq")
     rows = partial.shape[0] // count
-    total = take_block(partial, index, rows).astype(jnp.float32)
-    for mask in range(1, count):
-        piece = swap(take_block(partial, index ^ mask, rows), "seq", mask)
+    return [
+        swap(take_block(partial, index ^ mask, rows), "seq", mask) for mask in range(1, count)
+    ]
+
+
+def seq_scatter(partial, pieces):
+    rows = partial.shape[0] // lax.axis_size("seq")
+    total = take_block(partial, lax.axis_index("seq"), rows).astype(jnp.float32)
+    for piece in pieces:
         total = total + piece.astype(jnp.float32)
     return total
 
 
-def seq_scatter_near(partial):
+def near_first(partial):
     count = lax.axis_size("seq")
-    if count != 4:
-        return seq_scatter(partial)
-    index = lax.axis_index("seq")
+    parity = lax.axis_index("seq") % 2
     rows = partial.shape[0] // count
-
-    def near(mask):
-        arrived = swap(take_block(partial, index ^ 1 ^ mask, rows), "seq", 1)
-        mine = take_block(partial, index ^ mask, rows)
-        return arrived.astype(jnp.float32) + mine.astype(jnp.float32)
-
-    far = swap(low(near(2)), "seq", 2)
-    return near(0) + far.astype(jnp.float32)
+    split = partial.reshape(count // 2, 2, rows, partial.shape[1])
+
+    def half(parity):
+        chosen = lax.dynamic_index_in_dim(split, parity, 1, keepdims=False)
+        return chosen.reshape(count // 2 * rows, partial.shape[1])
+
+    return half(parity), swap(half(1 - parity), "seq", 1)
+
+
+def far_piece(mine, arrived):
+    other = 1 - lax.axis_index("seq") // 2
+    rows = mine.shape[0] // 2
+    total = take_block(mine, other, rows).astype(jnp.float32)
+    return swap(low(total + take_block(arrived, other, rows).astype(jnp.float32)), "seq", 2)
+
+
+def near_sum(mine, arrived, far):
+    here = lax.axis_index("seq") // 2
+    rows = mine.shape[0] // 2
+    total = take_block(mine, here, rows).astype(jnp.float32)
+    total = total + take_block(arrived, here, rows).astype(jnp.float32)
+    return total + far.astype(jnp.float32)
 
 
 def ring_route(count):
     return [(i, (i + 2) % count) for i in range(count)]
 
 
-def shard_gather(rows):
+def shard_gather(rows, late=0):
     count = lax.axis_size("wshard")
     if count != 8:
-        return lax.all_gather(rows, "wshard", axis=0, tiled=True)
+        return lax.all_gather(rows, "wshard", axis=0, tiled=True), [], []
     index = lax.axis_index("wshard")
     result = jnp.zeros((count * rows.shape[0],) + rows.shape[1:], rows.dtype)
     held = rows
+    blocks = []
+    missing = []
     for step in range(count // 2):
         source = (index + count - 2 * step) % count
+        swapped = swap(held, "wshard", 1)
         result = put_block(result, held, source)
-        result = put_block(result, swap(held, "wshard", 1), source ^ 1)
+        blocks = blocks + [held]
+        if step < count // 2 - late:
+            result = put_block(result, swapped, source ^ 1)
+            blocks = blocks + [swapped]
+        else:
+            missing = missing + [(source ^ 1, swapped)]
         if step < count // 2 - 1:
             held = lax.ppermute(held, "wshard", ring_route(count))
-    return result
-
-
-def shard_scatter(partial):
+    return result, blocks, missing
+
+
+def add_kernel(target_ref, mine_ref, *refs):
+    total = mine_ref[...].astype(jnp.float32)
+    for ref in refs[:-1]:
+        total = total + ref[...].astype(jnp.float32)
+    refs[-1][...] = low(total)
+
+
+def add_block(partial, target, pieces, arrived):
+    rows, columns = pieces[0].shape
+    spec = pl.BlockSpec((rows, columns), lambda q, target_ref: (0, 0))
+    return pl.pallas_call(
+        after(add_kernel, 2 + len(pieces), len(arrived)),
+        grid_spec=pltpu.PrefetchScalarGridSpec(
+            num_scalar_prefetch=1,
+            grid=(1,),
+            in_specs=[pl.BlockSpec((rows, columns), lambda q, target_ref: (target_ref[0], 0))]
+            + [spec] * len(pieces)
+            + anywhere(arrived),
+            out_specs=spec,
+        ),
+        out_shape=jax.ShapeDtypeStruct((rows, columns), jnp.bfloat16),
+        compiler_params=kernel_params(),
+        cost_estimate=cost(200_000, 900_000, 0),
+        name="add",
+    )(jnp.reshape(target, (1,)).astype(jnp.int32), partial, *pieces, *arrived)
+
+
+def place_kernel(target_ref, first_ref, second_ref, whole_ref, result_ref):
+    result_ref[...] = jnp.where(pl.program_id(0) == 0, first_ref[...], second_ref[...])
+
+
+def place_blocks(whole_array, targets, first, second, arrived):
+    rows, columns = first.shape
+    spec = pl.BlockSpec((rows, columns), lambda q, target_ref: (0, 0))
+    return pl.pallas_call(
+        after(place_kernel, 4, len(arrived)),
+        grid_spec=pltpu.PrefetchScalarGridSpec(
+            num_scalar_prefetch=1,
+            grid=(2,),
+            in_specs=[spec, spec, pl.BlockSpec(memory_space=pl.ANY)] + anywhere(arrived),
+            out_specs=pl.BlockSpec((rows, columns), lambda q, target_ref: (target_ref[q], 0)),
+        ),
+        out_shape=jax.ShapeDtypeStruct(whole_array.shape, whole_array.dtype),
+        input_output_aliases={3: 0},
+        compiler_params=kernel_params(),
+        cost_estimate=cost(1000, 1_000_000, 0),
+        name="place",
+    )(jnp.stack(targets).astype(jnp.int32), first, second, whole_array, *arrived)
+
+
+def sum_kernel(*refs):
+    total = refs[0][...]
+    for ref in refs[1:-1]:
+        total = total + ref[...]
+    refs[-1][...] = total
+
+
+def sum_after(terms, arrived):
+    return pl.pallas_call(
+        after(sum_kernel, len(terms), len(arrived)),
+        in_specs=[pl.BlockSpec(memory_space=pltpu.VMEM)] * len(terms) + anywhere(arrived),
+        out_specs=pl.BlockSpec(memory_space=pltpu.VMEM),
+        out_shape=jax.ShapeDtypeStruct(terms[0].shape, terms[0].dtype),
+        compiler_params=pltpu.CompilerParams(vmem_limit_bytes=50 * 1024 * 1024),
+        cost_estimate=cost(10_000, 60_000, 0),
+        name="sum",
+    )(*terms, *arrived)
+
+
+def ring_target(step):
     count = lax.axis_size("wshard")
-    if count != 8:
-        return lax.psum_scatter(partial, "wshard", scatter_dimension=0, tiled=True)
+    return (lax.axis_index("wshard") + count - 2 * step) % count
+
+
+def ring_swap(partial, step):
+    rows = partial.shape[0] // lax.axis_size("wshard")
+    return swap(take_block(partial, ring_target(step) ^ 1, rows), "wshard", 1)
+
+
+def ring_step(held):
+    return lax.ppermute(held, "wshard", ring_route(lax.axis_size("wshard")))
+
+
+def y_first(partial):
+    count = lax.axis_size("wshard")
+    parity = lax.axis_index("wshard") % 2
+    rows = partial.shape[0] // count
+    split = partial.reshape(count // 2, 2, rows, partial.shape[1])
+
+    def half(parity):
+        chosen = lax.dynamic_index_in_dim(split, parity, 1, keepdims=False)
+        return chosen.reshape(count // 2 * rows, partial.shape[1])
+
+    arrived = swap(half(1 - parity), "wshard", 1)
+    return half(parity), arrived
+
+
+def z_pieces(paired):
+    count = lax.axis_size("wshard")
     index = lax.axis_index("wshard")
-    rows = partial.shape[0] // count
-    total = None
-    for step in range(1, count // 2 + 1):
-        target = (index + count - 2 * step) % count
-        arrived = swap(take_block(partial, target ^ 1, rows), "wshard", 1)
-        mine = take_block(partial, target, rows).astype(jnp.float32)
-        mine = mine + arrived.astype(jnp.float32)
-        if total is not None:
-            mine = mine + lax.ppermute(total, "wshard", ring_route(count)).astype(jnp.float32)
-        total = low(mine)
-    return total
-
-
-def shard_total(values):
-    count = lax.axis_size("wshard")
-    mask = 1
-    while mask < count:
-        values = values + swap(values, "wshard", mask)
-        mask = 2 * mask
-    return values
+    rows = paired.shape[0] // (count // 2)
+    return [
+        swap(take_block(paired, (index ^ mask) // 2, rows), "wshard", mask)
+        for mask in range(2, count, 2)
+    ]
 
 
 def pack_out(rows):
@@ -826,7 +968,7 @@
 
     lanes = 128
     channels = local_di + 2 * STATE
-    packs = out_weight.shape[0] == groups * HEADDIM
+    packs = out_weight.shape[0] == groups * HEADDIM and lax.axis_size("wshard") == 8
     in_low = low(in_weight)
     rest_mine = jnp.concatenate(
         [
@@ -837,14 +979,13 @@
         1,
     )
     gate_mine = heads_of(in_low[:, :DI], 1, HEADDIM)
-    rest_weight = shard_gather(rest_mine)
+    rest_weight, _, _ = shard_gather(rest_mine)
     hidden_low = seq_gather(hidden_rows)
     if packs:
         out_mine = pack_out(pick_rows(low(out_weight), seq_index, groups))
-        gate_out = lax.all_gather(
-            jnp.concatenate([gate_mine, out_mine], 1), "wshard", axis=0, tiled=True
-        )
+        gate_out, arrived, late = shard_gather(jnp.concatenate([gate_mine, out_mine], 1), 2)
     else:
+        arrived = []
         gate_out = jnp.concatenate(
             [
                 lax.all_gather(gate_mine, "wshard", axis=0, tiled=True),
@@ -875,7 +1016,12 @@
         (my_kernel, my_bias[None, :]),
         heads_vectors,
         expand,
-    )
+        arrived,
+    )
+    if packs:
+        gate_out = place_blocks(
+            gate_out, [late[0][0], late[1][0]], late[0][1], late[1][1], [scanned]
+        )
     gating, d_gnorm, sums = run_gate(normed_low, scanned, cot, gate_out, my_gain_two)
     sums = sums[:2]
     for mask in (1, 2) if groups == 4 else ():
@@ -896,9 +1042,18 @@
         gate_out,
         my_gain_two,
     )
-    block_out = hidden_rows.astype(jnp.float32) + seq_scatter(block_part)
-    d_rest, grad_rest, d_kernel, d_conv_bias, d_skip_wide, d_head = run_backward(
-        normed_low,
+    if groups == 4:
+        block_near = near_first(block_part)
+        early = [block_near[1]]
+    else:
+        block_rows = seq_scatter(block_part, seq_pieces(block_part))
+        early = []
+    if packs:
+        grad_gate, grad_out = grad_gate_out[:, :local_di], grad_gate_out[:, local_di:]
+        gate_pieces = z_pieces(grad_gate)
+        out_mine, out_arrived = y_first(grad_out)
+        early = early + gate_pieces + [out_arrived]
+    d_rest, d_kernel, d_conv_bias, d_skip_wide, d_head = run_backward(
         conv_in,
         conv_pre,
         dt_raw,
@@ -909,22 +1064,30 @@
         heads_vectors,
         expand,
     )
-    rest_part = shard_scatter(grad_rest)
-    d_normed_part, d_gain_one = run_normed(hidden_low, d_gating, d_rest, gate_out, rest_weight)
-    d_normed = seq_scatter_near(d_normed_part)
-    own_hidden = hidden_rows.astype(jnp.float32)
-    own_scale = lax.rsqrt(jnp.mean(own_hidden * own_hidden, axis=-1, keepdims=True) + norm_eps)
-    own_unit = own_hidden * own_scale
-    d_own = d_normed * gain_one[None, :]
-    d_hidden = own_scale * (
-        d_own - own_unit * jnp.mean(d_own * own_unit, axis=-1, keepdims=True)
-    )
-    block_grad = cot_rows.astype(jnp.float32) + d_hidden
-
-    d_skip_part = jnp.sum(d_skip_wide.reshape(local_heads, HEADDIM), axis=1)
+    grad_rest = run_rest(normed_low, d_rest, early)
+    before_normed = [grad_rest]
+    between_normed = []
+    if packs:
+        gate_paired = add_block(
+            grad_gate, lax.axis_index("wshard") // 2, gate_pieces, [grad_rest]
+        )
+        out_paired = add_block(out_mine, jnp.int32(0), [out_arrived], [grad_rest])
+        rest_swaps = [ring_swap(grad_rest, 1)]
+        held = add_block(grad_rest, ring_target(1), rest_swaps, [gate_paired, out_paired])
+        before_normed = [held]
+        ring_arrived = ring_step(held)
+        rest_swaps = [ring_swap(grad_rest, 2)]
+        between_normed = [ring_arrived] + rest_swaps
+    normed_half = run_normed(
+        hidden_low, d_gating, d_rest, gate_out, rest_weight, [], before_normed
+    )
+    d_normed_part, d_gain_one = run_normed(
+        hidden_low, d_gating, d_rest, gate_out, rest_weight, normed_half, between_normed
+    )
     shared = jnp.concatenate(
         [d_gain_one[0], d_kernel[:, local_di:].reshape(-1), d_conv_bias[0, local_di:]]
     )
+    d_skip_part = jnp.sum(d_skip_wide.reshape(local_heads, HEADDIM), axis=1)
     apart = jnp.concatenate(
         [
             d_gain_two[0],
@@ -934,13 +1097,67 @@
             d_skip_part,
         ]
     )
-    vec_part = shard_total(jnp.concatenate([shared, apart]))
-    shared = vec_part[: shared.shape[0]]
-    every = seq_gather(vec_part[None, shared.shape[0] :])
-    for mask in (1, 2) if groups == 4 else ():
-        shared = shared + swap(shared, "seq", mask)
-    if groups != 4:
-        shared = lax.psum(shared, "seq")
+    vec_part = jnp.concatenate([shared, apart])[None]
+    if packs:
+        out_pieces = z_pieces(out_paired)
+        shard_rows = gate_paired.shape[0] // 2
+        parity = lax.axis_index("wshard") % 2
+        gate_arrived = swap(take_block(gate_paired, 1 - parity, shard_rows), "wshard", 1)
+        vec_swap = swap(vec_part, "wshard", 1)
+        block_far = far_piece(*block_near)
+        near = near_first(d_normed_part)
+        pieces = rest_swaps + [ring_arrived]
+        rest_swaps = [ring_swap(grad_rest, 3)]
+        held = add_block(
+            grad_rest,
+            ring_target(2),
+            pieces,
+            out_pieces + [gate_arrived, vec_swap, near[1]] + rest_swaps,
+        )
+        gate_part = add_block(gate_paired, parity, [gate_arrived], [held])
+        out_part = add_block(
+            out_paired, lax.axis_index("wshard") // 2, out_pieces, [held]
+        )
+        gate_out_part = jnp.concatenate([gate_part, out_part], 1)
+        gate_out_far = swap(gate_out_part, "seq", 2)
+        vec_part = sum_after([vec_part, vec_swap], [held])
+        vec_swap = swap(vec_part, "wshard", 2)
+        pieces = rest_swaps + [ring_step(held)]
+        rest_swaps = [ring_swap(grad_rest, 4)]
+        held = add_block(
+            grad_rest, ring_target(3), pieces, [vec_swap, block_far] + rest_swaps
+        )
+        vec_part = sum_after([vec_part, vec_swap], [held])
+        vec_swap = swap(vec_part, "wshard", 4)
+        far = far_piece(*near)
+        pieces = rest_swaps + [ring_step(held)]
+        rest_part = add_block(
+            grad_rest, ring_target(4), pieces, [vec_swap, far, gate_out_far]
+        )
+        vec_part = sum_after([vec_part, vec_swap], [rest_part])
+        block_rows = near_sum(*block_near, block_far)
+        d_normed = near_sum(*near, far)
+    else:
+        if groups == 4:
+            block_rows = near_sum(*block_near, far_piece(*block_near))
+        rest_part = lax.psum_scatter(grad_rest, "wshard", scatter_dimension=0, tiled=True)
+        vec_part = lax.psum(vec_part, "wshard")
+        d_normed = seq_scatter(d_normed_part, seq_pieces(d_normed_part))
+    block_out = hidden_rows.astype(jnp.float32) + block_rows
+    own_hidden = hidden_rows.astype(jnp.float32)
+    own_scale = lax.rsqrt(jnp.mean(own_hidden * own_hidden, axis=-1, keepdims=True) + norm_eps)
+    own_unit = own_hidden * own_scale
+    d_own = d_normed * gain_one[None, :]
+    d_hidden = own_scale * (
+        d_own - own_unit * jnp.mean(d_own * own_unit, axis=-1, keepdims=True)
+    )
+    block_grad = cot_rows.astype(jnp.float32) + d_hidden
+
+    every = seq_gather(vec_part)
+    shared, every = (
+        jnp.sum(every[:, : shared.shape[0]], axis=0),
+        every[:, shared.shape[0] :],
+    )
     kernel_end = local_di * (1 + WIDTH)
     heads_at = kernel_end + local_di
     both_kernel = D + 2 * STATE * WIDTH
@@ -969,8 +1186,7 @@
     )
     rows_in = in_weight.shape[0]
     if packs:
-        gate_out_part = lax.psum_scatter(grad_gate_out, "wshard", scatter_dimension=0, tiled=True)
-        gate_out_every = seq_gather(gate_out_part).reshape(groups, rows_in, -1)
+        gate_out_every = seq_gather(gate_out_part, gate_out_far).reshape(groups, rows_in, -1)
         gate_every = gate_out_every[:, :, :local_di]
         out_total = unpack_out(
             gate_out_every[:, :, local_di:].reshape(groups * rows_in, -1)

time: 261 us -> 279 us (1.069)
  waiting for transfers between devices: 79.3 us -> 49.5 us
  local copies, waits for them, and re-layouts: 46.4 us -> 75.8 us
  starting transfers between devices: 29.8 us -> 45.9 us
  Pallas kernels: 67 us -> 80.4 us
  between operations: 15.1 us -> 2.11 us
    ppermute x3, waiting for transfers between devices: 26.6 us -> 2.76 us  [ring_step(): return lax.ppermute(held, 'wshard', ring_route(lax.axis_size('wshard')))]
    ppermute x36 -> x44, waiting for transfers between devices: 47.2 us -> 32.6 us  [swap(): return lax.ppermute(values, axis, route)]
    pallas_call x3 -> x17, Pallas kernels: 47.5 us -> 61.5 us  [the longest x1 25.6 us: run_backward(): pl.pallas_call(backward_kernel, grid=(chunks,), in_specs=[back(channels),...]
    ppermute x36 -> x44, starting transfers between devices: 26.7 us -> 39 us  [swap(): return lax.ppermute(values, axis, route)]
    ppermute x3 -> x6, waiting for transfers between devices: 5.44 us -> 14.1 us  [shard_gather(): held = lax.ppermute(held, 'wshard', ring_route(count))]
    dynamic_slice x0 -> x3, local copies, waits for them, and re-layouts: none -> 5.25 us  [half(): chosen = lax.dynamic_index_in_dim(split, parity, 1, keepdims=False)]
    unnamed x58 -> x158, local copies, waits for them, and re-layouts: 9.65 us -> 14.2 us
    ppermute x3 -> x6, starting transfers between devices: 2 us -> 5.53 us  [shard_gather(): held = lax.ppermute(held, 'wshard', ring_route(count))]
  transfers between devices with their start and end apart: 44 -> 53, of which waited for: 19 -> 16; matrix products, arithmetic and copies ran while one was open for 16% -> 19% of each run, Pallas kernels for 6% -> 18%
where the time goes in v4:
time: 279 us; the launch traced here: 278 us
  Pallas kernels  80.4 us (29%)
  local copies, waits for them, and re-layouts  75.8 us (27%)
  waiting for transfers between devices  49.5 us (18%)
  starting transfers between devices  45.9 us (16%)
  other arithmetic  24.1 us (9%)
    ppermute x44, starting transfers between devices, swap(): return lax.ppermute(values, axis, route)  39 us
    ppermute x44, waiting for transfers between devices, swap(): return lax.ppermute(values, axis, route)  32.6 us
    pallas_call x1, Pallas kernels, run_backward(): pl.pallas_call(backward_kernel, grid=(chunks,), in_specs=[back(channels),...  25.6 us
    dynamic_update_slice x31, local copies, waits for them, and re-layouts, put_block(): lax.dynamic_update_slice_in_dim(buffer, block, index * block.shape[0], 0)  20.7 us
    pallas_call x1, Pallas kernels, run_forward(): pl.pallas_call(after(forward_kernel, 10, len(arrived)), grid=(chunks,), i...  14.3 us
    unnamed x158, local copies, waits for them, and re-layouts  14.2 us
    ppermute x6, waiting for transfers between devices, shard_gather(): held = lax.ppermute(held, 'wshard', ring_route(count))  14.1 us
    pallas_call x1, Pallas kernels, run_middle(): pl.pallas_call(middle_kernel, grid=(length // BLOCK,), in_specs=[wide(loc...  9.83 us
  transfers between devices with their start and end apart: 53, of which 16 were waited for; matrix products, arithmetic and copies ran while one was open for 19% of the time, Pallas kernels for 18%

profile of v4, /device:TPU:0, one launch (start us, length us, event | category | flops | bytes accessed | tf_op | source)
XLA Modules:
  0.0 277.8 jit_solution(9735367515272364844)
XLA Ops:
  6.3 3.0 %collective-permute-start.10 = (bf16[128,1024]{1,0:T(8,128)(2,1)S(1)}, bf16[128,1024]{1,0:T(8,128)(2,1)S(1)}, u32[]{:S(2)}, u32[]{:S(2)}) collective-permute-start(bf16[128,1024]{1,0:T(8,128)(2,1)S(1)} %get-tuple-element.95.refs_10_), channel_id=1, source_target_pairs={{0,1},{1,0},{2,3},{3,2},{4,5},{5,4},{6,7},{7,6},{8,9},{9,8},{10,11... | collective-permute-start | bytes 786440 | tf_op jit(solution)/shard_map/ppermute | solution.py:699
  35.8 4.8 %collective-permute-done.5 = bf16[128,896]{1,0:T(8,128)(2,1)S(1)} collective-permute-done((bf16[128,896]{1,0:T(8,128)(2,1)}, bf16[128,896]{1,0:T(8,128)(2,1)S(1)}, u32[]{:S(2)}, u32[]{:S(2)}) %collective-permute-start.5) | collective-permute-done | bytes 229408 | tf_op jit(solution)/shard_map/ppermute | solution.py:699
  48.6 7.4 %collective-permute-done.13.refs_14_ = bf16[128,1024]{1,0:T(8,128)(2,1)S(1)} collective-permute-done((bf16[128,1024]{1,0:T(8,128)(2,1)S(1)}, bf16[128,1024]{1,0:T(8,128)(2,1)S(1)}, u32[]{:S(2)}, u32[]{:S(2)}) %collective-permute-start.13) | collective-permute-done | bytes 262176 | tf_op jit(solution)/shard_map/ppermute | solution.py:792
  61.7 4.8 %collective-permute-done.14.refs_15_ = bf16[128,1024]{1,0:T(8,128)(2,1)S(1)} collective-permute-done((bf16[128,1024]{1,0:T(8,128)(2,1)S(1)}, bf16[128,1024]{1,0:T(8,128)(2,1)S(1)}, u32[]{:S(2)}, u32[]{:S(2)}) %collective-permute-start.14) | collective-permute-done | bytes 262176 | tf_op jit(solution)/shard_map/ppermute | solution.py:792
  68.1 2.9 %collective-permute-done.9 = bf16[128,896]{1,0:T(8,128)(2,1)S(1)} collective-permute-done((bf16[128,896]{1,0:T(8,128)(2,1)S(1)}, bf16[128,896]{1,0:T(8,128)(2,1)S(1)}, u32[]{:S(2)}, u32[]{:S(2)}) %collective-permute-start.9) | collective-permute-done | bytes 229408 | tf_op jit(solution)/shard_map/ppermute | solution.py:699
  73.1 14.3 %forward.1 = (bf16[1024,1024]{1,0:T(8,128)(2,1)}, f32[1024,768]{1,0:T(8,128)}, f32[1024,768]{1,0:T(8,128)}, f32[1024,128]{1,0:T(8,128)S(1)}, f32[1024,512]{1,0:T...) custom-call(bf16[1024,1024]{1,0:T(8,128)(2,1)} %copy-done.54, ...), custom_call_target="tpu_custom_call" | custom-call | flops 6000000000 | bytes 30000000 | tf_op jit(solution)/shard_map/forward/pallas_call | solution.py:456
  90.3 9.1 %gate.1 = (f32[1024,512]{1,0:T(8,128)S(1)}, f32[1024,512]{1,0:T(8,128)}, f32[8,1024]{1,0:T(8,128)S(1)}) custom-call(bf16[1024,1024]{1,0:T(8,128)(2,1)} %get-tuple-element.36.normed_ref.refs_0_, bf16[1024,512]{1,0:T(8,128)(2,1)S(1)} %get-tuple-element.35.refs_4_.scanned_ref, bf16[1024,1024]{1,0:T(8,128)(2,1)} %constant_dynamic-update-slice_fusion.14.cot_ref, ...), custom_call_target="tpu_custom_call" | custom-call | flops 2500000000 | bytes 12000000 | tf_op jit(solution)/shard_map/gate/pallas_call | solution.py:504
  102.4 3.1 %collective-permute-done.21 = f32[2,1024]{1,0:T(2,128)S(1)} collective-permute-done((f32[2,1024]{1,0:T(2,128)S(1)}, f32[2,1024]{1,0:T(2,128)S(1)}, u32[]{:S(2)}, u32[]{:S(2)}) %collective-permute-start.21) | collective-permute-done | bytes 8224 | tf_op jit(solution)/shard_map/ppermute | solution.py:699
  106.4 9.8 %middle.1 = (bf16[1024,1024]{1,0:T(8,128)(2,1)}, bf16[1024,512]{1,0:T(8,128)(2,1)S(1)}, bf16[1024,512]{1,0:T(8,128)(2,1)S(1)}, bf16[1024,1024]{1,0:T(8,128)(2,1)}, f32[1,512]{1,0:T(1,128)S(1)}) custom-call(bf16[1024,512]{1,0:T(8,128)(2,1)} %copy-done.4, f32[1024,512]{1,0:T(8,128)} %copy-done.46, f32[1024,512]{1,0:T(8,128)} %get-tuple-element.38.d_gnorm_ref, ...), custom_call_target="tpu_custom_call" | custom-call | flops 4000000000 | bytes 15000000 | tf_op jit(solution)/shard_map/middle/pallas_call | solution.py:536
  116.2 2.1 fusion.30
  120.9 4.4 %collective-permute-start.25 = (bf16[256,512]{1,0:T(8,128)(2,1)S(1)}, bf16[256,512]{1,0:T(8,128)(2,1)S(1)}, u32[]{:S(2)}, u32[]{:S(2)}) collective-permute-start(bf16[256,512]{1,0:T(8,128)(2,1)S(1)} %get-tuple-element.85), channel_id=1, source_target_pairs={{0,4},{1,5},{2,6},{3,7},{4,0},{5,1},{6,2},{7,3},{8,12},{9,13},{10,... | collective-permute-start | bytes 786440 | tf_op jit(solution)/shard_map/ppermute | solution.py:699
  127.1 25.6 %backward.1 = (bf16[1024,896]{1,0:T(8,128)(2,1)}, f32[4,768]{1,0:T(4,128)S(1)}, f32[1,768]{1,0:T(1,128)S(1)}, f32[1,512]{1,0:T(1,128)S(1)}, f32[2,128]{1,0:T(2,128)S(1)}) custom-call(f32[1024,768]{1,0:T(8,128)} %get-tuple-element.42.conv_in_ref, f32[1024,768]{1,0:T(8,128)} %get-tuple-element.43.conv_pre_ref, f32[1024,128]{1,0:T(8,128)S(1)} %copy-done.51, ...), custom_call_target="tpu_custom_call" | custom-call | flops 14000000000 | bytes 40000000 | tf_op jit(solution)/shard_map/backward/pallas_call | solution.py:588
  152.8 6.5 %rest.1.refs_5_.refs_3_.refs_1_ = bf16[1024,896]{1,0:T(8,128)(2,1)} custom-call(bf16[1024,1024]{1,0:T(8,128)(2,1)} %get-tuple-element.36.normed_ref.refs_0_, bf16[1024,896]{1,0:T(8,128)(2,1)} %get-tuple-element.48.refs_1_.refs_2_, bf16[512,1024]{1,0:T(8,128)(2,1)S(1)} %collective-permute-done.22.refs_2_, ...), custom_call_target="tpu_custom_call" | custom-call | flops 2000000000 | bytes 6000000 | tf_op jit(solution)/shard_map/rest/pallas_call | solution.py:632
  159.4 2.3 constant_dynamic-slice_fusion.1
  167.0 3.6 %collective-permute-done.28.refs_2_ = bf16[128,896]{1,0:T(8,128)(2,1)} collective-permute-done((bf16[128,896]{1,0:T(8,128)(2,1)}, bf16[128,896]{1,0:T(8,128)(2,1)}, u32[]{:S(2)}, u32[]{:S(2)}) %collective-permute-start.28) | collective-permute-done | bytes 229408 | tf_op jit(solution)/shard_map/ppermute | solution.py:699
  172.1 4.9 %normed.2 = (bf16[1024,1024]{1,0:T(8,128)(2,1)}, f32[1,1024]{1,0:T(1,128)S(1)}) custom-call(bf16[1024,1024]{1,0:T(8,128)(2,1)} %copy-done.54, bf16[1024,512]{1,0:T(8,128)(2,1)S(1)} %copy-done.6, bf16[1024,896]{1,0:T(8,128)(2,1)S(1)} %copy-done.3, bf16[1024,1024]{1,0:T(8,128)(2,1)} %copy-done.2, ...), custom_call_target="tpu_custom_call" | custom-call | flops 1500000000 | bytes 6000000 | tf_op jit(solution)/shard_map/normed/pallas_call | solution.py:655
  177.0 2.8 collective-permute-done.29.refs_7_.refs_3_
  179.8 4.9 %normed.3 = (bf16[1024,1024]{1,0:T(8,128)(2,1)}, f32[1,1024]{1,0:T(1,128)S(1)}) custom-call(bf16[1024,1024]{1,0:T(8,128)(2,1)} %copy-done.54, bf16[1024,512]{1,0:T(8,128)(2,1)S(1)} %copy-done.6, bf16[1024,896]{1,0:T(8,128)(2,1)S(1)} %copy-done.3, bf16[1024,1024]{1,0:T(8,128)(2,1)} %copy-done.2, ...), custom_call_target="tpu_custom_call", output_to_operand_aliasing={{0}: (5, {})} | custom-call | flops 1500000000 | bytes 6000000 | tf_op jit(solution)/shard_map/normed/pallas_call | solution.py:655
  184.6 3.1 %constant_dynamic-slice_fusion.7 = (bf16[2,1,256,1024]{3,2,1,0:T(8,128)(2,1)}, bf16[2,1,256,1024]{3,2,1,0:T(8,128)(2,1)}) fusion(bf16[2,2,256,1024]{3,2,1,0:T(8,128)(2,1)} %bitcast.131, s32[]{:T(128)S(6)} %select_n.256, s32[]{:T(128)S(6)} %select_n.259), kind=kLoop, calls=%fused_computation.57 | loop fusion | bytes 4194312 | tf_op jit(solution)/shard_map/jit(dynamic_index_in_dim)/dynamic_slice | solution.py:747
  188.6 2.3 collective-permute-start.35
  190.9 2.1 collective-permute-start.36
  193.0 2.0 add_convert_fusion.1
  197.4 4.1 %collective-permute-done.35.refs_5_.refs_3_ = bf16[128,512]{1,0:T(8,128)(2,1)S(1)} collective-permute-done((bf16[128,512]{1,0:T(8,128)(2,1)S(1)}, bf16[128,512]{1,0:T(8,128)(2,1)S(1)}, u32[]{:S(2)}, u32[]{:S(2)}) %collective-permute-start.35) | collective-permute-done | bytes 131104 | tf_op jit(solution)/shard_map/ppermute | solution.py:699
  206.4 3.2 %collective-permute-done.38.refs_10_.refs_2_ = bf16[128,896]{1,0:T(8,128)(2,1)S(1)} collective-permute-done((bf16[128,896]{1,0:T(8,128)(2,1)}, bf16[128,896]{1,0:T(8,128)(2,1)S(1)}, u32[]{:S(2)}, u32[]{:S(2)}) %collective-permute-start.38) | collective-permute-done | bytes 229408 | tf_op jit(solution)/shard_map/ppermute | solution.py:699
  217.8 3.5 %collective-permute-done.44.refs_4_.refs_1_ = f32[1,5400]{1,0:T(1,128)S(1)} collective-permute-done((f32[1,5400]{1,0:T(1,128)S(1)}, f32[1,5400]{1,0:T(1,128)S(1)}, u32[]{:S(2)}, u32[]{:S(2)}) %collective-permute-start.44) | collective-permute-done | bytes 21632 | tf_op jit(solution)/shard_map/ppermute | solution.py:699
  221.9 4.3 %collective-permute-start.46 = (f32[1,5400]{1,0:T(1,128)S(1)}, f32[1,5400]{1,0:T(1,128)S(1)}, u32[]{:S(2)}, u32[]{:S(2)}) collective-permute-start(f32[1,5400]{1,0:T(1,128)S(1)} %sum.4.refs_0_), channel_id=1, source_target_pairs={{0,4},{1,5},{2,6},{3,7},{4,0},{5,1},{6,2},{7,3},{8,12},{9,13},{10,... | collective-permute-start | bytes 64808 | tf_op jit(solution)/shard_map/ppermute | solution.py:699
  226.2 3.9 %collective-permute-done.40.refs_6_ = bf16[128,1024]{1,0:T(8,128)(2,1)S(1)} collective-permute-done((bf16[128,1024]{1,0:T(8,128)(2,1)}, bf16[128,1024]{1,0:T(8,128)(2,1)S(1)}, u32[]{:S(2)}, u32[]{:S(2)}) %collective-permute-start.40) | collective-permute-done | bytes 262176 | tf_op jit(solution)/shard_map/ppermute | solution.py:699
  240.9 3.3 %fusion.7 = (f32[1,256,1024]{2,1,0:T(8,128)}, f32[1,256,1024]{2,1,0:T(8,128)}) fusion(bf16[256,1024]{1,0:T(8,128)(2,1)} %collective-permute-done.32.refs_5_, f32[256]{0:T(256)S(1)} %broadcast_multiply_fusion, f32[1024]{0:T(1024)S(1)} %slice.164, f32[256]{0:T(256)S(1)} %add_rsqrt_fusion, bf16[512,1024]{1,0:T(8,128)(2,1)S(1)} %collective-permute-done.31.refs_9_, ...), kind=kLoop, calls=%fused_computation.15 | loop fusion | flops 4980736 | bytes 6297604 | tf_op jit(solution)/shard_map/reshape | solution.py:1221
  247.3 2.3 multiply_subtract_fusion.1
  262.6 2.7 copy.142
  265.3 2.3 copy.143
  271.5 6.3 %multiply_subtract_fusion = (f32[128,4384]{0,1:T(8,128)}, f32[128,4384]{0,1:T(8,128)}, f32[128,4384]{0,1:T(8,128)}) fusion(f32[128,4384]{0,1:T(8,128)S(1)} %copy-done.55, f32[128,32]{0,1:T(8,128)} %bitcast.162, f32[128,256]{0,1:T(8,128)} %copy.145, f32[128,2048]{0,1:T(8,128)} %bitcast.139, f32[128,2048]{0,1:T(8,128)S(1)} %bitcast.137, f32[128,4384]{0,1:T(8,128)} %param.15, ...), kind=kLoop, calls=%fused_computation.3 | loop fusion | flops 10100736 | bytes 15712256 | tf_op jit(solution)/shard_map/sub | solution.py:679
  (418 shorter events, 114.2 us)
Async XLA Ops:
  6.3 26.3 %collective-permute-start.10 = (bf16[128,1024]{1,0:T(8,128)(2,1)S(1)}, bf16[128,1024]{1,0:T(8,128)(2,1)S(1)}, u32[]{:S(2)}, u32[]{:S(2)}) collective-permute-start(bf16[128,1024]{1,0:T(8,128)(2,1)S(1)} %get-tuple-element.95.refs_10_), channel_id=1, source_target_pairs={{0,1},{1,0},{2,3},{3,2},{4,5},{5,4},{6,7},{7,6},{8,9},{9,8},{10,11... | collective-permute-start | bytes 786440 | tf_op jit(solution)/shard_map/ppermute | solution.py:699
  9.4 24.8 %collective-permute-start.11 = (bf16[128,1024]{1,0:T(8,128)(2,1)S(1)}, bf16[128,1024]{1,0:T(8,128)(2,1)S(1)}, u32[]{:S(2)}, u32[]{:S(2)}) collective-permute-start(bf16[128,1024]{1,0:T(8,128)(2,1)S(1)} %get-tuple-element.95.refs_10_), channel_id=1, source_target_pairs={{0,2},{1,3},{2,4},{3,5},{4,6},{5,7},{6,0},{7,1},{8,10},{9,11},{10,... | collective-permute-start | bytes 786440 | tf_op jit(solution)/shard_map/ppermute | solution.py:792
  16.0 11.6 %collective-permute-start.3 = (bf16[128,896]{1,0:T(8,128)(2,1)}, bf16[128,896]{1,0:T(8,128)(2,1)}, u32[]{:S(2)}, u32[]{:S(2)}) collective-permute-start(bf16[128,896]{1,0:T(8,128)(2,1)} %get-tuple-element.96), channel_id=1, source_target_pairs={{0,1},{1,0},{2,3},{3,2},{4,5},{5,4},{6,7},{7,6},{8,9},{9,8},{10,11... | collective-permute-start | bytes 688136 | tf_op jit(solution)/shard_map/ppermute | solution.py:699
  16.5 14.3 %collective-permute-start.4 = (bf16[128,896]{1,0:T(8,128)(2,1)}, bf16[128,896]{1,0:T(8,128)(2,1)}, u32[]{:S(2)}, u32[]{:S(2)}) collective-permute-start(bf16[128,896]{1,0:T(8,128)(2,1)} %get-tuple-element.96), channel_id=1, source_target_pairs={{0,2},{1,3},{2,4},{3,5},{4,6},{5,7},{6,0},{7,1},{8,10},{9,11},{10,... | collective-permute-start | bytes 688136 | tf_op jit(solution)/shard_map/ppermute | solution.py:792
  18.1 26.9 %collective-permute-start = (bf16[256,1024]{1,0:T(8,128)(2,1)S(1)}, bf16[256,1024]{1,0:T(8,128)(2,1)}, u32[]{:S(2)}, u32[]{:S(2)}) collective-permute-start(bf16[256,1024]{1,0:T(8,128)(2,1)S(1)} %bitcast.132), channel_id=1, source_target_pairs={{0,8},{8,0},{16,24},{24,16},{1,9},{9,1},{17,25},{25,17},{2,10},{10... | collective-permute-start | bytes 1572872 | tf_op jit(solution)/shard_map/ppermute | solution.py:699
  27.6 21.0 %collective-permute-start.1 = (bf16[256,1024]{1,0:T(8,128)(2,1)S(1)}, bf16[256,1024]{1,0:T(8,128)(2,1)S(1)}, u32[]{:S(2)}, u32[]{:S(2)}) collective-permute-start(bf16[256,1024]{1,0:T(8,128)(2,1)S(1)} %bitcast.133), channel_id=1, source_target_pairs={{0,16},{8,24},{16,0},{24,8},{1,17},{9,25},{17,1},{25,9},{2,18},{10... | collective-permute-start | bytes 1572872 | tf_op jit(solution)/shard_map/ppermute | solution.py:699
  30.8 16.0 %collective-permute-start.15 = (bf16[256,1024]{1,0:T(8,128)(2,1)}, bf16[256,1024]{1,0:T(8,128)(2,1)S(1)}, u32[]{:S(2)}, u32[]{:S(2)}) collective-permute-start(bf16[256,1024]{1,0:T(8,128)(2,1)} %bitcast.149), channel_id=1, source_target_pairs={{0,8},{8,0},{16,24},{24,16},{1,9},{9,1},{17,25},{25,17},{2,10},{10... | collective-permute-start | bytes 1572872 | tf_op jit(solution)/shard_map/ppermute | solution.py:699
  40.6 15.4 %collective-permute-start.16 = (bf16[256,1024]{1,0:T(8,128)(2,1)}, bf16[256,1024]{1,0:T(8,128)(2,1)S(1)}, u32[]{:S(2)}, u32[]{:S(2)}) collective-permute-start(bf16[256,1024]{1,0:T(8,128)(2,1)} %bitcast.150), channel_id=1, source_target_pairs={{0,16},{8,24},{16,0},{24,8},{1,17},{9,25},{17,1},{25,9},{2,18},{10... | collective-permute-start | bytes 1572872 | tf_op jit(solution)/shard_map/ppermute | solution.py:699
  43.8 13.1 %collective-permute-start.12 = (bf16[128,1024]{1,0:T(8,128)(2,1)S(1)}, bf16[128,1024]{1,0:T(8,128)(2,1)S(1)}, u32[]{:S(2)}, u32[]{:S(2)}) collective-permute-start(bf16[128,1024]{1,0:T(8,128)(2,1)S(1)} %collective-permute-done.11.refs_12_), channel_id=1, source_target_pairs={{0,1},{1,0},{2,3},{3,2},{4,5},{5,4},{6,7},{7,6},{8,9},{9,8},{10,11... | collective-permute-start | bytes 786440 | tf_op jit(solution)/shard_map/ppermute | solution.py:699
  46.8 11.7 %collective-permute-start.7 = (bf16[128,896]{1,0:T(8,128)(2,1)S(1)}, bf16[128,896]{1,0:T(8,128)(2,1)S(1)}, u32[]{:S(2)}, u32[]{:S(2)}) collective-permute-start(bf16[128,896]{1,0:T(8,128)(2,1)S(1)} %collective-permute-done.6), channel_id=1, source_target_pairs={{0,1},{1,0},{2,3},{3,2},{4,5},{5,4},{6,7},{7,6},{8,9},{9,8},{10,11... | collective-permute-start | bytes 688136 | tf_op jit(solution)/shard_map/ppermute | solution.py:699
  56.0 15.7 %collective-permute-start.2 = (bf16[256,1024]{1,0:T(8,128)(2,1)S(1)}, bf16[256,1024]{1,0:T(8,128)(2,1)S(1)}, u32[]{:S(2)}, u32[]{:S(2)}) collective-permute-start(bf16[256,1024]{1,0:T(8,128)(2,1)S(1)} %collective-permute-done.1), channel_id=1, source_target_pairs={{0,8},{8,0},{16,24},{24,16},{1,9},{9,1},{17,25},{25,17},{2,10},{10... | collective-permute-start | bytes 1572872 | tf_op jit(solution)/shard_map/ppermute | solution.py:699
  56.9 31.4 %collective-permute-start.18 = (bf16[128,1024]{1,0:T(8,128)(2,1)S(1)}, bf16[128,1024]{1,0:T(8,128)(2,1)S(1)}, u32[]{:S(2)}, u32[]{:S(2)}) collective-permute-start(bf16[128,1024]{1,0:T(8,128)(2,1)S(1)} %collective-permute-done.13.refs_14_), channel_id=1, source_target_pairs={{0,1},{1,0},{2,3},{3,2},{4,5},{5,4},{6,7},{7,6},{8,9},{9,8},{10,11... | collective-permute-start | bytes 786440 | tf_op jit(solution)/shard_map/ppermute | solution.py:699
  58.5 28.8 %collective-permute-start.17 = (bf16[256,1024]{1,0:T(8,128)(2,1)S(1)}, bf16[256,1024]{1,0:T(8,128)(2,1)S(1)}, u32[]{:S(2)}, u32[]{:S(2)}) collective-permute-start(bf16[256,1024]{1,0:T(8,128)(2,1)S(1)} %collective-permute-done.16), channel_id=1, source_target_pairs={{0,8},{8,0},{16,24},{24,16},{1,9},{9,1},{17,25},{25,17},{2,10},{10... | collective-permute-start | bytes 1572872 | tf_op jit(solution)/shard_map/ppermute | solution.py:699
  58.8 12.1 %collective-permute-start.9 = (bf16[128,896]{1,0:T(8,128)(2,1)S(1)}, bf16[128,896]{1,0:T(8,128)(2,1)S(1)}, u32[]{:S(2)}, u32[]{:S(2)}) collective-permute-start(bf16[128,896]{1,0:T(8,128)(2,1)S(1)} %collective-permute-done.8), channel_id=1, source_target_pairs={{0,1},{1,0},{2,3},{3,2},{4,5},{5,4},{6,7},{7,6},{8,9},{9,8},{10,11... | collective-permute-start | bytes 688136 | tf_op jit(solution)/shard_map/ppermute | solution.py:699
  66.5 21.7 %collective-permute-start.19 = (bf16[128,1024]{1,0:T(8,128)(2,1)S(1)}, bf16[128,1024]{1,0:T(8,128)(2,1)S(1)}, u32[]{:S(2)}, u32[]{:S(2)}) collective-permute-start(bf16[128,1024]{1,0:T(8,128)(2,1)S(1)} %collective-permute-done.14.refs_15_), channel_id=1, source_target_pairs={{0,1},{1,0},{2,3},{3,2},{4,5},{5,4},{6,7},{7,6},{8,9},{9,8},{10,11... | collective-permute-start | bytes 786440 | tf_op jit(solution)/shard_map/ppermute | solution.py:699
  119.2 33.5 %collective-permute-start.27 = (bf16[512,512]{1,0:T(8,128)(2,1)S(1)}, bf16[512,512]{1,0:T(8,128)(2,1)S(1)}, u32[]{:S(2)}, u32[]{:S(2)}) collective-permute-start(bf16[512,512]{1,0:T(8,128)(2,1)S(1)} %bitcast.159), channel_id=1, source_target_pairs={{0,1},{1,0},{2,3},{3,2},{4,5},{5,4},{6,7},{7,6},{8,9},{9,8},{10,11... | collective-permute-start | bytes 1572872 | tf_op jit(solution)/shard_map/ppermute | solution.py:699
  120.8 31.9 %collective-permute-start.24 = (bf16[256,512]{1,0:T(8,128)(2,1)S(1)}, bf16[256,512]{1,0:T(8,128)(2,1)S(1)}, u32[]{:S(2)}, u32[]{:S(2)}) collective-permute-start(bf16[256,512]{1,0:T(8,128)(2,1)S(1)} %get-tuple-element.86), channel_id=1, source_target_pairs={{0,2},{1,3},{2,0},{3,1},{4,6},{5,7},{6,4},{7,5},{8,10},{9,11},{10,... | collective-permute-start | bytes 786440 | tf_op jit(solution)/shard_map/ppermute | solution.py:699
  120.9 31.8 %collective-permute-start.25 = (bf16[256,512]{1,0:T(8,128)(2,1)S(1)}, bf16[256,512]{1,0:T(8,128)(2,1)S(1)}, u32[]{:S(2)}, u32[]{:S(2)}) collective-permute-start(bf16[256,512]{1,0:T(8,128)(2,1)S(1)} %get-tuple-element.85), channel_id=1, source_target_pairs={{0,4},{1,5},{2,6},{3,7},{4,0},{5,1},{6,2},{7,3},{8,12},{9,13},{10,... | collective-permute-start | bytes 786440 | tf_op jit(solution)/shard_map/ppermute | solution.py:699
  125.3 27.5 %collective-permute-start.26 = (bf16[256,512]{1,0:T(8,128)(2,1)S(1)}, bf16[256,512]{1,0:T(8,128)(2,1)S(1)}, u32[]{:S(2)}, u32[]{:S(2)}) collective-permute-start(bf16[256,512]{1,0:T(8,128)(2,1)S(1)} %get-tuple-element.84), channel_id=1, source_target_pairs={{0,6},{1,7},{2,4},{3,5},{4,2},{5,3},{6,0},{7,1},{8,14},{9,15},{10,... | collective-permute-start | bytes 786440 | tf_op jit(solution)/shard_map/ppermute | solution.py:699
  126.5 26.3 %collective-permute-start.22 = (bf16[512,1024]{1,0:T(8,128)(2,1)S(1)}, bf16[512,1024]{1,0:T(8,128)(2,1)S(1)}, u32[]{:S(2)}, u32[]{:S(2)}) collective-permute-start(bf16[512,1024]{1,0:T(8,128)(2,1)S(1)} %bitcast.151), channel_id=1, source_target_pairs={{0,8},{8,0},{16,24},{24,16},{1,9},{9,1},{17,25},{25,17},{2,10},{10... | collective-permute-start | bytes 3145736 | tf_op jit(solution)/shard_map/ppermute | solution.py:699
  162.3 14.7 %collective-permute-start.30 = (bf16[128,896]{1,0:T(8,128)(2,1)}, bf16[128,896]{1,0:T(8,128)(2,1)S(1)}, u32[]{:S(2)}, u32[]{:S(2)}) collective-permute-start(bf16[128,896]{1,0:T(8,128)(2,1)} %get-tuple-element.76), channel_id=1, source_target_pairs={{0,1},{1,0},{2,3},{3,2},{4,5},{5,4},{6,7},{7,6},{8,9},{9,8},{10,11... | collective-permute-start | bytes 688136 | tf_op jit(solution)/shard_map/ppermute | solution.py:699
  187.8 22.0 %collective-permute-start.31 = (bf16[512,1024]{1,0:T(8,128)(2,1)}, bf16[512,1024]{1,0:T(8,128)(2,1)S(1)}, u32[]{:S(2)}, u32[]{:S(2)}) collective-permute-start(bf16[512,1024]{1,0:T(8,128)(2,1)} %bitcast.29), channel_id=1, source_target_pairs={{0,8},{8,0},{16,24},{24,16},{1,9},{9,1},{17,25},{25,17},{2,10},{10... | collective-permute-start | bytes 3145736 | tf_op jit(solution)/shard_map/ppermute | solution.py:699
  188.6 12.9 %collective-permute-start.35 = (bf16[128,512]{1,0:T(8,128)(2,1)S(1)}, bf16[128,512]{1,0:T(8,128)(2,1)S(1)}, u32[]{:S(2)}, u32[]{:S(2)}) collective-permute-start(bf16[128,512]{1,0:T(8,128)(2,1)S(1)} %get-tuple-element.88), channel_id=1, source_target_pairs={{0,4},{1,5},{2,6},{3,7},{4,0},{5,1},{6,2},{7,3},{8,12},{9,13},{10,... | collective-permute-start | bytes 393224 | tf_op jit(solution)/shard_map/ppermute | solution.py:699
  190.9 13.3 %collective-permute-start.36 = (bf16[128,512]{1,0:T(8,128)(2,1)}, bf16[128,512]{1,0:T(8,128)(2,1)}, u32[]{:S(2)}, u32[]{:S(2)}) collective-permute-start(bf16[128,512]{1,0:T(8,128)(2,1)} %get-tuple-element.87), channel_id=1, source_target_pairs={{0,6},{1,7},{2,4},{3,5},{4,2},{5,3},{6,0},{7,1},{8,14},{9,15},{10,... | collective-permute-start | bytes 393224 | tf_op jit(solution)/shard_map/ppermute | solution.py:699
  195.0 22.4 %collective-permute-start.23 = (bf16[256,1024]{1,0:T(8,128)(2,1)}, bf16[256,1024]{1,0:T(8,128)(2,1)}, u32[]{:S(2)}, u32[]{:S(2)}) collective-permute-start(bf16[256,1024]{1,0:T(8,128)(2,1)} %add_convert_fusion.1), channel_id=1, source_target_pairs={{0,16},{8,24},{16,0},{24,8},{1,17},{9,25},{17,1},{25,9},{2,18},{10... | collective-permute-start | bytes 1572872 | tf_op jit(solution)/shard_map/ppermute | solution.py:699
  213.3 18.8 %collective-permute-start.32 = (bf16[256,1024]{1,0:T(8,128)(2,1)}, bf16[256,1024]{1,0:T(8,128)(2,1)}, u32[]{:S(2)}, u32[]{:S(2)}) collective-permute-start(bf16[256,1024]{1,0:T(8,128)(2,1)} %add_convert_fusion), channel_id=1, source_target_pairs={{0,16},{8,24},{16,0},{24,8},{1,17},{9,25},{17,1},{25,9},{2,18},{10... | collective-permute-start | bytes 1572872 | tf_op jit(solution)/shard_map/ppermute | solution.py:699
  215.4 14.6 %collective-permute-start.40 = (bf16[128,1024]{1,0:T(8,128)(2,1)}, bf16[128,1024]{1,0:T(8,128)(2,1)S(1)}, u32[]{:S(2)}, u32[]{:S(2)}) collective-permute-start(bf16[128,1024]{1,0:T(8,128)(2,1)} %get-tuple-element.93), channel_id=1, source_target_pairs={{0,16},{8,24},{16,0},{24,8},{1,17},{9,25},{17,1},{25,9},{2,18},{10... | collective-permute-start | bytes 786440 | tf_op jit(solution)/shard_map/ppermute | solution.py:699
  217.3 12.7 %collective-permute-start.39 = (bf16[128,1024]{1,0:T(8,128)(2,1)}, bf16[128,1024]{1,0:T(8,128)(2,1)}, u32[]{:S(2)}, u32[]{:S(2)}) collective-permute-start(bf16[128,1024]{1,0:T(8,128)(2,1)} %get-tuple-element.93), channel_id=1, source_target_pairs={{0,8},{8,0},{16,24},{24,16},{1,9},{9,1},{17,25},{25,17},{2,10},{10... | collective-permute-start | bytes 786440 | tf_op jit(solution)/shard_map/ppermute | solution.py:699
  230.0 14.1 %collective-permute-start.41 = (bf16[128,1024]{1,0:T(8,128)(2,1)S(1)}, bf16[128,1024]{1,0:T(8,128)(2,1)}, u32[]{:S(2)}, u32[]{:S(2)}) collective-permute-start(bf16[128,1024]{1,0:T(8,128)(2,1)S(1)} %collective-permute-done.40.refs_6_), channel_id=1, source_target_pairs={{0,8},{8,0},{16,24},{24,16},{1,9},{9,1},{17,25},{25,17},{2,10},{10... | collective-permute-start | bytes 786440 | tf_op jit(solution)/shard_map/ppermute | solution.py:699
  234.8 17.4 %collective-permute-start.50 = (f32[1,5400]{1,0:T(1,128)S(1)}, f32[1,5400]{1,0:T(1,128)}, u32[]{:S(2)}, u32[]{:S(2)}) collective-permute-start(f32[1,5400]{1,0:T(1,128)S(1)} %sum.5), channel_id=1, source_target_pairs={{0,8},{8,0},{16,24},{24,16},{1,9},{9,1},{17,25},{25,17},{2,10},{10... | collective-permute-start | bytes 64808 | tf_op jit(solution)/shard_map/ppermute | solution.py:699
  235.2 21.0 %collective-permute-start.47 = (bf16[128,896]{1,0:T(8,128)(2,1)S(1)}, bf16[128,896]{1,0:T(8,128)(2,1)}, u32[]{:S(2)}, u32[]{:S(2)}) collective-permute-start(bf16[128,896]{1,0:T(8,128)(2,1)S(1)} %add.492.refs_2_), channel_id=1, source_target_pairs={{0,8},{8,0},{16,24},{24,16},{1,9},{9,1},{17,25},{25,17},{2,10},{10... | collective-permute-start | bytes 688136 | tf_op jit(solution)/shard_map/ppermute | solution.py:699
  235.3 20.7 %collective-permute-start.48 = (bf16[128,896]{1,0:T(8,128)(2,1)S(1)}, bf16[128,896]{1,0:T(8,128)(2,1)S(1)}, u32[]{:S(2)}, u32[]{:S(2)}) collective-permute-start(bf16[128,896]{1,0:T(8,128)(2,1)S(1)} %add.492.refs_2_), channel_id=1, source_target_pairs={{0,16},{8,24},{16,0},{24,8},{1,17},{9,25},{17,1},{25,9},{2,18},{10... | collective-permute-start | bytes 688136 | tf_op jit(solution)/shard_map/ppermute | solution.py:699
  (101 other events, 651.1 us)

commit v5 on v3

v5 whole, which is shorter than its diff:
```python
import jax
import jax.numpy as jnp
from jax import lax
from jax.experimental import pallas as pl
from jax.experimental.pallas import tpu as pltpu
from jax.sharding import PartitionSpec as P

D = 1024
HEADS = 32
HEADDIM = 64
STATE = 128
WIDTH = 4
BLOCK = 256
STEP = 10
DI = 2048
CONVCH = 2304


precise = lax.Precision.HIGHEST
norm_eps = 1e-05
beta_one = 0.9
beta_two = 0.95
adam_eps = 1e-08
matrix_rate = 0.05
matrix_decay = 0.1
vector_rate = 0.5


def rms_scale(values):
    return values * lax.rsqrt(jnp.mean(values * values, axis=-1, keepdims=True) + norm_eps)


def split_vector(vector):
    extents = [D, DI, WIDTH * CONVCH, CONVCH, HEADS, HEADS, HEADS]
    pieces = []
    offset = 0
    for extent in extents:
        pieces.append(vector[offset : offset + extent])
        offset = offset + extent
    pieces[2] = pieces[2].reshape(WIDTH, CONVCH)
    return pieces


def wide_back(extent, count):
    return pl.BlockSpec((BLOCK, extent), lambda q: (count - 1 - q, 0))


def whole(*shape):
    return pl.BlockSpec(shape, lambda q: (0,) * len(shape))


def dot_nt(left, right, precision=None):
    return lax.dot_general(
        left,
        right,
        (((1,), (1,)), ((), ())),
        precision=precision,
        preferred_element_type=jnp.float32,
    )


def dot_tn(left, right):
    return lax.dot_general(
        left, right, (((0,), (0,)), ((), ())), preferred_element_type=jnp.float32
    )


def dot_nn(left, right, precision=None):
    return jnp.dot(left, right, precision=precision, preferred_element_type=jnp.float32)


def sigmoid(values):
    return 1.0 / (1.0 + jnp.exp(-values))


def low(values):
    return values.astype(jnp.bfloat16)


def lower_mask():
    rows = lax.broadcasted_iota(jnp.int32, (BLOCK, BLOCK), 0)
    return rows >= lax.broadcasted_iota(jnp.int32, (BLOCK, BLOCK), 1)


def decay_sums(dt_raw, dt_bias, a_log, expand):
    shifted = dt_raw + dt_bias
    step = jnp.maximum(shifted, 0.0) + jnp.log1p(jnp.exp(-jnp.abs(shifted)))
    log_decay = -jnp.exp(a_log) * step
    ones = jnp.where(lower_mask(), 1.0, 0.0)
    running = dot_nn(ones, log_decay, precise)
    step_wide = dot_nn(step, expand, precise)
    running_wide = dot_nn(running, expand, precise)
    return shifted, step, log_decay, running, step_wide, running_wide


def place(result_ref, places_ref, first, blocks):
    for number, block in enumerate(blocks):
        rows = block.shape[0]
        start = pl.multiple_of(places_ref[first + number] * rows, rows)
        result_ref[pl.ds(start, rows), :] = block[...]


def forward_kernel(hidden_count, rest_count, places_ref, *refs):
    hidden_blocks = refs[:hidden_count]
    rest_blocks = refs[hidden_count : hidden_count + rest_count]
    (
        gain_one_ref,
        conv_ref,
        bias_ref,
        a_log_ref,
        dt_bias_ref,
        skip_ref,
        expand_ref,
        hidden_ref,
        rest_ref,
        normed_ref,
        normed_t_ref,
        conv_in_ref,
        conv_pre_ref,
        dt_ref,
        y_ref,
        scanned_ref,
        state_ref,
        ext,
        state,
    ) = refs[hidden_count + rest_count :]
    local_di = y_ref.shape[1]
    heads = local_di // HEADDIM
    channels = conv_in_ref.shape[1]

    @pl.when(pl.program_id(0) == 0)
    def _():
        ext[0:8, :] = jnp.zeros((8, ext.shape[1]), jnp.float32)
        state[...] = jnp.zeros_like(state)
        place(hidden_ref, places_ref, 0, hidden_blocks)
        place(rest_ref, places_ref, hidden_count, rest_blocks)

    chunk = pl.ds(pl.multiple_of(pl.program_id(0) * BLOCK, BLOCK), BLOCK)
    hidden = hidden_ref[chunk, :].astype(jnp.float32)
    normed = rms_scale(hidden) * gain_one_ref[...]
    normed_t_ref[...] = low(normed.T)
    normed = low(normed)
    normed_ref[...] = normed
    conv_in = dot_nn(normed, rest_ref[:, :channels])
    conv_in_ref[...] = conv_in
    ext[8 : 8 + BLOCK, :] = conv_in
    conv_pre = bias_ref[...] + conv_ref[WIDTH - 1 : WIDTH, :] * conv_in
    for tap in range(WIDTH - 1):
        first = 8 - WIDTH + 1 + tap
        conv_pre = conv_pre + conv_ref[tap : tap + 1, :] * ext[first : first + BLOCK, :]
    conv_pre_ref[...] = conv_pre
    ext[8 - WIDTH + 1 : 8, :] = ext[8 + BLOCK - WIDTH + 1 : 8 + BLOCK, :]
    conv_low = low(conv_pre * sigmoid(conv_pre))
    inner = conv_low[:, :local_di]
    b_rows = conv_low[:, local_di : local_di + STATE]
    c_rows = conv_low[:, local_di + STATE :]
    dt_raw = low(dot_nn(normed, rest_ref[:, channels:])).astype(jnp.float32)
    dt_ref[...] = dt_raw

    _, _, _, running, step_wide, running_wide = decay_sums(
        dt_raw, dt_bias_ref[...], a_log_ref[...], expand_ref[...]
    )
    running_t = running.T
    b_t = low(b_rows.astype(jnp.float32).T)
    scores = dot_nn(c_rows, b_t)
    mask = lower_mask()
    inner_wide = inner.astype(jnp.float32)
    stepped = step_wide * inner_wide
    stepped_low = low(stepped)
    first_half = lax.broadcasted_iota(jnp.int32, (BLOCK, 2 * HEADDIM), 1) < HEADDIM
    zero = jnp.zeros((), jnp.bfloat16)
    state_ref[...] = state[...].reshape(state_ref.shape)
    held = state[...]
    carried = jnp.exp(running_wide) * dot_nn(c_rows, low(held))
    for pair in range(heads // 2):
        span = slice(pair * 2 * HEADDIM, (pair + 1) * 2 * HEADDIM)
        both = stepped_low[:, span]
        total = carried[:, span]
        for half in range(2):
            head = 2 * pair + half
            differ = running[:, head : head + 1] - running_t[head : head + 1, :]
            mixed = low(jnp.exp(jnp.where(mask, differ, -jnp.inf)) * scores)
            mine = jnp.where(first_half if half == 0 else ~first_half, both, zero)
            total = total + dot_nn(mixed, mine)
        y_ref[:, span] = total
    last = running_wide[BLOCK - 1 : BLOCK, :]
    to_end = jnp.exp(last - running_wide)
    state[...] = jnp.exp(last) * held + dot_nn(b_t, low(to_end * stepped))
    scanned_ref[...] = low(y_ref[...] + skip_ref[...] * inner_wide)


def out_halves(packed):
    split = packed.reshape(-1, 2, HEADDIM, packed.shape[1])
    extent = packed.shape[0] // 2
    return (
        split[:, 0].reshape(extent, packed.shape[1]),
        split[:, 1].reshape(extent, packed.shape[1]),
    )


def gate_kernel(cot_count, gate_out_count, places_ref, *refs):
    cot_blocks = refs[:cot_count]
    gate_out_blocks = refs[cot_count : cot_count + gate_out_count]
    (
        normed_ref,
        scanned_ref,
        gain_two_ref,
        cot_ref,
        gate_out_ref,
        gating_ref,
        d_gnorm_ref,
        sums_ref,
    ) = refs[cot_count + gate_out_count :]
    local_di = gating_ref.shape[1]

    @pl.when(pl.program_id(0) == 0)
    def _():
        place(cot_ref, places_ref, 0, cot_blocks)
        place(gate_out_ref, places_ref, cot_count, gate_out_blocks)

    chunk = pl.ds(pl.multiple_of(pl.program_id(0) * BLOCK, BLOCK), BLOCK)
    gating = dot_nn(normed_ref[...], gate_out_ref[:, :local_di])
    gating_ref[...] = gating
    out_left, out_right = out_halves(gate_out_ref[:, local_di:])
    half = out_left.shape[1]
    d_gnorm = dot_nt(cot_ref[chunk, :half], out_left)
    d_gnorm = d_gnorm + dot_nt(cot_ref[chunk, half:], out_right)
    d_gnorm_ref[...] = d_gnorm
    gated = scanned_ref[...].astype(jnp.float32) * (gating * sigmoid(gating))
    ones = jnp.ones((8, local_di), jnp.float32)
    squares = dot_nt(ones, gated * gated, precise)
    products = dot_nt(ones, d_gnorm * gain_two_ref[...] * gated, precise)
    sums_ref[...] = jnp.where(
        lax.broadcasted_iota(jnp.int32, squares.shape, 0) == 0, squares, products
    )


def keep_chunk(value, here, number, mine_ref, send_ref):
    rows = pl.ds(pl.multiple_of(number * BLOCK, BLOCK), BLOCK)

    @pl.when(here)
    def _():
        mine_ref[rows, :] = value

    @pl.when(jnp.logical_not(here))
    def _():
        send_ref[rows, :] = value


def middle_kernel(gate_count, out_count, places_ref, *refs):
    (
        scanned_ref,
        gating_ref,
        d_gnorm_ref,
        cot_ref,
        normed_t_ref,
        scale_ref,
        slope_ref,
        out_ref,
        gain_two_ref,
        mine_ref,
        send_ref,
        d_gating_ref,
        d_scanned_ref,
        d_gain_two_ref,
    ) = refs[:14]
    gate_refs = refs[14 : 14 + gate_count]
    out_refs = refs[14 + gate_count : 14 + gate_count + out_count]
    left_sum, right_sum, gate_sum = refs[14 + gate_count + out_count :]
    chunk = pl.program_id(0)

    @pl.when(chunk == 0)
    def _():
        left_sum[...] = jnp.zeros_like(left_sum)
        right_sum[...] = jnp.zeros_like(right_sum)
        gate_sum[...] = jnp.zeros_like(gate_sum)
        d_gain_two_ref[...] = jnp.zeros_like(d_gain_two_ref)

    gating = gating_ref[...]
    open_part = sigmoid(gating)
    gate = gating * open_part
    scanned = scanned_ref[...].astype(jnp.float32)
    scale = scale_ref[:, :1]
    unit = scanned * gate * scale
    d_gnorm = d_gnorm_ref[...]
    gain_two = gain_two_ref[...]
    gnorm = low(unit * gain_two)
    out_left, out_right = out_halves(out_ref[...])
    half = out_left.shape[1]
    block_part = jnp.concatenate([low(dot_nn(gnorm, out_left)), low(dot_nn(gnorm, out_right))], 1)
    keep_chunk(block_part, chunk % 2 == places_ref[0], chunk // 2, mine_ref, send_ref)
    left_sum[...] += dot_tn(gnorm, cot_ref[:, :half])
    right_sum[...] += dot_tn(gnorm, cot_ref[:, half:])
    d_gain_two_ref[...] += jnp.sum(d_gnorm * unit, axis=0, keepdims=True)
    d_gated = scale * (d_gnorm * gain_two) - unit * slope_ref[:, :1]
    d_gating = low(d_gated * scanned * (open_part * (1.0 + gating * (1.0 - open_part))))
    d_gating_ref[...] = d_gating
    d_scanned_ref[...] = low(d_gated * gate)
    gate_sum[...] += dot_nn(normed_t_ref[...], d_gating)

    @pl.when(chunk == pl.num_programs(0) - 1)
    def _():
        for number, gate_ref in enumerate(gate_refs):
            rows = gate_ref.shape[0]
            start = pl.multiple_of(places_ref[1 + number] * rows, rows)
            gate_ref[...] = low(gate_sum[pl.ds(start, rows), :])
        for number, grad_ref in enumerate(out_refs):
            first = places_ref[1 + gate_count + number]
            for step in range(grad_ref.shape[0] // (2 * HEADDIM)):
                head = first + step * out_count
                rows = pl.ds(pl.multiple_of(head * HEADDIM, HEADDIM), HEADDIM)
                base = 2 * step * HEADDIM
                grad_ref[base : base + HEADDIM, :] = low(left_sum[rows, :])
                grad_ref[base + HEADDIM : base + 2 * HEADDIM, :] = low(right_sum[rows, :])


def backward_kernel(
    conv_in_ref,
    conv_pre_ref,
    dt_ref,
    y_ref,
    state_ref,
    d_scanned_ref,
    conv_ref,
    a_log_ref,
    dt_bias_ref,
    skip_ref,
    expand_ref,
    d_rest_ref,
    d_kernel_ref,
    d_conv_bias_ref,
    d_skip_ref,
    d_head_ref,
    ext,
    d_state,
    later_state,
):
    local_di = y_ref.shape[1]
    heads = local_di // HEADDIM
    chunk = pl.program_id(0)

    @pl.when(chunk == 0)
    def _():
        ext[BLOCK : BLOCK + 8, :] = jnp.zeros((8, ext.shape[1]), jnp.float32)
        d_state[...] = jnp.zeros_like(d_state)
        later_state[...] = jnp.zeros_like(later_state)
        d_kernel_ref[...] = jnp.zeros_like(d_kernel_ref)
        d_conv_bias_ref[...] = jnp.zeros_like(d_conv_bias_ref)
        d_skip_ref[...] = jnp.zeros_like(d_skip_ref)
        d_head_ref[...] = jnp.zeros_like(d_head_ref)

    expand = expand_ref[...]
    conv_pre = conv_pre_ref[...]
    open_part = sigmoid(conv_pre)
    conv_low = low(conv_pre * open_part)
    inner = conv_low[:, :local_di].astype(jnp.float32)
    b_rows = conv_low[:, local_di : local_di + STATE]
    c_rows = conv_low[:, local_di + STATE :]
    a_log = a_log_ref[...]
    shifted, _, log_decay, running, step_wide, running_wide = decay_sums(
        dt_ref[...], dt_bias_ref[...], a_log, expand
    )
    running_t = running.T
    b_t = low(b_rows.astype(jnp.float32).T)
    c_t = low(c_rows.astype(jnp.float32).T)
    scores = dot_nn(c_rows, b_t)
    scores_t = dot_nn(b_rows, c_t)
    mask = lower_mask()
    rows = lax.broadcasted_iota(jnp.int32, (BLOCK, BLOCK), 0)
    mask_t = rows <= lax.broadcasted_iota(jnp.int32, (BLOCK, BLOCK), 1)
    d_y_low = d_scanned_ref[...]
    d_y = d_y_low.astype(jnp.float32)
    stepped_low = low(step_wide * inner)
    stepped = stepped_low.astype(jnp.float32)
    last = running_wide[BLOCK - 1 : BLOCK, :]
    to_end = jnp.exp(last - running_wide)
    d_later = d_state[...]
    d_later_low = low(d_later)
    held = state_ref[...].reshape(d_state.shape)
    decayed_dy = low(jnp.exp(running_wide) * d_y)
    d_c = dot_nt(decayed_dy, low(held))
    d_b = dot_nt(low(to_end * stepped), d_later_low)
    d_stepped = to_end * dot_nn(b_rows, d_later_low)
    cross = jnp.sum(later_state[...] * d_later, axis=0, keepdims=True)
    d_state[...] = jnp.exp(last) * d_later + dot_nn(c_t, decayed_dy)
    later_state[...] = held
    first_half = lax.broadcasted_iota(jnp.int32, (BLOCK, 2 * HEADDIM), 1) < HEADDIM
    zero = jnp.zeros((), jnp.bfloat16)
    d_scores = jnp.zeros((BLOCK, BLOCK), jnp.float32)
    pieces = []
    for pair in range(heads // 2):
        span = slice(pair * 2 * HEADDIM, (pair + 1) * 2 * HEADDIM)
        total = d_stepped[:, span]
        for half in range(2):
            head = 2 * pair + half
            mine = jnp.where(first_half if half == 0 else ~first_half, d_y_low[:, span], zero)
            column = running[:, head : head + 1]
            row = running_t[head : head + 1, :]
            decay = jnp.exp(jnp.where(mask, column - row, -jnp.inf))
            decay_t = jnp.exp(jnp.where(mask_t, row - column, -jnp.inf))
            d_scores = d_scores + dot_nt(mine, stepped_low[:, span]) * decay
            total = total + dot_nn(low(decay_t * scores_t), mine)
        pieces.append(total)
    d_stepped = jnp.concatenate(pieces, 1)
    d_scores_low = low(d_scores)
    d_c = d_c + dot_nn(d_scores_low, b_rows)
    d_b = d_b + dot_nn(low(d_scores.T), c_rows)
    d_inner = step_wide * d_stepped + skip_ref[...] * d_y
    d_running = dot_nt(d_y * y_ref[...] - d_stepped * stepped, expand, precise)
    upper = jnp.where(mask_t, 1.0, 0.0)
    d_log = dot_nn(upper, d_running, precise) + dot_nt(cross, expand, precise)
    d_step = dot_nt(d_stepped * inner, expand, precise) - jnp.exp(a_log) * d_log
    d_dt = d_step * sigmoid(shifted)
    d_head_ref[0:1, :] += jnp.sum(d_log * log_decay, axis=0, keepdims=True)
    d_head_ref[1:2, :] += jnp.sum(d_dt, axis=0, keepdims=True)
    d_skip_ref[...] += jnp.sum(d_y * inner, axis=0, keepdims=True)

    d_conv_out = jnp.concatenate([d_inner, d_b, d_c], 1)
    d_pre = d_conv_out * (open_part * (1.0 + conv_pre * (1.0 - open_part)))
    ext[0:BLOCK, :] = d_pre
    d_conv_bias_ref[...] += jnp.sum(d_pre, axis=0, keepdims=True)
    conv_in = conv_in_ref[...]
    d_conv_in = jnp.zeros_like(conv_in)
    for tap in range(WIDTH):
        moved = ext[WIDTH - 1 - tap : WIDTH - 1 - tap + BLOCK, :]
        d_conv_in = d_conv_in + conv_ref[tap : tap + 1, :] * moved
        d_kernel_ref[tap : tap + 1, :] += jnp.sum(moved * conv_in, axis=0, keepdims=True)
    ext[BLOCK : BLOCK + 8, :] = ext[0:8, :]
    d_rest_ref[...] = jnp.concatenate([low(d_conv_in), low(d_dt)], 1)


def rest_kernel(places_ref, normed_t_ref, d_rest_ref, *grad_refs):
    for number, grad_ref in enumerate(grad_refs):
        rows = grad_ref.shape[0]
        start = pl.multiple_of(places_ref[number] * rows, rows)
        grad_ref[...] = low(dot_nn(normed_t_ref[pl.ds(start, rows), :], d_rest_ref[...]))


def normed_kernel(
    places_ref,
    hidden_ref,
    d_gating_ref,
    d_rest_ref,
    gate_weight_ref,
    rest_weight_ref,
    before_ref,
    mine_ref,
    send_ref,
    d_gain_one_ref,
):
    chunk = pl.program_id(0)

    @pl.when(chunk == 0)
    def _():
        d_gain_one_ref[...] = before_ref[...]

    d_normed = dot_nt(d_gating_ref[...], gate_weight_ref[...])
    d_normed = d_normed + dot_nt(d_rest_ref[...], rest_weight_ref[...])
    keep_chunk(low(d_normed), chunk == places_ref[0], 0, mine_ref, send_ref)
    unit = rms_scale(hidden_ref[...].astype(jnp.float32))
    d_gain_one_ref[...] += jnp.sum(d_normed * unit, axis=0, keepdims=True)


def first_lanes(shape):
    return lax.broadcasted_iota(jnp.int32, shape, 1) < HEADDIM


def prepare_kernel(places_ref, in_ref, out_ref, rest_ref, gate_out_ref):
    index = places_ref[0]
    local_di = gate_out_ref.shape[1] // 2
    lanes = 2 * HEADDIM
    rows = in_ref.shape[0]
    first = first_lanes((rows, lanes))
    odd = lax.broadcasted_iota(jnp.int32, (rows, lanes), 1) * 0 + index % 2 == 1

    def head(base, number):
        start = pl.multiple_of(base + (2 * number + index // 2) * lanes, lanes)
        return in_ref[:, pl.ds(start, lanes)]

    for base, result_ref in ((0, gate_out_ref), (DI, rest_ref)):
        for tile in range(local_di // lanes):
            left, right = head(base, 2 * tile), head(base, 2 * tile + 1)
            left = jnp.where(odd, pltpu.roll(left, HEADDIM, 1), left)
            right = jnp.where(odd, right, pltpu.roll(right, HEADDIM, 1))
            span = slice(tile * lanes, (tile + 1) * lanes)
            result_ref[:, span] = low(jnp.where(first, left, right))
    channels = local_di + 2 * STATE
    rest_ref[:, local_di:channels] = low(in_ref[:, 2 * DI : 2 * DI + 2 * STATE])
    source = lax.broadcasted_iota(jnp.int32, (HEADS, lanes), 0)
    target = lax.broadcasted_iota(jnp.int32, (HEADS, lanes), 1)
    groups = DI // local_di
    chosen = (source == groups * target + index) & (target < HEADS // groups)
    steps = low(in_ref[:, DI + CONVCH :])
    rest_ref[:, channels:] = low(dot_nn(steps, jnp.where(chosen, 1.0, 0.0).astype(jnp.bfloat16)))
    mine = out_ref[pl.ds(pl.multiple_of(index * HEADDIM, HEADDIM), HEADDIM), :]
    gate_out_ref[:HEADDIM, local_di:] = low(mine[:, : D // 2])
    gate_out_ref[HEADDIM:, local_di:] = low(mine[:, D // 2 :])


def update_kernel(groups, places_ref, *refs):
    gate_out_blocks = refs[:groups]
    rest_blocks = refs[groups : 2 * groups]
    (
        in_ref,
        in_first_ref,
        in_second_ref,
        out_ref,
        out_first_ref,
        out_second_ref,
        in_first_new_ref,
        in_second_new_ref,
        in_new_ref,
        out_first_new_ref,
        out_second_new_ref,
        out_new_ref,
        gate_out,
        rest,
    ) = refs[2 * groups :]
    chunk = pl.program_id(0)

    @pl.when(chunk == 0)
    def _():
        for number in range(groups):
            gate_out[places_ref[number]] = gate_out_blocks[number][...]
            rest[places_ref[number]] = rest_blocks[number][...]

    rows = in_ref.shape[0]
    here = pl.ds(pl.multiple_of(chunk * rows, rows), rows)
    lanes = 2 * HEADDIM
    local_di = gate_out.shape[2] // 2
    channels = local_di + 2 * STATE
    first = first_lanes((rows, lanes))

    def step_in(span, grad):
        first_new, second_new, new = adamw_step(
            in_ref[:, span],
            in_first_ref[:, span],
            in_second_ref[:, span],
            grad,
            matrix_rate,
            matrix_decay,
        )
        in_first_new_ref[:, span] = first_new
        in_second_new_ref[:, span] = second_new
        in_new_ref[:, span] = new

    for base, source in ((0, gate_out), (DI, rest)):
        for tile in range(DI // lanes):
            head, group = 2 * tile // groups, 2 * tile % groups
            start = head // 2 * lanes
            left = source[group, here, start : start + lanes].astype(jnp.float32)
            right = source[group + 1, here, start : start + lanes].astype(jnp.float32)
            if head % 2 == 0:
                right = pltpu.roll(right, HEADDIM, 1)
            else:
                left = pltpu.roll(left, HEADDIM, 1)
            step_in(
                slice(base + tile * lanes, base + (tile + 1) * lanes),
                jnp.where(first, left, right),
            )
    both = rest[0, here, local_di:channels].astype(jnp.float32)
    steps = jnp.zeros((rows, lanes), jnp.float32)
    source_lane = lax.broadcasted_iota(jnp.int32, (lanes, lanes), 0)
    target_lane = lax.broadcasted_iota(jnp.int32, (lanes, lanes), 1)
    for group in range(groups):
        if group > 0:
            both = both + rest[group, here, local_di:channels].astype(jnp.float32)
        chosen = (target_lane == groups * source_lane + group) & (target_lane < HEADS)
        spread = jnp.where(chosen, 1.0, 0.0).astype(jnp.bfloat16)
        steps = steps + dot_nn(rest[group, here, channels:], spread)
    step_in(slice(2 * DI, 2 * DI + 2 * STATE), both)
    step_in(slice(DI + CONVCH, DI + CONVCH + HEADS), steps[:, :HEADS])
    packed = gate_out[chunk, :, local_di:].astype(jnp.float32)
    for half in range(2):
        span = slice(half * D // 2, (half + 1) * D // 2)
        first_new, second_new, new = adamw_step(
            out_ref[:, span],
            out_first_ref[:, span],
            out_second_ref[:, span],
            packed[half * HEADDIM : (half + 1) * HEADDIM, :],
            matrix_rate,
            matrix_decay,
        )
        out_first_new_ref[:, span] = first_new
        out_second_new_ref[:, span] = second_new
        out_new_ref[:, span] = new


def kernel_params():
    return pltpu.CompilerParams(
        dimension_semantics=("arbitrary",), vmem_limit_bytes=56 * 1024 * 1024
    )


def cost(flops, moved, transcendentals):
    return pl.CostEstimate(flops=flops, bytes_accessed=moved, transcendentals=transcendentals)


def after(kernel, inputs, arrived):
    def run(*refs):
        kernel(*refs[:inputs], *refs[inputs + arrived :])

    return run


def corner(array):
    return pl.BlockSpec((min(16, array.shape[0]), 128), lambda *_: (0, 0))


def fixed(shape):
    return pl.BlockSpec(shape, lambda *_: (0,) * len(shape))


def rows_of(extent, first=0):
    return pl.BlockSpec((BLOCK, extent), lambda q, *_: (q + first, 0))


def struct(shape, dtype=jnp.float32):
    return jax.ShapeDtypeStruct(shape, dtype)


def call(kernel, places, inputs, in_specs, outputs, out_specs, scratch, grid, arrived, price, name):
    return pl.pallas_call(
        after(kernel, 1 + len(inputs), len(arrived)),
        grid_spec=pltpu.PrefetchScalarGridSpec(
            num_scalar_prefetch=1,
            grid=(grid,),
            in_specs=list(in_specs) + [corner(array) for array in arrived],
            out_specs=out_specs,
            scratch_shapes=scratch,
        ),
        out_shape=outputs,
        compiler_params=kernel_params(),
        cost_estimate=cost(*price),
        name=name,
    )(jnp.stack(places).astype(jnp.int32), *inputs, *arrived)


def run_prepare(index, in_weight, out_weight, lanes):
    rows = in_weight.shape[0]
    local_di = DI // 4
    rest = local_di + 2 * STATE + lanes
    return call(
        prepare_kernel,
        [index],
        [in_weight, out_weight],
        [fixed(in_weight.shape), fixed(out_weight.shape)],
        [struct((rows, rest), jnp.bfloat16), struct((rows, 2 * local_di), jnp.bfloat16)],
        [fixed((rows, rest)), fixed((rows, 2 * local_di))],
        [],
        1,
        [],
        (100_000_000, 4_000_000, 0),
        "prepare",
    )


def run_forward(hidden, rest, gain_one, conv, heads_vectors, expand):
    hidden_places, hidden_blocks = hidden
    rest_places, rest_blocks = rest
    length = hidden_blocks[0].shape[0] * len(hidden_blocks)
    chunks = length // BLOCK
    lanes, local_di = expand.shape
    rest_extent = rest_blocks[0].shape[1]
    channels = rest_extent - lanes
    vectors = [gain_one, *conv, *heads_vectors, expand]
    inputs = [*hidden_blocks, *rest_blocks, *vectors]
    return call(
        lambda *refs: forward_kernel(len(hidden_blocks), len(rest_blocks), *refs),
        hidden_places + rest_places,
        inputs,
        [fixed(array.shape) for array in inputs],
        [
            struct((length, D), jnp.bfloat16),
            struct((D, rest_extent), jnp.bfloat16),
            struct((length, D), jnp.bfloat16),
            struct((D, length), jnp.bfloat16),
            struct((length, channels)),
            struct((length, channels)),
            struct((length, lanes)),
            struct((length, local_di)),
            struct((length, local_di), jnp.bfloat16),
            struct((chunks, STATE, local_di)),
        ],
        [
            fixed((length, D)),
            fixed((D, rest_extent)),
            rows_of(D),
            pl.BlockSpec((D, BLOCK), lambda q, *_: (0, q)),
            rows_of(channels),
            rows_of(channels),
            rows_of(lanes),
            rows_of(local_di),
            rows_of(local_di),
            pl.BlockSpec((1, STATE, local_di), lambda q, *_: (q, 0, 0)),
        ],
        [
            pltpu.VMEM((8 + BLOCK, channels), jnp.float32),
            pltpu.VMEM((STATE, local_di), jnp.float32),
        ],
        chunks,
        [],
        (6_000_000_000, 30_000_000, 8_000_000),
        "forward",
    )


def run_gate(cot, gate_out, normed, scanned, gain_two):
    cot_places, cot_blocks = cot
    gate_out_places, gate_out_blocks = gate_out
    length, local_di = scanned.shape
    whole_blocks = [*cot_blocks, *gate_out_blocks]
    gate_out_shape = (D, gate_out_blocks[0].shape[1])
    return call(
        lambda *refs: gate_kernel(len(cot_blocks), len(gate_out_blocks), *refs),
        cot_places + gate_out_places,
        [*whole_blocks, normed, scanned, gain_two],
        [fixed(array.shape) for array in whole_blocks]
        + [rows_of(D), rows_of(local_di), fixed((1, local_di))],
        [
            struct((length, D), jnp.bfloat16),
            struct(gate_out_shape, jnp.bfloat16),
            struct((length, local_di)),
            struct((length, local_di)),
            struct((8, length)),
        ],
        [
            fixed((length, D)),
            fixed(gate_out_shape),
            rows_of(local_di),
            rows_of(local_di),
            pl.BlockSpec((8, BLOCK), lambda q, *_: (0, q)),
        ],
        [],
        length // BLOCK,
        [],
        (2_500_000_000, 12_000_000, 1_000_000),
        "gate",
    )


def run_middle(
    parity, gate_places, out_places, scanned, gating, d_gnorm, cot, normed_t, columns, gate_out, gain
):
    length, local_di = scanned.shape
    half = D // 2
    gate_shape = (D // len(gate_places), local_di)
    out_shape = (2 * local_di // len(out_places), half)
    shapes = [gate_shape] * len(gate_places) + [out_shape] * len(out_places)
    return call(
        lambda *refs: middle_kernel(len(gate_places), len(out_places), *refs),
        [parity] + gate_places + out_places,
        [scanned, gating, d_gnorm, cot, normed_t, *columns, gate_out, gain],
        [
            rows_of(local_di),
            rows_of(local_di),
            rows_of(local_di),
            rows_of(D),
            pl.BlockSpec((D, BLOCK), lambda q, *_: (0, q)),
            rows_of(1),
            rows_of(1),
            pl.BlockSpec((2 * local_di, half), lambda q, *_: (0, local_di // half)),
            fixed((1, local_di)),
        ],
        [
            struct((length // 2, D), jnp.bfloat16),
            struct((length // 2, D), jnp.bfloat16),
            struct((length, local_di), jnp.bfloat16),
            struct((length, local_di), jnp.bfloat16),
            struct((1, local_di)),
        ]
        + [struct(shape, jnp.bfloat16) for shape in shapes],
        [
            fixed((length // 2, D)),
            fixed((length // 2, D)),
            rows_of(local_di),
            rows_of(local_di),
            fixed((1, local_di)),
        ]
        + [fixed(shape) for shape in shapes],
        [
            pltpu.VMEM((local_di, half), jnp.float32),
            pltpu.VMEM((local_di, half), jnp.float32),
            pltpu.VMEM((D, local_di), jnp.float32),
        ],
        length // BLOCK,
        [],
        (4_000_000_000, 15_000_000, 500_000),
        "middle",
    )


def run_backward(
    conv_in, conv_pre, dt_raw, y, states, d_scanned, kernel, heads_vectors, expand
):
    length, local_di = y.shape
    chunks = length // BLOCK
    channels = conv_in.shape[1]
    lanes = expand.shape[0]
    shape = jax.ShapeDtypeStruct
    f32, bf16 = jnp.float32, jnp.bfloat16

    def back(extent):
        return wide_back(extent, chunks)

    return pl.pallas_call(
        backward_kernel,
        grid=(chunks,),
        in_specs=[
            back(channels),
            back(channels),
            back(lanes),
            back(local_di),
            pl.BlockSpec((1, STATE, local_di), lambda q: (chunks - 1 - q, 0, 0)),
            back(local_di),
            whole(WIDTH, channels),
            whole(1, lanes),
            whole(1, lanes),
            whole(1, local_di),
            whole(lanes, local_di),
        ],
        out_specs=[
            back(channels + lanes),
            whole(WIDTH, channels),
            whole(1, channels),
            whole(1, local_di),
            whole(2, lanes),
        ],
        out_shape=[
            shape((length, channels + lanes), bf16),
            shape((WIDTH, channels), f32),
            shape((1, channels), f32),
            shape((1, local_di), f32),
            shape((2, lanes), f32),
        ],
        scratch_shapes=[
            pltpu.VMEM((BLOCK + 8, channels), f32),
            pltpu.VMEM((STATE, local_di), f32),
            pltpu.VMEM((STATE, local_di), f32),
        ],
        compiler_params=kernel_params(),
        cost_estimate=cost(14_000_000_000, 40_000_000, 10_000_000),
        name="backward",
    )(conv_in, conv_pre, dt_raw, y, states, d_scanned, kernel, *heads_vectors, expand)


def run_rest(places, normed_t, d_rest, arrived):
    rest = d_rest.shape[1]
    shape = (D // len(places), rest)
    return call(
        rest_kernel,
        places,
        [normed_t, d_rest],
        [fixed(normed_t.shape), fixed(d_rest.shape)],
        [struct(shape, jnp.bfloat16)] * len(places),
        [fixed(shape)] * len(places),
        [],
        1,
        arrived,
        (2_000_000_000, 6_000_000, 0),
        "rest",
    )


def run_normed(half, parity, hidden, d_gating, d_rest, gate_out, rest_weight, before, arrived):
    length, local_di = d_gating.shape
    rest = d_rest.shape[1]
    return call(
        normed_kernel,
        [parity],
        [hidden, d_gating, d_rest, gate_out, rest_weight, before],
        [
            rows_of(D, 2 * half),
            rows_of(local_di, 2 * half),
            rows_of(rest, 2 * half),
            fixed((D, local_di)),
            fixed((D, rest)),
            fixed((1, D)),
        ],
        [
            struct((BLOCK, D), jnp.bfloat16),
            struct((BLOCK, D), jnp.bfloat16),
            struct((1, D)),
        ],
        [fixed((BLOCK, D)), fixed((BLOCK, D)), fixed((1, D))],
        [],
        2,
        arrived,
        (1_500_000_000, 6_000_000, 1000),
        "normed",
    )


def run_update(places, gate_out_blocks, rest_blocks, in_arrays, out_arrays):
    groups = len(places)
    blocks = [*gate_out_blocks, *rest_blocks]
    rows_in = in_arrays[0].shape[0] // groups
    rows_out = out_arrays[0].shape[0] // groups
    arrays = [*in_arrays, *out_arrays]
    specs = [
        pl.BlockSpec((rows, array.shape[1]), lambda q, *_: (q, 0))
        for rows, array in zip([rows_in] * 3 + [rows_out] * 3, arrays)
    ]
    return call(
        lambda *refs: update_kernel(groups, *refs),
        places,
        [*blocks, *arrays],
        [fixed(array.shape) for array in blocks] + specs,
        [struct(array.shape) for array in arrays],
        specs,
        [
            pltpu.VMEM((groups,) + gate_out_blocks[0].shape, jnp.bfloat16),
            pltpu.VMEM((groups,) + rest_blocks[0].shape, jnp.bfloat16),
        ],
        groups,
        [],
        (20_000_000, 22_000_000, 1_000_000),
        "update",
    )


def adamw_step(weight, first, second, grad, rate, decay):
    first_new = beta_one * first + (1.0 - beta_one) * grad
    second_new = beta_two * second + (1.0 - beta_two) * grad * grad
    fix_one = 1.0 - beta_one**STEP
    fix_two = 1.0 - beta_two**STEP
    normalized = first_new / fix_one / (jnp.sqrt(second_new / fix_two) + adam_eps)
    return (first_new, second_new, weight - rate * (normalized + decay * weight))


def pick_heads(values, axis, width, index, groups):
    shape = values.shape
    split = shape[:axis] + (HEADS // groups, groups, width) + shape[axis + 1 :]
    taken = lax.dynamic_index_in_dim(values.reshape(split), index, axis + 1, keepdims=False)
    return taken.reshape(shape[:axis] + (HEADS // groups * width,) + shape[axis + 1 :])


def merge_heads(stacked, axis, width):
    groups = stacked.shape[0]
    shape = stacked.shape[1:]
    split = (groups,) + shape[:axis] + (HEADS // groups, width) + shape[axis + 1 :]
    moved = jnp.moveaxis(stacked.reshape(split), 0, axis + 1)
    return moved.reshape(shape[:axis] + (HEADS * width,) + shape[axis + 1 :])


def swap(values, axis, mask):
    route = [(i, i ^ mask) for i in range(lax.axis_size(axis))]
    return lax.ppermute(values, axis, route)


def seq_blocks(rows, far=None):
    index = lax.axis_index("seq")
    far = swap(rows, "seq", 2) if far is None else far
    blocks = [rows, swap(rows, "seq", 1), far, swap(far, "seq", 1)]
    return [index ^ mask for mask in range(4)], blocks


def ring_step(held):
    count = lax.axis_size("wshard")
    return lax.ppermute(held, "wshard", [(i, (i + 2) % count) for i in range(count)])


def ring_blocks(rows):
    count = lax.axis_size("wshard")
    index = lax.axis_index("wshard")
    places, blocks = [], []
    for step in range(count // 2):
        source = (index + count - 2 * step) % count
        places = places + [source, source ^ 1]
        blocks = blocks + [rows, swap(rows, "wshard", 1)]
        if step < count // 2 - 1:
            rows = ring_step(rows)
    return places, blocks


def add_kernel(places_ref, *refs):
    total = refs[0][...].astype(jnp.float32)
    for ref in refs[1:-1]:
        total = total + ref[...].astype(jnp.float32)
    refs[-1][...] = total.astype(refs[-1].dtype)


def add(terms, arrived):
    spec = fixed(terms[0].shape)
    return call(
        add_kernel,
        [jnp.int32(0)],
        terms,
        [spec] * len(terms),
        struct(terms[0].shape, terms[0].dtype),
        spec,
        [],
        1,
        arrived,
        (200_000, 900_000, 0),
        "add",
    )


def take_block(values, index, rows):
    return lax.dynamic_slice_in_dim(values, index * rows, rows, 0)


def pack_out(rows):
    split = rows.reshape(-1, HEADDIM, 2, rows.shape[1] // 2)
    return jnp.swapaxes(split, 1, 2).reshape(2 * rows.shape[0], rows.shape[1] // 2)


def unpack_out(packed):
    split = packed.reshape(-1, 2, HEADDIM, packed.shape[1])
    return jnp.swapaxes(split, 1, 2).reshape(packed.shape[0] // 2, 2 * packed.shape[1])


def gather_out(out_low, seq_index, groups):
    rows = out_low.shape[0]
    if rows % (groups * HEADDIM) == 0:
        mine = pick_rows(out_low, seq_index, groups)
        return lax.all_gather(mine, "wshard", axis=0, tiled=True)
    whole = lax.all_gather(out_low, "wshard", axis=0, tiled=True)
    return pick_heads(whole, 0, HEADDIM, seq_index, groups)


def pick_rows(values, seq_index, groups):
    rows = values.shape[0]
    split = values.reshape(rows // (groups * HEADDIM), groups, HEADDIM, values.shape[1])
    return lax.dynamic_index_in_dim(split, seq_index, 1, keepdims=False).reshape(
        rows // groups, values.shape[1]
    )


def sum_out_grad(grad, rows, seq_index, groups):
    grad = grad.astype(jnp.bfloat16)
    if rows % (groups * HEADDIM) == 0:
        mine = lax.psum_scatter(grad, "wshard", scatter_dimension=0, tiled=True)
        every = lax.all_gather(mine, "seq", axis=0, tiled=False)
        split = every.reshape(groups, rows // (groups * HEADDIM), HEADDIM, grad.shape[1])
        return jnp.moveaxis(split, 0, 1).reshape(rows, grad.shape[1]).astype(jnp.float32)
    blocks = grad.reshape(HEADS // groups, 1, HEADDIM, grad.shape[1])
    here = (jnp.arange(groups) == seq_index)[None, :, None, None]
    spread = jnp.where(here, blocks, jnp.zeros((), jnp.bfloat16)).reshape(DI, grad.shape[1])
    mine = lax.psum_scatter(spread, "wshard", scatter_dimension=0, tiled=True)
    return lax.psum(mine.astype(jnp.float32), "seq")


def shards(
    block_in,
    cotangent,
    in_weight,
    in_first,
    in_second,
    out_weight,
    out_first,
    out_second,
    vec_weight,
    vec_first,
    vec_second,
):
    rows_here = block_in.shape[1]
    groups = lax.axis_size("seq")
    seq_index = lax.axis_index("seq")
    local_heads = HEADS // groups
    local_di = DI // groups
    hidden_rows = block_in.reshape(rows_here, D)
    cot_rows = cotangent.reshape(rows_here, D)
    gain_one, gain_two, kernel, conv_bias, a_log, dt_bias, d_skip = split_vector(vec_weight)

    def heads_of(values, axis, width):
        return pick_heads(values, axis, width, seq_index, groups)

    lanes = 128
    channels = local_di + 2 * STATE
    shard_index = lax.axis_index("wshard")
    rings = lax.axis_size("wshard") == 8
    near = seq_index % 2
    far = seq_index // 2
    if rings:
        y, z = shard_index % 2, shard_index // 2
        rest_mine, gate_out_mine = run_prepare(seq_index, in_weight, out_weight, lanes)
        rest = ring_blocks(rest_mine)
        hidden = seq_blocks(hidden_rows)
        gate_out = ring_blocks(gate_out_mine)
        cot = seq_blocks(cot_rows)
        gate_places = [z ^ mask for mask in range(4)]
        out_places = [y, 1 - y]
        rest_places = [
            (shard_index + 8 - 2 * step) % 8 ^ other for step in range(1, 5) for other in (0, 1)
        ]
    else:
        in_low = low(in_weight)
        steps_mine = heads_of(in_low[:, DI + CONVCH :], 1, 1)
        rest_mine = jnp.concatenate(
            [
                heads_of(in_low[:, DI : 2 * DI], 1, HEADDIM),
                in_low[:, 2 * DI : 2 * DI + 2 * STATE],
                jnp.pad(steps_mine, ((0, 0), (0, lanes - local_heads))),
            ],
            1,
        )
        gate_mine = heads_of(in_low[:, :DI], 1, HEADDIM)
        origin = [jnp.int32(0)]
        rest = (origin, [lax.all_gather(rest_mine, "wshard", axis=0, tiled=True)])
        hidden = (origin, [lax.all_gather(hidden_rows, "seq", axis=0, tiled=True)])
        cot = (origin, [lax.all_gather(cot_rows, "seq", axis=0, tiled=True)])
        gate_mine = lax.all_gather(gate_mine, "wshard", axis=0, tiled=True)
        out_mine = pack_out(gather_out(low(out_weight), seq_index, groups))
        gate_out = (origin, [jnp.concatenate([gate_mine, out_mine], 1)])
        gate_places, out_places, rest_places = origin, origin, origin
    my_gain_two = heads_of(gain_two, 0, HEADDIM)[None, :]
    my_kernel = jnp.concatenate([heads_of(kernel[:, :DI], 1, HEADDIM), kernel[:, DI:]], 1)
    my_bias = jnp.concatenate([heads_of(conv_bias[:DI], 0, HEADDIM), conv_bias[DI:]], 0)

    def on_lanes(values):
        return jnp.pad(values, (0, lanes - local_heads))[None, :]

    heads_vectors = (
        on_lanes(heads_of(a_log, 0, 1)),
        on_lanes(heads_of(dt_bias, 0, 1)),
        jnp.repeat(heads_of(d_skip, 0, 1), HEADDIM)[None, :],
    )
    expand = (
        jnp.arange(lanes)[:, None] == jnp.arange(local_di)[None, :] // HEADDIM
    ).astype(jnp.float32)
    (
        hidden_low,
        rest_weight,
        normed_low,
        normed_t,
        conv_in,
        conv_pre,
        dt_raw,
        y_part,
        scanned,
        states,
    ) = run_forward(
        hidden, rest, gain_one[None, :], (my_kernel, my_bias[None, :]), heads_vectors, expand
    )
    cot_low, gate_out_weight, gating, d_gnorm, sums = run_gate(
        cot, gate_out, normed_low, scanned, my_gain_two
    )
    sums = sums[:2]
    for mask in (1, 2):
        sums = sums + swap(sums, "seq", mask)
    sums = sums / DI
    scale = lax.rsqrt(sums[0] + norm_eps)
    slope = scale * scale * sums[1]
    middle = run_middle(
        near,
        gate_places,
        out_places,
        scanned,
        gating,
        d_gnorm,
        cot_low,
        normed_t,
        (scale[:, None], slope[:, None]),
        gate_out_weight,
        my_gain_two,
    )
    block_mine, block_send, d_gating, d_scanned, d_gain_two = middle[:5]
    gate_grads = middle[5 : 5 + len(gate_places)]
    out_grads = middle[5 + len(gate_places) :]
    block_arrived = swap(block_send, "seq", 1)
    early = [block_arrived]
    if rings:
        gate_pieces = [swap(gate_grads[mask], "wshard", 2 * mask) for mask in range(1, 4)]
        out_arrived = swap(out_grads[1], "wshard", 1)
        early = early + gate_pieces + [out_arrived]
    d_rest, d_kernel, d_conv_bias, d_skip_wide, d_head = run_backward(
        conv_in,
        conv_pre,
        dt_raw,
        y_part,
        states,
        d_scanned,
        my_kernel,
        heads_vectors,
        expand,
    )
    rest_grads = run_rest(rest_places, normed_t, d_rest, early)

    def sum_of(one, two):
        return low(one.astype(jnp.float32) + two.astype(jnp.float32))

    block_sum = sum_of(block_mine, block_arrived)
    block_far = swap(take_block(block_sum, 1 - far, rows_here), "seq", 2)
    before_first, before_second = [rest_grads[0]], []
    if rings:
        rest_arrived = swap(rest_grads[1], "wshard", 1)
        gate_paired = add([gate_grads[0]] + gate_pieces, [rest_grads[0]])
        out_paired = add([out_grads[0], out_arrived], [rest_grads[0]])
        held = add([rest_grads[0], rest_arrived], [gate_paired, out_paired])
        ring_arrived = ring_step(held)
        rows_shard = in_weight.shape[0]
        out_pieces = [
            swap(take_block(out_paired, z ^ mask, rows_shard), "wshard", 2 * mask)
            for mask in range(1, 4)
        ]
        before_first = [held]
        before_second = [ring_arrived, block_far] + out_pieces
    mine_one, send_one, d_gain_one = run_normed(
        0,
        near,
        hidden_low,
        d_gating,
        d_rest,
        gate_out_weight,
        rest_weight,
        jnp.zeros((1, D), jnp.float32),
        before_first,
    )
    arrived_one = swap(send_one, "seq", 1)
    mine_two, send_two, d_gain_one = run_normed(
        1,
        near,
        hidden_low,
        d_gating,
        d_rest,
        gate_out_weight,
        rest_weight,
        d_gain_one,
        before_second,
    )
    arrived_two = swap(send_two, "seq", 1)
    normed_one = mine_one.astype(jnp.float32) + arrived_one.astype(jnp.float32)
    normed_two = mine_two.astype(jnp.float32) + arrived_two.astype(jnp.float32)
    normed_far = swap(low(jnp.where(far == 0, normed_two, normed_one)), "seq", 2)
    normed_here = jnp.where(far == 0, normed_one, normed_two)
    shared = jnp.concatenate(
        [d_gain_one[0], d_kernel[:, local_di:].reshape(-1), d_conv_bias[0, local_di:]]
    )
    d_skip_part = jnp.sum(d_skip_wide.reshape(local_heads, HEADDIM), axis=1)
    apart = jnp.concatenate(
        [
            d_gain_two[0],
            d_kernel[:, :local_di].reshape(-1),
            d_conv_bias[0, :local_di],
            d_head[:, :local_heads].reshape(-1),
            d_skip_part,
        ]
    )
    vec_part = jnp.concatenate([shared, apart])[None]
    if rings:
        gate_arrived = swap(take_block(gate_paired, 1 - y, rows_shard), "wshard", 1)
        rest_arrived = swap(rest_grads[3], "wshard", 1)
        held = add(
            [rest_grads[2], rest_arrived, ring_arrived],
            [gate_arrived, arrived_one, arrived_two],
        )
        ring_arrived = ring_step(held)
        rest_arrived = swap(rest_grads[5], "wshard", 1)
        vec_arrived = swap(vec_part, "wshard", 1)
        gate_part = add([take_block(gate_paired, y, rows_shard), gate_arrived], [held])
        out_part = add([take_block(out_paired, z, rows_shard)] + out_pieces, [held])
        gate_out_part = jnp.concatenate([gate_part, out_part], 1)
        held = add([rest_grads[4], rest_arrived, ring_arrived], [vec_arrived])
        ring_arrived = ring_step(held)
        rest_arrived = swap(rest_grads[7], "wshard", 1)
        vec_part = add([vec_part, vec_arrived], [held])
        vec_arrived = swap(vec_part, "wshard", 2)
        gate_out_far = swap(gate_out_part, "seq", 2)
        rest_part = add(
            [rest_grads[6], rest_arrived, ring_arrived],
            [vec_arrived, normed_far, gate_out_far],
        )
        vec_part = add([vec_part, vec_arrived], [rest_part])
        vec_part = vec_part + swap(vec_part, "wshard", 4)
        vec_places, vec_blocks = seq_blocks(vec_part)
        every = jnp.zeros((groups, vec_part.shape[1]), jnp.float32)
        for spot, block in zip(vec_places, vec_blocks):
            every = lax.dynamic_update_slice_in_dim(every, block, spot, 0)
    else:
        vec_part = lax.psum(vec_part, "wshard")
        every = lax.all_gather(vec_part, "seq", axis=0, tiled=True)
    block_here = take_block(block_sum, far, rows_here).astype(jnp.float32)
    block_out = hidden_rows.astype(jnp.float32) + (block_here + block_far.astype(jnp.float32))
    d_normed = normed_here + normed_far.astype(jnp.float32)
    own_hidden = hidden_rows.astype(jnp.float32)
    own_scale = lax.rsqrt(jnp.mean(own_hidden * own_hidden, axis=-1, keepdims=True) + norm_eps)
    own_unit = own_hidden * own_scale
    d_own = d_normed * gain_one[None, :]
    d_hidden = own_scale * (
        d_own - own_unit * jnp.mean(d_own * own_unit, axis=-1, keepdims=True)
    )
    block_grad = cot_rows.astype(jnp.float32) + d_hidden
    shared, every = (
        jnp.sum(every[:, : shared.shape[0]], axis=0),
        every[:, shared.shape[0] :],
    )
    kernel_end = local_di * (1 + WIDTH)
    heads_at = kernel_end + local_di
    both_kernel = D + 2 * STATE * WIDTH
    vec_total = jnp.concatenate(
        [
            shared[:D],
            merge_heads(every[:, :local_di], 0, HEADDIM),
            jnp.concatenate(
                [
                    merge_heads(
                        every[:, local_di:kernel_end].reshape(groups, WIDTH, local_di), 1, HEADDIM
                    ),
                    shared[D:both_kernel].reshape(WIDTH, 2 * STATE),
                ],
                1,
            ).reshape(-1),
            merge_heads(every[:, kernel_end:heads_at], 0, HEADDIM),
            shared[both_kernel:],
            merge_heads(every[:, heads_at : heads_at + local_heads], 0, 1),
            merge_heads(every[:, heads_at + local_heads : heads_at + 2 * local_heads], 0, 1),
            merge_heads(every[:, heads_at + 2 * local_heads :], 0, 1),
        ]
    )
    vec_first_new, vec_second_new, vec_weight_new = adamw_step(
        vec_weight, vec_first, vec_second, vec_total, vector_rate, 0.0
    )
    if rings:
        rest_spots, rest_blocks = seq_blocks(rest_part)
        _, gate_out_blocks = seq_blocks(gate_out_part, gate_out_far)
        (
            in_first_new,
            in_second_new,
            in_weight_new,
            out_first_new,
            out_second_new,
            out_weight_new,
        ) = run_update(
            rest_spots,
            gate_out_blocks,
            rest_blocks,
            (in_weight, in_first, in_second),
            (out_weight, out_first, out_second),
        )
    else:
        rest_part = lax.psum_scatter(rest_grads[0], "wshard", scatter_dimension=0, tiled=True)
        gate_part = lax.psum_scatter(gate_grads[0], "wshard", scatter_dimension=0, tiled=True)
        gate_every = lax.all_gather(gate_part, "seq", axis=0, tiled=False).astype(jnp.float32)
        rest_every = lax.all_gather(rest_part, "seq", axis=0, tiled=False).astype(jnp.float32)
        out_total = sum_out_grad(
            unpack_out(out_grads[0]), out_weight.shape[0], seq_index, groups
        )
        in_total = jnp.concatenate(
            [
                merge_heads(gate_every, 1, HEADDIM),
                merge_heads(rest_every[:, :, :local_di], 1, HEADDIM),
                jnp.sum(rest_every[:, :, local_di:channels], axis=0),
                merge_heads(rest_every[:, :, channels : channels + local_heads], 1, 1),
            ],
            1,
        )
        in_first_new, in_second_new, in_weight_new = adamw_step(
            in_weight, in_first, in_second, in_total, matrix_rate, matrix_decay
        )
        out_first_new, out_second_new, out_weight_new = adamw_step(
            out_weight, out_first, out_second, out_total, matrix_rate, matrix_decay
        )
    return (
        block_out.reshape(1, rows_here, D),
        block_grad.reshape(1, rows_here, D),
        in_first_new,
        in_second_new,
        in_weight_new,
        out_first_new,
        out_second_new,
        out_weight_new,
        vec_first_new,
        vec_second_new,
        vec_weight_new,
    )


def solution(mesh):
    return jax.shard_map(
        shards,
        mesh=mesh,
        in_specs=(
            P("wshard", "seq", None),
            P("wshard", "seq", None),
            P("wshard", None),
            P("wshard", None),
            P("wshard", None),
            P("wshard", None),
            P("wshard", None),
            P("wshard", None),
            P(),
            P(),
            P(),
        ),
        out_specs=(
            P("wshard", "seq", None),
            P("wshard", "seq", None),
            P("wshard", None),
            P("wshard", None),
            P("wshard", None),
            P("wshard", None),
            P("wshard", None),
            P("wshard", None),
            P(),
            P(),
            P(),
        ),
        check_vma=False,
    )
```

time: 261 us -> 266 us (1.019)
  Pallas kernels: 67 us -> 116 us
  waiting for transfers between devices: 79.3 us -> 39.7 us
  starting transfers between devices: 29.8 us -> 51.2 us
  between operations: 15.1 us -> 1.5 us
  other arithmetic: 22.6 us -> 14.7 us
  local copies, waits for them, and re-layouts: 46.4 us -> 42.5 us
    pallas_call x5 -> x19, Pallas kernels: 67 us -> 116 us  [the longest x18 90 us: call(): pl.pallas_call(after(kernel, 1 + len(inputs), len(arrived)), grid_spec=pl...]
    ppermute x36 -> x45, waiting for transfers between devices: 47.2 us -> 25.4 us  [swap(): return lax.ppermute(values, axis, route)]
    ppermute x6 -> x9, waiting for transfers between devices: 32 us -> 14.3 us  [ring_step(): lax.ppermute(held, 'wshard', [(i, (i + 2) % count) for i in range(count)])]
    unnamed x58 -> x140, local copies, waits for them, and re-layouts: 9.65 us -> 26.7 us
    ppermute x36 -> x45, starting transfers between devices: 26.7 us -> 43 us  [swap(): return lax.ppermute(values, axis, route)]
    dynamic_update_slice x26 -> x4, local copies, waits for them, and re-layouts: 17.8 us -> 2.74 us  [shards(): every = lax.dynamic_update_slice_in_dim(every, block, spot, 0)]
    sub x3 -> x1, other arithmetic: 8.78 us -> 1.52 us  [adamw_step(): weight - rate * (normalized + decay * weight)]
    ppermute x6 -> x9, starting transfers between devices: 3.01 us -> 8.15 us  [ring_step(): lax.ppermute(held, 'wshard', [(i, (i + 2) % count) for i in range(count)])]
  transfers between devices with their start and end apart: 44 -> 54, of which waited for: 19 -> 16; matrix products, arithmetic and copies ran while one was open for 16% -> 12% of each run, Pallas kernels for 6% -> 29%
where the time goes in v5:
time: 266 us; the launch traced here: 265 us
  Pallas kernels  116 us (44%)
  starting transfers between devices  51.2 us (19%)
  local copies, waits for them, and re-layouts  42.5 us (16%)
  waiting for transfers between devices  39.7 us (15%)
  other arithmetic  14.7 us (6%)
    pallas_call x18, Pallas kernels, call(): pl.pallas_call(after(kernel, 1 + len(inputs), len(arrived)), grid_spec=pl...  90 us
    ppermute x45, starting transfers between devices, swap(): return lax.ppermute(values, axis, route)  43 us
    unnamed x140, local copies, waits for them, and re-layouts  26.7 us
    pallas_call x1, Pallas kernels, run_backward(): pl.pallas_call(backward_kernel, grid=(chunks,), in_specs=[back(channels),...  25.6 us
    ppermute x45, waiting for transfers between devices, swap(): return lax.ppermute(values, axis, route)  25.4 us
    ppermute x9, waiting for transfers between devices, ring_step(): lax.ppermute(held, 'wshard', [(i, (i + 2) % count) for i in range(count)])  14.3 us
    ppermute x9, starting transfers between devices, ring_step(): lax.ppermute(held, 'wshard', [(i, (i + 2) % count) for i in range(count)])  8.15 us
  transfers between devices with their start and end apart: 54, of which 16 were waited for; matrix products, arithmetic and copies ran while one was open for 12% of the time, Pallas kernels for 29%

profile of v5, /device:TPU:0, one launch (start us, length us, event | category | flops | bytes accessed | tf_op | source)
XLA Modules:
  0.0 265.3 jit_solution(17447835567790874150)
XLA Ops:
  0.6 3.1 %copy.49.refs_1_.refs_9_ = f32[128,4384]{1,0:T(8,128)} copy(f32[128,4384]{0,1:T(8,128)} %param.13) | data formatting | bytes 4489216 | tf_op args[2]
  3.8 3.0 %prepare.1 = (bf16[128,896]{1,0:T(8,128)(2,1)}, bf16[128,1024]{1,0:T(8,128)(2,1)}) custom-call(s32[1]{0:T(128)} %bitcast.8.refs_0_, f32[128,4384]{1,0:T(8,128)} %copy.49.refs_1_.refs_9_, f32[256,1024]{1,0:T(8,128)} %refs_12_.1), custom_call_target="tpu_custom_call" | custom-call | flops 100000000 | bytes 4000000 | tf_op jit(solution)/shard_map/prepare/pallas_call | solution.py:623
  6.8 3.0 %collective-permute-start.4 = (bf16[128,896]{1,0:T(8,128)(2,1)}, bf16[128,896]{1,0:T(8,128)(2,1)}, u32[]{:S(2)}, u32[]{:S(2)}) collective-permute-start(bf16[128,896]{1,0:T(8,128)(2,1)} %get-tuple-element.64.refs_5_), channel_id=1, source_target_pairs={{0,2},{1,3},{2,4},{3,5},{4,6},{5,7},{6,0},{7,1},{8,10},{9,11},{10,... | collective-permute-start | bytes 688136 | tf_op jit(solution)/shard_map/ppermute | solution.py:960
  14.9 3.7 %collective-permute-done.4.refs_7_ = bf16[128,896]{1,0:T(8,128)(2,1)} collective-permute-done((bf16[128,896]{1,0:T(8,128)(2,1)}, bf16[128,896]{1,0:T(8,128)(2,1)}, u32[]{:S(2)}, u32[]{:S(2)}) %collective-permute-start.4) | collective-permute-done | bytes 229408 | tf_op jit(solution)/shard_map/ppermute | solution.py:960
  18.9 5.3 %collective-permute-done.14.refs_7_ = bf16[128,1024]{1,0:T(8,128)(2,1)} collective-permute-done((bf16[128,1024]{1,0:T(8,128)(2,1)}, bf16[128,1024]{1,0:T(8,128)(2,1)}, u32[]{:S(2)}, u32[]{:S(2)}) %collective-permute-start.14) | collective-permute-done | bytes 262176 | tf_op jit(solution)/shard_map/ppermute | solution.py:960
  41.5 2.3 collective-permute-start.9
  44.6 2.9 %collective-permute-done.7.refs_10_ = bf16[128,896]{1,0:T(8,128)(2,1)S(1)} collective-permute-done((bf16[128,896]{1,0:T(8,128)(2,1)}, bf16[128,896]{1,0:T(8,128)(2,1)S(1)}, u32[]{:S(2)}, u32[]{:S(2)}) %collective-permute-start.7) | collective-permute-done | bytes 229408 | tf_op jit(solution)/shard_map/ppermute | solution.py:948
  49.5 2.9 %collective-permute-done.9.refs_12_ = bf16[128,896]{1,0:T(8,128)(2,1)S(1)} collective-permute-done((bf16[128,896]{1,0:T(8,128)(2,1)}, bf16[128,896]{1,0:T(8,128)(2,1)S(1)}, u32[]{:S(2)}, u32[]{:S(2)}) %collective-permute-start.9) | collective-permute-done | bytes 229408 | tf_op jit(solution)/shard_map/ppermute | solution.py:948
  53.6 17.1 %forward.1 = (bf16[1024,1024]{1,0:T(8,128)(2,1)}, bf16[1024,896]{1,0:T(8,128)(2,1)}, bf16[1024,1024]{1,0:T(8,128)(2,1)}, bf16[1024,1024]{1,0:T(8,128)(2,1)}, f32...) custom-call(s32[12]{0:T(128)} %stack.121.refs_0_, ...), custom_call_target="tpu_custom_call" | custom-call | flops 6000000000 | bytes 30000000 | tf_op jit(solution)/shard_map/forward/pallas_call | solution.py:623
  71.9 11.5 %gate.1 = (bf16[1024,1024]{1,0:T(8,128)(2,1)}, bf16[1024,1024]{1,0:T(8,128)(2,1)}, f32[1024,512]{1,0:T(8,128)}, f32[1024,512]{1,0:T(8,128)}, f32[8,1024]{1,0:T(8,128)}) custom-call(s32[12]{0:T(128)} %stack.121.refs_0_, bf16[256,1024]{1,0:T(8,128)(2,1)} %bitcast.84, bf16[256,1024]{1,0:T(8,128)(2,1)} %copy-done.55, bf16[256,1024]{1,0:T(8,128)(2,1)} %copy-done.53, ...), custom_call_target="tpu_custom_call" | custom-call | flops 2500000000 | bytes 12000000 | tf_op jit(solution)/shard_map/gate/pallas_call | solution.py:623
  92.1 12.8 %middle.1 = (bf16[512,1024]{1,0:T(8,128)(2,1)}, bf16[512,1024]{1,0:T(8,128)(2,1)}, bf16[1024,512]{1,0:T(8,128)(2,1)}, bf16[1024,512]{1,0:T(8,128)(2,1)}, f32[1,5...) custom-call(s32[7]{0:T(128)} %stack.108.refs_0_, ...), custom_call_target="tpu_custom_call" | custom-call | flops 4000000000 | bytes 15000000 | tf_op jit(solution)/shard_map/middle/pallas_call | solution.py:623
  107.4 2.9 %collective-permute-start.25 = (bf16[256,512]{1,0:T(8,128)(2,1)}, bf16[256,512]{1,0:T(8,128)(2,1)S(1)}, u32[]{:S(2)}, u32[]{:S(2)}) collective-permute-start(bf16[256,512]{1,0:T(8,128)(2,1)} %get-tuple-element.87), channel_id=1, source_target_pairs={{0,4},{1,5},{2,6},{3,7},{4,0},{5,1},{6,2},{7,3},{8,12},{9,13},{10,... | collective-permute-start | bytes 786440 | tf_op jit(solution)/shard_map/ppermute | solution.py:948
  110.4 25.6 %backward.1 = (bf16[1024,896]{1,0:T(8,128)(2,1)}, f32[4,768]{1,0:T(4,128)}, f32[1,768]{1,0:T(1,128)}, f32[1,512]{1,0:T(1,128)}, f32[2,128]{1,0:T(2,128)}) custom-call(f32[1024,768]{1,0:T(8,128)} %get-tuple-element.78.conv_in_ref, f32[1024,768]{1,0:T(8,128)} %get-tuple-element.79.conv_pre_ref, f32[1024,128]{1,0:T(8,128)} %get-tuple-element.80.dt_ref, ...), custom_call_target="tpu_custom_call" | custom-call | flops 14000000000 | bytes 40000000 | tf_op jit(solution)/shard_map/backward/pallas_call | solution.py:806
  139.9 5.9 %rest.1 = (bf16[128,896]{1,0:T(8,128)(2,1)}, bf16[128,896]{1,0:T(8,128)(2,1)}, bf16[128,896]{1,0:T(8,128)(2,1)}, bf16[128,896]{1,0:T(8,128)(2,1)}, bf16[128,896]...) custom-call(s32[8]{0:T(128)} %stack.124.refs_0_, ...), custom_call_target="tpu_custom_call" | custom-call | flops 2000000000 | bytes 6000000 | tf_op jit(solution)/shard_map/rest/pallas_call | solution.py:623
  146.9 2.1 add.318.refs_4_
  149.0 2.1 add.317.refs_3_
  157.9 2.4 collective-permute-start.32
  162.1 5.6 %normed.2 = (bf16[256,1024]{1,0:T(8,128)(2,1)}, bf16[256,1024]{1,0:T(8,128)(2,1)}, f32[1,1024]{1,0:T(1,128)}) custom-call(s32[1]{0:T(128)} %bitcast.1.refs_0_, bf16[1024,1024]{1,0:T(8,128)(2,1)} %get-tuple-element.76.refs_1_, bf16[1024,512]{1,0:T(8,128)(2,1)} %get-tuple-element.77.refs_2_, bf16[1024,896]{1,0:T(8,128)(2,1)} %get-tuple-element.84.refs_2_.refs_3_, ...), custom_call_target="tpu_custom_call" | custom-call | flops 1500000000 | bytes 6000000 | tf_op jit(solution)/shard_map/normed/pallas_call | solution.py:623
  168.5 4.1 %collective-permute-done.32.refs_10_.refs_3_ = bf16[128,512]{1,0:T(8,128)(2,1)S(1)} collective-permute-done((bf16[128,512]{1,0:T(8,128)(2,1)S(1)}, bf16[128,512]{1,0:T(8,128)(2,1)S(1)}, u32[]{:S(2)}, u32[]{:S(2)}) %collective-permute-start.32) | collective-permute-done | bytes 131104 | tf_op jit(solution)/shard_map/ppermute | solution.py:948
  173.5 5.7 %normed.3 = (bf16[256,1024]{1,0:T(8,128)(2,1)}, bf16[256,1024]{1,0:T(8,128)(2,1)}, f32[1,1024]{1,0:T(1,128)}) custom-call(s32[1]{0:T(128)} %bitcast.1.refs_0_, bf16[1024,1024]{1,0:T(8,128)(2,1)} %get-tuple-element.76.refs_1_, bf16[1024,512]{1,0:T(8,128)(2,1)} %get-tuple-element.77.refs_2_, bf16[1024,896]{1,0:T(8,128)(2,1)} %get-tuple-element.84.refs_2_.refs_3_, ...), custom_call_target="tpu_custom_call" | custom-call | flops 1500000000 | bytes 6000000 | tf_op jit(solution)/shard_map/normed/pallas_call | solution.py:623
  183.5 7.5 %collective-permute-done.36.refs_4_.refs_2_ = bf16[128,512]{1,0:T(8,128)(2,1)S(1)} collective-permute-done((bf16[128,512]{1,0:T(8,128)(2,1)S(1)}, bf16[128,512]{1,0:T(8,128)(2,1)S(1)}, u32[]{:S(2)}, u32[]{:S(2)}) %collective-permute-start.36) | collective-permute-done | bytes 131104 | tf_op jit(solution)/shard_map/ppermute | solution.py:948
  194.1 2.1 collective-permute-start.43
  196.2 2.4 select_convert_fusion
  214.1 3.1 %copy.54.refs_10_ = f32[128,4384]{1,0:T(8,128)} copy(f32[128,4384]{0,1:T(8,128)} %param.14) | data formatting | bytes 4489216 | tf_op args[3]
  217.2 3.1 %copy.55.refs_11_ = f32[128,4384]{1,0:T(8,128)} copy(f32[128,4384]{0,1:T(8,128)} %param.15) | data formatting | bytes 4489216 | tf_op args[4]
  221.7 2.1 add.325.refs_5_.refs_3_
  226.2 4.4 %collective-permute-start.50 = (f32[1,5400]{1,0:T(1,128)}, f32[1,5400]{1,0:T(1,128)S(1)}, u32[]{:S(2)}, u32[]{:S(2)}) collective-permute-start(f32[1,5400]{1,0:T(1,128)} %add.326), channel_id=1, source_target_pairs={{0,4},{1,5},{2,6},{3,7},{4,0},{5,1},{6,2},{7,3},{8,12},{9,13},{10,... | collective-permute-start | bytes 64808 | tf_op jit(solution)/shard_map/ppermute | solution.py:948
  234.0 2.7 %collective-permute-done.52 = f32[1,5400]{1,0:T(1,128)S(1)} collective-permute-done((f32[1,5400]{1,0:T(1,128)S(1)}, f32[1,5400]{1,0:T(1,128)S(1)}, u32[]{:S(2)}, u32[]{:S(2)}) %collective-permute-start.52) | collective-permute-done | bytes 21632 | tf_op jit(solution)/shard_map/ppermute | solution.py:948
  236.7 2.5 fusion.6
  246.9 10.2 %update.1 = (f32[128,4384]{1,0:T(8,128)}, f32[128,4384]{1,0:T(8,128)}, f32[128,4384]{1,0:T(8,128)}, f32[256,1024]{1,0:T(8,128)}, f32[256,1024]{1,0:T(8,128)}, /*index=5*/f32[256,1024]{1,0:T(8,128)}) custom-call(s32[4]{0:T(128)} %pad_add_fusion.refs_0_, bf16[128,1024]{1,0:T(8,128)(2,1)} %pad_maximum_fusion.refs_1_, ...), custom_call_target="tpu_custom_call" | custom-call | flops 20000000 | bytes 22000000 | tf_op jit(solution)/shard_map/update/pallas_call | solution.py:623
  257.2 3.0 %copy.62 = f32[128,4384]{0,1:T(8,128)} copy(f32[128,4384]{1,0:T(8,128)} %get-tuple-element.141) | data formatting | bytes 4489216
  260.2 3.2 %copy.63 = f32[128,4384]{0,1:T(8,128)} copy(f32[128,4384]{1,0:T(8,128)} %get-tuple-element.142) | data formatting | bytes 4489216
  (334 shorter events, 93.5 us)
Async XLA Ops:
  11.3 12.9 %collective-permute-start.14 = (bf16[128,1024]{1,0:T(8,128)(2,1)}, bf16[128,1024]{1,0:T(8,128)(2,1)}, u32[]{:S(2)}, u32[]{:S(2)}) collective-permute-start(bf16[128,1024]{1,0:T(8,128)(2,1)} %get-tuple-element.66.refs_5_), channel_id=1, source_target_pairs={{0,2},{1,3},{2,4},{3,5},{4,6},{5,7},{6,0},{7,1},{8,10},{9,11},{10,... | collective-permute-start | bytes 786440 | tf_op jit(solution)/shard_map/ppermute | solution.py:960
  12.9 13.1 %collective-permute-start.13 = (bf16[128,1024]{1,0:T(8,128)(2,1)}, bf16[128,1024]{1,0:T(8,128)(2,1)S(1)}, u32[]{:S(2)}, u32[]{:S(2)}) collective-permute-start(bf16[128,1024]{1,0:T(8,128)(2,1)} %get-tuple-element.66.refs_5_), channel_id=1, source_target_pairs={{0,1},{1,0},{2,3},{3,2},{4,5},{5,4},{6,7},{7,6},{8,9},{9,8},{10,11... | collective-permute-start | bytes 786440 | tf_op jit(solution)/shard_map/ppermute | solution.py:948
  13.4 17.0 %collective-permute-start.1 = (bf16[256,1024]{1,0:T(8,128)(2,1)S(1)}, bf16[256,1024]{1,0:T(8,128)(2,1)S(1)}, u32[]{:S(2)}, u32[]{:S(2)}) collective-permute-start(bf16[256,1024]{1,0:T(8,128)(2,1)S(1)} %bitcast.82), channel_id=1, source_target_pairs={{0,16},{8,24},{16,0},{24,8},{1,17},{9,25},{17,1},{25,9},{2,18},{10... | collective-permute-start | bytes 1572872 | tf_op jit(solution)/shard_map/ppermute | solution.py:948
  18.9 19.8 %collective-permute-start = (bf16[256,1024]{1,0:T(8,128)(2,1)S(1)}, bf16[256,1024]{1,0:T(8,128)(2,1)S(1)}, u32[]{:S(2)}, u32[]{:S(2)}) collective-permute-start(bf16[256,1024]{1,0:T(8,128)(2,1)S(1)} %bitcast.83), channel_id=1, source_target_pairs={{0,8},{8,0},{16,24},{24,16},{1,9},{9,1},{17,25},{25,17},{2,10},{10... | collective-permute-start | bytes 1572872 | tf_op jit(solution)/shard_map/ppermute | solution.py:948
  28.9 15.7 %collective-permute-start.11 = (bf16[256,1024]{1,0:T(8,128)(2,1)S(1)}, bf16[256,1024]{1,0:T(8,128)(2,1)S(1)}, u32[]{:S(2)}, u32[]{:S(2)}) collective-permute-start(bf16[256,1024]{1,0:T(8,128)(2,1)S(1)} %bitcast.85), channel_id=1, source_target_pairs={{0,16},{8,24},{16,0},{24,8},{1,17},{9,25},{17,1},{25,9},{2,18},{10... | collective-permute-start | bytes 1572872 | tf_op jit(solution)/shard_map/ppermute | solution.py:948
  30.4 22.0 %collective-permute-start.2 = (bf16[256,1024]{1,0:T(8,128)(2,1)S(1)}, bf16[256,1024]{1,0:T(8,128)(2,1)S(1)}, u32[]{:S(2)}, u32[]{:S(2)}) collective-permute-start(bf16[256,1024]{1,0:T(8,128)(2,1)S(1)} %collective-permute-done.1.refs_3_), channel_id=1, source_target_pairs={{0,8},{8,0},{16,24},{24,16},{1,9},{9,1},{17,25},{25,17},{2,10},{10... | collective-permute-start | bytes 1572872 | tf_op jit(solution)/shard_map/ppermute | solution.py:948
  34.5 14.0 %collective-permute-start.18 = (bf16[128,1024]{1,0:T(8,128)(2,1)}, bf16[128,1024]{1,0:T(8,128)(2,1)}, u32[]{:S(2)}, u32[]{:S(2)}) collective-permute-start(bf16[128,1024]{1,0:T(8,128)(2,1)} %collective-permute-done.16.refs_9_), channel_id=1, source_target_pairs={{0,2},{1,3},{2,4},{3,5},{4,6},{5,7},{6,0},{7,1},{8,10},{9,11},{10,... | collective-permute-start | bytes 786440 | tf_op jit(solution)/shard_map/ppermute | solution.py:960
  44.6 26.1 %collective-permute-start.10 = (bf16[256,1024]{1,0:T(8,128)(2,1)S(1)}, bf16[256,1024]{1,0:T(8,128)(2,1)S(1)}, u32[]{:S(2)}, u32[]{:S(2)}) collective-permute-start(bf16[256,1024]{1,0:T(8,128)(2,1)S(1)} %bitcast.86), channel_id=1, source_target_pairs={{0,8},{8,0},{16,24},{24,16},{1,9},{9,1},{17,25},{25,17},{2,10},{10... | collective-permute-start | bytes 1572872 | tf_op jit(solution)/shard_map/ppermute | solution.py:948
  47.4 23.2 %collective-permute-start.15 = (bf16[128,1024]{1,0:T(8,128)(2,1)}, bf16[128,1024]{1,0:T(8,128)(2,1)S(1)}, u32[]{:S(2)}, u32[]{:S(2)}) collective-permute-start(bf16[128,1024]{1,0:T(8,128)(2,1)} %collective-permute-done.14.refs_7_), channel_id=1, source_target_pairs={{0,1},{1,0},{2,3},{3,2},{4,5},{5,4},{6,7},{7,6},{8,9},{9,8},{10,11... | collective-permute-start | bytes 786440 | tf_op jit(solution)/shard_map/ppermute | solution.py:948
  48.5 22.1 %collective-permute-start.17 = (bf16[128,1024]{1,0:T(8,128)(2,1)}, bf16[128,1024]{1,0:T(8,128)(2,1)S(1)}, u32[]{:S(2)}, u32[]{:S(2)}) collective-permute-start(bf16[128,1024]{1,0:T(8,128)(2,1)} %collective-permute-done.16.refs_9_), channel_id=1, source_target_pairs={{0,1},{1,0},{2,3},{3,2},{4,5},{5,4},{6,7},{7,6},{8,9},{9,8},{10,11... | collective-permute-start | bytes 786440 | tf_op jit(solution)/shard_map/ppermute | solution.py:948
  52.4 18.4 %collective-permute-start.12 = (bf16[256,1024]{1,0:T(8,128)(2,1)S(1)}, bf16[256,1024]{1,0:T(8,128)(2,1)S(1)}, u32[]{:S(2)}, u32[]{:S(2)}) collective-permute-start(bf16[256,1024]{1,0:T(8,128)(2,1)S(1)} %collective-permute-done.11.refs_3_), channel_id=1, source_target_pairs={{0,8},{8,0},{16,24},{24,16},{1,9},{9,1},{17,25},{25,17},{2,10},{10... | collective-permute-start | bytes 1572872 | tf_op jit(solution)/shard_map/ppermute | solution.py:948
  52.4 18.3 %collective-permute-start.19 = (bf16[128,1024]{1,0:T(8,128)(2,1)}, bf16[128,1024]{1,0:T(8,128)(2,1)S(1)}, u32[]{:S(2)}, u32[]{:S(2)}) collective-permute-start(bf16[128,1024]{1,0:T(8,128)(2,1)} %collective-permute-done.18.refs_11_), channel_id=1, source_target_pairs={{0,1},{1,0},{2,3},{3,2},{4,5},{5,4},{6,7},{7,6},{8,9},{9,8},{10,11... | collective-permute-start | bytes 786440 | tf_op jit(solution)/shard_map/ppermute | solution.py:948
  104.9 31.1 %collective-permute-start.22 = (bf16[512,1024]{1,0:T(8,128)(2,1)}, bf16[512,1024]{1,0:T(8,128)(2,1)S(1)}, u32[]{:S(2)}, u32[]{:S(2)}) collective-permute-start(bf16[512,1024]{1,0:T(8,128)(2,1)} %get-tuple-element.75), channel_id=1, source_target_pairs={{0,8},{8,0},{16,24},{24,16},{1,9},{9,1},{17,25},{25,17},{2,10},{10... | collective-permute-start | bytes 3145736 | tf_op jit(solution)/shard_map/ppermute | solution.py:948
  105.0 34.0 %collective-permute-start.27 = (bf16[512,512]{1,0:T(8,128)(2,1)}, bf16[512,512]{1,0:T(8,128)(2,1)S(1)}, u32[]{:S(2)}, u32[]{:S(2)}) collective-permute-start(bf16[512,512]{1,0:T(8,128)(2,1)} %get-tuple-element.89), channel_id=1, source_target_pairs={{0,1},{1,0},{2,3},{3,2},{4,5},{5,4},{6,7},{7,6},{8,9},{9,8},{10,11... | collective-permute-start | bytes 1572872 | tf_op jit(solution)/shard_map/ppermute | solution.py:948
  106.0 32.9 %collective-permute-start.24 = (bf16[256,512]{1,0:T(8,128)(2,1)}, bf16[256,512]{1,0:T(8,128)(2,1)S(1)}, u32[]{:S(2)}, u32[]{:S(2)}) collective-permute-start(bf16[256,512]{1,0:T(8,128)(2,1)} %get-tuple-element.86), channel_id=1, source_target_pairs={{0,2},{1,3},{2,0},{3,1},{4,6},{5,7},{6,4},{7,5},{8,10},{9,11},{10,... | collective-permute-start | bytes 786440 | tf_op jit(solution)/shard_map/ppermute | solution.py:948
  107.4 31.5 %collective-permute-start.25 = (bf16[256,512]{1,0:T(8,128)(2,1)}, bf16[256,512]{1,0:T(8,128)(2,1)S(1)}, u32[]{:S(2)}, u32[]{:S(2)}) collective-permute-start(bf16[256,512]{1,0:T(8,128)(2,1)} %get-tuple-element.87), channel_id=1, source_target_pairs={{0,4},{1,5},{2,6},{3,7},{4,0},{5,1},{6,2},{7,3},{8,12},{9,13},{10,... | collective-permute-start | bytes 786440 | tf_op jit(solution)/shard_map/ppermute | solution.py:948
  110.3 28.5 %collective-permute-start.26 = (bf16[256,512]{1,0:T(8,128)(2,1)}, bf16[256,512]{1,0:T(8,128)(2,1)S(1)}, u32[]{:S(2)}, u32[]{:S(2)}) collective-permute-start(bf16[256,512]{1,0:T(8,128)(2,1)} %get-tuple-element.88), channel_id=1, source_target_pairs={{0,6},{1,7},{2,4},{3,5},{4,2},{5,3},{6,0},{7,1},{8,14},{9,15},{10,... | collective-permute-start | bytes 786440 | tf_op jit(solution)/shard_map/ppermute | solution.py:948
  137.4 35.1 %collective-permute-start.23 = (bf16[256,1024]{1,0:T(8,128)(2,1)S(1)}, bf16[256,1024]{1,0:T(8,128)(2,1)S(1)}, u32[]{:S(2)}, u32[]{:S(2)}) collective-permute-start(bf16[256,1024]{1,0:T(8,128)(2,1)S(1)} %constant_dynamic-slice_fusion.6), channel_id=1, source_target_pairs={{0,16},{8,24},{16,0},{24,8},{1,17},{9,25},{17,1},{25,9},{2,18},{10... | collective-permute-start | bytes 1572872 | tf_op jit(solution)/shard_map/ppermute | solution.py:948
  155.2 17.4 %collective-permute-start.30 = (bf16[128,896]{1,0:T(8,128)(2,1)}, bf16[128,896]{1,0:T(8,128)(2,1)S(1)}, u32[]{:S(2)}, u32[]{:S(2)}) collective-permute-start(bf16[128,896]{1,0:T(8,128)(2,1)} %add.319.refs_7_), channel_id=1, source_target_pairs={{0,2},{1,3},{2,4},{3,5},{4,6},{5,7},{6,0},{7,1},{8,10},{9,11},{10,... | collective-permute-start | bytes 688136 | tf_op jit(solution)/shard_map/ppermute | solution.py:960
  156.5 12.0 %collective-permute-start.31 = (bf16[128,512]{1,0:T(8,128)(2,1)S(1)}, bf16[128,512]{1,0:T(8,128)(2,1)S(1)}, u32[]{:S(2)}, u32[]{:S(2)}) collective-permute-start(bf16[128,512]{1,0:T(8,128)(2,1)S(1)} %get-tuple-element.156), channel_id=1, source_target_pairs={{0,2},{1,3},{2,0},{3,1},{4,6},{5,7},{6,4},{7,5},{8,10},{9,11},{10,... | collective-permute-start | bytes 393224 | tf_op jit(solution)/shard_map/ppermute | solution.py:948
  157.9 14.6 %collective-permute-start.32 = (bf16[128,512]{1,0:T(8,128)(2,1)S(1)}, bf16[128,512]{1,0:T(8,128)(2,1)S(1)}, u32[]{:S(2)}, u32[]{:S(2)}) collective-permute-start(bf16[128,512]{1,0:T(8,128)(2,1)S(1)} %get-tuple-element.155), channel_id=1, source_target_pairs={{0,4},{1,5},{2,6},{3,7},{4,0},{5,1},{6,2},{7,3},{8,12},{9,13},{10,... | collective-permute-start | bytes 393224 | tf_op jit(solution)/shard_map/ppermute | solution.py:948
  160.3 12.3 %collective-permute-start.33 = (bf16[128,512]{1,0:T(8,128)(2,1)S(1)}, bf16[128,512]{1,0:T(8,128)(2,1)S(1)}, u32[]{:S(2)}, u32[]{:S(2)}) collective-permute-start(bf16[128,512]{1,0:T(8,128)(2,1)S(1)} %get-tuple-element.154), channel_id=1, source_target_pairs={{0,6},{1,7},{2,4},{3,5},{4,2},{5,3},{6,0},{7,1},{8,14},{9,15},{10,... | collective-permute-start | bytes 393224 | tf_op jit(solution)/shard_map/ppermute | solution.py:948
  168.4 22.6 %collective-permute-start.29 = (bf16[256,1024]{1,0:T(8,128)(2,1)}, bf16[256,1024]{1,0:T(8,128)(2,1)S(1)}, u32[]{:S(2)}, u32[]{:S(2)}) collective-permute-start(bf16[256,1024]{1,0:T(8,128)(2,1)} %get-tuple-element.95), channel_id=1, source_target_pairs={{0,8},{8,0},{16,24},{24,16},{1,9},{9,1},{17,25},{25,17},{2,10},{10... | collective-permute-start | bytes 1572872 | tf_op jit(solution)/shard_map/ppermute | solution.py:948
  179.3 11.8 %collective-permute-start.34 = (bf16[256,1024]{1,0:T(8,128)(2,1)}, bf16[256,1024]{1,0:T(8,128)(2,1)S(1)}, u32[]{:S(2)}, u32[]{:S(2)}) collective-permute-start(bf16[256,1024]{1,0:T(8,128)(2,1)} %get-tuple-element.98), channel_id=1, source_target_pairs={{0,8},{8,0},{16,24},{24,16},{1,9},{9,1},{17,25},{25,17},{2,10},{10... | collective-permute-start | bytes 1572872 | tf_op jit(solution)/shard_map/ppermute | solution.py:948
  182.3 26.2 %collective-permute-start.42 = (bf16[128,896]{1,0:T(8,128)(2,1)}, bf16[128,896]{1,0:T(8,128)(2,1)S(1)}, u32[]{:S(2)}, u32[]{:S(2)}) collective-permute-start(bf16[128,896]{1,0:T(8,128)(2,1)} %get-tuple-element.104), channel_id=1, source_target_pairs={{0,1},{1,0},{2,3},{3,2},{4,5},{5,4},{6,7},{7,6},{8,9},{9,8},{10,11... | collective-permute-start | bytes 688136 | tf_op jit(solution)/shard_map/ppermute | solution.py:948
  194.1 15.4 %collective-permute-start.43 = (bf16[128,896]{1,0:T(8,128)(2,1)}, bf16[128,896]{1,0:T(8,128)(2,1)S(1)}, u32[]{:S(2)}, u32[]{:S(2)}) collective-permute-start(bf16[128,896]{1,0:T(8,128)(2,1)} %add.320.refs_3_.refs_5_), channel_id=1, source_target_pairs={{0,2},{1,3},{2,4},{3,5},{4,6},{5,7},{6,0},{7,1},{8,10},{9,11},{10,... | collective-permute-start | bytes 688136 | tf_op jit(solution)/shard_map/ppermute | solution.py:960
  198.6 22.3 %collective-permute-start.35 = (bf16[256,1024]{1,0:T(8,128)(2,1)}, bf16[256,1024]{1,0:T(8,128)(2,1)S(1)}, u32[]{:S(2)}, u32[]{:S(2)}) collective-permute-start(bf16[256,1024]{1,0:T(8,128)(2,1)} %select_convert_fusion), channel_id=1, source_target_pairs={{0,16},{8,24},{16,0},{24,8},{1,17},{9,25},{17,1},{25,9},{2,18},{10... | collective-permute-start | bytes 1572872 | tf_op jit(solution)/shard_map/ppermute | solution.py:948
  201.2 19.2 %collective-permute-start.41 = (bf16[128,896]{1,0:T(8,128)(2,1)}, bf16[128,896]{1,0:T(8,128)(2,1)S(1)}, u32[]{:S(2)}, u32[]{:S(2)}) collective-permute-start(bf16[128,896]{1,0:T(8,128)(2,1)} %get-tuple-element.102), channel_id=1, source_target_pairs={{0,1},{1,0},{2,3},{3,2},{4,5},{5,4},{6,7},{7,6},{8,9},{9,8},{10,11... | collective-permute-start | bytes 688136 | tf_op jit(solution)/shard_map/ppermute | solution.py:948
  208.5 11.8 %collective-permute-start.39 = (bf16[128,1024]{1,0:T(8,128)(2,1)}, bf16[128,1024]{1,0:T(8,128)(2,1)}, u32[]{:S(2)}, u32[]{:S(2)}) collective-permute-start(bf16[128,1024]{1,0:T(8,128)(2,1)} %pad_maximum_fusion.refs_1_), channel_id=1, source_target_pairs={{0,16},{8,24},{16,0},{24,8},{1,17},{9,25},{17,1},{25,9},{2,18},{10... | collective-permute-start | bytes 786440 | tf_op jit(solution)/shard_map/ppermute | solution.py:948
  220.3 25.2 %collective-permute-start.38 = (bf16[128,1024]{1,0:T(8,128)(2,1)}, bf16[128,1024]{1,0:T(8,128)(2,1)}, u32[]{:S(2)}, u32[]{:S(2)}) collective-permute-start(bf16[128,1024]{1,0:T(8,128)(2,1)} %pad_maximum_fusion.refs_1_), channel_id=1, source_target_pairs={{0,8},{8,0},{16,24},{24,16},{1,9},{9,1},{17,25},{25,17},{2,10},{10... | collective-permute-start | bytes 786440 | tf_op jit(solution)/shard_map/ppermute | solution.py:948
  220.4 25.2 %collective-permute-start.40 = (bf16[128,1024]{1,0:T(8,128)(2,1)}, bf16[128,1024]{1,0:T(8,128)(2,1)}, u32[]{:S(2)}, u32[]{:S(2)}) collective-permute-start(bf16[128,1024]{1,0:T(8,128)(2,1)} %collective-permute-done.39.refs_6_.refs_3_), channel_id=1, source_target_pairs={{0,8},{8,0},{16,24},{24,16},{1,9},{9,1},{17,25},{25,17},{2,10},{10... | collective-permute-start | bytes 786440 | tf_op jit(solution)/shard_map/ppermute | solution.py:948
  223.8 20.1 %collective-permute-start.48 = (bf16[128,896]{1,0:T(8,128)(2,1)}, bf16[128,896]{1,0:T(8,128)(2,1)}, u32[]{:S(2)}, u32[]{:S(2)}) collective-permute-start(bf16[128,896]{1,0:T(8,128)(2,1)} %add.325.refs_5_.refs_3_), channel_id=1, source_target_pairs={{0,16},{8,24},{16,0},{24,8},{1,17},{9,25},{17,1},{25,9},{2,18},{10... | collective-permute-start | bytes 688136 | tf_op jit(solution)/shard_map/ppermute | solution.py:948
  (89 other events, 632.3 us)

commit v6 on v5

v6 whole, which is shorter than its diff:
```python
import jax
import jax.numpy as jnp
from jax import lax
from jax.experimental import pallas as pl
from jax.experimental.pallas import tpu as pltpu
from jax.sharding import PartitionSpec as P

D = 1024
HEADS = 32
HEADDIM = 64
STATE = 128
WIDTH = 4
BLOCK = 256
STEP = 10
DI = 2048
CONVCH = 2304


precise = lax.Precision.HIGHEST
norm_eps = 1e-05
beta_one = 0.9
beta_two = 0.95
adam_eps = 1e-08
matrix_rate = 0.05
matrix_decay = 0.1
vector_rate = 0.5


def rms_scale(values):
    return values * lax.rsqrt(jnp.mean(values * values, axis=-1, keepdims=True) + norm_eps)


def split_vector(vector):
    extents = [D, DI, WIDTH * CONVCH, CONVCH, HEADS, HEADS, HEADS]
    pieces = []
    offset = 0
    for extent in extents:
        pieces.append(vector[offset : offset + extent])
        offset = offset + extent
    pieces[2] = pieces[2].reshape(WIDTH, CONVCH)
    return pieces


def dot_nt(left, right, precision=None):
    return lax.dot_general(
        left,
        right,
        (((1,), (1,)), ((), ())),
        precision=precision,
        preferred_element_type=jnp.float32,
    )


def dot_tn(left, right):
    return lax.dot_general(
        left, right, (((0,), (0,)), ((), ())), preferred_element_type=jnp.float32
    )


def dot_nn(left, right, precision=None):
    return jnp.dot(left, right, precision=precision, preferred_element_type=jnp.float32)


def sigmoid(values):
    return 1.0 / (1.0 + jnp.exp(-values))


def low(values):
    return values.astype(jnp.bfloat16)


def lower_mask():
    rows = lax.broadcasted_iota(jnp.int32, (BLOCK, BLOCK), 0)
    return rows >= lax.broadcasted_iota(jnp.int32, (BLOCK, BLOCK), 1)


def decay_sums(dt_raw, dt_bias, a_log, expand):
    shifted = dt_raw + dt_bias
    step = jnp.maximum(shifted, 0.0) + jnp.log1p(jnp.exp(-jnp.abs(shifted)))
    log_decay = -jnp.exp(a_log) * step
    ones = jnp.where(lower_mask(), 1.0, 0.0)
    running = dot_nn(ones, log_decay, precise)
    step_wide = dot_nn(step, expand, precise)
    running_wide = dot_nn(running, expand, precise)
    return shifted, step, log_decay, running, step_wide, running_wide


def place_rows(result_ref, place, block):
    rows = block.shape[0]
    result_ref[pl.ds(pl.multiple_of(place * rows, rows), rows), :] = block


def place_columns(result_ref, place, block):
    rows, columns = block.shape
    start = pl.multiple_of(place * columns, columns)
    result_ref[:rows, pl.ds(start, columns)] = block


def forward_kernel(both_count, rest_count, places_ref, *refs):
    both_blocks = refs[:both_count]
    rest_blocks = refs[both_count : both_count + rest_count]
    (
        gain_one_ref,
        conv_ref,
        bias_ref,
        a_log_ref,
        dt_bias_ref,
        skip_ref,
        expand_ref,
        hidden_ref,
        cot_ref,
        rest_ref,
        normed_ref,
        conv_in_ref,
        conv_pre_ref,
        dt_ref,
        y_ref,
        scanned_ref,
        state_ref,
        ext,
        state,
    ) = refs[both_count + rest_count :]
    local_di = y_ref.shape[1]
    heads = local_di // HEADDIM
    channels = conv_in_ref.shape[1]

    @pl.when(pl.program_id(0) == 0)
    def _():
        ext[0:8, :] = jnp.zeros((8, ext.shape[1]), jnp.float32)
        state[...] = jnp.zeros_like(state)
        for number, block in enumerate(both_blocks):
            half = block.shape[0] // 2
            place_rows(hidden_ref, places_ref[number], block[:half, :])
            place_rows(cot_ref, places_ref[number], block[half:, :])
        rest_ref[channels:, :] = jnp.zeros_like(rest_ref[channels:, :])
        for number, block in enumerate(rest_blocks):
            place_columns(rest_ref, places_ref[both_count + number], block[...])

    chunk = pl.ds(pl.multiple_of(pl.program_id(0) * BLOCK, BLOCK), BLOCK)
    hidden = hidden_ref[chunk, :].astype(jnp.float32)
    normed = low(rms_scale(hidden) * gain_one_ref[...])
    normed_ref[...] = normed
    conv_in = dot_nt(normed, rest_ref[:channels, :])
    conv_in_ref[...] = conv_in
    ext[8 : 8 + BLOCK, :] = conv_in
    conv_pre = bias_ref[...] + conv_ref[WIDTH - 1 : WIDTH, :] * conv_in
    for tap in range(WIDTH - 1):
        first = 8 - WIDTH + 1 + tap
        conv_pre = conv_pre + conv_ref[tap : tap + 1, :] * ext[first : first + BLOCK, :]
    conv_pre_ref[...] = conv_pre
    ext[8 - WIDTH + 1 : 8, :] = ext[8 + BLOCK - WIDTH + 1 : 8 + BLOCK, :]
    conv_low = low(conv_pre * sigmoid(conv_pre))
    inner = conv_low[:, :local_di]
    b_rows = conv_low[:, local_di : local_di + STATE]
    c_rows = conv_low[:, local_di + STATE :]
    dt_raw = low(dot_nt(normed, rest_ref[channels:, :])).astype(jnp.float32)
    dt_ref[...] = dt_raw

    _, _, _, running, step_wide, running_wide = decay_sums(
        dt_raw, dt_bias_ref[...], a_log_ref[...], expand_ref[...]
    )
    running_t = running.T
    b_t = low(b_rows.astype(jnp.float32).T)
    scores = dot_nn(c_rows, b_t)
    mask = lower_mask()
    inner_wide = inner.astype(jnp.float32)
    stepped = step_wide * inner_wide
    stepped_low = low(stepped)
    first_half = lax.broadcasted_iota(jnp.int32, (BLOCK, 2 * HEADDIM), 1) < HEADDIM
    zero = jnp.zeros((), jnp.bfloat16)
    state_ref[...] = state[...].reshape(state_ref.shape)
    held = state[...]
    carried = jnp.exp(running_wide) * dot_nn(c_rows, low(held))
    for pair in range(heads // 2):
        span = slice(pair * 2 * HEADDIM, (pair + 1) * 2 * HEADDIM)
        both = stepped_low[:, span]
        total = carried[:, span]
        for half in range(2):
            head = 2 * pair + half
            differ = running[:, head : head + 1] - running_t[head : head + 1, :]
            mixed = low(jnp.exp(jnp.where(mask, differ, -jnp.inf)) * scores)
            mine = jnp.where(first_half if half == 0 else ~first_half, both, zero)
            total = total + dot_nn(mixed, mine)
        y_ref[:, span] = total
    last = running_wide[BLOCK - 1 : BLOCK, :]
    to_end = jnp.exp(last - running_wide)
    state[...] = jnp.exp(last) * held + dot_nn(b_t, low(to_end * stepped))
    scanned_ref[...] = low(y_ref[...] + skip_ref[...] * inner_wide)


def gate_kernel(count, places_ref, *refs):
    blocks = refs[:count]
    (
        cot_ref,
        normed_ref,
        scanned_ref,
        gain_two_ref,
        gate_ref,
        out_ref,
        gating_ref,
        d_gnorm_ref,
        sums_ref,
    ) = refs[count:]
    local_di = gating_ref.shape[1]

    @pl.when(pl.program_id(0) == 0)
    def _():
        if count == 2:
            gate_ref[...] = blocks[0][...]
            out_ref[...] = blocks[1][...]
        else:
            for number, block in enumerate(blocks):
                spot = places_ref[number]
                place_columns(gate_ref, spot, block[:local_di, :])
                for tile in range(D // block.shape[1]):
                    first = local_di + tile * HEADDIM
                    columns = slice(tile * block.shape[1], (tile + 1) * block.shape[1])
                    place_rows(out_ref.at[:, columns], spot, block[first : first + HEADDIM, :])

    gating = dot_nt(normed_ref[...], gate_ref[...])
    gating_ref[...] = gating
    d_gnorm = dot_nt(cot_ref[...], out_ref[...])
    d_gnorm_ref[...] = d_gnorm
    gated = scanned_ref[...].astype(jnp.float32) * (gating * sigmoid(gating))
    ones = jnp.ones((8, local_di), jnp.float32)
    squares = dot_nt(ones, gated * gated, precise)
    products = dot_nt(ones, d_gnorm * gain_two_ref[...] * gated, precise)
    sums_ref[...] = jnp.where(
        lax.broadcasted_iota(jnp.int32, squares.shape, 0) == 0, squares, products
    )


def keep_chunk(value, here, number, mine_ref, send_ref):
    rows = pl.ds(pl.multiple_of(number * BLOCK, BLOCK), BLOCK)

    @pl.when(here)
    def _():
        mine_ref[rows, :] = value

    @pl.when(jnp.logical_not(here))
    def _():
        send_ref[rows, :] = value


def middle_kernel(gate_count, out_count, places_ref, *refs):
    (
        scanned_ref,
        gating_ref,
        d_gnorm_ref,
        cot_ref,
        normed_ref,
        sums_one_ref,
        sums_two_ref,
        sums_three_ref,
        sums_four_ref,
        out_ref,
        gain_two_ref,
        mine_ref,
        send_ref,
        d_gating_ref,
        d_scanned_ref,
        d_gain_two_ref,
    ) = refs[:16]
    gate_refs = refs[16 : 16 + gate_count]
    out_refs = refs[16 + gate_count : 16 + gate_count + out_count]
    out_sum, gate_sum = refs[16 + gate_count + out_count :]
    chunk = pl.program_id(0)

    @pl.when(chunk == 0)
    def _():
        out_sum[...] = jnp.zeros_like(out_sum)
        gate_sum[...] = jnp.zeros_like(gate_sum)
        d_gain_two_ref[...] = jnp.zeros_like(d_gain_two_ref)

    sums = (sums_one_ref[...] + sums_two_ref[...]) + (sums_three_ref[...] + sums_four_ref[...])
    sums = (sums / DI).T
    scale = lax.rsqrt(sums[:, 0:1] + norm_eps)
    slope = scale * scale * sums[:, 1:2]
    gating = gating_ref[...]
    open_part = sigmoid(gating)
    gate = gating * open_part
    scanned = scanned_ref[...].astype(jnp.float32)
    unit = scanned * gate * scale
    d_gnorm = d_gnorm_ref[...]
    gain_two = gain_two_ref[...]
    gnorm = low(unit * gain_two)
    block_part = low(dot_nn(gnorm, out_ref[...]))
    keep_chunk(block_part, chunk % 2 == places_ref[0], chunk // 2, mine_ref, send_ref)
    out_sum[...] += dot_tn(gnorm, cot_ref[...])
    d_gain_two_ref[...] += jnp.sum(d_gnorm * unit, axis=0, keepdims=True)
    d_gated = scale * (d_gnorm * gain_two) - unit * slope
    d_gating = low(d_gated * scanned * (open_part * (1.0 + gating * (1.0 - open_part))))
    d_gating_ref[...] = d_gating
    d_scanned_ref[...] = low(d_gated * gate)
    gate_sum[...] += dot_tn(d_gating, normed_ref[...])

    @pl.when(chunk == pl.num_programs(0) - 1)
    def _():
        for number, gate_ref in enumerate(gate_refs):
            columns = gate_ref.shape[1]
            start = pl.multiple_of(places_ref[1 + number] * columns, columns)
            gate_ref[...] = low(gate_sum[:, pl.ds(start, columns)])
        for number, grad_ref in enumerate(out_refs):
            columns = grad_ref.shape[1]
            first = places_ref[1 + gate_count + number]
            for step in range(out_sum.shape[0] // HEADDIM // out_count):
                head = first + step * out_count
                rows = pl.ds(pl.multiple_of(head * HEADDIM, HEADDIM), HEADDIM)
                for tile in range(D // columns):
                    base = (step * (D // columns) + tile) * HEADDIM
                    grad_ref[base : base + HEADDIM, :] = low(
                        out_sum[rows, tile * columns : (tile + 1) * columns]
                    )


def backward_kernel(
    grad_count,
    places_ref,
    normed_ref,
    conv_in_ref,
    conv_pre_ref,
    dt_ref,
    y_ref,
    state_ref,
    d_scanned_ref,
    conv_ref,
    a_log_ref,
    dt_bias_ref,
    skip_ref,
    expand_ref,
    d_rest_ref,
    d_kernel_ref,
    d_conv_bias_ref,
    d_skip_ref,
    d_head_ref,
    *refs,
):
    grad_refs = refs[:grad_count]
    ext, d_state, later_state, rest_sum = refs[grad_count:]
    local_di = y_ref.shape[1]
    heads = local_di // HEADDIM
    chunk = pl.program_id(0)

    @pl.when(chunk == 0)
    def _():
        ext[BLOCK : BLOCK + 8, :] = jnp.zeros((8, ext.shape[1]), jnp.float32)
        d_state[...] = jnp.zeros_like(d_state)
        later_state[...] = jnp.zeros_like(later_state)
        rest_sum[...] = jnp.zeros_like(rest_sum)
        d_kernel_ref[...] = jnp.zeros_like(d_kernel_ref)
        d_conv_bias_ref[...] = jnp.zeros_like(d_conv_bias_ref)
        d_skip_ref[...] = jnp.zeros_like(d_skip_ref)
        d_head_ref[...] = jnp.zeros_like(d_head_ref)

    expand = expand_ref[...]
    conv_pre = conv_pre_ref[...]
    open_part = sigmoid(conv_pre)
    conv_low = low(conv_pre * open_part)
    inner = conv_low[:, :local_di].astype(jnp.float32)
    b_rows = conv_low[:, local_di : local_di + STATE]
    c_rows = conv_low[:, local_di + STATE :]
    a_log = a_log_ref[...]
    shifted, _, log_decay, running, step_wide, running_wide = decay_sums(
        dt_ref[...], dt_bias_ref[...], a_log, expand
    )
    running_t = running.T
    b_t = low(b_rows.astype(jnp.float32).T)
    c_t = low(c_rows.astype(jnp.float32).T)
    scores = dot_nn(c_rows, b_t)
    scores_t = dot_nn(b_rows, c_t)
    mask = lower_mask()
    rows = lax.broadcasted_iota(jnp.int32, (BLOCK, BLOCK), 0)
    mask_t = rows <= lax.broadcasted_iota(jnp.int32, (BLOCK, BLOCK), 1)
    d_y_low = d_scanned_ref[...]
    d_y = d_y_low.astype(jnp.float32)
    stepped_low = low(step_wide * inner)
    stepped = stepped_low.astype(jnp.float32)
    last = running_wide[BLOCK - 1 : BLOCK, :]
    to_end = jnp.exp(last - running_wide)
    d_later = d_state[...]
    d_later_low = low(d_later)
    held = state_ref[...].reshape(d_state.shape)
    decayed_dy = low(jnp.exp(running_wide) * d_y)
    d_c = dot_nt(decayed_dy, low(held))
    d_b = dot_nt(low(to_end * stepped), d_later_low)
    d_stepped = to_end * dot_nn(b_rows, d_later_low)
    cross = jnp.sum(later_state[...] * d_later, axis=0, keepdims=True)
    d_state[...] = jnp.exp(last) * d_later + dot_nn(c_t, decayed_dy)
    later_state[...] = held
    first_half = lax.broadcasted_iota(jnp.int32, (BLOCK, 2 * HEADDIM), 1) < HEADDIM
    zero = jnp.zeros((), jnp.bfloat16)
    d_scores = jnp.zeros((BLOCK, BLOCK), jnp.float32)
    pieces = []
    for pair in range(heads // 2):
        span = slice(pair * 2 * HEADDIM, (pair + 1) * 2 * HEADDIM)
        total = d_stepped[:, span]
        for half in range(2):
            head = 2 * pair + half
            mine = jnp.where(first_half if half == 0 else ~first_half, d_y_low[:, span], zero)
            column = running[:, head : head + 1]
            row = running_t[head : head + 1, :]
            decay = jnp.exp(jnp.where(mask, column - row, -jnp.inf))
            decay_t = jnp.exp(jnp.where(mask_t, row - column, -jnp.inf))
            d_scores = d_scores + dot_nt(mine, stepped_low[:, span]) * decay
            total = total + dot_nn(low(decay_t * scores_t), mine)
        pieces.append(total)
    d_stepped = jnp.concatenate(pieces, 1)
    d_scores_low = low(d_scores)
    d_c = d_c + dot_nn(d_scores_low, b_rows)
    d_b = d_b + dot_nn(low(d_scores.T), c_rows)
    d_inner = step_wide * d_stepped + skip_ref[...] * d_y
    d_running = dot_nt(d_y * y_ref[...] - d_stepped * stepped, expand, precise)
    upper = jnp.where(mask_t, 1.0, 0.0)
    d_log = dot_nn(upper, d_running, precise) + dot_nt(cross, expand, precise)
    d_step = dot_nt(d_stepped * inner, expand, precise) - jnp.exp(a_log) * d_log
    d_dt = d_step * sigmoid(shifted)
    d_head_ref[0:1, :] += jnp.sum(d_log * log_decay, axis=0, keepdims=True)
    d_head_ref[1:2, :] += jnp.sum(d_dt, axis=0, keepdims=True)
    d_skip_ref[...] += jnp.sum(d_y * inner, axis=0, keepdims=True)

    d_conv_out = jnp.concatenate([d_inner, d_b, d_c], 1)
    d_pre = d_conv_out * (open_part * (1.0 + conv_pre * (1.0 - open_part)))
    ext[0:BLOCK, :] = d_pre
    d_conv_bias_ref[...] += jnp.sum(d_pre, axis=0, keepdims=True)
    conv_in = conv_in_ref[...]
    d_conv_in = jnp.zeros_like(conv_in)
    for tap in range(WIDTH):
        moved = ext[WIDTH - 1 - tap : WIDTH - 1 - tap + BLOCK, :]
        d_conv_in = d_conv_in + conv_ref[tap : tap + 1, :] * moved
        d_kernel_ref[tap : tap + 1, :] += jnp.sum(moved * conv_in, axis=0, keepdims=True)
    ext[BLOCK : BLOCK + 8, :] = ext[0:8, :]
    d_rest = jnp.concatenate([low(d_conv_in), low(d_dt)], 1)
    d_rest_ref[...] = d_rest
    rest_sum[...] += dot_tn(d_rest, normed_ref[...])

    @pl.when(chunk == pl.num_programs(0) - 1)
    def _():
        for number, grad_ref in enumerate(grad_refs):
            rows, columns = grad_ref.shape
            start = pl.multiple_of(places_ref[number] * columns, columns)
            grad_ref[...] = low(rest_sum[:rows, pl.ds(start, columns)])


def sum_of(*refs):
    total = refs[0][...].astype(jnp.float32)
    for ref in refs[1:]:
        total = total + ref[...].astype(jnp.float32)
    return total


def pair_kernel(places_ref, *refs):
    gate, out, block = refs[:4], refs[4:6], refs[6:8]
    gate_keep_ref, gate_send_ref, block_keep_ref, block_send_ref = refs[8:12]
    out_refs = refs[12:]
    paired = sum_of(*gate)
    columns = gate_keep_ref.shape[1]
    even = places_ref[0] == 0
    first, second = low(paired[:, :columns]), low(paired[:, columns:])
    gate_keep_ref[...] = jnp.where(even, first, second)
    gate_send_ref[...] = jnp.where(even, second, first)
    rows = block_keep_ref.shape[0]
    for ref, place in ((block_keep_ref, places_ref[1]), (block_send_ref, 1 - places_ref[1])):
        here = pl.ds(pl.multiple_of(place * rows, rows), rows)
        ref[...] = low(sum_of(block[0].at[here, :], block[1].at[here, :]))
    for number, ref in enumerate(out_refs):
        rows = ref.shape[0]
        start = pl.multiple_of(places_ref[2 + number] * rows, rows)
        here = pl.ds(start, rows)
        ref[...] = low(sum_of(out[0].at[here, :], out[1].at[here, :]))


def normed_kernel(
    places_ref,
    hidden_ref,
    d_gating_ref,
    d_rest_ref,
    gate_weight_ref,
    rest_weight_ref,
    mine_ref,
    send_ref,
    d_gain_one_ref,
):
    chunk = pl.program_id(0)

    @pl.when(chunk == 0)
    def _():
        d_gain_one_ref[...] = jnp.zeros_like(d_gain_one_ref)

    d_normed = dot_nn(d_gating_ref[...], gate_weight_ref[...])
    d_normed = d_normed + dot_nn(d_rest_ref[...], rest_weight_ref[...])
    keep_chunk(low(d_normed), chunk % 2 == places_ref[0], chunk // 2, mine_ref, send_ref)
    unit = rms_scale(hidden_ref[...].astype(jnp.float32))
    d_gain_one_ref[...] += jnp.sum(d_normed * unit, axis=0, keepdims=True)


def prepare_kernel(places_ref, in_ref, out_ref, hidden_ref, cot_ref, rest_ref, gate_out_ref, both_ref):
    index = places_ref[0]
    local_di = gate_out_ref.shape[0] // 2
    groups = DI // local_di
    for head in range(HEADS // groups):
        rows = slice(head * HEADDIM, (head + 1) * HEADDIM)
        for base, result_ref in ((0, gate_out_ref), (DI, rest_ref)):
            start = pl.multiple_of(base + (groups * head + index) * HEADDIM, HEADDIM)
            result_ref[rows, :] = low(in_ref[pl.ds(start, HEADDIM), :])
    channels = local_di + 2 * STATE
    rest_ref[local_di:channels, :] = low(in_ref[2 * DI : 2 * DI + 2 * STATE, :])
    rows = rest_ref.shape[0] - channels
    target = lax.broadcasted_iota(jnp.int32, (rows, HEADS), 0)
    source = lax.broadcasted_iota(jnp.int32, (rows, HEADS), 1)
    chosen = (source == groups * target + index) & (target < HEADS // groups)
    steps = low(in_ref[DI + CONVCH :, :])
    rest_ref[channels:, :] = low(dot_nn(jnp.where(chosen, 1.0, 0.0).astype(jnp.bfloat16), steps))
    mine = pl.ds(pl.multiple_of(index * HEADDIM, HEADDIM), HEADDIM)
    columns = gate_out_ref.shape[1]
    for tile in range(D // columns):
        first = local_di + tile * HEADDIM
        gate_out_ref[first : first + HEADDIM, :] = low(
            out_ref[mine, tile * columns : (tile + 1) * columns]
        )
    half = hidden_ref.shape[0]
    both_ref[:half, :] = hidden_ref[...]
    both_ref[half:, :] = cot_ref[...]


def update_kernel(groups, places_ref, *refs):
    gate_out_blocks = refs[:groups]
    rest_blocks = refs[groups : 2 * groups]
    in_refs = refs[2 * groups : 2 * groups + 3]
    out_refs = refs[2 * groups + 3 : 2 * groups + 6]
    in_new_refs = refs[2 * groups + 6 : 2 * groups + 9]
    out_new_refs = refs[2 * groups + 9 : 2 * groups + 12]
    gate_out, rest = refs[2 * groups + 12 :]
    chunk = pl.program_id(0)
    local_di = gate_out.shape[1] // 2
    channels = local_di + 2 * STATE
    parts = DI // in_refs[0].shape[0]

    @pl.when(chunk == 0)
    def _():
        for number in range(groups):
            gate_out[places_ref[number]] = gate_out_blocks[number][...]
            rest[places_ref[number]] = rest_blocks[number][...]

    def step(old_refs, new_refs, rows, columns, grad):
        results = adamw_step(
            *[ref[rows, columns] for ref in old_refs], grad, matrix_rate, matrix_decay
        )
        for ref, result in zip(new_refs, results):
            ref[rows, columns] = result

    def step_heads(source, part):
        heads = local_di // HEADDIM // parts
        for head in range(heads):
            start = pl.multiple_of((part * heads + head) * HEADDIM, HEADDIM)
            for group in range(groups):
                first = (head * groups + group) * HEADDIM
                grad = source[group, pl.ds(start, HEADDIM), :].astype(jnp.float32)
                step(in_refs, in_new_refs, slice(first, first + HEADDIM), slice(None), grad)

    @pl.when(chunk < parts)
    def _():
        step_heads(gate_out, chunk)

    @pl.when((chunk >= parts) & (chunk < 2 * parts))
    def _():
        step_heads(rest, chunk - parts)

    @pl.when(chunk == 2 * parts)
    def _():
        both = rest[0, local_di:channels, :].astype(jnp.float32)
        rows = rest.shape[1] - channels
        steps = jnp.zeros((HEADS, rest.shape[2]), jnp.float32)
        target = lax.broadcasted_iota(jnp.int32, (HEADS, rows), 0)
        source = lax.broadcasted_iota(jnp.int32, (HEADS, rows), 1)
        for group in range(groups):
            if group > 0:
                both = both + rest[group, local_di:channels, :].astype(jnp.float32)
            chosen = jnp.where(target == groups * source + group, 1.0, 0.0).astype(jnp.bfloat16)
            steps = steps + dot_nn(chosen, rest[group, channels:, :])
        step(in_refs, in_new_refs, slice(0, 2 * STATE), slice(None), both)
        step(in_refs, in_new_refs, slice(2 * STATE, 2 * STATE + HEADS), slice(None), steps)

    @pl.when(chunk < groups)
    def _():
        columns = gate_out.shape[2]
        for tile in range(D // columns):
            first = local_di + tile * HEADDIM
            grad = gate_out[chunk, first : first + HEADDIM, :].astype(jnp.float32)
            span = slice(tile * columns, (tile + 1) * columns)
            step(out_refs, out_new_refs, slice(None), span, grad)


def kernel_params():
    return pltpu.CompilerParams(
        dimension_semantics=("arbitrary",), vmem_limit_bytes=56 * 1024 * 1024
    )


def cost(flops, moved, transcendentals):
    return pl.CostEstimate(flops=flops, bytes_accessed=moved, transcendentals=transcendentals)


def after(kernel, inputs, arrived):
    def run(*refs):
        kernel(*refs[:inputs], *refs[inputs + arrived :])

    return run


def corner(array):
    return pl.BlockSpec((min(16, array.shape[0]), 128), lambda *_: (0, 0))


def fixed(shape):
    return pl.BlockSpec(shape, lambda *_: (0,) * len(shape))


def rows_of(extent, first=0):
    return pl.BlockSpec((BLOCK, extent), lambda q, *_: (q + first, 0))


def struct(shape, dtype=jnp.float32):
    return jax.ShapeDtypeStruct(shape, dtype)


def call(kernel, places, inputs, in_specs, outputs, out_specs, scratch, grid, arrived, price, name):
    return pl.pallas_call(
        after(kernel, 1 + len(inputs), len(arrived)),
        grid_spec=pltpu.PrefetchScalarGridSpec(
            num_scalar_prefetch=1,
            grid=(grid,),
            in_specs=list(in_specs) + [corner(array) for array in arrived],
            out_specs=out_specs,
            scratch_shapes=scratch,
        ),
        out_shape=outputs,
        compiler_params=kernel_params(),
        cost_estimate=cost(*price),
        name=name,
    )(jnp.stack(places).astype(jnp.int32), *inputs, *arrived)


def run_prepare(index, in_t, out_weight, hidden, cot):
    columns = in_t.shape[1]
    local_di = DI // 4
    shapes = [
        (local_di + 2 * STATE + 16, columns),
        (2 * local_di, columns),
        (2 * hidden.shape[0], D),
    ]
    inputs = [in_t, out_weight, hidden, cot]
    return call(
        prepare_kernel,
        [index],
        inputs,
        [fixed(array.shape) for array in inputs],
        [struct(shape, jnp.bfloat16) for shape in shapes],
        [fixed(shape) for shape in shapes],
        [],
        1,
        [],
        (100_000_000, 4_000_000, 0),
        "prepare",
    )


def run_forward(both, rest, gain_one, conv, heads_vectors, expand):
    both_places, both_blocks = both
    rest_places, rest_blocks = rest
    length = both_blocks[0].shape[0] // 2 * len(both_blocks)
    chunks = length // BLOCK
    lanes, local_di = expand.shape
    channels = local_di + 2 * STATE
    vectors = [gain_one, *conv, *heads_vectors, expand]
    inputs = [*both_blocks, *rest_blocks, *vectors]
    return call(
        lambda *refs: forward_kernel(len(both_blocks), len(rest_blocks), *refs),
        both_places + rest_places,
        inputs,
        [fixed(array.shape) for array in inputs],
        [
            struct((length, D), jnp.bfloat16),
            struct((length, D), jnp.bfloat16),
            struct((channels + lanes, D), jnp.bfloat16),
            struct((length, D), jnp.bfloat16),
            struct((length, channels)),
            struct((length, channels)),
            struct((length, lanes)),
            struct((length, local_di)),
            struct((length, local_di), jnp.bfloat16),
            struct((chunks, STATE, local_di)),
        ],
        [
            fixed((length, D)),
            fixed((length, D)),
            fixed((channels + lanes, D)),
            rows_of(D),
            rows_of(channels),
            rows_of(channels),
            rows_of(lanes),
            rows_of(local_di),
            rows_of(local_di),
            pl.BlockSpec((1, STATE, local_di), lambda q, *_: (q, 0, 0)),
        ],
        [
            pltpu.VMEM((8 + BLOCK, channels), jnp.float32),
            pltpu.VMEM((STATE, local_di), jnp.float32),
        ],
        chunks,
        [],
        (6_000_000_000, 30_000_000, 8_000_000),
        "forward",
    )


def run_gate(gate_out, cot, normed, scanned, gain_two):
    places, blocks = gate_out
    length, local_di = scanned.shape
    return call(
        lambda *refs: gate_kernel(len(blocks), *refs),
        places,
        [*blocks, cot, normed, scanned, gain_two],
        [fixed(array.shape) for array in blocks]
        + [rows_of(D), rows_of(D), rows_of(local_di), fixed((1, local_di))],
        [
            struct((local_di, D), jnp.bfloat16),
            struct((local_di, D), jnp.bfloat16),
            struct((length, local_di)),
            struct((length, local_di)),
            struct((8, length)),
        ],
        [
            fixed((local_di, D)),
            fixed((local_di, D)),
            rows_of(local_di),
            rows_of(local_di),
            pl.BlockSpec((8, BLOCK), lambda q, *_: (0, q)),
        ],
        [],
        length // BLOCK,
        [],
        (2_500_000_000, 12_000_000, 1_000_000),
        "gate",
    )


def run_middle(parity, gate_places, out_places, scanned, gating, d_gnorm, cot, normed, sums, out, gain):
    length, local_di = scanned.shape
    gate_shape = (local_di, D // len(gate_places))
    out_shape = (local_di, D) if len(out_places) == 1 else (local_di * D // 256, 128)
    shapes = [gate_shape] * len(gate_places) + [out_shape] * len(out_places)
    return call(
        lambda *refs: middle_kernel(len(gate_places), len(out_places), *refs),
        [parity] + gate_places + out_places,
        [scanned, gating, d_gnorm, cot, normed, *sums, out, gain],
        [
            rows_of(local_di),
            rows_of(local_di),
            rows_of(local_di),
            rows_of(D),
            rows_of(D),
        ]
        + [pl.BlockSpec((8, BLOCK), lambda q, *_: (0, q))] * 4
        + [fixed((local_di, D)), fixed((1, local_di))],
        [
            struct((length // 2, D), jnp.bfloat16),
            struct((length // 2, D), jnp.bfloat16),
            struct((length, local_di), jnp.bfloat16),
            struct((length, local_di), jnp.bfloat16),
            struct((1, local_di)),
        ]
        + [struct(shape, jnp.bfloat16) for shape in shapes],
        [
            fixed((length // 2, D)),
            fixed((length // 2, D)),
            rows_of(local_di),
            rows_of(local_di),
            fixed((1, local_di)),
        ]
        + [fixed(shape) for shape in shapes],
        [pltpu.VMEM((local_di, D), jnp.float32), pltpu.VMEM((local_di, D), jnp.float32)],
        length // BLOCK,
        [],
        (4_000_000_000, 15_000_000, 500_000),
        "middle",
    )


def run_backward(
    places, normed, conv_in, conv_pre, dt_raw, y, states, d_scanned, kernel, heads_vectors, expand
):
    length, local_di = y.shape
    chunks = length // BLOCK
    channels = conv_in.shape[1]
    lanes = expand.shape[0]
    grad = (channels + 16, D // len(places))

    def back(extent):
        return pl.BlockSpec((BLOCK, extent), lambda q, *_: (chunks - 1 - q, 0))

    return call(
        lambda *refs: backward_kernel(len(places), *refs),
        places,
        [normed, conv_in, conv_pre, dt_raw, y, states, d_scanned, kernel, *heads_vectors, expand],
        [
            back(D),
            back(channels),
            back(channels),
            back(lanes),
            back(local_di),
            pl.BlockSpec((1, STATE, local_di), lambda q, *_: (chunks - 1 - q, 0, 0)),
            back(local_di),
            fixed((WIDTH, channels)),
            fixed((1, lanes)),
            fixed((1, lanes)),
            fixed((1, local_di)),
            fixed((lanes, local_di)),
        ],
        [
            struct((length, channels + lanes), jnp.bfloat16),
            struct((WIDTH, channels)),
            struct((1, channels)),
            struct((1, local_di)),
            struct((2, lanes)),
        ]
        + [struct(grad, jnp.bfloat16)] * len(places),
        [
            back(channels + lanes),
            fixed((WIDTH, channels)),
            fixed((1, channels)),
            fixed((1, local_di)),
            fixed((2, lanes)),
        ]
        + [fixed(grad)] * len(places),
        [
            pltpu.VMEM((BLOCK + 8, channels), jnp.float32),
            pltpu.VMEM((STATE, local_di), jnp.float32),
            pltpu.VMEM((STATE, local_di), jnp.float32),
            pltpu.VMEM((channels + lanes, D), jnp.float32),
        ],
        chunks,
        [],
        (14_000_000_000, 40_000_000, 10_000_000),
        "backward",
    )


def run_pair(y, far, out_places, gate, out, block):
    columns = gate[0].shape[1] // 2
    shapes = [
        (gate[0].shape[0], columns),
        (gate[0].shape[0], columns),
        (block[0].shape[0] // 2, D),
        (block[0].shape[0] // 2, D),
    ] + [(out[0].shape[0] // len(out_places), out[0].shape[1])] * len(out_places)
    inputs = [*gate, *out, *block]
    return call(
        pair_kernel,
        [y, far] + out_places,
        inputs,
        [fixed(array.shape) for array in inputs],
        [struct(shape, jnp.bfloat16) for shape in shapes],
        [fixed(shape) for shape in shapes],
        [],
        1,
        [],
        (3_000_000, 7_000_000, 0),
        "pair",
    )


def run_normed(parity, hidden, d_gating, d_rest, gate_weight, rest_weight, arrived):
    length, local_di = d_gating.shape
    rest = d_rest.shape[1]
    return call(
        normed_kernel,
        [parity],
        [hidden, d_gating, d_rest, gate_weight, rest_weight],
        [
            rows_of(D),
            rows_of(local_di),
            rows_of(rest),
            fixed((local_di, D)),
            fixed((rest, D)),
        ],
        [
            struct((length // 2, D), jnp.bfloat16),
            struct((length // 2, D), jnp.bfloat16),
            struct((1, D)),
        ],
        [fixed((length // 2, D)), fixed((length // 2, D)), fixed((1, D))],
        [],
        length // BLOCK,
        arrived,
        (3_000_000_000, 9_000_000, 1000),
        "normed",
    )


def run_update(places, gate_out_blocks, rest_blocks, in_arrays, out_arrays):
    groups = len(places)
    blocks = [*gate_out_blocks, *rest_blocks]
    rows_in = DI // 4
    rows_out = out_arrays[0].shape[0] // groups
    arrays = [*in_arrays, *out_arrays]
    in_spec = pl.BlockSpec((rows_in, in_arrays[0].shape[1]), lambda q, *_: (q, 0))
    out_spec = pl.BlockSpec((rows_out, D), lambda q, *_: (jnp.minimum(q, groups - 1), 0))
    specs = [in_spec] * 3 + [out_spec] * 3
    return call(
        lambda *refs: update_kernel(groups, *refs),
        places,
        [*blocks, *arrays],
        [fixed(array.shape) for array in blocks] + specs,
        [struct(array.shape) for array in arrays],
        specs,
        [
            pltpu.VMEM((groups,) + gate_out_blocks[0].shape, jnp.bfloat16),
            pltpu.VMEM((groups,) + rest_blocks[0].shape, jnp.bfloat16),
        ],
        2 * (DI // rows_in) + 1,
        [],
        (20_000_000, 22_000_000, 1_000_000),
        "update",
    )


def adamw_step(weight, first, second, grad, rate, decay):
    first_new = beta_one * first + (1.0 - beta_one) * grad
    second_new = beta_two * second + (1.0 - beta_two) * grad * grad
    fix_one = 1.0 - beta_one**STEP
    fix_two = 1.0 - beta_two**STEP
    normalized = first_new / fix_one / (jnp.sqrt(second_new / fix_two) + adam_eps)
    return (first_new, second_new, weight - rate * (normalized + decay * weight))


def pick_heads(values, axis, width, index, groups):
    shape = values.shape
    split = shape[:axis] + (HEADS // groups, groups, width) + shape[axis + 1 :]
    taken = lax.dynamic_index_in_dim(values.reshape(split), index, axis + 1, keepdims=False)
    return taken.reshape(shape[:axis] + (HEADS // groups * width,) + shape[axis + 1 :])


def merge_heads(stacked, axis, width):
    groups = stacked.shape[0]
    shape = stacked.shape[1:]
    split = (groups,) + shape[:axis] + (HEADS // groups, width) + shape[axis + 1 :]
    moved = jnp.moveaxis(stacked.reshape(split), 0, axis + 1)
    return moved.reshape(shape[:axis] + (HEADS * width,) + shape[axis + 1 :])


def swap(values, axis, mask):
    route = [(i, i ^ mask) for i in range(lax.axis_size(axis))]
    return lax.ppermute(values, axis, route)


def seq_blocks(rows, far=None):
    index = lax.axis_index("seq")
    far = swap(rows, "seq", 2) if far is None else far
    blocks = [rows, swap(rows, "seq", 1), far, swap(far, "seq", 1)]
    return [index ^ mask for mask in range(4)], blocks


def ring_step(held):
    count = lax.axis_size("wshard")
    return lax.ppermute(held, "wshard", [(i, (i + 2) % count) for i in range(count)])


def ring_blocks(rows):
    count = lax.axis_size("wshard")
    index = lax.axis_index("wshard")
    places, blocks = [], []
    for step in range(count // 2):
        source = (index + count - 2 * step) % count
        places = places + [source, source ^ 1]
        blocks = blocks + [rows, swap(rows, "wshard", 1)]
        if step < count // 2 - 1:
            rows = ring_step(rows)
    return places, blocks


def add_kernel(counts, places_ref, *refs):
    terms, results = refs[: sum(counts)], refs[sum(counts) :]
    first = 0
    for count, result in zip(counts, results):
        total = sum_of(*terms[first : first + count])
        result[...] = total.astype(result.dtype)
        first = first + count


def add(groups, arrived):
    terms = [term for group in groups for term in group]
    return call(
        lambda *refs: add_kernel([len(group) for group in groups], *refs),
        [jnp.int32(0)],
        terms,
        [fixed(term.shape) for term in terms],
        [struct(group[0].shape, group[0].dtype) for group in groups],
        [fixed(group[0].shape) for group in groups],
        [],
        1,
        arrived,
        (200_000, 900_000, 0),
        "add",
    )


def take_block(values, index, rows):
    return lax.dynamic_slice_in_dim(values, index * rows, rows, 0)


def gather_out(out_low, seq_index, groups):
    rows = out_low.shape[0]
    if rows % (groups * HEADDIM) == 0:
        mine = pick_rows(out_low, seq_index, groups)
        return lax.all_gather(mine, "wshard", axis=0, tiled=True)
    whole = lax.all_gather(out_low, "wshard", axis=0, tiled=True)
    return pick_heads(whole, 0, HEADDIM, seq_index, groups)


def pick_rows(values, seq_index, groups):
    rows = values.shape[0]
    split = values.reshape(rows // (groups * HEADDIM), groups, HEADDIM, values.shape[1])
    return lax.dynamic_index_in_dim(split, seq_index, 1, keepdims=False).reshape(
        rows // groups, values.shape[1]
    )


def sum_out_grad(grad, rows, seq_index, groups):
    grad = grad.astype(jnp.bfloat16)
    if rows % (groups * HEADDIM) == 0:
        mine = lax.psum_scatter(grad, "wshard", scatter_dimension=0, tiled=True)
        every = lax.all_gather(mine, "seq", axis=0, tiled=False)
        split = every.reshape(groups, rows // (groups * HEADDIM), HEADDIM, grad.shape[1])
        return jnp.moveaxis(split, 0, 1).reshape(rows, grad.shape[1]).astype(jnp.float32)
    blocks = grad.reshape(HEADS // groups, 1, HEADDIM, grad.shape[1])
    here = (jnp.arange(groups) == seq_index)[None, :, None, None]
    spread = jnp.where(here, blocks, jnp.zeros((), jnp.bfloat16)).reshape(DI, grad.shape[1])
    mine = lax.psum_scatter(spread, "wshard", scatter_dimension=0, tiled=True)
    return lax.psum(mine.astype(jnp.float32), "seq")


def shards(
    block_in,
    cotangent,
    in_weight,
    in_first,
    in_second,
    out_weight,
    out_first,
    out_second,
    vec_weight,
    vec_first,
    vec_second,
):
    rows_here = block_in.shape[1]
    groups = lax.axis_size("seq")
    seq_index = lax.axis_index("seq")
    local_heads = HEADS // groups
    local_di = DI // groups
    hidden_rows = block_in.reshape(rows_here, D)
    cot_rows = cotangent.reshape(rows_here, D)
    gain_one, gain_two, kernel, conv_bias, a_log, dt_bias, d_skip = split_vector(vec_weight)

    def heads_of(values, axis, width):
        return pick_heads(values, axis, width, seq_index, groups)

    lanes = 128
    channels = local_di + 2 * STATE
    shard_index = lax.axis_index("wshard")
    rings = lax.axis_size("wshard") == 8
    near = seq_index % 2
    far = seq_index // 2
    if rings:
        y, z = shard_index % 2, shard_index // 2
        rest_mine, gate_out_mine, both_mine = run_prepare(
            seq_index, in_weight.T, out_weight, hidden_rows, cot_rows
        )
        rest = ring_blocks(rest_mine)
        both = seq_blocks(both_mine)
        gate_out = ring_blocks(gate_out_mine)
        gate_places = [z ^ mask for mask in range(4)]
        out_places = [y, 1 - y]
        rest_places = [
            (shard_index + 8 - 2 * step) % 8 ^ other for step in range(1, 5) for other in (0, 1)
        ]
    else:
        in_low = low(in_weight)
        steps_mine = heads_of(in_low[:, DI + CONVCH :], 1, 1)
        rest_mine = jnp.concatenate(
            [
                heads_of(in_low[:, DI : 2 * DI], 1, HEADDIM),
                in_low[:, 2 * DI : 2 * DI + 2 * STATE],
                jnp.pad(steps_mine, ((0, 0), (0, 16 - local_heads))),
            ],
            1,
        )
        gate_mine = heads_of(in_low[:, :DI], 1, HEADDIM)
        origin = [jnp.int32(0)]
        rest = (origin, [lax.all_gather(rest_mine, "wshard", axis=0, tiled=True).T])
        hidden_low = lax.all_gather(hidden_rows, "seq", axis=0, tiled=True)
        cot_low = lax.all_gather(cot_rows, "seq", axis=0, tiled=True)
        both = (origin, [jnp.concatenate([hidden_low, cot_low], 0)])
        gate_mine = lax.all_gather(gate_mine, "wshard", axis=0, tiled=True).T
        gate_out = (origin, [gate_mine, gather_out(low(out_weight), seq_index, groups)])
        gate_places, out_places, rest_places = origin, origin, origin
    my_gain_two = heads_of(gain_two, 0, HEADDIM)[None, :]
    my_kernel = jnp.concatenate([heads_of(kernel[:, :DI], 1, HEADDIM), kernel[:, DI:]], 1)
    my_bias = jnp.concatenate([heads_of(conv_bias[:DI], 0, HEADDIM), conv_bias[DI:]], 0)

    def on_lanes(values):
        return jnp.pad(values, (0, lanes - local_heads))[None, :]

    heads_vectors = (
        on_lanes(heads_of(a_log, 0, 1)),
        on_lanes(heads_of(dt_bias, 0, 1)),
        jnp.repeat(heads_of(d_skip, 0, 1), HEADDIM)[None, :],
    )
    expand = (
        jnp.arange(lanes)[:, None] == jnp.arange(local_di)[None, :] // HEADDIM
    ).astype(jnp.float32)
    (
        hidden_low,
        cot_low,
        rest_weight,
        normed_low,
        conv_in,
        conv_pre,
        dt_raw,
        y_part,
        scanned,
        states,
    ) = run_forward(
        both, rest, gain_one[None, :], (my_kernel, my_bias[None, :]), heads_vectors, expand
    )
    gate_weight, out_low, gating, d_gnorm, sums = run_gate(
        gate_out, cot_low, normed_low, scanned, my_gain_two
    )
    middle = run_middle(
        near,
        gate_places,
        out_places,
        scanned,
        gating,
        d_gnorm,
        cot_low,
        normed_low,
        [sums] + [swap(sums, "seq", mask) for mask in range(1, 4)],
        out_low,
        my_gain_two,
    )
    block_mine, block_send, d_gating, d_scanned, d_gain_two = middle[:5]
    gate_grads = middle[5 : 5 + len(gate_places)]
    out_grads = middle[5 + len(gate_places) :]
    block_arrived = swap(block_send, "seq", 1)
    if rings:
        gate_pieces = [swap(gate_grads[mask], "wshard", 2 * mask) for mask in range(1, 4)]
        out_arrived = swap(out_grads[1], "wshard", 1)
    backward = run_backward(
        rest_places,
        normed_low,
        conv_in,
        conv_pre,
        dt_raw,
        y_part,
        states,
        d_scanned,
        my_kernel,
        heads_vectors,
        expand,
    )
    d_rest, d_kernel, d_conv_bias, d_skip_wide, d_head = backward[:5]
    rest_grads = backward[5:]
    before_normed = []
    if rings:
        rest_arrived = swap(rest_grads[1], "wshard", 1)
        gate_keep, gate_send, block_keep, block_send, *out_sums = run_pair(
            y,
            far,
            gate_places,
            [gate_grads[0]] + gate_pieces,
            [out_grads[0], out_arrived],
            [block_mine, block_arrived],
        )
        gate_arrived = swap(gate_send, "wshard", 1)
        out_pieces = [swap(out_sums[mask], "wshard", 2 * mask) for mask in range(1, 4)]
        before_normed = [gate_keep]
    else:
        block_sum = low(block_mine.astype(jnp.float32) + block_arrived.astype(jnp.float32))
        block_keep = take_block(block_sum, far, rows_here)
        block_send = take_block(block_sum, 1 - far, rows_here)
    block_far = swap(block_send, "seq", 2)
    normed_mine, normed_send, d_gain_one = run_normed(
        near, hidden_low, d_gating, d_rest, gate_weight, rest_weight, before_normed
    )
    normed_arrived = swap(normed_send, "seq", 1)
    normed_sum = normed_mine.astype(jnp.float32) + normed_arrived.astype(jnp.float32)
    normed_far = swap(low(take_block(normed_sum, 1 - far, rows_here)), "seq", 2)
    shared = jnp.concatenate(
        [d_gain_one[0], d_kernel[:, local_di:].reshape(-1), d_conv_bias[0, local_di:]]
    )
    d_skip_part = jnp.sum(d_skip_wide.reshape(local_heads, HEADDIM), axis=1)
    apart = jnp.concatenate(
        [
            d_gain_two[0],
            d_kernel[:, :local_di].reshape(-1),
            d_conv_bias[0, :local_di],
            d_head[:, :local_heads].reshape(-1),
            d_skip_part,
        ]
    )
    vec_part = jnp.concatenate([shared, apart])[None]
    if rings:
        (held,) = add(
            [[rest_grads[0], rest_arrived]], [d_gain_one, gate_arrived, block_far] + out_pieces
        )
        vec_arrived = swap(vec_part, "wshard", 1)
        held, gate_part, out_part, vec_part = add(
            [
                [rest_grads[2], swap(rest_grads[3], "wshard", 1), ring_step(held)],
                [gate_keep, gate_arrived],
                [out_sums[0]] + out_pieces,
                [vec_part, vec_arrived],
            ],
            [normed_arrived],
        )
        gate_out_part = jnp.concatenate([gate_part, out_part], 0)
        gate_out_far = swap(gate_out_part, "seq", 2)
        held, vec_part = add(
            [
                [rest_grads[4], swap(rest_grads[5], "wshard", 1), ring_step(held)],
                [vec_part, swap(vec_part, "wshard", 2)],
            ],
            [gate_out_far],
        )
        rest_part, vec_part = add(
            [
                [rest_grads[6], swap(rest_grads[7], "wshard", 1), ring_step(held)],
                [vec_part, swap(vec_part, "wshard", 4)],
            ],
            [normed_far],
        )
        vec_places, vec_blocks = seq_blocks(vec_part)
        every = jnp.zeros((groups, vec_part.shape[1]), jnp.float32)
        for spot, block in zip(vec_places, vec_blocks):
            every = lax.dynamic_update_slice_in_dim(every, block, spot, 0)
    else:
        vec_part = lax.psum(vec_part, "wshard")
        every = lax.all_gather(vec_part, "seq", axis=0, tiled=True)
    block_here = block_keep.astype(jnp.float32) + block_far.astype(jnp.float32)
    block_out = hidden_rows.astype(jnp.float32) + block_here
    d_normed = take_block(normed_sum, far, rows_here) + normed_far.astype(jnp.float32)
    own_hidden = hidden_rows.astype(jnp.float32)
    own_scale = lax.rsqrt(jnp.mean(own_hidden * own_hidden, axis=-1, keepdims=True) + norm_eps)
    own_unit = own_hidden * own_scale
    d_own = d_normed * gain_one[None, :]
    d_hidden = own_scale * (
        d_own - own_unit * jnp.mean(d_own * own_unit, axis=-1, keepdims=True)
    )
    block_grad = cot_rows.astype(jnp.float32) + d_hidden
    shared, every = (
        jnp.sum(every[:, : shared.shape[0]], axis=0),
        every[:, shared.shape[0] :],
    )
    kernel_end = local_di * (1 + WIDTH)
    heads_at = kernel_end + local_di
    both_kernel = D + 2 * STATE * WIDTH
    vec_total = jnp.concatenate(
        [
            shared[:D],
            merge_heads(every[:, :local_di], 0, HEADDIM),
            jnp.concatenate(
                [
                    merge_heads(
                        every[:, local_di:kernel_end].reshape(groups, WIDTH, local_di), 1, HEADDIM
                    ),
                    shared[D:both_kernel].reshape(WIDTH, 2 * STATE),
                ],
                1,
            ).reshape(-1),
            merge_heads(every[:, kernel_end:heads_at], 0, HEADDIM),
            shared[both_kernel:],
            merge_heads(every[:, heads_at : heads_at + local_heads], 0, 1),
            merge_heads(every[:, heads_at + local_heads : heads_at + 2 * local_heads], 0, 1),
            merge_heads(every[:, heads_at + 2 * local_heads :], 0, 1),
        ]
    )
    vec_first_new, vec_second_new, vec_weight_new = adamw_step(
        vec_weight, vec_first, vec_second, vec_total, vector_rate, 0.0
    )
    if rings:
        rest_spots, rest_blocks = seq_blocks(rest_part)
        _, gate_out_blocks = seq_blocks(gate_out_part, gate_out_far)
        updated = run_update(
            rest_spots,
            gate_out_blocks,
            rest_blocks,
            (in_weight.T, in_first.T, in_second.T),
            (out_weight, out_first, out_second),
        )
        in_first_new, in_second_new, in_weight_new = [array.T for array in updated[:3]]
        out_first_new, out_second_new, out_weight_new = updated[3:]
    else:
        rest_part = lax.psum_scatter(rest_grads[0].T, "wshard", scatter_dimension=0, tiled=True)
        gate_part = lax.psum_scatter(gate_grads[0].T, "wshard", scatter_dimension=0, tiled=True)
        gate_every = lax.all_gather(gate_part, "seq", axis=0, tiled=False).astype(jnp.float32)
        rest_every = lax.all_gather(rest_part, "seq", axis=0, tiled=False).astype(jnp.float32)
        out_total = sum_out_grad(out_grads[0], out_weight.shape[0], seq_index, groups)
        in_total = jnp.concatenate(
            [
                merge_heads(gate_every, 1, HEADDIM),
                merge_heads(rest_every[:, :, :local_di], 1, HEADDIM),
                jnp.sum(rest_every[:, :, local_di:channels], axis=0),
                merge_heads(rest_every[:, :, channels : channels + local_heads], 1, 1),
            ],
            1,
        )
        in_first_new, in_second_new, in_weight_new = adamw_step(
            in_weight, in_first, in_second, in_total, matrix_rate, matrix_decay
        )
        out_first_new, out_second_new, out_weight_new = adamw_step(
            out_weight, out_first, out_second, out_total, matrix_rate, matrix_decay
        )
    return (
        block_out.reshape(1, rows_here, D),
        block_grad.reshape(1, rows_here, D),
        in_first_new,
        in_second_new,
        in_weight_new,
        out_first_new,
        out_second_new,
        out_weight_new,
        vec_first_new,
        vec_second_new,
        vec_weight_new,
    )


def solution(mesh):
    return jax.shard_map(
        shards,
        mesh=mesh,
        in_specs=(
            P("wshard", "seq", None),
            P("wshard", "seq", None),
            P("wshard", None),
            P("wshard", None),
            P("wshard", None),
            P("wshard", None),
            P("wshard", None),
            P("wshard", None),
            P(),
            P(),
            P(),
        ),
        out_specs=(
            P("wshard", "seq", None),
            P("wshard", "seq", None),
            P("wshard", None),
            P("wshard", None),
            P("wshard", None),
            P("wshard", None),
            P("wshard", None),
            P("wshard", None),
            P(),
            P(),
            P(),
        ),
        check_vma=False,
    )
```

time: 266 us -> 252 us (0.947)
  local copies, waits for them, and re-layouts: 42.5 us -> 22.6 us
  waiting for transfers between devices: 39.7 us -> 57.7 us
  Pallas kernels: 116 us -> 110 us
  other arithmetic: 14.7 us -> 9.71 us
    pallas_call x1 -> x0, Pallas kernels: 25.6 us -> none  [run_backward(): pl.pallas_call(backward_kernel, grid=(chunks,), in_specs=[back(channels),...]
    ppermute x45 -> x42, waiting for transfers between devices: 25.4 us -> 45.9 us  [swap(): return lax.ppermute(values, axis, route)]
    pallas_call x18 -> x12, Pallas kernels: 90 us -> 110 us  [call(): pl.pallas_call(after(kernel, 1 + len(inputs), len(arrived)), grid_spec=pl...]
    unnamed x140 -> x127, local copies, waits for them, and re-layouts: 26.7 us -> 8.77 us
    ppermute x45 -> x42, starting transfers between devices: 43 us -> 40 us  [swap(): return lax.ppermute(values, axis, route)]
    convert_element_type x2 -> x0, other arithmetic: 2.75 us -> none  [low(): return values.astype(jnp.bfloat16)]
  transfers between devices with their start and end apart: 54 -> 51, of which waited for: 16 -> 16; matrix products, arithmetic and copies ran while one was open for 12% -> 10% of each run, Pallas kernels for 29% -> 22%
where the time goes in v6:
time: 252 us
  Pallas kernels  110 us (44%)
  waiting for transfers between devices  57.7 us (23%)
  starting transfers between devices  50.3 us (20%)
  local copies, waits for them, and re-layouts  22.6 us (9%)
  other arithmetic  9.71 us (4%)
    pallas_call x12, Pallas kernels, call(): pl.pallas_call(after(kernel, 1 + len(inputs), len(arrived)), grid_spec=pl...  110 us
    ppermute x42, waiting for transfers between devices, swap(): return lax.ppermute(values, axis, route)  45.9 us
    ppermute x42, starting transfers between devices, swap(): return lax.ppermute(values, axis, route)  40 us
    ppermute x9, waiting for transfers between devices, ring_step(): lax.ppermute(held, 'wshard', [(i, (i + 2) % count) for i in range(count)])  11.7 us
    ppermute x9, starting transfers between devices, ring_step(): lax.ppermute(held, 'wshard', [(i, (i + 2) % count) for i in range(count)])  10.3 us
    unnamed x127, local copies, waits for them, and re-layouts  8.77 us
  transfers between devices with their start and end apart: 51, of which 16 were waited for; matrix products, arithmetic and copies ran while one was open for 10% of the time, Pallas kernels for 22%

profile of v6, /device:TPU:0, one launch (start us, length us, event | category | flops | bytes accessed | tf_op | source)
XLA Modules:
  0.0 251.7 jit_solution(17325772487651244332)
XLA Ops:
  0.7 3.4 %prepare.1 = (bf16[784,128]{1,0:T(8,128)(2,1)}, bf16[1024,128]{1,0:T(8,128)(2,1)}, bf16[512,1024]{1,0:T(8,128)(2,1)}) custom-call(s32[1]{0:T(128)} %bitcast.9.refs_0_, f32[4384,128]{1,0:T(8,128)} %bitcast.82, f32[256,1024]{1,0:T(8,128)} %refs_12_.1, bf16[256,1024]{1,0:T(8,128)(2,1)} %bitcast.84, bf16[256,1024]{1,0:T(8,128)(2,1)} %bitcast.87), custom_call_target="tpu_custom_call" | custom-call | flops 100000000 | bytes 4000000 | tf_op jit(solution)/shard_map/prepare/pallas_call | solution.py:627
  4.1 2.9 %collective-permute-start.1 = (bf16[512,1024]{1,0:T(8,128)(2,1)}, bf16[512,1024]{1,0:T(8,128)(2,1)S(1)}, u32[]{:S(2)}, u32[]{:S(2)}) collective-permute-start(bf16[512,1024]{1,0:T(8,128)(2,1)} %get-tuple-element.78.refs_1_), channel_id=1, source_target_pairs={{0,16},{8,24},{16,0},{24,8},{1,17},{9,25},{17,1},{25,9},{2,18},{10... | collective-permute-start | bytes 3145736 | tf_op jit(solution)/shard_map/ppermute | solution.py:953
  11.7 18.7 %collective-permute-done.1.refs_3_ = bf16[512,1024]{1,0:T(8,128)(2,1)S(1)} collective-permute-done((bf16[512,1024]{1,0:T(8,128)(2,1)}, bf16[512,1024]{1,0:T(8,128)(2,1)S(1)}, u32[]{:S(2)}, u32[]{:S(2)}) %collective-permute-start.1) | collective-permute-done | bytes 1048608 | tf_op jit(solution)/shard_map/ppermute | solution.py:953
  30.7 1.8 collective-permute-start.6
  36.9 3.8 %collective-permute-done.6.refs_9_ = bf16[784,128]{1,0:T(8,128)(2,1)} collective-permute-done((bf16[784,128]{1,0:T(8,128)(2,1)}, bf16[784,128]{1,0:T(8,128)(2,1)}, u32[]{:S(2)}, u32[]{:S(2)}) %collective-permute-start.6) | collective-permute-done | bytes 200736 | tf_op jit(solution)/shard_map/ppermute | solution.py:965
  41.2 5.1 %collective-permute-done.13.refs_5_ = bf16[1024,128]{1,0:T(8,128)(2,1)} collective-permute-done((bf16[1024,128]{1,0:T(8,128)(2,1)}, bf16[1024,128]{1,0:T(8,128)(2,1)}, u32[]{:S(2)}, u32[]{:S(2)}) %collective-permute-start.13) | collective-permute-done | bytes 262176 | tf_op jit(solution)/shard_map/ppermute | solution.py:965
  53.7 5.3 %collective-permute-done.7.refs_10_ = bf16[784,128]{1,0:T(8,128)(2,1)S(1)} collective-permute-done((bf16[784,128]{1,0:T(8,128)(2,1)}, bf16[784,128]{1,0:T(8,128)(2,1)S(1)}, u32[]{:S(2)}, u32[]{:S(2)}) %collective-permute-start.7) | collective-permute-done | bytes 200736 | tf_op jit(solution)/shard_map/ppermute | solution.py:953
  59.1 1.7 collective-permute-start.10
  61.1 2.3 collective-permute-done.9.refs_12_
  63.4 1.7 collective-permute-start.14
  66.4 17.6 %forward.1 = (bf16[1024,1024]{1,0:T(8,128)(2,1)}, bf16[1024,1024]{1,0:T(8,128)(2,1)}, bf16[896,1024]{1,0:T(8,128)(2,1)}, bf16[1024,1024]{1,0:T(8,128)(2,1)}, f32...) custom-call(s32[12]{0:T(128)} %stack.131.refs_0_, ...), custom_call_target="tpu_custom_call" | custom-call | flops 6000000000 | bytes 30000000 | tf_op jit(solution)/shard_map/forward/pallas_call | solution.py:627
  85.3 11.3 %gate.1 = (bf16[512,1024]{1,0:T(8,128)(2,1)}, bf16[512,1024]{1,0:T(8,128)(2,1)}, f32[1024,512]{1,0:T(8,128)}, f32[1024,512]{1,0:T(8,128)}, f32[8,1024]{1,0:T(8,128)}) custom-call(s32[8]{0:T(128)} %stack.132.refs_0_, bf16[1024,128]{1,0:T(8,128)(2,1)} %get-tuple-element.81.refs_1_, bf16[1024,128]{1,0:T(8,128)(2,1)} %copy-done.45, ...), custom_call_target="tpu_custom_call" | custom-call | flops 2500000000 | bytes 12000000 | tf_op jit(solution)/shard_map/gate/pallas_call | solution.py:627
  102.2 13.3 %middle.1 = (bf16[512,1024]{1,0:T(8,128)(2,1)}, bf16[512,1024]{1,0:T(8,128)(2,1)}, bf16[1024,512]{1,0:T(8,128)(2,1)}, bf16[1024,512]{1,0:T(8,128)(2,1)}, f32[1,5...) custom-call(s32[7]{0:T(128)} %stack.118.refs_0_, ...), custom_call_target="tpu_custom_call" | custom-call | flops 4000000000 | bytes 15000000 | tf_op jit(solution)/shard_map/middle/pallas_call | solution.py:627
  118.5 3.0 %collective-permute-start.21 = (bf16[512,256]{1,0:T(8,128)(2,1)}, bf16[512,256]{1,0:T(8,128)(2,1)S(1)}, u32[]{:S(2)}, u32[]{:S(2)}) collective-permute-start(bf16[512,256]{1,0:T(8,128)(2,1)} %get-tuple-element.90), channel_id=1, source_target_pairs={{0,4},{1,5},{2,6},{3,7},{4,0},{5,1},{6,2},{7,3},{8,12},{9,13},{10,... | collective-permute-start | bytes 786440 | tf_op jit(solution)/shard_map/ppermute | solution.py:953
  121.6 31.0 %backward.1 = (bf16[1024,896]{1,0:T(8,128)(2,1)}, f32[4,768]{1,0:T(4,128)}, f32[1,768]{1,0:T(1,128)}, f32[1,512]{1,0:T(1,128)}, f32[2,128]{1,0:T(2,128)}, /*inde...) custom-call(s32[8]{0:T(128)} %stack.135.refs_0_, ...), custom_call_target="tpu_custom_call" | custom-call | flops 14000000000 | bytes 40000000 | tf_op jit(solution)/shard_map/backward/pallas_call | solution.py:627
  154.0 4.3 %pair.1 = (bf16[512,128]{1,0:T(8,128)(2,1)}, bf16[512,128]{1,0:T(8,128)(2,1)}, bf16[256,1024]{1,0:T(8,128)(2,1)}, bf16[256,1024]{1,0:T(8,128)(2,1)}, bf16[512,12...) custom-call(s32[6]{0:T(128)} %stack.115.refs_0_, ...), custom_call_target="tpu_custom_call" | custom-call | flops 3000000 | bytes 7000000 | tf_op jit(solution)/shard_map/pair/pallas_call | solution.py:627
  158.4 8.7 %normed.1 = (bf16[512,1024]{1,0:T(8,128)(2,1)}, bf16[512,1024]{1,0:T(8,128)(2,1)}, f32[1,1024]{1,0:T(1,128)}) custom-call(s32[1]{0:T(128)} %bitcast.7.refs_0_, bf16[1024,1024]{1,0:T(8,128)(2,1)} %get-tuple-element.98.refs_1_, bf16[1024,512]{1,0:T(8,128)(2,1)} %get-tuple-element.99.refs_2_, bf16[1024,896]{1,0:T(8,128)(2,1)} %get-tuple-element.106.refs_3_, ...), custom_call_target="tpu_custom_call" | custom-call | flops 3000000000 | bytes 9000000 | tf_op jit(solution)/shard_map/normed/pallas_call | solution.py:627
  170.6 5.2 %collective-permute-done.29.refs_2_ = bf16[784,128]{1,0:T(8,128)(2,1)S(1)} collective-permute-done((bf16[784,128]{1,0:T(8,128)(2,1)S(1)}, bf16[784,128]{1,0:T(8,128)(2,1)S(1)}, u32[]{:S(2)}, u32[]{:S(2)}) %collective-permute-start.29) | collective-permute-done | bytes 200736 | tf_op jit(solution)/shard_map/ppermute | solution.py:953
  177.9 3.8 %collective-permute-start.33 = (bf16[512,128]{1,0:T(8,128)(2,1)S(1)}, bf16[512,128]{1,0:T(8,128)(2,1)S(1)}, u32[]{:S(2)}, u32[]{:S(2)}) collective-permute-start(bf16[512,128]{1,0:T(8,128)(2,1)S(1)} %copy-done.53), channel_id=1, source_target_pairs={{0,6},{1,7},{2,4},{3,5},{4,2},{5,3},{6,0},{7,1},{8,14},{9,15},{10,... | collective-permute-start | bytes 393224 | tf_op jit(solution)/shard_map/ppermute | solution.py:953
  182.2 5.5 %collective-permute-done.32.refs_7_.refs_8_ = bf16[512,128]{1,0:T(8,128)(2,1)S(1)} collective-permute-done((bf16[512,128]{1,0:T(8,128)(2,1)S(1)}, bf16[512,128]{1,0:T(8,128)(2,1)S(1)}, u32[]{:S(2)}, u32[]{:S(2)}) %collective-permute-start.32) | collective-permute-done | bytes 131104 | tf_op jit(solution)/shard_map/ppermute | solution.py:953
  188.5 1.8 add.217
  190.3 2.0 collective-permute-start.34
  196.7 2.1 collective-permute-done.35.refs_11_
  199.8 2.3 add.218
  206.6 2.0 convert_add_fusion
  211.0 3.1 %collective-permute-done.42.refs_5_ = f32[1,5400]{1,0:T(1,128)S(1)} collective-permute-done((f32[1,5400]{1,0:T(1,128)S(1)}, f32[1,5400]{1,0:T(1,128)S(1)}, u32[]{:S(2)}, u32[]{:S(2)}) %collective-permute-start.42) | collective-permute-done | bytes 21632 | tf_op jit(solution)/shard_map/ppermute | solution.py:953
  214.9 1.9 add.219
  216.8 2.9 %collective-permute-start.44 = (f32[1,5400]{1,0:T(1,128)}, f32[1,5400]{1,0:T(1,128)S(1)}, u32[]{:S(2)}, u32[]{:S(2)}) collective-permute-start(f32[1,5400]{1,0:T(1,128)} %get-tuple-element.136.refs_4_), channel_id=1, source_target_pairs={{0,4},{1,5},{2,6},{3,7},{4,0},{5,1},{6,2},{7,3},{8,12},{9,13},{10,... | collective-permute-start | bytes 64808 | tf_op jit(solution)/shard_map/ppermute | solution.py:953
  221.8 2.8 %collective-permute-done.43.refs_3_ = bf16[784,128]{1,0:T(8,128)(2,1)} collective-permute-done((bf16[784,128]{1,0:T(8,128)(2,1)}, bf16[784,128]{1,0:T(8,128)(2,1)}, u32[]{:S(2)}, u32[]{:S(2)}) %collective-permute-start.43) | collective-permute-done | bytes 200736 | tf_op jit(solution)/shard_map/ppermute | solution.py:965
  225.4 1.9 add.220
  231.5 1.9 fusion.6
  239.0 12.5 %update.1 = (f32[4384,128]{1,0:T(8,128)}, f32[4384,128]{1,0:T(8,128)}, f32[4384,128]{1,0:T(8,128)}, f32[256,1024]{1,0:T(8,128)}, f32[256,1024]{1,0:T(8,128)}, /*index=5*/f32[256,1024]{1,0:T(8,128)}) custom-call(s32[4]{0:T(128)} %pad_add_fusion.refs_0_, bf16[1024,128]{1,0:T(8,128)(2,1)} %copy-done.9, bf16[1024,128]{1,0:T(8,128)(2,1)} %collective-permute-done.36.refs_2_, ...), custom_call_target="tpu_custom_call" | custom-call | flops 20000000 | bytes 22000000 | tf_op jit(solution)/shard_map/update/pallas_call | solution.py:627
  (296 shorter events, 62.7 us)
Async XLA Ops:
  4.1 26.3 %collective-permute-start.1 = (bf16[512,1024]{1,0:T(8,128)(2,1)}, bf16[512,1024]{1,0:T(8,128)(2,1)S(1)}, u32[]{:S(2)}, u32[]{:S(2)}) collective-permute-start(bf16[512,1024]{1,0:T(8,128)(2,1)} %get-tuple-element.78.refs_1_), channel_id=1, source_target_pairs={{0,16},{8,24},{16,0},{24,8},{1,17},{9,25},{17,1},{25,9},{2,18},{10... | collective-permute-start | bytes 3145736 | tf_op jit(solution)/shard_map/ppermute | solution.py:953
  7.0 58.1 %collective-permute-start = (bf16[512,1024]{1,0:T(8,128)(2,1)}, bf16[512,1024]{1,0:T(8,128)(2,1)S(1)}, u32[]{:S(2)}, u32[]{:S(2)}) collective-permute-start(bf16[512,1024]{1,0:T(8,128)(2,1)} %get-tuple-element.78.refs_1_), channel_id=1, source_target_pairs={{0,8},{8,0},{16,24},{24,16},{1,9},{9,1},{17,25},{25,17},{2,10},{10... | collective-permute-start | bytes 3145736 | tf_op jit(solution)/shard_map/ppermute | solution.py:953
  7.0 23.7 %collective-permute-start.4 = (bf16[784,128]{1,0:T(8,128)(2,1)}, bf16[784,128]{1,0:T(8,128)(2,1)}, u32[]{:S(2)}, u32[]{:S(2)}) collective-permute-start(bf16[784,128]{1,0:T(8,128)(2,1)} %get-tuple-element.79.refs_5_), channel_id=1, source_target_pairs={{0,2},{1,3},{2,4},{3,5},{4,6},{5,7},{6,0},{7,1},{8,10},{9,11},{10,... | collective-permute-start | bytes 602120 | tf_op jit(solution)/shard_map/ppermute | solution.py:965
  8.6 26.8 %collective-permute-start.3 = (bf16[784,128]{1,0:T(8,128)(2,1)}, bf16[784,128]{1,0:T(8,128)(2,1)}, u32[]{:S(2)}, u32[]{:S(2)}) collective-permute-start(bf16[784,128]{1,0:T(8,128)(2,1)} %get-tuple-element.79.refs_5_), channel_id=1, source_target_pairs={{0,1},{1,0},{2,3},{3,2},{4,5},{5,4},{6,7},{7,6},{8,9},{9,8},{10,11... | collective-permute-start | bytes 602120 | tf_op jit(solution)/shard_map/ppermute | solution.py:953
  10.1 22.4 %collective-permute-start.11 = (bf16[1024,128]{1,0:T(8,128)(2,1)}, bf16[1024,128]{1,0:T(8,128)(2,1)}, u32[]{:S(2)}, u32[]{:S(2)}) collective-permute-start(bf16[1024,128]{1,0:T(8,128)(2,1)} %get-tuple-element.81.refs_1_), channel_id=1, source_target_pairs={{0,2},{1,3},{2,4},{3,5},{4,6},{5,7},{6,0},{7,1},{8,10},{9,11},{10,... | collective-permute-start | bytes 786440 | tf_op jit(solution)/shard_map/ppermute | solution.py:965
  30.4 35.1 %collective-permute-start.2 = (bf16[512,1024]{1,0:T(8,128)(2,1)S(1)}, bf16[512,1024]{1,0:T(8,128)(2,1)S(1)}, u32[]{:S(2)}, u32[]{:S(2)}) collective-permute-start(bf16[512,1024]{1,0:T(8,128)(2,1)S(1)} %collective-permute-done.1.refs_3_), channel_id=1, source_target_pairs={{0,8},{8,0},{16,24},{24,16},{1,9},{9,1},{17,25},{25,17},{2,10},{10... | collective-permute-start | bytes 3145736 | tf_op jit(solution)/shard_map/ppermute | solution.py:953
  30.7 10.0 %collective-permute-start.6 = (bf16[784,128]{1,0:T(8,128)(2,1)}, bf16[784,128]{1,0:T(8,128)(2,1)}, u32[]{:S(2)}, u32[]{:S(2)}) collective-permute-start(bf16[784,128]{1,0:T(8,128)(2,1)} %collective-permute-done.4.refs_7_), channel_id=1, source_target_pairs={{0,2},{1,3},{2,4},{3,5},{4,6},{5,7},{6,0},{7,1},{8,10},{9,11},{10,... | collective-permute-start | bytes 602120 | tf_op jit(solution)/shard_map/ppermute | solution.py:965
  32.5 13.8 %collective-permute-start.13 = (bf16[1024,128]{1,0:T(8,128)(2,1)}, bf16[1024,128]{1,0:T(8,128)(2,1)}, u32[]{:S(2)}, u32[]{:S(2)}) collective-permute-start(bf16[1024,128]{1,0:T(8,128)(2,1)} %collective-permute-done.11.refs_3_), channel_id=1, source_target_pairs={{0,2},{1,3},{2,4},{3,5},{4,6},{5,7},{6,0},{7,1},{8,10},{9,11},{10,... | collective-permute-start | bytes 786440 | tf_op jit(solution)/shard_map/ppermute | solution.py:965
  35.4 15.6 %collective-permute-start.5 = (bf16[784,128]{1,0:T(8,128)(2,1)}, bf16[784,128]{1,0:T(8,128)(2,1)}, u32[]{:S(2)}, u32[]{:S(2)}) collective-permute-start(bf16[784,128]{1,0:T(8,128)(2,1)} %collective-permute-done.4.refs_7_), channel_id=1, source_target_pairs={{0,1},{1,0},{2,3},{3,2},{4,5},{5,4},{6,7},{7,6},{8,9},{9,8},{10,11... | collective-permute-start | bytes 602120 | tf_op jit(solution)/shard_map/ppermute | solution.py:953
  40.7 12.0 %collective-permute-start.8 = (bf16[784,128]{1,0:T(8,128)(2,1)}, bf16[784,128]{1,0:T(8,128)(2,1)}, u32[]{:S(2)}, u32[]{:S(2)}) collective-permute-start(bf16[784,128]{1,0:T(8,128)(2,1)} %collective-permute-done.6.refs_9_), channel_id=1, source_target_pairs={{0,2},{1,3},{2,4},{3,5},{4,6},{5,7},{6,0},{7,1},{8,10},{9,11},{10,... | collective-permute-start | bytes 602120 | tf_op jit(solution)/shard_map/ppermute | solution.py:965
  46.3 14.5 %collective-permute-start.15 = (bf16[1024,128]{1,0:T(8,128)(2,1)}, bf16[1024,128]{1,0:T(8,128)(2,1)}, u32[]{:S(2)}, u32[]{:S(2)}) collective-permute-start(bf16[1024,128]{1,0:T(8,128)(2,1)} %collective-permute-done.13.refs_5_), channel_id=1, source_target_pairs={{0,2},{1,3},{2,4},{3,5},{4,6},{5,7},{6,0},{7,1},{8,10},{9,11},{10,... | collective-permute-start | bytes 786440 | tf_op jit(solution)/shard_map/ppermute | solution.py:965
  52.6 10.7 %collective-permute-start.9 = (bf16[784,128]{1,0:T(8,128)(2,1)}, bf16[784,128]{1,0:T(8,128)(2,1)S(1)}, u32[]{:S(2)}, u32[]{:S(2)}) collective-permute-start(bf16[784,128]{1,0:T(8,128)(2,1)} %collective-permute-done.8.refs_11_), channel_id=1, source_target_pairs={{0,1},{1,0},{2,3},{3,2},{4,5},{5,4},{6,7},{7,6},{8,9},{9,8},{10,11... | collective-permute-start | bytes 602120 | tf_op jit(solution)/shard_map/ppermute | solution.py:953
  59.1 24.9 %collective-permute-start.10 = (bf16[1024,128]{1,0:T(8,128)(2,1)}, bf16[1024,128]{1,0:T(8,128)(2,1)S(1)}, u32[]{:S(2)}, u32[]{:S(2)}) collective-permute-start(bf16[1024,128]{1,0:T(8,128)(2,1)} %get-tuple-element.81.refs_1_), channel_id=1, source_target_pairs={{0,1},{1,0},{2,3},{3,2},{4,5},{5,4},{6,7},{7,6},{8,9},{9,8},{10,11... | collective-permute-start | bytes 786440 | tf_op jit(solution)/shard_map/ppermute | solution.py:953
  60.8 23.2 %collective-permute-start.12 = (bf16[1024,128]{1,0:T(8,128)(2,1)}, bf16[1024,128]{1,0:T(8,128)(2,1)S(1)}, u32[]{:S(2)}, u32[]{:S(2)}) collective-permute-start(bf16[1024,128]{1,0:T(8,128)(2,1)} %collective-permute-done.11.refs_3_), channel_id=1, source_target_pairs={{0,1},{1,0},{2,3},{3,2},{4,5},{5,4},{6,7},{7,6},{8,9},{9,8},{10,11... | collective-permute-start | bytes 786440 | tf_op jit(solution)/shard_map/ppermute | solution.py:953
  63.4 20.6 %collective-permute-start.14 = (bf16[1024,128]{1,0:T(8,128)(2,1)}, bf16[1024,128]{1,0:T(8,128)(2,1)S(1)}, u32[]{:S(2)}, u32[]{:S(2)}) collective-permute-start(bf16[1024,128]{1,0:T(8,128)(2,1)} %collective-permute-done.13.refs_5_), channel_id=1, source_target_pairs={{0,1},{1,0},{2,3},{3,2},{4,5},{5,4},{6,7},{7,6},{8,9},{9,8},{10,11... | collective-permute-start | bytes 786440 | tf_op jit(solution)/shard_map/ppermute | solution.py:953
  65.1 19.5 %collective-permute-start.16 = (bf16[1024,128]{1,0:T(8,128)(2,1)}, bf16[1024,128]{1,0:T(8,128)(2,1)S(1)}, u32[]{:S(2)}, u32[]{:S(2)}) collective-permute-start(bf16[1024,128]{1,0:T(8,128)(2,1)} %collective-permute-done.15.refs_7_), channel_id=1, source_target_pairs={{0,1},{1,0},{2,3},{3,2},{4,5},{5,4},{6,7},{7,6},{8,9},{9,8},{10,11... | collective-permute-start | bytes 786440 | tf_op jit(solution)/shard_map/ppermute | solution.py:953
  115.5 37.2 %collective-permute-start.24 = (bf16[512,1024]{1,0:T(8,128)(2,1)}, bf16[512,1024]{1,0:T(8,128)(2,1)S(1)}, u32[]{:S(2)}, u32[]{:S(2)}) collective-permute-start(bf16[512,1024]{1,0:T(8,128)(2,1)} %get-tuple-element.95), channel_id=1, source_target_pairs={{0,8},{8,0},{16,24},{24,16},{1,9},{9,1},{17,25},{25,17},{2,10},{10... | collective-permute-start | bytes 3145736 | tf_op jit(solution)/shard_map/ppermute | solution.py:953
  115.7 36.9 %collective-permute-start.23 = (bf16[2048,128]{1,0:T(8,128)(2,1)}, bf16[2048,128]{1,0:T(8,128)(2,1)S(1)}, u32[]{:S(2)}, u32[]{:S(2)}) collective-permute-start(bf16[2048,128]{1,0:T(8,128)(2,1)} %get-tuple-element.93), channel_id=1, source_target_pairs={{0,1},{1,0},{2,3},{3,2},{4,5},{5,4},{6,7},{7,6},{8,9},{9,8},{10,11... | collective-permute-start | bytes 1572872 | tf_op jit(solution)/shard_map/ppermute | solution.py:953
  117.2 35.4 %collective-permute-start.20 = (bf16[512,256]{1,0:T(8,128)(2,1)}, bf16[512,256]{1,0:T(8,128)(2,1)S(1)}, u32[]{:S(2)}, u32[]{:S(2)}) collective-permute-start(bf16[512,256]{1,0:T(8,128)(2,1)} %get-tuple-element.89), channel_id=1, source_target_pairs={{0,2},{1,3},{2,0},{3,1},{4,6},{5,7},{6,4},{7,5},{8,10},{9,11},{10,... | collective-permute-start | bytes 786440 | tf_op jit(solution)/shard_map/ppermute | solution.py:953
  118.5 34.1 %collective-permute-start.21 = (bf16[512,256]{1,0:T(8,128)(2,1)}, bf16[512,256]{1,0:T(8,128)(2,1)S(1)}, u32[]{:S(2)}, u32[]{:S(2)}) collective-permute-start(bf16[512,256]{1,0:T(8,128)(2,1)} %get-tuple-element.90), channel_id=1, source_target_pairs={{0,4},{1,5},{2,6},{3,7},{4,0},{5,1},{6,2},{7,3},{8,12},{9,13},{10,... | collective-permute-start | bytes 786440 | tf_op jit(solution)/shard_map/ppermute | solution.py:953
  121.6 31.1 %collective-permute-start.22 = (bf16[512,256]{1,0:T(8,128)(2,1)}, bf16[512,256]{1,0:T(8,128)(2,1)S(1)}, u32[]{:S(2)}, u32[]{:S(2)}) collective-permute-start(bf16[512,256]{1,0:T(8,128)(2,1)} %get-tuple-element.91), channel_id=1, source_target_pairs={{0,6},{1,7},{2,4},{3,5},{4,2},{5,3},{6,0},{7,1},{8,14},{9,15},{10,... | collective-permute-start | bytes 786440 | tf_op jit(solution)/shard_map/ppermute | solution.py:953
  167.1 31.7 %collective-permute-start.26 = (bf16[512,1024]{1,0:T(8,128)(2,1)}, bf16[512,1024]{1,0:T(8,128)(2,1)S(1)}, u32[]{:S(2)}, u32[]{:S(2)}) collective-permute-start(bf16[512,1024]{1,0:T(8,128)(2,1)} %get-tuple-element.111), channel_id=1, source_target_pairs={{0,8},{8,0},{16,24},{24,16},{1,9},{9,1},{17,25},{25,17},{2,10},{10... | collective-permute-start | bytes 3145736 | tf_op jit(solution)/shard_map/ppermute | solution.py:953
  167.1 20.6 %collective-permute-start.25 = (bf16[256,1024]{1,0:T(8,128)(2,1)S(1)}, bf16[256,1024]{1,0:T(8,128)(2,1)S(1)}, u32[]{:S(2)}, u32[]{:S(2)}) collective-permute-start(bf16[256,1024]{1,0:T(8,128)(2,1)S(1)} %copy-done.44), channel_id=1, source_target_pairs={{0,16},{8,24},{16,0},{24,8},{1,17},{9,25},{17,1},{25,9},{2,18},{10... | collective-permute-start | bytes 1572872 | tf_op jit(solution)/shard_map/ppermute | solution.py:953
  170.1 11.6 %collective-permute-start.31 = (bf16[512,128]{1,0:T(8,128)(2,1)S(1)}, bf16[512,128]{1,0:T(8,128)(2,1)S(1)}, u32[]{:S(2)}, u32[]{:S(2)}) collective-permute-start(bf16[512,128]{1,0:T(8,128)(2,1)S(1)} %copy-done.55), channel_id=1, source_target_pairs={{0,2},{1,3},{2,0},{3,1},{4,6},{5,7},{6,4},{7,5},{8,10},{9,11},{10,... | collective-permute-start | bytes 393224 | tf_op jit(solution)/shard_map/ppermute | solution.py:953
  175.9 11.8 %collective-permute-start.32 = (bf16[512,128]{1,0:T(8,128)(2,1)S(1)}, bf16[512,128]{1,0:T(8,128)(2,1)S(1)}, u32[]{:S(2)}, u32[]{:S(2)}) collective-permute-start(bf16[512,128]{1,0:T(8,128)(2,1)S(1)} %copy-done.54), channel_id=1, source_target_pairs={{0,4},{1,5},{2,6},{3,7},{4,0},{5,1},{6,2},{7,3},{8,12},{9,13},{10,... | collective-permute-start | bytes 393224 | tf_op jit(solution)/shard_map/ppermute | solution.py:953
  181.7 15.0 %collective-permute-start.28 = (bf16[784,128]{1,0:T(8,128)(2,1)S(1)}, bf16[784,128]{1,0:T(8,128)(2,1)S(1)}, u32[]{:S(2)}, u32[]{:S(2)}) collective-permute-start(bf16[784,128]{1,0:T(8,128)(2,1)S(1)} %copy-done.49), channel_id=1, source_target_pairs={{0,1},{1,0},{2,3},{3,2},{4,5},{5,4},{6,7},{7,6},{8,9},{9,8},{10,11... | collective-permute-start | bytes 602120 | tf_op jit(solution)/shard_map/ppermute | solution.py:953
  195.2 15.3 %collective-permute-start.40 = (bf16[784,128]{1,0:T(8,128)(2,1)}, bf16[784,128]{1,0:T(8,128)(2,1)S(1)}, u32[]{:S(2)}, u32[]{:S(2)}) collective-permute-start(bf16[784,128]{1,0:T(8,128)(2,1)} %get-tuple-element.132), channel_id=1, source_target_pairs={{0,1},{1,0},{2,3},{3,2},{4,5},{5,4},{6,7},{7,6},{8,9},{9,8},{10,11... | collective-permute-start | bytes 602120 | tf_op jit(solution)/shard_map/ppermute | solution.py:953
  203.9 10.2 %collective-permute-start.37 = (bf16[1024,128]{1,0:T(8,128)(2,1)S(1)}, bf16[1024,128]{1,0:T(8,128)(2,1)S(1)}, u32[]{:S(2)}, u32[]{:S(2)}) collective-permute-start(bf16[1024,128]{1,0:T(8,128)(2,1)S(1)} %constant_dynamic-update-slice_fusion.refs_1_), channel_id=1, source_target_pairs={{0,16},{8,24},{16,0},{24,8},{1,17},{9,25},{17,1},{25,9},{2,18},{10... | collective-permute-start | bytes 786440 | tf_op jit(solution)/shard_map/ppermute | solution.py:953
  209.5 15.1 %collective-permute-start.27 = (bf16[256,1024]{1,0:T(8,128)(2,1)}, bf16[256,1024]{1,0:T(8,128)(2,1)S(1)}, u32[]{:S(2)}, u32[]{:S(2)}) collective-permute-start(bf16[256,1024]{1,0:T(8,128)(2,1)} %dynamic-slice_convert_fusion), channel_id=1, source_target_pairs={{0,16},{8,24},{16,0},{24,8},{1,17},{9,25},{17,1},{25,9},{2,18},{10... | collective-permute-start | bytes 1572872 | tf_op jit(solution)/shard_map/ppermute | solution.py:953
  210.6 9.9 %collective-permute-start.39 = (bf16[784,128]{1,0:T(8,128)(2,1)}, bf16[784,128]{1,0:T(8,128)(2,1)}, u32[]{:S(2)}, u32[]{:S(2)}) collective-permute-start(bf16[784,128]{1,0:T(8,128)(2,1)} %get-tuple-element.130), channel_id=1, source_target_pairs={{0,1},{1,0},{2,3},{3,2},{4,5},{5,4},{6,7},{7,6},{8,9},{9,8},{10,11... | collective-permute-start | bytes 602120 | tf_op jit(solution)/shard_map/ppermute | solution.py:953
  220.4 17.9 %collective-permute-start.36 = (bf16[1024,128]{1,0:T(8,128)(2,1)S(1)}, bf16[1024,128]{1,0:T(8,128)(2,1)}, u32[]{:S(2)}, u32[]{:S(2)}) collective-permute-start(bf16[1024,128]{1,0:T(8,128)(2,1)S(1)} %constant_dynamic-update-slice_fusion.refs_1_), channel_id=1, source_target_pairs={{0,8},{8,0},{16,24},{24,16},{1,9},{9,1},{17,25},{25,17},{2,10},{10... | collective-permute-start | bytes 786440 | tf_op jit(solution)/shard_map/ppermute | solution.py:953
  220.4 17.8 %collective-permute-start.38 = (bf16[1024,128]{1,0:T(8,128)(2,1)}, bf16[1024,128]{1,0:T(8,128)(2,1)}, u32[]{:S(2)}, u32[]{:S(2)}) collective-permute-start(bf16[1024,128]{1,0:T(8,128)(2,1)} %copy-done.8), channel_id=1, source_target_pairs={{0,8},{8,0},{16,24},{24,16},{1,9},{9,1},{17,25},{25,17},{2,10},{10... | collective-permute-start | bytes 786440 | tf_op jit(solution)/shard_map/ppermute | solution.py:953
  (82 other events, 645.1 us)

commit v7 on v6

--- a/solution.py
+++ b/solution.py
@@ -96,10 +96,10 @@
     result_ref[:rows, pl.ds(start, columns)] = block
 
 
-def forward_kernel(both_count, rest_count, places_ref, *refs):
-    both_blocks = refs[:both_count]
-    rest_blocks = refs[both_count : both_count + rest_count]
+def forward_kernel(rest_count, places_ref, *refs):
+    rest_blocks = refs[:rest_count]
     (
+        hidden_ref,
         gain_one_ref,
         conv_ref,
         bias_ref,
@@ -107,8 +107,6 @@
         dt_bias_ref,
         skip_ref,
         expand_ref,
-        hidden_ref,
-        cot_ref,
         rest_ref,
         normed_ref,
         conv_in_ref,
@@ -119,7 +117,7 @@
         state_ref,
         ext,
         state,
-    ) = refs[both_count + rest_count :]
+    ) = refs[rest_count:]
     local_di = y_ref.shape[1]
     heads = local_di // HEADDIM
     channels = conv_in_ref.shape[1]
@@ -128,16 +126,11 @@
     def _():
         ext[0:8, :] = jnp.zeros((8, ext.shape[1]), jnp.float32)
         state[...] = jnp.zeros_like(state)
-        for number, block in enumerate(both_blocks):
-            half = block.shape[0] // 2
-            place_rows(hidden_ref, places_ref[number], block[:half, :])
-            place_rows(cot_ref, places_ref[number], block[half:, :])
         rest_ref[channels:, :] = jnp.zeros_like(rest_ref[channels:, :])
         for number, block in enumerate(rest_blocks):
-            place_columns(rest_ref, places_ref[both_count + number], block[...])
-
-    chunk = pl.ds(pl.multiple_of(pl.program_id(0) * BLOCK, BLOCK), BLOCK)
-    hidden = hidden_ref[chunk, :].astype(jnp.float32)
+            place_columns(rest_ref, places_ref[number], block[...])
+
+    hidden = hidden_ref[...].astype(jnp.float32)
     normed = low(rms_scale(hidden) * gain_one_ref[...])
     normed_ref[...] = normed
     conv_in = dot_nt(normed, rest_ref[:channels, :])
@@ -436,9 +429,15 @@
     @pl.when(chunk == pl.num_programs(0) - 1)
     def _():
         for number, grad_ref in enumerate(grad_refs):
-            rows, columns = grad_ref.shape
-            start = pl.multiple_of(places_ref[number] * columns, columns)
-            grad_ref[...] = low(rest_sum[:rows, pl.ds(start, columns)])
+            columns = grad_ref.shape[1]
+            blocks = rest_sum.shape[1] // columns // grad_count
+            rows = grad_ref.shape[0] // blocks
+            for step in range(blocks):
+                place = places_ref[number] + step * grad_count
+                start = pl.multiple_of(place * columns, columns)
+                grad_ref[step * rows : (step + 1) * rows, :] = low(
+                    rest_sum[:rows, pl.ds(start, columns)]
+                )
 
 
 def sum_of(*refs):
@@ -469,6 +468,27 @@
         ref[...] = low(sum_of(out[0].at[here, :], out[1].at[here, :]))
 
 
+def rest_pair_kernel(places_ref, mine_ref, arrived_ref, *rest_refs):
+    for number, ref in enumerate(rest_refs):
+        rows = ref.shape[0]
+        here = pl.ds(pl.multiple_of(places_ref[number] * rows, rows), rows)
+        ref[...] = low(sum_of(mine_ref.at[here, :], arrived_ref.at[here, :]))
+
+
+def join_kernel(places_ref, *refs):
+    joined_ref, vec_ref = refs[-2:]
+    rows = refs[0].shape[0]
+    joined_ref[:rows, :] = low(sum_of(*refs[:2]))
+    joined_ref[rows:, :] = low(sum_of(*refs[2:6]))
+    vec_ref[...] = refs[6][...] + refs[7][...]
+
+
+def final_kernel(places_ref, *refs):
+    rest_ref, vec_ref = refs[6:]
+    rest_ref[...] = low(sum_of(*refs[:4]))
+    vec_ref[...] = refs[4][...] + refs[5][...]
+
+
 def normed_kernel(
     places_ref,
     hidden_ref,
@@ -493,7 +513,7 @@
     d_gain_one_ref[...] += jnp.sum(d_normed * unit, axis=0, keepdims=True)
 
 
-def prepare_kernel(places_ref, in_ref, out_ref, hidden_ref, cot_ref, rest_ref, gate_out_ref, both_ref):
+def prepare_kernel(places_ref, in_ref, out_ref, rest_ref, gate_out_ref):
     index = places_ref[0]
     local_di = gate_out_ref.shape[0] // 2
     groups = DI // local_di
@@ -517,56 +537,64 @@
         gate_out_ref[first : first + HEADDIM, :] = low(
             out_ref[mine, tile * columns : (tile + 1) * columns]
         )
-    half = hidden_ref.shape[0]
-    both_ref[:half, :] = hidden_ref[...]
-    both_ref[half:, :] = cot_ref[...]
-
-
-def update_kernel(groups, places_ref, *refs):
-    gate_out_blocks = refs[:groups]
-    rest_blocks = refs[groups : 2 * groups]
-    in_refs = refs[2 * groups : 2 * groups + 3]
-    out_refs = refs[2 * groups + 3 : 2 * groups + 6]
-    in_new_refs = refs[2 * groups + 6 : 2 * groups + 9]
-    out_new_refs = refs[2 * groups + 9 : 2 * groups + 12]
-    gate_out, rest = refs[2 * groups + 12 :]
+
+
+def adamw_store(old_refs, new_refs, rows, columns, grad):
+    results = adamw_step(*[ref[rows, columns] for ref in old_refs], grad, matrix_rate, matrix_decay)
+    for ref, result in zip(new_refs, results):
+        ref[rows, columns] = result
+
+
+def update_heads(old_refs, new_refs, source, part):
+    groups = source.shape[0]
+    heads = old_refs[0].shape[0] // HEADDIM // groups
+    for head in range(heads):
+        start = pl.multiple_of((part * heads + head) * HEADDIM, HEADDIM)
+        for group in range(groups):
+            first = (head * groups + group) * HEADDIM
+            grad = source[group, pl.ds(start, HEADDIM), :].astype(jnp.float32)
+            adamw_store(old_refs, new_refs, slice(first, first + HEADDIM), slice(None), grad)
+
+
+def update_gate_kernel(groups, places_ref, *refs):
+    blocks, in_refs, out_refs = refs[:groups], refs[groups : groups + 3], refs[groups + 3 : groups + 6]
+    in_new_refs, out_new_refs = refs[groups + 6 : groups + 9], refs[groups + 9 : groups + 12]
+    (gate_out,) = refs[groups + 12 :]
     chunk = pl.program_id(0)
-    local_di = gate_out.shape[1] // 2
-    channels = local_di + 2 * STATE
-    parts = DI // in_refs[0].shape[0]
 
     @pl.when(chunk == 0)
     def _():
         for number in range(groups):
-            gate_out[places_ref[number]] = gate_out_blocks[number][...]
-            rest[places_ref[number]] = rest_blocks[number][...]
-
-    def step(old_refs, new_refs, rows, columns, grad):
-        results = adamw_step(
-            *[ref[rows, columns] for ref in old_refs], grad, matrix_rate, matrix_decay
-        )
-        for ref, result in zip(new_refs, results):
-            ref[rows, columns] = result
-
-    def step_heads(source, part):
-        heads = local_di // HEADDIM // parts
-        for head in range(heads):
-            start = pl.multiple_of((part * heads + head) * HEADDIM, HEADDIM)
-            for group in range(groups):
-                first = (head * groups + group) * HEADDIM
-                grad = source[group, pl.ds(start, HEADDIM), :].astype(jnp.float32)
-                step(in_refs, in_new_refs, slice(first, first + HEADDIM), slice(None), grad)
-
-    @pl.when(chunk < parts)
+            gate_out[places_ref[number]] = blocks[number][...]
+
+    update_heads(in_refs, in_new_refs, gate_out, chunk)
+    local_di = gate_out.shape[1] // 2
+    columns = gate_out.shape[2]
+    for tile in range(D // columns):
+        first = local_di + tile * HEADDIM
+        grad = gate_out[chunk, first : first + HEADDIM, :].astype(jnp.float32)
+        span = slice(tile * columns, (tile + 1) * columns)
+        adamw_store(out_refs, out_new_refs, slice(None), span, grad)
+
+
+def update_rest_kernel(groups, places_ref, *refs):
+    blocks, in_refs = refs[:groups], refs[groups : groups + 3]
+    in_new_refs, (rest,) = refs[groups + 6 : groups + 9], refs[groups + 9 :]
+    chunk = pl.program_id(0)
+
+    @pl.when(chunk == 0)
     def _():
-        step_heads(gate_out, chunk)
-
-    @pl.when((chunk >= parts) & (chunk < 2 * parts))
+        for number in range(groups):
+            rest[places_ref[number]] = blocks[number][...]
+
+    @pl.when(chunk < pl.num_programs(0) - 1)
     def _():
-        step_heads(rest, chunk - parts)
-
-    @pl.when(chunk == 2 * parts)
+        update_heads(in_refs, in_new_refs, rest, chunk)
+
+    @pl.when(chunk == pl.num_programs(0) - 1)
     def _():
+        local_di = DI // groups
+        channels = local_di + 2 * STATE
         both = rest[0, local_di:channels, :].astype(jnp.float32)
         rows = rest.shape[1] - channels
         steps = jnp.zeros((HEADS, rest.shape[2]), jnp.float32)
@@ -577,17 +605,9 @@
                 both = both + rest[group, local_di:channels, :].astype(jnp.float32)
             chosen = jnp.where(target == groups * source + group, 1.0, 0.0).astype(jnp.bfloat16)
             steps = steps + dot_nn(chosen, rest[group, channels:, :])
-        step(in_refs, in_new_refs, slice(0, 2 * STATE), slice(None), both)
-        step(in_refs, in_new_refs, slice(2 * STATE, 2 * STATE + HEADS), slice(None), steps)
-
-    @pl.when(chunk < groups)
-    def _():
-        columns = gate_out.shape[2]
-        for tile in range(D // columns):
-            first = local_di + tile * HEADDIM
-            grad = gate_out[chunk, first : first + HEADDIM, :].astype(jnp.float32)
-            span = slice(tile * columns, (tile + 1) * columns)
-            step(out_refs, out_new_refs, slice(None), span, grad)
+        after_both = slice(2 * STATE, 2 * STATE + HEADS)
+        adamw_store(in_refs, in_new_refs, slice(0, 2 * STATE), slice(None), both)
+        adamw_store(in_refs, in_new_refs, after_both, slice(None), steps)
 
 
 def kernel_params():
@@ -623,7 +643,9 @@
     return jax.ShapeDtypeStruct(shape, dtype)
 
 
-def call(kernel, places, inputs, in_specs, outputs, out_specs, scratch, grid, arrived, price, name):
+def call(
+    kernel, places, inputs, in_specs, outputs, out_specs, scratch, grid, arrived, price, name, same=()
+):
     return pl.pallas_call(
         after(kernel, 1 + len(inputs), len(arrived)),
         grid_spec=pltpu.PrefetchScalarGridSpec(
@@ -634,21 +656,21 @@
             scratch_shapes=scratch,
         ),
         out_shape=outputs,
+        input_output_aliases=dict(same),
         compiler_params=kernel_params(),
         cost_estimate=cost(*price),
         name=name,
     )(jnp.stack(places).astype(jnp.int32), *inputs, *arrived)
 
 
-def run_prepare(index, in_t, out_weight, hidden, cot):
+def run_prepare(index, in_t, out_weight):
     columns = in_t.shape[1]
     local_di = DI // 4
     shapes = [
         (local_di + 2 * STATE + 16, columns),
         (2 * local_di, columns),
-        (2 * hidden.shape[0], D),
     ]
-    inputs = [in_t, out_weight, hidden, cot]
+    inputs = [in_t, out_weight]
     return call(
         prepare_kernel,
         [index],
@@ -664,23 +686,21 @@
     )
 
 
-def run_forward(both, rest, gain_one, conv, heads_vectors, expand):
-    both_places, both_blocks = both
-    rest_places, rest_blocks = rest
-    length = both_blocks[0].shape[0] // 2 * len(both_blocks)
+def run_forward(hidden, rest, gain_one, conv, heads_vectors, expand):
+    places, blocks = rest
+    length = hidden.shape[0]
     chunks = length // BLOCK
     lanes, local_di = expand.shape
     channels = local_di + 2 * STATE
     vectors = [gain_one, *conv, *heads_vectors, expand]
-    inputs = [*both_blocks, *rest_blocks, *vectors]
     return call(
-        lambda *refs: forward_kernel(len(both_blocks), len(rest_blocks), *refs),
-        both_places + rest_places,
-        inputs,
-        [fixed(array.shape) for array in inputs],
-        [
-            struct((length, D), jnp.bfloat16),
-            struct((length, D), jnp.bfloat16),
+        lambda *refs: forward_kernel(len(blocks), *refs),
+        places,
+        [*blocks, hidden, *vectors],
+        [fixed(array.shape) for array in blocks]
+        + [rows_of(D)]
+        + [fixed(array.shape) for array in vectors],
+        [
             struct((channels + lanes, D), jnp.bfloat16),
             struct((length, D), jnp.bfloat16),
             struct((length, channels)),
@@ -691,8 +711,6 @@
             struct((chunks, STATE, local_di)),
         ],
         [
-            fixed((length, D)),
-            fixed((length, D)),
             fixed((channels + lanes, D)),
             rows_of(D),
             rows_of(channels),
@@ -793,7 +811,7 @@
     chunks = length // BLOCK
     channels = conv_in.shape[1]
     lanes = expand.shape[0]
-    grad = (channels + 16, D // len(places))
+    grad = (channels + 16, D) if len(places) == 1 else ((channels + 16) * D // 256, 128)
 
     def back(extent):
         return pl.BlockSpec((BLOCK, extent), lambda q, *_: (chunks - 1 - q, 0))
@@ -897,30 +915,100 @@
     )
 
 
-def run_update(places, gate_out_blocks, rest_blocks, in_arrays, out_arrays):
+def run_rest_pair(places, mine, arrived, there):
+    rest = (mine.shape[0] // len(places), mine.shape[1])
+    shapes = [struct(rest, jnp.bfloat16)] * len(places)
+    inputs = [mine, arrived]
+    return call(
+        rest_pair_kernel,
+        places,
+        inputs,
+        [fixed(array.shape) for array in inputs],
+        shapes,
+        [fixed(shape.shape) for shape in shapes],
+        [],
+        1,
+        there,
+        (2_000_000, 3_000_000, 0),
+        "rest_pair",
+    )
+
+
+def run_join(gate, out, vec, there):
+    inputs = [*gate, *out, *vec]
+    shape = (gate[0].shape[0] + out[0].shape[0], gate[0].shape[1])
+    return call(
+        join_kernel,
+        [jnp.int32(0)],
+        inputs,
+        [fixed(array.shape) for array in inputs],
+        [struct(shape, jnp.bfloat16), struct(vec[0].shape)],
+        [fixed(shape), fixed(vec[0].shape)],
+        [],
+        1,
+        there,
+        (500_000, 1_000_000, 0),
+        "join",
+    )
+
+
+def run_final(rest, vec, there):
+    inputs = [*rest, *vec]
+    return call(
+        final_kernel,
+        [jnp.int32(0)],
+        inputs,
+        [fixed(array.shape) for array in inputs],
+        [struct(rest[0].shape, jnp.bfloat16), struct(vec[0].shape)],
+        [fixed(rest[0].shape), fixed(vec[0].shape)],
+        [],
+        1,
+        there,
+        (500_000, 1_000_000, 0),
+        "final",
+    )
+
+
+def run_update_gate(places, blocks, in_arrays, out_arrays, there):
     groups = len(places)
-    blocks = [*gate_out_blocks, *rest_blocks]
-    rows_in = DI // 4
     rows_out = out_arrays[0].shape[0] // groups
     arrays = [*in_arrays, *out_arrays]
-    in_spec = pl.BlockSpec((rows_in, in_arrays[0].shape[1]), lambda q, *_: (q, 0))
-    out_spec = pl.BlockSpec((rows_out, D), lambda q, *_: (jnp.minimum(q, groups - 1), 0))
+    in_spec = pl.BlockSpec((DI // groups, in_arrays[0].shape[1]), lambda q, *_: (q, 0))
+    out_spec = pl.BlockSpec((rows_out, D), lambda q, *_: (q, 0))
     specs = [in_spec] * 3 + [out_spec] * 3
     return call(
-        lambda *refs: update_kernel(groups, *refs),
+        lambda *refs: update_gate_kernel(groups, *refs),
         places,
         [*blocks, *arrays],
         [fixed(array.shape) for array in blocks] + specs,
         [struct(array.shape) for array in arrays],
         specs,
-        [
-            pltpu.VMEM((groups,) + gate_out_blocks[0].shape, jnp.bfloat16),
-            pltpu.VMEM((groups,) + rest_blocks[0].shape, jnp.bfloat16),
-        ],
-        2 * (DI // rows_in) + 1,
+        [pltpu.VMEM((groups,) + blocks[0].shape, jnp.bfloat16)],
+        groups,
+        there,
+        (10_000_000, 13_000_000, 500_000),
+        "update_gate",
+    )
+
+
+def run_update_rest(places, blocks, in_arrays, so_far):
+    groups = len(places)
+    spec = pl.BlockSpec((DI // groups, in_arrays[0].shape[1]), lambda q, *_: (q + groups, 0))
+    return call(
+        lambda *refs: update_rest_kernel(groups, *refs),
+        places,
+        [*blocks, *in_arrays, *so_far],
+        [fixed(array.shape) for array in blocks]
+        + [spec] * 3
+        + [pl.BlockSpec(memory_space=pl.ANY)] * 3,
+        [struct(array.shape) for array in in_arrays],
+        [spec] * 3,
+        [pltpu.VMEM((groups,) + blocks[0].shape, jnp.bfloat16)],
+        groups + 1,
         [],
-        (20_000_000, 22_000_000, 1_000_000),
-        "update",
+        (10_000_000, 8_000_000, 500_000),
+        "update_rest",
+        [(1 + groups + 3 + number, number) for number in range(3)],
     )
 
 
@@ -976,32 +1064,6 @@
         if step < count // 2 - 1:
             rows = ring_step(rows)
     return places, blocks
-
-
-def add_kernel(counts, places_ref, *refs):
-    terms, results = refs[: sum(counts)], refs[sum(counts) :]
-    first = 0
-    for count, result in zip(counts, results):
-        total = sum_of(*terms[first : first + count])
-        result[...] = total.astype(result.dtype)
-        first = first + count
-
-
-def add(groups, arrived):
-    terms = [term for group in groups for term in group]
-    return call(
-        lambda *refs: add_kernel([len(group) for group in groups], *refs),
-        [jnp.int32(0)],
-        terms,
-        [fixed(term.shape) for term in terms],
-        [struct(group[0].shape, group[0].dtype) for group in groups],
-        [fixed(group[0].shape) for group in groups],
-        [],
-        1,
-        arrived,
-        (200_000, 900_000, 0),
-        "add",
-    )
 
 
 def take_block(values, index, rows):
@@ -1072,17 +1134,11 @@
     far = seq_index // 2
     if rings:
         y, z = shard_index % 2, shard_index // 2
-        rest_mine, gate_out_mine, both_mine = run_prepare(
-            seq_index, in_weight.T, out_weight, hidden_rows, cot_rows
-        )
+        rest_mine, gate_out_mine = run_prepare(seq_index, in_weight.T, out_weight)
         rest = ring_blocks(rest_mine)
-        both = seq_blocks(both_mine)
         gate_out = ring_blocks(gate_out_mine)
         gate_places = [z ^ mask for mask in range(4)]
         out_places = [y, 1 - y]
-        rest_places = [
-            (shard_index + 8 - 2 * step) % 8 ^ other for step in range(1, 5) for other in (0, 1)
-        ]
     else:
         in_low = low(in_weight)
         steps_mine = heads_of(in_low[:, DI + CONVCH :], 1, 1)
@@ -1097,12 +1153,11 @@
         gate_mine = heads_of(in_low[:, :DI], 1, HEADDIM)
         origin = [jnp.int32(0)]
         rest = (origin, [lax.all_gather(rest_mine, "wshard", axis=0, tiled=True).T])
-        hidden_low = lax.all_gather(hidden_rows, "seq", axis=0, tiled=True)
-        cot_low = lax.all_gather(cot_rows, "seq", axis=0, tiled=True)
-        both = (origin, [jnp.concatenate([hidden_low, cot_low], 0)])
         gate_mine = lax.all_gather(gate_mine, "wshard", axis=0, tiled=True).T
         gate_out = (origin, [gate_mine, gather_out(low(out_weight), seq_index, groups)])
-        gate_places, out_places, rest_places = origin, origin, origin
+        gate_places, out_places = origin, origin
+    hidden_low = lax.all_gather(hidden_rows, "seq", axis=0, tiled=True)
+    cot_low = lax.all_gather(cot_rows, "seq", axis=0, tiled=True)
     my_gain_two = heads_of(gain_two, 0, HEADDIM)[None, :]
     my_kernel = jnp.concatenate([heads_of(kernel[:, :DI], 1, HEADDIM), kernel[:, DI:]], 1)
     my_bias = jnp.concatenate([heads_of(conv_bias[:DI], 0, HEADDIM), conv_bias[DI:]], 0)
@@ -1119,8 +1174,6 @@
         jnp.arange(lanes)[:, None] == jnp.arange(local_di)[None, :] // HEADDIM
     ).astype(jnp.float32)
     (
-        hidden_low,
-        cot_low,
         rest_weight,
         normed_low,
         conv_in,
@@ -1130,7 +1183,7 @@
         scanned,
         states,
     ) = run_forward(
-        both, rest, gain_one[None, :], (my_kernel, my_bias[None, :]), heads_vectors, expand
+        hidden_low, rest, gain_one[None, :], (my_kernel, my_bias[None, :]), heads_vectors, expand
     )
     gate_weight, out_low, gating, d_gnorm, sums = run_gate(
         gate_out, cot_low, normed_low, scanned, my_gain_two
@@ -1156,7 +1209,7 @@
         gate_pieces = [swap(gate_grads[mask], "wshard", 2 * mask) for mask in range(1, 4)]
         out_arrived = swap(out_grads[1], "wshard", 1)
     backward = run_backward(
-        rest_places,
+        out_places,
         normed_low,
         conv_in,
         conv_pre,
@@ -1210,34 +1263,32 @@
     )
     vec_part = jnp.concatenate([shared, apart])[None]
     if rings:
-        (held,) = add(
-            [[rest_grads[0], rest_arrived]], [d_gain_one, gate_arrived, block_far] + out_pieces
+        rest_sums = run_rest_pair(
+            gate_places, rest_grads[0], rest_arrived, [d_gain_one, block_far] + out_pieces
         )
-        vec_arrived = swap(vec_part, "wshard", 1)
-        held, gate_part, out_part, vec_part = add(
-            [
-                [rest_grads[2], swap(rest_grads[3], "wshard", 1), ring_step(held)],
-                [gate_keep, gate_arrived],
-                [out_sums[0]] + out_pieces,
-                [vec_part, vec_arrived],
-            ],
-            [normed_arrived],
+        rest_pieces = [swap(rest_sums[mask], "wshard", 2 * mask) for mask in range(1, 4)]
+        gate_out_part, vec_part = run_join(
+            [gate_keep, gate_arrived],
+            [out_sums[0]] + out_pieces,
+            [vec_part, swap(vec_part, "wshard", 1)],
+            [rest_sums[0]],
         )
-        gate_out_part = jnp.concatenate([gate_part, out_part], 0)
-        gate_out_far = swap(gate_out_part, "seq", 2)
-        held, vec_part = add(
-            [
-                [rest_grads[4], swap(rest_grads[5], "wshard", 1), ring_step(held)],
-                [vec_part, swap(vec_part, "wshard", 2)],
-            ],
-            [gate_out_far],
+        vec_arrived = swap(vec_part, "wshard", 2)
+        spots, gate_out_blocks = seq_blocks(gate_out_part)
+        in_arrays = (in_weight.T, in_first.T, in_second.T)
+        updated = run_update_gate(
+            spots,
+            gate_out_blocks,
+            in_arrays,
+            (out_weight, out_first, out_second),
+            [vec_arrived],
         )
-        rest_part, vec_part = add(
-            [
-                [rest_grads[6], swap(rest_grads[7], "wshard", 1), ring_step(held)],
-                [vec_part, swap(vec_part, "wshard", 4)],
-            ],
-            [normed_far],
+        out_first_new, out_second_new, out_weight_new = updated[3:]
+        vec_part = vec_part + vec_arrived
+        rest_part, vec_part = run_final(
+            [rest_sums[0]] + rest_pieces,
+            [vec_part, swap(vec_part, "wshard", 4)],
+            [out_first_new],
         )
         vec_places, vec_blocks = seq_blocks(vec_part)
         every = jnp.zeros((groups, vec_part.shape[1]), jnp.float32)
@@ -1288,17 +1339,9 @@
         vec_weight, vec_first, vec_second, vec_total, vector_rate, 0.0
     )
     if rings:
-        rest_spots, rest_blocks = seq_blocks(rest_part)
-        _, gate_out_blocks = seq_blocks(gate_out_part, gate_out_far)
-        updated = run_update(
-            rest_spots,
-            gate_out_blocks,
-            rest_blocks,
-            (in_weight.T, in_first.T, in_second.T),
-            (out_weight, out_first, out_second),
-        )
-        in_first_new, in_second_new, in_weight_new = [array.T for array in updated[:3]]
-        out_first_new, out_second_new, out_weight_new = updated[3:]
+        spots, rest_blocks = seq_blocks(rest_part)
+        updated = run_update_rest(spots, rest_blocks, in_arrays, updated[:3])
+        in_first_new, in_second_new, in_weight_new = [array.T for array in updated]
     else:
         rest_part = lax.psum_scatter(rest_grads[0].T, "wshard", scatter_dimension=0, tiled=True)
         gate_part = lax.psum_scatter(gate_grads[0].T, "wshard", scatter_dimension=0, tiled=True)

time: 252 us -> 265 us (1.052)
  between operations: 1.64 us -> 14.8 us
  waiting for transfers between devices: 57.7 us -> 64.8 us
  starting transfers between devices: 50.3 us -> 46.2 us
  local copies, waits for them, and re-layouts: 22.6 us -> 19.7 us
    ppermute x9 -> x6, waiting for transfers between devices: 11.7 us -> 19 us  [ring_step(): lax.ppermute(held, 'wshard', [(i, (i + 2) % count) for i in range(count)])]
    ppermute x9 -> x6, starting transfers between devices: 10.3 us -> 4.98 us  [ring_step(): lax.ppermute(held, 'wshard', [(i, (i + 2) % count) for i in range(count)])]
    ppermute x42 -> x39, waiting for transfers between devices: 45.9 us -> 44.4 us  [swap(): return lax.ppermute(values, axis, route)]
    ppermute x42 -> x39, starting transfers between devices: 40 us -> 41.1 us  [swap(): return lax.ppermute(values, axis, route)]
    unnamed x127 -> x108, local copies, waits for them, and re-layouts: 8.77 us -> 7.93 us
  transfers between devices with their start and end apart: 51 -> 47, of which waited for: 16 -> 15; matrix products, arithmetic and copies ran while one was open for 10% -> 8% of each run, Pallas kernels for 22% -> 32%
where the time goes in v7:
time: 265 us; the launch traced here: 264 us
  Pallas kernels  108 us (41%)
  waiting for transfers between devices  64.8 us (24%)
  starting transfers between devices  46.2 us (17%)
  local copies, waits for them, and re-layouts  19.7 us (7%)
  between operations  14.8 us (6%)
  other arithmetic  10.4 us (4%)
    pallas_call x12, Pallas kernels, call(): pl.pallas_call(after(kernel, 1 + len(inputs), len(arrived)), grid_spec=pl...  108 us
    ppermute x39, waiting for transfers between devices, swap(): return lax.ppermute(values, axis, route)  44.4 us
    ppermute x39, starting transfers between devices, swap(): return lax.ppermute(values, axis, route)  41.1 us
    ppermute x6, waiting for transfers between devices, ring_step(): lax.ppermute(held, 'wshard', [(i, (i + 2) % count) for i in range(count)])  19 us
    unnamed x108, local copies, waits for them, and re-layouts  7.93 us
  transfers between devices with their start and end apart: 47, of which 15 were waited for; matrix products, arithmetic and copies ran while one was open for 8% of the time, Pallas kernels for 32%

profile of v7, /device:TPU:0, one launch (start us, length us, event | category | flops | bytes accessed | tf_op | source)
XLA Modules:
  0.0 264.0 jit_solution(6632743391639626264)
XLA Ops:
  8.7 2.7 %prepare.1 = (bf16[784,128]{1,0:T(8,128)(2,1)}, bf16[1024,128]{1,0:T(8,128)(2,1)}) custom-call(s32[1]{0:T(128)} %bitcast.17.refs_0_, f32[4384,128]{1,0:T(8,128)} %bitcast.84, f32[256,1024]{1,0:T(8,128)} %refs_8_.1), custom_call_target="tpu_custom_call" | custom-call | flops 100000000 | bytes 4000000 | tf_op jit(solution)/shard_map/prepare/pallas_call | solution.py:649
  11.4 3.0 %collective-permute-start.1 = (bf16[784,128]{1,0:T(8,128)(2,1)}, bf16[784,128]{1,0:T(8,128)(2,1)S(1)}, u32[]{:S(2)}, u32[]{:S(2)}) collective-permute-start(bf16[784,128]{1,0:T(8,128)(2,1)} %get-tuple-element.72.refs_1_), channel_id=1, source_target_pairs={{0,2},{1,3},{2,4},{3,5},{4,6},{5,7},{6,0},{7,1},{8,10},{9,11},{10,... | collective-permute-start | bytes 602120 | tf_op jit(solution)/shard_map/ppermute | solution.py:1053
  17.8 4.7 %collective-permute-done.1.refs_3_ = bf16[784,128]{1,0:T(8,128)(2,1)S(1)} collective-permute-done((bf16[784,128]{1,0:T(8,128)(2,1)}, bf16[784,128]{1,0:T(8,128)(2,1)S(1)}, u32[]{:S(2)}, u32[]{:S(2)}) %collective-permute-start.1) | collective-permute-done | bytes 200736 | tf_op jit(solution)/shard_map/ppermute | solution.py:1053
  22.5 5.6 %collective-permute-done.8.refs_3_ = bf16[1024,128]{1,0:T(8,128)(2,1)S(1)} collective-permute-done((bf16[1024,128]{1,0:T(8,128)(2,1)}, bf16[1024,128]{1,0:T(8,128)(2,1)S(1)}, u32[]{:S(2)}, u32[]{:S(2)}) %collective-permute-start.8) | collective-permute-done | bytes 262176 | tf_op jit(solution)/shard_map/ppermute | solution.py:1053
  29.4 2.7 %collective-permute-done.3.refs_5_ = bf16[784,128]{1,0:T(8,128)(2,1)S(1)} collective-permute-done((bf16[784,128]{1,0:T(8,128)(2,1)S(1)}, bf16[784,128]{1,0:T(8,128)(2,1)S(1)}, u32[]{:S(2)}, u32[]{:S(2)}) %collective-permute-start.3) | collective-permute-done | bytes 200736 | tf_op jit(solution)/shard_map/ppermute | solution.py:1053
  33.0 6.0 %collective-permute-done.10.refs_5_ = bf16[1024,128]{1,0:T(8,128)(2,1)S(1)} collective-permute-done((bf16[1024,128]{1,0:T(8,128)(2,1)S(1)}, bf16[1024,128]{1,0:T(8,128)(2,1)S(1)}, u32[]{:S(2)}, u32[]{:S(2)}) %collective-permute-start.10) | collective-permute-done | bytes 262176 | tf_op jit(solution)/shard_map/ppermute | solution.py:1053
  43.2 1.8 collective-permute-start.2
  45.2 1.8 collective-permute-start.6
  48.0 3.1 %collective-permute-done.2.refs_4_ = bf16[784,128]{1,0:T(8,128)(2,1)S(1)} collective-permute-done((bf16[784,128]{1,0:T(8,128)(2,1)S(1)}, bf16[784,128]{1,0:T(8,128)(2,1)S(1)}, u32[]{:S(2)}, u32[]{:S(2)}) %collective-permute-start.2) | collective-permute-done | bytes 200736 | tf_op jit(solution)/shard_map/ppermute | solution.py:1041
  51.1 1.8 collective-permute-start.9
  52.9 2.5 collective-permute-done.4.refs_6_
  55.4 1.8 collective-permute-start.11
  57.4 2.4 collective-permute-done.6.refs_8_
  59.8 15.6 %forward.1 = (bf16[896,1024]{1,0:T(8,128)(2,1)}, bf16[1024,1024]{1,0:T(8,128)(2,1)}, f32[1024,768]{1,0:T(8,128)}, f32[1024,768]{1,0:T(8,128)}, f32[1024,128]{1,0...) custom-call(s32[8]{0:T(128)} %stack.123.refs_0_, ...), custom_call_target="tpu_custom_call" | custom-call | flops 6000000000 | bytes 30000000 | tf_op jit(solution)/shard_map/forward/pallas_call | solution.py:649
  75.6 2.0 collective-permute-done.13.refs_8_
  78.4 11.2 %gate.1 = (bf16[512,1024]{1,0:T(8,128)(2,1)}, bf16[512,1024]{1,0:T(8,128)(2,1)}, f32[1024,512]{1,0:T(8,128)}, f32[1024,512]{1,0:T(8,128)}, f32[8,1024]{1,0:T(8,128)}) custom-call(s32[8]{0:T(128)} %stack.123.refs_0_, bf16[1024,128]{1,0:T(8,128)(2,1)} %get-tuple-element.74.refs_1_, bf16[1024,128]{1,0:T(8,128)(2,1)} %copy-done.38, ...), custom_call_target="tpu_custom_call" | custom-call | flops 2500000000 | bytes 12000000 | tf_op jit(solution)/shard_map/gate/pallas_call | solution.py:649
  95.3 13.3 %middle.1 = (bf16[512,1024]{1,0:T(8,128)(2,1)}, bf16[512,1024]{1,0:T(8,128)(2,1)}, bf16[1024,512]{1,0:T(8,128)(2,1)}, bf16[1024,512]{1,0:T(8,128)(2,1)}, f32[1,5...) custom-call(s32[7]{0:T(128)} %stack.114.refs_0_, ...), custom_call_target="tpu_custom_call" | custom-call | flops 4000000000 | bytes 15000000 | tf_op jit(solution)/shard_map/middle/pallas_call | solution.py:649
  111.9 30.9 %backward.1 = (bf16[1024,896]{1,0:T(8,128)(2,1)}, f32[4,768]{1,0:T(4,128)}, f32[1,768]{1,0:T(1,128)}, f32[1,512]{1,0:T(1,128)}, f32[2,128]{1,0:T(2,128)}, /*inde...) custom-call(s32[2]{0:T(128)} %pad_add_fusion.refs_0_, bf16[1024,1024]{1,0:T(8,128)(2,1)} %get-tuple-element.75.refs_10_.refs_5_.refs_1_, ...), custom_call_target="tpu_custom_call" | custom-call | flops 14000000000 | bytes 40000000 | tf_op jit(solution)/shard_map/backward/pallas_call | solution.py:649
  143.4 2.0 collective-permute-start.18
  147.5 15.9 %collective-permute-done.18.refs_3_ = bf16[512,256]{1,0:T(8,128)(2,1)S(1)} collective-permute-done((bf16[512,256]{1,0:T(8,128)(2,1)}, bf16[512,256]{1,0:T(8,128)(2,1)S(1)}, u32[]{:S(2)}, u32[]{:S(2)}) %collective-permute-start.18) | collective-permute-done | bytes 262176 | tf_op jit(solution)/shard_map/ppermute | solution.py:1041
  164.7 4.3 %pair.1 = (bf16[512,128]{1,0:T(8,128)(2,1)}, bf16[512,128]{1,0:T(8,128)(2,1)}, bf16[256,1024]{1,0:T(8,128)(2,1)}, bf16[256,1024]{1,0:T(8,128)(2,1)}, bf16[512,12...) custom-call(s32[6]{0:T(128)} %stack.111.refs_0_, ...), custom_call_target="tpu_custom_call" | custom-call | flops 3000000 | bytes 7000000 | tf_op jit(solution)/shard_map/pair/pallas_call | solution.py:649
  169.9 6.0 %collective-permute-start.26 = (bf16[512,128]{1,0:T(8,128)(2,1)}, bf16[512,128]{1,0:T(8,128)(2,1)S(1)}, u32[]{:S(2)}, u32[]{:S(2)}) collective-permute-start(bf16[512,128]{1,0:T(8,128)(2,1)} %get-tuple-element.106), channel_id=1, source_target_pairs={{0,2},{1,3},{2,0},{3,1},{4,6},{5,7},{6,4},{7,5},{8,10},{9,11},{10,... | collective-permute-start | bytes 393224 | tf_op jit(solution)/shard_map/ppermute | solution.py:1041
  178.5 8.6 %normed.1 = (bf16[512,1024]{1,0:T(8,128)(2,1)}, bf16[512,1024]{1,0:T(8,128)(2,1)}, f32[1,1024]{1,0:T(1,128)}) custom-call(s32[1]{0:T(128)} %bitcast.7.refs_0_, bf16[1024,1024]{1,0:T(8,128)(2,1)} %bitcast.105, bf16[1024,512]{1,0:T(8,128)(2,1)} %get-tuple-element.90.refs_2_, bf16[1024,896]{1,0:T(8,128)(2,1)} %get-tuple-element.97.refs_3_, ...), custom_call_target="tpu_custom_call" | custom-call | flops 3000000000 | bytes 9000000 | tf_op jit(solution)/shard_map/normed/pallas_call | solution.py:649
  193.8 3.1 %rest_pair.1 = (bf16[784,128]{1,0:T(8,128)(2,1)}, bf16[784,128]{1,0:T(8,128)(2,1)}, bf16[784,128]{1,0:T(8,128)(2,1)}, bf16[784,128]{1,0:T(8,128)(2,1)}) custom-call(s32[4]{0:T(128)} %pad_add_fusion.2.refs_0_, bf16[3136,128]{1,0:T(8,128)(2,1)} %get-tuple-element.103.refs_1_, bf16[3136,128]{1,0:T(8,128)(2,1)} %copy-done.7, ...), custom_call_target="tpu_custom_call" | custom-call | flops 2000000 | bytes 3000000 | tf_op jit(solution)/shard_map/rest_pair/pallas_call | solution.py:649
  197.5 2.0 join.1
  201.5 6.6 %collective-permute-done.37.refs_3_ = bf16[1024,128]{1,0:T(8,128)(2,1)S(1)} collective-permute-done((bf16[1024,128]{1,0:T(8,128)(2,1)}, bf16[1024,128]{1,0:T(8,128)(2,1)S(1)}, u32[]{:S(2)}, u32[]{:S(2)}) %collective-permute-start.37) | collective-permute-done | bytes 262176 | tf_op jit(solution)/shard_map/ppermute | solution.py:1041
  209.3 2.0 collective-permute-start.30
  215.4 7.5 %update_gate.1 = (f32[4384,128]{1,0:T(8,128)}, f32[4384,128]{1,0:T(8,128)}, f32[4384,128]{1,0:T(8,128)}, f32[256,1024]{1,0:T(8,128)}, f32[256,1024]{1,0:T(8,128)}, /*index=5*/f32[256,1024]{1,0:T(8,128)}) custom-call(s32[4]{0:T(128)} %pad_add_fusion.1.refs_0_, bf16[1024,128]{1,0:T(8,128)(2,1)} %get-tuple-element.121.refs_1_, bf16[1024,128]{1,0:T(8,128)(2,1)} %copy-done.14, ...), custom_call_target="tpu_custom_call" | custom-call | flops 10000000 | bytes 13000000 | tf_op jit(solution)/shard_map/update_gate/pallas_call | solution.py:649
  222.9 8.5 %collective-permute-done.35.refs_6_ = f32[1,5400]{1,0:T(1,128)S(1)} collective-permute-done((f32[1,5400]{1,0:T(1,128)S(1)}, f32[1,5400]{1,0:T(1,128)S(1)}, u32[]{:S(2)}, u32[]{:S(2)}) %collective-permute-start.35) | collective-permute-done | bytes 21632 | tf_op jit(solution)/shard_map/ppermute | solution.py:1041
  232.2 2.0 final.1
  246.6 6.9 %update_rest.1 = (f32[4384,128]{1,0:T(8,128)}, f32[4384,128]{1,0:T(8,128)}, f32[4384,128]{1,0:T(8,128)}) custom-call(s32[4]{0:T(128)} %pad_add_fusion.1.refs_0_, bf16[784,128]{1,0:T(8,128)(2,1)} %get-tuple-element.123.refs_1_, bf16[784,128]{1,0:T(8,128)(2,1)} %collective-permute-done.39.refs_2_, ...), custom_call_target="tpu_custom_call", output_to_operand_aliasing={{0}: (8, {}), {1}: (9, {}), {2}: (10, {})} | custom-call | flops 10000000 | bytes 8000000 | tf_op jit(solution)/shard_map/update_rest/pallas_call | solution.py:649
  255.2 1.9 fusion.6
  (271 shorter events, 58.8 us)
Async XLA Ops:
  7.2 52.6 %all-gather.5.cloned.1.call-start = ((), (), s32[]{:S(2)}) async-start(), calls=%async_computation | async-start | bytes 2621440 | tf_op jit(solution)/shard_map/all_gather | solution.py:1159
  7.9 69.7 %all-gather.7.cloned.1.call-start = ((), (), s32[]{:S(2)}) async-start(), calls=%async_computation.1 | async-start | bytes 2621440 | tf_op jit(solution)/shard_map/all_gather | solution.py:1160
  11.4 11.1 %collective-permute-start.1 = (bf16[784,128]{1,0:T(8,128)(2,1)}, bf16[784,128]{1,0:T(8,128)(2,1)S(1)}, u32[]{:S(2)}, u32[]{:S(2)}) collective-permute-start(bf16[784,128]{1,0:T(8,128)(2,1)} %get-tuple-element.72.refs_1_), channel_id=1, source_target_pairs={{0,2},{1,3},{2,4},{3,5},{4,6},{5,7},{6,0},{7,1},{8,10},{9,11},{10,... | collective-permute-start | bytes 602120 | tf_op jit(solution)/shard_map/ppermute | solution.py:1053
  14.4 33.3 %collective-permute-start = (bf16[784,128]{1,0:T(8,128)(2,1)}, bf16[784,128]{1,0:T(8,128)(2,1)S(1)}, u32[]{:S(2)}, u32[]{:S(2)}) collective-permute-start(bf16[784,128]{1,0:T(8,128)(2,1)} %get-tuple-element.72.refs_1_), channel_id=1, source_target_pairs={{0,1},{1,0},{2,3},{3,2},{4,5},{5,4},{6,7},{7,6},{8,9},{9,8},{10,11... | collective-permute-start | bytes 602120 | tf_op jit(solution)/shard_map/ppermute | solution.py:1041
  16.0 12.1 %collective-permute-start.8 = (bf16[1024,128]{1,0:T(8,128)(2,1)}, bf16[1024,128]{1,0:T(8,128)(2,1)S(1)}, u32[]{:S(2)}, u32[]{:S(2)}) collective-permute-start(bf16[1024,128]{1,0:T(8,128)(2,1)} %get-tuple-element.74.refs_1_), channel_id=1, source_target_pairs={{0,2},{1,3},{2,4},{3,5},{4,6},{5,7},{6,0},{7,1},{8,10},{9,11},{10,... | collective-permute-start | bytes 786440 | tf_op jit(solution)/shard_map/ppermute | solution.py:1053
  28.1 11.0 %collective-permute-start.10 = (bf16[1024,128]{1,0:T(8,128)(2,1)S(1)}, bf16[1024,128]{1,0:T(8,128)(2,1)S(1)}, u32[]{:S(2)}, u32[]{:S(2)}) collective-permute-start(bf16[1024,128]{1,0:T(8,128)(2,1)S(1)} %collective-permute-done.8.refs_3_), channel_id=1, source_target_pairs={{0,2},{1,3},{2,4},{3,5},{4,6},{5,7},{6,0},{7,1},{8,10},{9,11},{10,... | collective-permute-start | bytes 786440 | tf_op jit(solution)/shard_map/ppermute | solution.py:1053
  32.1 13.1 %collective-permute-start.5 = (bf16[784,128]{1,0:T(8,128)(2,1)S(1)}, bf16[784,128]{1,0:T(8,128)(2,1)S(1)}, u32[]{:S(2)}, u32[]{:S(2)}) collective-permute-start(bf16[784,128]{1,0:T(8,128)(2,1)S(1)} %collective-permute-done.3.refs_5_), channel_id=1, source_target_pairs={{0,2},{1,3},{2,4},{3,5},{4,6},{5,7},{6,0},{7,1},{8,10},{9,11},{10,... | collective-permute-start | bytes 602120 | tf_op jit(solution)/shard_map/ppermute | solution.py:1053
  39.1 18.1 %collective-permute-start.12 = (bf16[1024,128]{1,0:T(8,128)(2,1)S(1)}, bf16[1024,128]{1,0:T(8,128)(2,1)S(1)}, u32[]{:S(2)}, u32[]{:S(2)}) collective-permute-start(bf16[1024,128]{1,0:T(8,128)(2,1)S(1)} %collective-permute-done.10.refs_5_), channel_id=1, source_target_pairs={{0,2},{1,3},{2,4},{3,5},{4,6},{5,7},{6,0},{7,1},{8,10},{9,11},{10,... | collective-permute-start | bytes 786440 | tf_op jit(solution)/shard_map/ppermute | solution.py:1053
  45.0 10.4 %collective-permute-start.4 = (bf16[784,128]{1,0:T(8,128)(2,1)S(1)}, bf16[784,128]{1,0:T(8,128)(2,1)S(1)}, u32[]{:S(2)}, u32[]{:S(2)}) collective-permute-start(bf16[784,128]{1,0:T(8,128)(2,1)S(1)} %collective-permute-done.3.refs_5_), channel_id=1, source_target_pairs={{0,1},{1,0},{2,3},{3,2},{4,5},{5,4},{6,7},{7,6},{8,9},{9,8},{10,11... | collective-permute-start | bytes 602120 | tf_op jit(solution)/shard_map/ppermute | solution.py:1041
  45.2 14.6 %collective-permute-start.6 = (bf16[784,128]{1,0:T(8,128)(2,1)S(1)}, bf16[784,128]{1,0:T(8,128)(2,1)}, u32[]{:S(2)}, u32[]{:S(2)}) collective-permute-start(bf16[784,128]{1,0:T(8,128)(2,1)S(1)} %collective-permute-done.5.refs_7_), channel_id=1, source_target_pairs={{0,1},{1,0},{2,3},{3,2},{4,5},{5,4},{6,7},{7,6},{8,9},{9,8},{10,11... | collective-permute-start | bytes 602120 | tf_op jit(solution)/shard_map/ppermute | solution.py:1041
  47.8 27.8 %collective-permute-start.7 = (bf16[1024,128]{1,0:T(8,128)(2,1)}, bf16[1024,128]{1,0:T(8,128)(2,1)S(1)}, u32[]{:S(2)}, u32[]{:S(2)}) collective-permute-start(bf16[1024,128]{1,0:T(8,128)(2,1)} %get-tuple-element.74.refs_1_), channel_id=1, source_target_pairs={{0,1},{1,0},{2,3},{3,2},{4,5},{5,4},{6,7},{7,6},{8,9},{9,8},{10,11... | collective-permute-start | bytes 786440 | tf_op jit(solution)/shard_map/ppermute | solution.py:1041
  51.1 24.5 %collective-permute-start.9 = (bf16[1024,128]{1,0:T(8,128)(2,1)S(1)}, bf16[1024,128]{1,0:T(8,128)(2,1)S(1)}, u32[]{:S(2)}, u32[]{:S(2)}) collective-permute-start(bf16[1024,128]{1,0:T(8,128)(2,1)S(1)} %collective-permute-done.8.refs_3_), channel_id=1, source_target_pairs={{0,1},{1,0},{2,3},{3,2},{4,5},{5,4},{6,7},{7,6},{8,9},{9,8},{10,11... | collective-permute-start | bytes 786440 | tf_op jit(solution)/shard_map/ppermute | solution.py:1041
  55.4 20.2 %collective-permute-start.11 = (bf16[1024,128]{1,0:T(8,128)(2,1)S(1)}, bf16[1024,128]{1,0:T(8,128)(2,1)S(1)}, u32[]{:S(2)}, u32[]{:S(2)}) collective-permute-start(bf16[1024,128]{1,0:T(8,128)(2,1)S(1)} %collective-permute-done.10.refs_5_), channel_id=1, source_target_pairs={{0,1},{1,0},{2,3},{3,2},{4,5},{5,4},{6,7},{7,6},{8,9},{9,8},{10,11... | collective-permute-start | bytes 786440 | tf_op jit(solution)/shard_map/ppermute | solution.py:1041
  57.2 20.4 %collective-permute-start.13 = (bf16[1024,128]{1,0:T(8,128)(2,1)S(1)}, bf16[1024,128]{1,0:T(8,128)(2,1)S(1)}, u32[]{:S(2)}, u32[]{:S(2)}) collective-permute-start(bf16[1024,128]{1,0:T(8,128)(2,1)S(1)} %collective-permute-done.12.refs_7_), channel_id=1, source_target_pairs={{0,1},{1,0},{2,3},{3,2},{4,5},{5,4},{6,7},{7,6},{8,9},{9,8},{10,11... | collective-permute-start | bytes 786440 | tf_op jit(solution)/shard_map/ppermute | solution.py:1041
  108.5 54.9 %collective-permute-start.21 = (bf16[512,1024]{1,0:T(8,128)(2,1)}, bf16[512,1024]{1,0:T(8,128)(2,1)S(1)}, u32[]{:S(2)}, u32[]{:S(2)}) collective-permute-start(bf16[512,1024]{1,0:T(8,128)(2,1)} %get-tuple-element.87), channel_id=1, source_target_pairs={{0,8},{8,0},{16,24},{24,16},{1,9},{9,1},{17,25},{25,17},{2,10},{10... | collective-permute-start | bytes 3145736 | tf_op jit(solution)/shard_map/ppermute | solution.py:1041
  108.8 54.6 %collective-permute-start.20 = (bf16[2048,128]{1,0:T(8,128)(2,1)}, bf16[2048,128]{1,0:T(8,128)(2,1)S(1)}, u32[]{:S(2)}, u32[]{:S(2)}) collective-permute-start(bf16[2048,128]{1,0:T(8,128)(2,1)} %get-tuple-element.85), channel_id=1, source_target_pairs={{0,1},{1,0},{2,3},{3,2},{4,5},{5,4},{6,7},{7,6},{8,9},{9,8},{10,11... | collective-permute-start | bytes 1572872 | tf_op jit(solution)/shard_map/ppermute | solution.py:1041
  110.3 35.1 %collective-permute-start.17 = (bf16[512,256]{1,0:T(8,128)(2,1)}, bf16[512,256]{1,0:T(8,128)(2,1)S(1)}, u32[]{:S(2)}, u32[]{:S(2)}) collective-permute-start(bf16[512,256]{1,0:T(8,128)(2,1)} %get-tuple-element.81), channel_id=1, source_target_pairs={{0,2},{1,3},{2,0},{3,1},{4,6},{5,7},{6,4},{7,5},{8,10},{9,11},{10,... | collective-permute-start | bytes 786440 | tf_op jit(solution)/shard_map/ppermute | solution.py:1041
  142.8 44.3 %collective-permute-start.25 = (bf16[3136,128]{1,0:T(8,128)(2,1)}, bf16[3136,128]{1,0:T(8,128)(2,1)S(1)}, u32[]{:S(2)}, u32[]{:S(2)}) collective-permute-start(bf16[3136,128]{1,0:T(8,128)(2,1)} %get-tuple-element.104), channel_id=1, source_target_pairs={{0,1},{1,0},{2,3},{3,2},{4,5},{5,4},{6,7},{7,6},{8,9},{9,8},{10,11... | collective-permute-start | bytes 2408456 | tf_op jit(solution)/shard_map/ppermute | solution.py:1041
  143.4 20.0 %collective-permute-start.18 = (bf16[512,256]{1,0:T(8,128)(2,1)}, bf16[512,256]{1,0:T(8,128)(2,1)S(1)}, u32[]{:S(2)}, u32[]{:S(2)}) collective-permute-start(bf16[512,256]{1,0:T(8,128)(2,1)} %get-tuple-element.82), channel_id=1, source_target_pairs={{0,4},{1,5},{2,6},{3,7},{4,0},{5,1},{6,2},{7,3},{8,12},{9,13},{10,... | collective-permute-start | bytes 786440 | tf_op jit(solution)/shard_map/ppermute | solution.py:1041
  145.4 18.0 %collective-permute-start.19 = (bf16[512,256]{1,0:T(8,128)(2,1)}, bf16[512,256]{1,0:T(8,128)(2,1)S(1)}, u32[]{:S(2)}, u32[]{:S(2)}) collective-permute-start(bf16[512,256]{1,0:T(8,128)(2,1)} %get-tuple-element.83), channel_id=1, source_target_pairs={{0,6},{1,7},{2,4},{3,5},{4,2},{5,3},{6,0},{7,1},{8,14},{9,15},{10,... | collective-permute-start | bytes 786440 | tf_op jit(solution)/shard_map/ppermute | solution.py:1041
  169.0 23.9 %collective-permute-start.22 = (bf16[256,1024]{1,0:T(8,128)(2,1)}, bf16[256,1024]{1,0:T(8,128)(2,1)S(1)}, u32[]{:S(2)}, u32[]{:S(2)}) collective-permute-start(bf16[256,1024]{1,0:T(8,128)(2,1)} %get-tuple-element.89), channel_id=1, source_target_pairs={{0,16},{8,24},{16,0},{24,8},{1,17},{9,25},{17,1},{25,9},{2,18},{10... | collective-permute-start | bytes 1572872 | tf_op jit(solution)/shard_map/ppermute | solution.py:1041
  169.9 18.8 %collective-permute-start.26 = (bf16[512,128]{1,0:T(8,128)(2,1)}, bf16[512,128]{1,0:T(8,128)(2,1)S(1)}, u32[]{:S(2)}, u32[]{:S(2)}) collective-permute-start(bf16[512,128]{1,0:T(8,128)(2,1)} %get-tuple-element.106), channel_id=1, source_target_pairs={{0,2},{1,3},{2,0},{3,1},{4,6},{5,7},{6,4},{7,5},{8,10},{9,11},{10,... | collective-permute-start | bytes 393224 | tf_op jit(solution)/shard_map/ppermute | solution.py:1041
  175.9 15.8 %collective-permute-start.27 = (bf16[512,128]{1,0:T(8,128)(2,1)}, bf16[512,128]{1,0:T(8,128)(2,1)S(1)}, u32[]{:S(2)}, u32[]{:S(2)}) collective-permute-start(bf16[512,128]{1,0:T(8,128)(2,1)} %get-tuple-element.107), channel_id=1, source_target_pairs={{0,4},{1,5},{2,6},{3,7},{4,0},{5,1},{6,2},{7,3},{8,12},{9,13},{10,... | collective-permute-start | bytes 393224 | tf_op jit(solution)/shard_map/ppermute | solution.py:1041
  177.0 15.9 %collective-permute-start.28 = (bf16[512,128]{1,0:T(8,128)(2,1)}, bf16[512,128]{1,0:T(8,128)(2,1)S(1)}, u32[]{:S(2)}, u32[]{:S(2)}) collective-permute-start(bf16[512,128]{1,0:T(8,128)(2,1)} %get-tuple-element.108), channel_id=1, source_target_pairs={{0,6},{1,7},{2,4},{3,5},{4,2},{5,3},{6,0},{7,1},{8,14},{9,15},{10,... | collective-permute-start | bytes 393224 | tf_op jit(solution)/shard_map/ppermute | solution.py:1041
  187.1 9.7 %collective-permute-start.32 = (bf16[512,128]{1,0:T(8,128)(2,1)}, bf16[512,128]{1,0:T(8,128)(2,1)}, u32[]{:S(2)}, u32[]{:S(2)}) collective-permute-start(bf16[512,128]{1,0:T(8,128)(2,1)} %get-tuple-element.113), channel_id=1, source_target_pairs={{0,1},{1,0},{2,3},{3,2},{4,5},{5,4},{6,7},{7,6},{8,9},{9,8},{10,11... | collective-permute-start | bytes 393224 | tf_op jit(solution)/shard_map/ppermute | solution.py:1041
  188.7 47.6 %collective-permute-start.23 = (bf16[512,1024]{1,0:T(8,128)(2,1)}, bf16[512,1024]{1,0:T(8,128)(2,1)S(1)}, u32[]{:S(2)}, u32[]{:S(2)}) collective-permute-start(bf16[512,1024]{1,0:T(8,128)(2,1)} %get-tuple-element.102), channel_id=1, source_target_pairs={{0,8},{8,0},{16,24},{24,16},{1,9},{9,1},{17,25},{25,17},{2,10},{10... | collective-permute-start | bytes 3145736 | tf_op jit(solution)/shard_map/ppermute | solution.py:1041
  200.6 10.7 %collective-permute-start.36 = (bf16[1024,128]{1,0:T(8,128)(2,1)}, bf16[1024,128]{1,0:T(8,128)(2,1)S(1)}, u32[]{:S(2)}, u32[]{:S(2)}) collective-permute-start(bf16[1024,128]{1,0:T(8,128)(2,1)} %get-tuple-element.121.refs_1_), channel_id=1, source_target_pairs={{0,8},{8,0},{16,24},{24,16},{1,9},{9,1},{17,25},{25,17},{2,10},{10... | collective-permute-start | bytes 786440 | tf_op jit(solution)/shard_map/ppermute | solution.py:1041
  208.3 23.1 %collective-permute-start.29 = (bf16[784,128]{1,0:T(8,128)(2,1)}, bf16[784,128]{1,0:T(8,128)(2,1)S(1)}, u32[]{:S(2)}, u32[]{:S(2)}) collective-permute-start(bf16[784,128]{1,0:T(8,128)(2,1)} %get-tuple-element.110), channel_id=1, source_target_pairs={{0,2},{1,3},{2,0},{3,1},{4,6},{5,7},{6,4},{7,5},{8,10},{9,11},{10,... | collective-permute-start | bytes 602120 | tf_op jit(solution)/shard_map/ppermute | solution.py:1041
  209.3 22.1 %collective-permute-start.30 = (bf16[784,128]{1,0:T(8,128)(2,1)}, bf16[784,128]{1,0:T(8,128)(2,1)S(1)}, u32[]{:S(2)}, u32[]{:S(2)}) collective-permute-start(bf16[784,128]{1,0:T(8,128)(2,1)} %get-tuple-element.111), channel_id=1, source_target_pairs={{0,4},{1,5},{2,6},{3,7},{4,0},{5,1},{6,2},{7,3},{8,12},{9,13},{10,... | collective-permute-start | bytes 602120 | tf_op jit(solution)/shard_map/ppermute | solution.py:1041
  211.3 20.1 %collective-permute-start.31 = (bf16[784,128]{1,0:T(8,128)(2,1)}, bf16[784,128]{1,0:T(8,128)(2,1)S(1)}, u32[]{:S(2)}, u32[]{:S(2)}) collective-permute-start(bf16[784,128]{1,0:T(8,128)(2,1)} %get-tuple-element.112), channel_id=1, source_target_pairs={{0,6},{1,7},{2,4},{3,5},{4,2},{5,3},{6,0},{7,1},{8,14},{9,15},{10,... | collective-permute-start | bytes 602120 | tf_op jit(solution)/shard_map/ppermute | solution.py:1041
  213.6 17.8 %collective-permute-start.35 = (f32[1,5400]{1,0:T(1,128)S(1)}, f32[1,5400]{1,0:T(1,128)S(1)}, u32[]{:S(2)}, u32[]{:S(2)}) collective-permute-start(f32[1,5400]{1,0:T(1,128)S(1)} %add.142.refs_5_), channel_id=1, source_target_pairs={{0,4},{1,5},{2,6},{3,7},{4,0},{5,1},{6,2},{7,3},{8,12},{9,13},{10,... | collective-permute-start | bytes 64808 | tf_op jit(solution)/shard_map/ppermute | solution.py:1041
  240.7 14.1 %collective-permute-start.24 = (bf16[256,1024]{1,0:T(8,128)(2,1)}, bf16[256,1024]{1,0:T(8,128)(2,1)S(1)}, u32[]{:S(2)}, u32[]{:S(2)}) collective-permute-start(bf16[256,1024]{1,0:T(8,128)(2,1)} %dynamic-slice_convert_fusion), channel_id=1, source_target_pairs={{0,16},{8,24},{16,0},{24,8},{1,17},{9,25},{17,1},{25,9},{2,18},{10... | collective-permute-start | bytes 1572872 | tf_op jit(solution)/shard_map/ppermute | solution.py:1041
  (69 other events, 528.4 us)
Sparse Core Ops, SparseCore 0:
  9.6 25.2 all-gather.4
  36.5 22.5 all-gather.6

commit v8 on v7

--- a/solution.py
+++ b/solution.py
@@ -201,14 +201,18 @@
         if count == 2:
             gate_ref[...] = blocks[0][...]
             out_ref[...] = blocks[1][...]
-        else:
-            for number, block in enumerate(blocks):
+            return
+        number = 0
+        for block in blocks:
+            columns = block.shape[1]
+            for base in range(0, block.shape[0], 2 * local_di):
                 spot = places_ref[number]
-                place_columns(gate_ref, spot, block[:local_di, :])
-                for tile in range(D // block.shape[1]):
-                    first = local_di + tile * HEADDIM
-                    columns = slice(tile * block.shape[1], (tile + 1) * block.shape[1])
-                    place_rows(out_ref.at[:, columns], spot, block[first : first + HEADDIM, :])
+                number = number + 1
+                place_columns(gate_ref, spot, block[base : base + local_di, :])
+                for tile in range(D // columns):
+                    first = base + local_di + tile * HEADDIM
+                    span = slice(tile * columns, (tile + 1) * columns)
+                    place_rows(out_ref.at[:, span], spot, block[first : first + HEADDIM, :])
 
     gating = dot_nt(normed_ref[...], gate_ref[...])
     gating_ref[...] = gating
@@ -221,18 +225,6 @@
     sums_ref[...] = jnp.where(
         lax.broadcasted_iota(jnp.int32, squares.shape, 0) == 0, squares, products
     )
-
-
-def keep_chunk(value, here, number, mine_ref, send_ref):
-    rows = pl.ds(pl.multiple_of(number * BLOCK, BLOCK), BLOCK)
-
-    @pl.when(here)
-    def _():
-        mine_ref[rows, :] = value
-
-    @pl.when(jnp.logical_not(here))
-    def _():
-        send_ref[rows, :] = value
 
 
 def middle_kernel(gate_count, out_count, places_ref, *refs):
@@ -248,15 +240,14 @@
         sums_four_ref,
         out_ref,
         gain_two_ref,
-        mine_ref,
-        send_ref,
+        block_ref,
         d_gating_ref,
         d_scanned_ref,
         d_gain_two_ref,
-    ) = refs[:16]
-    gate_refs = refs[16 : 16 + gate_count]
-    out_refs = refs[16 + gate_count : 16 + gate_count + out_count]
-    out_sum, gate_sum = refs[16 + gate_count + out_count :]
+    ) = refs[:15]
+    gate_refs = refs[15 : 15 + gate_count]
+    out_refs = refs[15 + gate_count : 15 + gate_count + out_count]
+    out_sum, gate_sum = refs[15 + gate_count + out_count :]
     chunk = pl.program_id(0)
 
     @pl.when(chunk == 0)
@@ -277,8 +268,7 @@
     d_gnorm = d_gnorm_ref[...]
     gain_two = gain_two_ref[...]
     gnorm = low(unit * gain_two)
-    block_part = low(dot_nn(gnorm, out_ref[...]))
-    keep_chunk(block_part, chunk % 2 == places_ref[0], chunk // 2, mine_ref, send_ref)
+    block_ref[...] = low(dot_nn(gnorm, out_ref[...]))
     out_sum[...] += dot_tn(gnorm, cot_ref[...])
     d_gain_two_ref[...] += jnp.sum(d_gnorm * unit, axis=0, keepdims=True)
     d_gated = scale * (d_gnorm * gain_two) - unit * slope
@@ -291,11 +281,11 @@
     def _():
         for number, gate_ref in enumerate(gate_refs):
             columns = gate_ref.shape[1]
-            start = pl.multiple_of(places_ref[1 + number] * columns, columns)
+            start = pl.multiple_of(places_ref[number] * columns, columns)
             gate_ref[...] = low(gate_sum[:, pl.ds(start, columns)])
         for number, grad_ref in enumerate(out_refs):
             columns = grad_ref.shape[1]
-            first = places_ref[1 + gate_count + number]
+            first = places_ref[gate_count + number]
             for step in range(out_sum.shape[0] // HEADDIM // out_count):
                 head = first + step * out_count
                 rows = pl.ds(pl.multiple_of(head * HEADDIM, HEADDIM), HEADDIM)
@@ -448,22 +438,18 @@
 
 
 def pair_kernel(places_ref, *refs):
-    gate, out, block = refs[:4], refs[4:6], refs[6:8]
-    gate_keep_ref, gate_send_ref, block_keep_ref, block_send_ref = refs[8:12]
-    out_refs = refs[12:]
+    gate, out = refs[:4], refs[4:6]
+    gate_keep_ref, gate_send_ref = refs[7:9]
+    out_refs = refs[9:-1]
     paired = sum_of(*gate)
     columns = gate_keep_ref.shape[1]
     even = places_ref[0] == 0
     first, second = low(paired[:, :columns]), low(paired[:, columns:])
     gate_keep_ref[...] = jnp.where(even, first, second)
     gate_send_ref[...] = jnp.where(even, second, first)
-    rows = block_keep_ref.shape[0]
-    for ref, place in ((block_keep_ref, places_ref[1]), (block_send_ref, 1 - places_ref[1])):
-        here = pl.ds(pl.multiple_of(place * rows, rows), rows)
-        ref[...] = low(sum_of(block[0].at[here, :], block[1].at[here, :]))
     for number, ref in enumerate(out_refs):
         rows = ref.shape[0]
-        start = pl.multiple_of(places_ref[2 + number] * rows, rows)
+        start = pl.multiple_of(places_ref[1 + number] * rows, rows)
         here = pl.ds(start, rows)
         ref[...] = low(sum_of(out[0].at[here, :], out[1].at[here, :]))
 
@@ -476,17 +462,18 @@
 
 
 def join_kernel(places_ref, *refs):
-    joined_ref, vec_ref = refs[-2:]
+    joined_ref = refs[-1]
     rows = refs[0].shape[0]
     joined_ref[:rows, :] = low(sum_of(*refs[:2]))
     joined_ref[rows:, :] = low(sum_of(*refs[2:6]))
-    vec_ref[...] = refs[6][...] + refs[7][...]
 
 
 def final_kernel(places_ref, *refs):
-    rest_ref, vec_ref = refs[6:]
-    rest_ref[...] = low(sum_of(*refs[:4]))
-    vec_ref[...] = refs[4][...] + refs[5][...]
+    refs[-2][...] = low(sum_of(*refs[:4]))
+
+
+def vec_kernel(places_ref, *refs):
+    refs[-1][...] = (refs[0][...] + refs[1][...]) + (refs[2][...] + refs[3][...])
 
 
 def normed_kernel(
@@ -496,8 +483,7 @@
     d_rest_ref,
     gate_weight_ref,
     rest_weight_ref,
-    mine_ref,
-    send_ref,
+    d_normed_ref,
     d_gain_one_ref,
 ):
     chunk = pl.program_id(0)
@@ -508,7 +494,7 @@
 
     d_normed = dot_nn(d_gating_ref[...], gate_weight_ref[...])
     d_normed = d_normed + dot_nn(d_rest_ref[...], rest_weight_ref[...])
-    keep_chunk(low(d_normed), chunk % 2 == places_ref[0], chunk // 2, mine_ref, send_ref)
+    d_normed_ref[...] = low(d_normed)
     unit = rms_scale(hidden_ref[...].astype(jnp.float32))
     d_gain_one_ref[...] += jnp.sum(d_normed * unit, axis=0, keepdims=True)
 
@@ -762,14 +748,14 @@
     )
 
 
-def run_middle(parity, gate_places, out_places, scanned, gating, d_gnorm, cot, normed, sums, out, gain):
+def run_middle(gate_places, out_places, scanned, gating, d_gnorm, cot, normed, sums, out, gain):
     length, local_di = scanned.shape
     gate_shape = (local_di, D // len(gate_places))
     out_shape = (local_di, D) if len(out_places) == 1 else (local_di * D // 256, 128)
     shapes = [gate_shape] * len(gate_places) + [out_shape] * len(out_places)
     return call(
         lambda *refs: middle_kernel(len(gate_places), len(out_places), *refs),
-        [parity] + gate_places + out_places,
+        gate_places + out_places,
         [scanned, gating, d_gnorm, cot, normed, *sums, out, gain],
         [
             rows_of(local_di),
@@ -781,16 +767,14 @@
         + [pl.BlockSpec((8, BLOCK), lambda q, *_: (0, q))] * 4
         + [fixed((local_di, D)), fixed((1, local_di))],
         [
-            struct((length // 2, D), jnp.bfloat16),
-            struct((length // 2, D), jnp.bfloat16),
+            struct((length, D), jnp.bfloat16),
             struct((length, local_di), jnp.bfloat16),
             struct((length, local_di), jnp.bfloat16),
             struct((1, local_di)),
         ]
         + [struct(shape, jnp.bfloat16) for shape in shapes],
         [
-            fixed((length // 2, D)),
-            fixed((length // 2, D)),
+            rows_of(D),
             rows_of(local_di),
             rows_of(local_di),
             fixed((1, local_di)),
@@ -863,36 +847,36 @@
     )
 
 
-def run_pair(y, far, out_places, gate, out, block):
+def run_pair(y, out_places, gate, out, through):
     columns = gate[0].shape[1] // 2
     shapes = [
         (gate[0].shape[0], columns),
         (gate[0].shape[0], columns),
-        (block[0].shape[0] // 2, D),
-        (block[0].shape[0] // 2, D),
     ] + [(out[0].shape[0] // len(out_places), out[0].shape[1])] * len(out_places)
-    inputs = [*gate, *out, *block]
+    inputs = [*gate, *out]
+    untouched = pl.BlockSpec(memory_space=pl.ANY)
     return call(
         pair_kernel,
-        [y, far] + out_places,
-        inputs,
-        [fixed(array.shape) for array in inputs],
-        [struct(shape, jnp.bfloat16) for shape in shapes],
-        [fixed(shape) for shape in shapes],
+        [y] + out_places,
+        [*inputs, through],
+        [fixed(array.shape) for array in inputs] + [untouched],
+        [struct(shape, jnp.bfloat16) for shape in shapes] + [struct(through.shape, through.dtype)],
+        [fixed(shape) for shape in shapes] + [untouched],
         [],
         1,
         [],
         (3_000_000, 7_000_000, 0),
         "pair",
-    )
-
-
-def run_normed(parity, hidden, d_gating, d_rest, gate_weight, rest_weight, arrived):
+        [(1 + len(inputs), len(shapes))],
+    )
+
+
+def run_normed(hidden, d_gating, d_rest, gate_weight, rest_weight, arrived):
     length, local_di = d_gating.shape
     rest = d_rest.shape[1]
     return call(
         normed_kernel,
-        [parity],
+        [jnp.int32(0)],
         [hidden, d_gating, d_rest, gate_weight, rest_weight],
         [
             rows_of(D),
@@ -902,11 +886,10 @@
             fixed((rest, D)),
         ],
         [
-            struct((length // 2, D), jnp.bfloat16),
-            struct((length // 2, D), jnp.bfloat16),
+            struct((length, D), jnp.bfloat16),
             struct((1, D)),
         ],
-        [fixed((length // 2, D)), fixed((length // 2, D)), fixed((1, D))],
+        [rows_of(D), fixed((1, D))],
         [],
         length // BLOCK,
         arrived,
@@ -934,16 +917,16 @@
     )
 
 
-def run_join(gate, out, vec, there):
-    inputs = [*gate, *out, *vec]
+def run_join(gate, out, there):
+    inputs = [*gate, *out]
     shape = (gate[0].shape[0] + out[0].shape[0], gate[0].shape[1])
     return call(
         join_kernel,
         [jnp.int32(0)],
         inputs,
         [fixed(array.shape) for array in inputs],
-        [struct(shape, jnp.bfloat16), struct(vec[0].shape)],
-        [fixed(shape), fixed(vec[0].shape)],
+        struct(shape, jnp.bfloat16),
+        fixed(shape),
         [],
         1,
         there,
@@ -952,20 +935,37 @@
     )
 
 
-def run_final(rest, vec, there):
-    inputs = [*rest, *vec]
+def run_final(rest, through, there):
+    untouched = pl.BlockSpec(memory_space=pl.ANY)
     return call(
         final_kernel,
         [jnp.int32(0)],
-        inputs,
-        [fixed(array.shape) for array in inputs],
-        [struct(rest[0].shape, jnp.bfloat16), struct(vec[0].shape)],
-        [fixed(rest[0].shape), fixed(vec[0].shape)],
+        [*rest, through],
+        [fixed(array.shape) for array in rest] + [untouched],
+        [struct(rest[0].shape, jnp.bfloat16), struct(through.shape, through.dtype)],
+        [fixed(rest[0].shape), untouched],
         [],
         1,
         there,
         (500_000, 1_000_000, 0),
         "final",
+        [(1 + len(rest), 1)],
+    )
+
+
+def run_vec(terms):
+    return call(
+        vec_kernel,
+        [jnp.int32(0)],
+        terms,
+        [fixed(array.shape) for array in terms],
+        struct(terms[0].shape),
+        fixed(terms[0].shape),
+        [],
+        1,
+        [],
+        (20_000, 100_000, 0),
+        "vec",
     )
 
 
@@ -1064,6 +1064,20 @@
         if step < count // 2 - 1:
             rows = ring_step(rows)
     return places, blocks
+
+
+def ring_pairs(rows):
+    count = lax.axis_size("wshard")
+    index = lax.axis_index("wshard")
+    places = [(index + count - 2 * step) % count for step in range(count // 2)]
+    blocks = [rows]
+    for _ in range(count // 2 - 1):
+        blocks = blocks + [ring_step(blocks[-1])]
+    swapped = [
+        swap(jnp.concatenate(blocks[first : first + 2], 0), "wshard", 1)
+        for first in range(0, count // 2, 2)
+    ]
+    return places + [place ^ 1 for place in places], blocks + swapped
 
 
 def take_block(values, index, rows):
@@ -1130,13 +1144,11 @@
     channels = local_di + 2 * STATE
     shard_index = lax.axis_index("wshard")
     rings = lax.axis_size("wshard") == 8
-    near = seq_index % 2
-    far = seq_index // 2
     if rings:
         y, z = shard_index % 2, shard_index // 2
         rest_mine, gate_out_mine = run_prepare(seq_index, in_weight.T, out_weight)
         rest = ring_blocks(rest_mine)
-        gate_out = ring_blocks(gate_out_mine)
+        gate_out = ring_pairs(gate_out_mine)
         gate_places = [z ^ mask for mask in range(4)]
         out_places = [y, 1 - y]
     else:
@@ -1189,7 +1201,6 @@
         gate_out, cot_low, normed_low, scanned, my_gain_two
     )
     middle = run_middle(
-        near,
         gate_places,
         out_places,
         scanned,
@@ -1201,10 +1212,10 @@
         out_low,
         my_gain_two,
     )
-    block_mine, block_send, d_gating, d_scanned, d_gain_two = middle[:5]
-    gate_grads = middle[5 : 5 + len(gate_places)]
-    out_grads = middle[5 + len(gate_places) :]
-    block_arrived = swap(block_send, "seq", 1)
+    block_part, d_gating, d_scanned, d_gain_two = middle[:4]
+    gate_grads = middle[4 : 4 + len(gate_places)]
+    out_grads = middle[4 + len(gate_places) :]
+    block_rows = lax.psum_scatter(block_part, "seq", scatter_dimension=0, tiled=True)
     if rings:
         gate_pieces = [swap(gate_grads[mask], "wshard", 2 * mask) for mask in range(1, 4)]
         out_arrived = swap(out_grads[1], "wshard", 1)
@@ -1225,29 +1236,21 @@
     rest_grads = backward[5:]
     before_normed = []
     if rings:
-        rest_arrived = swap(rest_grads[1], "wshard", 1)
-        gate_keep, gate_send, block_keep, block_send, *out_sums = run_pair(
+        gate_keep, gate_send, *out_sums, rest_send = run_pair(
             y,
-            far,
             gate_places,
             [gate_grads[0]] + gate_pieces,
             [out_grads[0], out_arrived],
-            [block_mine, block_arrived],
+            rest_grads[1],
         )
+        rest_arrived = swap(rest_send, "wshard", 1)
         gate_arrived = swap(gate_send, "wshard", 1)
         out_pieces = [swap(out_sums[mask], "wshard", 2 * mask) for mask in range(1, 4)]
         before_normed = [gate_keep]
-    else:
-        block_sum = low(block_mine.astype(jnp.float32) + block_arrived.astype(jnp.float32))
-        block_keep = take_block(block_sum, far, rows_here)
-        block_send = take_block(block_sum, 1 - far, rows_here)
-    block_far = swap(block_send, "seq", 2)
-    normed_mine, normed_send, d_gain_one = run_normed(
-        near, hidden_low, d_gating, d_rest, gate_weight, rest_weight, before_normed
-    )
-    normed_arrived = swap(normed_send, "seq", 1)
-    normed_sum = normed_mine.astype(jnp.float32) + normed_arrived.astype(jnp.float32)
-    normed_far = swap(low(take_block(normed_sum, 1 - far, rows_here)), "seq", 2)
+    d_normed_part, d_gain_one = run_normed(
+        hidden_low, d_gating, d_rest, gate_weight, rest_weight, before_normed
+    )
+    d_normed = lax.psum_scatter(d_normed_part, "seq", scatter_dimension=0, tiled=True)
     shared = jnp.concatenate(
         [d_gain_one[0], d_kernel[:, local_di:].reshape(-1), d_conv_bias[0, local_di:]]
     )
@@ -1263,33 +1266,33 @@
     )
     vec_part = jnp.concatenate([shared, apart])[None]
     if rings:
+        gate_out_part = run_join(
+            [gate_keep, gate_arrived], [out_sums[0]] + out_pieces, [d_gain_one]
+        )
+        gate_out_far = swap(gate_out_part, "seq", 2)
+        gate_out_near = swap(gate_out_part, "seq", 1)
         rest_sums = run_rest_pair(
-            gate_places, rest_grads[0], rest_arrived, [d_gain_one, block_far] + out_pieces
+            gate_places,
+            rest_grads[0],
+            rest_arrived,
+            [gate_out_far, gate_out_near, block_rows],
         )
         rest_pieces = [swap(rest_sums[mask], "wshard", 2 * mask) for mask in range(1, 4)]
-        gate_out_part, vec_part = run_join(
-            [gate_keep, gate_arrived],
-            [out_sums[0]] + out_pieces,
-            [vec_part, swap(vec_part, "wshard", 1)],
-            [rest_sums[0]],
-        )
-        vec_arrived = swap(vec_part, "wshard", 2)
-        spots, gate_out_blocks = seq_blocks(gate_out_part)
+        spots = [seq_index ^ mask for mask in range(4)]
+        gate_out_blocks = [
+            gate_out_part, gate_out_near, gate_out_far, swap(gate_out_far, "seq", 1)
+        ]
         in_arrays = (in_weight.T, in_first.T, in_second.T)
         updated = run_update_gate(
-            spots,
-            gate_out_blocks,
-            in_arrays,
-            (out_weight, out_first, out_second),
-            [vec_arrived],
+            spots, gate_out_blocks, in_arrays, (out_weight, out_first, out_second), []
         )
         out_first_new, out_second_new, out_weight_new = updated[3:]
-        vec_part = vec_part + vec_arrived
+        vec_part = vec_part + swap(vec_part, "wshard", 1)
         rest_part, vec_part = run_final(
-            [rest_sums[0]] + rest_pieces,
-            [vec_part, swap(vec_part, "wshard", 4)],
-            [out_first_new],
+            [rest_sums[0]] + rest_pieces, vec_part, [out_first_new]
         )
+        vec_pieces = [swap(vec_part, "wshard", 2 * mask) for mask in range(1, 4)]
+        vec_part = run_vec([vec_part] + vec_pieces)
         vec_places, vec_blocks = seq_blocks(vec_part)
         every = jnp.zeros((groups, vec_part.shape[1]), jnp.float32)
         for spot, block in zip(vec_places, vec_blocks):
@@ -1297,9 +1300,8 @@
     else:
         vec_part = lax.psum(vec_part, "wshard")
         every = lax.all_gather(vec_part, "seq", axis=0, tiled=True)
-    block_here = block_keep.astype(jnp.float32) + block_far.astype(jnp.float32)
-    block_out = hidden_rows.astype(jnp.float32) + block_here
-    d_normed = take_block(normed_sum, far, rows_here) + normed_far.astype(jnp.float32)
+    block_out = hidden_rows.astype(jnp.float32) + block_rows.astype(jnp.float32)
+    d_normed = d_normed.astype(jnp.float32)
     own_hidden = hidden_rows.astype(jnp.float32)
     own_scale = lax.rsqrt(jnp.mean(own_hidden * own_hidden, axis=-1, keepdims=True) + norm_eps)
     own_unit = own_hidden * own_scale

time: 265 us -> 273 us (1.030)
  waiting for transfers between devices: 64.8 us -> 80.2 us
  starting transfers between devices: 46.2 us -> 40 us
    ppermute x39 -> x34, waiting for transfers between devices: 44.4 us -> 55.9 us  [swap(): return lax.ppermute(values, axis, route)]
    ppermute x39 -> x34, starting transfers between devices: 41.1 us -> 34 us  [swap(): return lax.ppermute(values, axis, route)]
    ppermute x6, waiting for transfers between devices: 19 us -> 22.8 us  [ring_step(): lax.ppermute(held, 'wshard', [(i, (i + 2) % count) for i in range(count)])]
    pallas_call x12 -> x13, Pallas kernels: 108 us -> 106 us  [call(): pl.pallas_call(after(kernel, 1 + len(inputs), len(arrived)), grid_spec=pl...]
  transfers between devices with their start and end apart: 47 -> 44, of which waited for: 15 -> 14; matrix products, arithmetic and copies ran while one was open for 8% -> 8% of each run, Pallas kernels for 32% -> 28%
where the time goes in v8:
time: 273 us; the launch traced here: 272 us
  Pallas kernels  106 us (39%)
  waiting for transfers between devices  80.2 us (29%)
  starting transfers between devices  40 us (15%)
  local copies, waits for them, and re-layouts  20.1 us (7%)
  between operations  14.5 us (5%)
  other arithmetic  10.7 us (4%)
    pallas_call x13, Pallas kernels, call(): pl.pallas_call(after(kernel, 1 + len(inputs), len(arrived)), grid_spec=pl...  106 us
    ppermute x34, waiting for transfers between devices, swap(): return lax.ppermute(values, axis, route)  55.9 us
    ppermute x34, starting transfers between devices, swap(): return lax.ppermute(values, axis, route)  34 us
    ppermute x6, waiting for transfers between devices, ring_step(): lax.ppermute(held, 'wshard', [(i, (i + 2) % count) for i in range(count)])  22.8 us
    unnamed x108, local copies, waits for them, and re-layouts  8.54 us
    ppermute x6, starting transfers between devices, ring_step(): lax.ppermute(held, 'wshard', [(i, (i + 2) % count) for i in range(count)])  5.89 us
  transfers between devices with their start and end apart: 44, of which 14 were waited for; matrix products, arithmetic and copies ran while one was open for 8% of the time, Pallas kernels for 28%

profile of v8, /device:TPU:0, one launch (start us, length us, event | category | flops | bytes accessed | tf_op | source)
XLA Modules:
  0.0 271.7 jit_solution(11237256687009783451)
XLA Ops:
  8.7 2.7 prepare.1
  11.5 3.0 %collective-permute-start.1 = (bf16[784,128]{1,0:T(8,128)(2,1)}, bf16[784,128]{1,0:T(8,128)(2,1)S(1)}, u32[]{:S(2)}, u32[]{:S(2)}) collective-permute-start(bf16[784,128]{1,0:T(8,128)(2,1)} %get-tuple-element.67.refs_1_), channel_id=1, source_target_pairs={{0,2},{1,3},{2,4},{3,5},{4,6},{5,7},{6,0},{7,1},{8,10},{9,11},{10,... | collective-permute-start | bytes 602120 | tf_op jit(solution)/shard_map/ppermute | solution.py:1053
  16.0 1.6 collective-permute-start.7
  18.6 8.8 %collective-permute-done.7.refs_2_ = bf16[1024,128]{1,0:T(8,128)(2,1)S(1)} collective-permute-done((bf16[1024,128]{1,0:T(8,128)(2,1)}, bf16[1024,128]{1,0:T(8,128)(2,1)S(1)}, u32[]{:S(2)}, u32[]{:S(2)}) %collective-permute-start.7) | collective-permute-done | bytes 262176 | tf_op jit(solution)/shard_map/ppermute | solution.py:1053
  30.5 7.9 %collective-permute-done.8.refs_3_ = bf16[1024,128]{1,0:T(8,128)(2,1)S(1)} collective-permute-done((bf16[1024,128]{1,0:T(8,128)(2,1)S(1)}, bf16[1024,128]{1,0:T(8,128)(2,1)S(1)}, u32[]{:S(2)}, u32[]{:S(2)}) %collective-permute-start.8) | collective-permute-done | bytes 262176 | tf_op jit(solution)/shard_map/ppermute | solution.py:1053
  46.3 6.1 %collective-permute-done.5.refs_7_ = bf16[784,128]{1,0:T(8,128)(2,1)S(1)} collective-permute-done((bf16[784,128]{1,0:T(8,128)(2,1)}, bf16[784,128]{1,0:T(8,128)(2,1)S(1)}, u32[]{:S(2)}, u32[]{:S(2)}) %collective-permute-start.5) | collective-permute-done | bytes 200736 | tf_op jit(solution)/shard_map/ppermute | solution.py:1053
  55.8 10.9 %collective-permute-done.4.refs_6_ = bf16[784,128]{1,0:T(8,128)(2,1)S(1)} collective-permute-done((bf16[784,128]{1,0:T(8,128)(2,1)}, bf16[784,128]{1,0:T(8,128)(2,1)S(1)}, u32[]{:S(2)}, u32[]{:S(2)}) %collective-permute-start.4) | collective-permute-done | bytes 200736 | tf_op jit(solution)/shard_map/ppermute | solution.py:1041
  67.3 3.7 %collective-permute-done.6.refs_8_ = bf16[784,128]{1,0:T(8,128)(2,1)} collective-permute-done((bf16[784,128]{1,0:T(8,128)(2,1)S(1)}, bf16[784,128]{1,0:T(8,128)(2,1)}, u32[]{:S(2)}, u32[]{:S(2)}) %collective-permute-start.6) | collective-permute-done | bytes 200736 | tf_op jit(solution)/shard_map/ppermute | solution.py:1041
  71.0 15.6 %forward.1 = (bf16[896,1024]{1,0:T(8,128)(2,1)}, bf16[1024,1024]{1,0:T(8,128)(2,1)}, f32[1024,768]{1,0:T(8,128)}, f32[1024,768]{1,0:T(8,128)}, f32[1024,128]{1,0...) custom-call(s32[8]{0:T(128)} %stack.115.refs_0_, ...), custom_call_target="tpu_custom_call" | custom-call | flops 6000000000 | bytes 30000000 | tf_op jit(solution)/shard_map/forward/pallas_call | solution.py:635
  87.7 11.2 %gate.1 = (bf16[512,1024]{1,0:T(8,128)(2,1)}, bf16[512,1024]{1,0:T(8,128)(2,1)}, f32[1024,512]{1,0:T(8,128)}, f32[1024,512]{1,0:T(8,128)}, f32[8,1024]{1,0:T(8,128)}) custom-call(s32[8]{0:T(128)} %stack.117.refs_0_, bf16[1024,128]{1,0:T(8,128)(2,1)} %get-tuple-element.69.refs_1_, bf16[1024,128]{1,0:T(8,128)(2,1)} %copy-done.12, ...), custom_call_target="tpu_custom_call" | custom-call | flops 2500000000 | bytes 12000000 | tf_op jit(solution)/shard_map/gate/pallas_call | solution.py:635
  101.3 1.7 collective-permute-done.13.refs_8_
  104.6 11.6 %middle.1 = (bf16[1024,1024]{1,0:T(8,128)(2,1)}, bf16[1024,512]{1,0:T(8,128)(2,1)}, bf16[1024,512]{1,0:T(8,128)(2,1)}, f32[1,512]{1,0:T(1,128)}, bf16[512,256]{1...) custom-call(s32[6]{0:T(128)} %stack.106.refs_0_, ...), custom_call_target="tpu_custom_call" | custom-call | flops 4000000000 | bytes 15000000 | tf_op jit(solution)/shard_map/middle/pallas_call | solution.py:635
  119.1 4.3 %collective-permute-start.16 = (bf16[512,256]{1,0:T(8,128)(2,1)}, bf16[512,256]{1,0:T(8,128)(2,1)S(1)}, u32[]{:S(2)}, u32[]{:S(2)}) collective-permute-start(bf16[512,256]{1,0:T(8,128)(2,1)} %get-tuple-element.88), channel_id=1, source_target_pairs={{0,4},{1,5},{2,6},{3,7},{4,0},{5,1},{6,2},{7,3},{8,12},{9,13},{10,... | collective-permute-start | bytes 786440 | tf_op jit(solution)/shard_map/ppermute | solution.py:1041
  123.5 31.3 %backward.1 = (bf16[1024,896]{1,0:T(8,128)(2,1)}, f32[4,768]{1,0:T(4,128)}, f32[1,768]{1,0:T(1,128)}, f32[1,512]{1,0:T(1,128)}, f32[2,128]{1,0:T(2,128)}, /*inde...) custom-call(s32[2]{0:T(128)} %pad_add_fusion.refs_0_, bf16[1024,1024]{1,0:T(8,128)(2,1)} %get-tuple-element.70.refs_8_.refs_5_.refs_1_, ...), custom_call_target="tpu_custom_call" | custom-call | flops 14000000000 | bytes 40000000 | tf_op jit(solution)/shard_map/backward/pallas_call | solution.py:635
  155.8 3.2 %pair.1 = (bf16[512,128]{1,0:T(8,128)(2,1)}, bf16[512,128]{1,0:T(8,128)(2,1)}, bf16[512,128]{1,0:T(8,128)(2,1)}, bf16[512,128]{1,0:T(8,128)(2,1)}, bf16[512,128]...) custom-call(s32[5]{0:T(128)} %stack.119.refs_0_, ...), custom_call_target="tpu_custom_call", output_to_operand_aliasing={{6}: (7, {})} | custom-call | flops 3000000 | bytes 7000000 | tf_op jit(solution)/shard_map/pair/pallas_call | solution.py:635
  159.1 7.7 %normed.1 = (bf16[1024,1024]{1,0:T(8,128)(2,1)}, f32[1,1024]{1,0:T(1,128)}) custom-call(s32[1]{0:T(128)} %constant.130.clone.1.refs_0_, bf16[1024,1024]{1,0:T(8,128)(2,1)} %bitcast.103, bf16[1024,512]{1,0:T(8,128)(2,1)} %get-tuple-element.76.refs_2_, bf16[1024,896]{1,0:T(8,128)(2,1)} %get-tuple-element.83.refs_3_, ...), custom_call_target="tpu_custom_call" | custom-call | flops 3000000000 | bytes 9000000 | tf_op jit(solution)/shard_map/normed/pallas_call | solution.py:635
  170.3 3.7 %collective-permute-start.22 = (bf16[512,128]{1,0:T(8,128)(2,1)S(1)}, bf16[512,128]{1,0:T(8,128)(2,1)S(1)}, u32[]{:S(2)}, u32[]{:S(2)}) collective-permute-start(bf16[512,128]{1,0:T(8,128)(2,1)S(1)} %copy-done.45), channel_id=1, source_target_pairs={{0,4},{1,5},{2,6},{3,7},{4,0},{5,1},{6,2},{7,3},{8,12},{9,13},{10,... | collective-permute-start | bytes 393224 | tf_op jit(solution)/shard_map/ppermute | solution.py:1041
  174.1 14.9 %collective-permute-done.20.refs_2_ = bf16[512,128]{1,0:T(8,128)(2,1)S(1)} collective-permute-done((bf16[512,128]{1,0:T(8,128)(2,1)S(1)}, bf16[512,128]{1,0:T(8,128)(2,1)S(1)}, u32[]{:S(2)}, u32[]{:S(2)}) %collective-permute-start.20) | collective-permute-done | bytes 131104 | tf_op jit(solution)/shard_map/ppermute | solution.py:1041
  189.8 2.0 join.1.refs_1_
  195.3 7.6 %collective-permute-done.24.refs_3_ = bf16[1024,128]{1,0:T(8,128)(2,1)S(1)} collective-permute-done((bf16[1024,128]{1,0:T(8,128)(2,1)}, bf16[1024,128]{1,0:T(8,128)(2,1)S(1)}, u32[]{:S(2)}, u32[]{:S(2)}) %collective-permute-start.24) | collective-permute-done | bytes 262176 | tf_op jit(solution)/shard_map/ppermute | solution.py:1041
  204.0 3.1 %rest_pair.1 = (bf16[784,128]{1,0:T(8,128)(2,1)}, bf16[784,128]{1,0:T(8,128)(2,1)}, bf16[784,128]{1,0:T(8,128)(2,1)}, bf16[784,128]{1,0:T(8,128)(2,1)}) custom-call(s32[4]{0:T(128)} %pad_add_fusion.2.refs_0_, bf16[3136,128]{1,0:T(8,128)(2,1)} %get-tuple-element.95.refs_1_, bf16[3136,128]{1,0:T(8,128)(2,1)} %copy-done.5, bf16[1024,128]{1,0:T(8,128)(2,1)} %copy-done.3, ...), custom_call_target="tpu_custom_call" | custom-call | flops 2000000 | bytes 3000000 | tf_op jit(solution)/shard_map/rest_pair/pallas_call | solution.py:635
  208.5 2.4 collective-permute-start.27
  212.7 7.5 %update_gate.1 = (f32[4384,128]{1,0:T(8,128)}, f32[4384,128]{1,0:T(8,128)}, f32[4384,128]{1,0:T(8,128)}, f32[256,1024]{1,0:T(8,128)}, f32[256,1024]{1,0:T(8,128)}, /*index=5*/f32[256,1024]{1,0:T(8,128)}) custom-call(s32[4]{0:T(128)} %pad_add_fusion.1.refs_0_, bf16[1024,128]{1,0:T(8,128)(2,1)} %join.1.refs_1_, bf16[1024,128]{1,0:T(8,128)(2,1)} %copy-done.4, ...), custom_call_target="tpu_custom_call" | custom-call | flops 10000000 | bytes 13000000 | tf_op jit(solution)/shard_map/update_gate/pallas_call | solution.py:635
  220.3 5.8 %collective-permute-done.27.refs_3_ = bf16[784,128]{1,0:T(8,128)(2,1)S(1)} collective-permute-done((bf16[784,128]{1,0:T(8,128)(2,1)}, bf16[784,128]{1,0:T(8,128)(2,1)S(1)}, u32[]{:S(2)}, u32[]{:S(2)}) %collective-permute-start.27) | collective-permute-done | bytes 200736 | tf_op jit(solution)/shard_map/ppermute | solution.py:1041
  226.8 2.1 final.1
  228.9 4.0 %collective-permute-start.34 = (f32[1,5400]{1,0:T(1,128)}, f32[1,5400]{1,0:T(1,128)S(1)}, u32[]{:S(2)}, u32[]{:S(2)}) collective-permute-start(f32[1,5400]{1,0:T(1,128)} %get-tuple-element.122.refs_1_), channel_id=1, source_target_pairs={{0,2},{1,3},{2,0},{3,1},{4,6},{5,7},{6,4},{7,5},{8,10},{9,11},{10,... | collective-permute-start | bytes 64808 | tf_op jit(solution)/shard_map/ppermute | solution.py:1041
  235.3 2.7 collective-permute-done.35.refs_3_
  238.0 1.7 collective-permute-done.36.refs_4_
  242.5 3.2 %collective-permute-done.38 = f32[1,5400]{1,0:T(1,128)S(1)} collective-permute-done((f32[1,5400]{1,0:T(1,128)}, f32[1,5400]{1,0:T(1,128)S(1)}, u32[]{:S(2)}, u32[]{:S(2)}) %collective-permute-start.38) | collective-permute-done | bytes 21632 | tf_op jit(solution)/shard_map/ppermute | solution.py:1041
  250.7 2.6 collective-permute-done.32.refs_3_
  254.8 2.8 %fusion.6 = (f32[1,256,1024]{2,1,0:T(8,128)}, f32[1,256,1024]{2,1,0:T(8,128)}) fusion(bf16[256,1024]{1,0:T(8,128)(2,1)} %reduce-scatter.5.cloned.1.call-done, bf16[1,256,1024]{2,1,0:T(8,128)(2,1)S(1)} %copy-done.1, bf16[1,256,1024]{2,1,0:T(8,128)(2,1)S(1)} %copy-done, f32[256]{0:T(256)S(1)} %broadcast_multiply_fusion, f32[1024]{0:T(1024)S(1)} %copy-done.28, ...), kind=kLoop, calls=%fused_computation.9 | loop fusion | flops 2883584 | bytes 4200448 | tf_op jit(solution)/shard_map/reshape | solution.py:1370
  258.4 6.8 %update_rest.1 = (f32[4384,128]{1,0:T(8,128)}, f32[4384,128]{1,0:T(8,128)}, f32[4384,128]{1,0:T(8,128)}) custom-call(s32[4]{0:T(128)} %pad_add_fusion.1.refs_0_, bf16[784,128]{1,0:T(8,128)(2,1)} %get-tuple-element.113.refs_1_, bf16[784,128]{1,0:T(8,128)(2,1)} %copy-done.17, ...), custom_call_target="tpu_custom_call", output_to_operand_aliasing={{0}: (8, {}), {1}: (9, {}), {2}: (10, {})} | custom-call | flops 10000000 | bytes 8000000 | tf_op jit(solution)/shard_map/update_rest/pallas_call | solution.py:635
  (269 shorter events, 52.8 us)
Async XLA Ops:
  7.2 63.8 %all-gather.5.cloned.1.call-start = ((), (), s32[]{:S(2)}) async-start(), calls=%async_computation.4 | async-start | bytes 2621440 | tf_op jit(solution)/shard_map/all_gather | solution.py:1171
  7.9 78.8 %all-gather.7.cloned.1.call-start = ((), (), s32[]{:S(2)}) async-start(), calls=%async_computation.5 | async-start | bytes 2621440 | tf_op jit(solution)/shard_map/all_gather | solution.py:1172
  8.7 194.3 %reduce-scatter.3.cloned.1.call-start = ((), (), s32[]{:S(2)}) async-start(), calls=%async_computation.2 | async-start | bytes 2621440 | tf_op jit(solution)/shard_map/reduce_scatter | solution.py:1218
  11.5 17.2 %collective-permute-start.1 = (bf16[784,128]{1,0:T(8,128)(2,1)}, bf16[784,128]{1,0:T(8,128)(2,1)S(1)}, u32[]{:S(2)}, u32[]{:S(2)}) collective-permute-start(bf16[784,128]{1,0:T(8,128)(2,1)} %get-tuple-element.67.refs_1_), channel_id=1, source_target_pairs={{0,2},{1,3},{2,4},{3,5},{4,6},{5,7},{6,0},{7,1},{8,10},{9,11},{10,... | collective-permute-start | bytes 602120 | tf_op jit(solution)/shard_map/ppermute | solution.py:1053
  14.5 40.0 %collective-permute-start = (bf16[784,128]{1,0:T(8,128)(2,1)}, bf16[784,128]{1,0:T(8,128)(2,1)S(1)}, u32[]{:S(2)}, u32[]{:S(2)}) collective-permute-start(bf16[784,128]{1,0:T(8,128)(2,1)} %get-tuple-element.67.refs_1_), channel_id=1, source_target_pairs={{0,1},{1,0},{2,3},{3,2},{4,5},{5,4},{6,7},{7,6},{8,9},{9,8},{10,11... | collective-permute-start | bytes 602120 | tf_op jit(solution)/shard_map/ppermute | solution.py:1041
  16.0 11.3 %collective-permute-start.7 = (bf16[1024,128]{1,0:T(8,128)(2,1)}, bf16[1024,128]{1,0:T(8,128)(2,1)S(1)}, u32[]{:S(2)}, u32[]{:S(2)}) collective-permute-start(bf16[1024,128]{1,0:T(8,128)(2,1)} %get-tuple-element.69.refs_1_), channel_id=1, source_target_pairs={{0,2},{1,3},{2,4},{3,5},{4,6},{5,7},{6,0},{7,1},{8,10},{9,11},{10,... | collective-permute-start | bytes 786440 | tf_op jit(solution)/shard_map/ppermute | solution.py:1053
  27.3 11.0 %collective-permute-start.8 = (bf16[1024,128]{1,0:T(8,128)(2,1)S(1)}, bf16[1024,128]{1,0:T(8,128)(2,1)S(1)}, u32[]{:S(2)}, u32[]{:S(2)}) collective-permute-start(bf16[1024,128]{1,0:T(8,128)(2,1)S(1)} %collective-permute-done.7.refs_2_), channel_id=1, source_target_pairs={{0,2},{1,3},{2,4},{3,5},{4,6},{5,7},{6,0},{7,1},{8,10},{9,11},{10,... | collective-permute-start | bytes 786440 | tf_op jit(solution)/shard_map/ppermute | solution.py:1053
  28.6 16.0 %collective-permute-start.3 = (bf16[784,128]{1,0:T(8,128)(2,1)S(1)}, bf16[784,128]{1,0:T(8,128)(2,1)}, u32[]{:S(2)}, u32[]{:S(2)}) collective-permute-start(bf16[784,128]{1,0:T(8,128)(2,1)S(1)} %collective-permute-done.1.refs_3_), channel_id=1, source_target_pairs={{0,2},{1,3},{2,4},{3,5},{4,6},{5,7},{6,0},{7,1},{8,10},{9,11},{10,... | collective-permute-start | bytes 602120 | tf_op jit(solution)/shard_map/ppermute | solution.py:1053
  38.4 14.5 %collective-permute-start.9 = (bf16[1024,128]{1,0:T(8,128)(2,1)S(1)}, bf16[1024,128]{1,0:T(8,128)(2,1)S(1)}, u32[]{:S(2)}, u32[]{:S(2)}) collective-permute-start(bf16[1024,128]{1,0:T(8,128)(2,1)S(1)} %collective-permute-done.8.refs_3_), channel_id=1, source_target_pairs={{0,2},{1,3},{2,4},{3,5},{4,6},{5,7},{6,0},{7,1},{8,10},{9,11},{10,... | collective-permute-start | bytes 786440 | tf_op jit(solution)/shard_map/ppermute | solution.py:1053
  43.2 11.9 %collective-permute-start.2 = (bf16[784,128]{1,0:T(8,128)(2,1)S(1)}, bf16[784,128]{1,0:T(8,128)(2,1)S(1)}, u32[]{:S(2)}, u32[]{:S(2)}) collective-permute-start(bf16[784,128]{1,0:T(8,128)(2,1)S(1)} %collective-permute-done.1.refs_3_), channel_id=1, source_target_pairs={{0,1},{1,0},{2,3},{3,2},{4,5},{5,4},{6,7},{7,6},{8,9},{9,8},{10,11... | collective-permute-start | bytes 602120 | tf_op jit(solution)/shard_map/ppermute | solution.py:1041
  45.7 41.0 %collective-permute-start.10 = (bf16[2048,128]{1,0:T(8,128)(2,1)S(1)}, bf16[2048,128]{1,0:T(8,128)(2,1)S(1)}, u32[]{:S(2)}, u32[]{:S(2)}) collective-permute-start(bf16[2048,128]{1,0:T(8,128)(2,1)S(1)} %pad_maximum_fusion), channel_id=1, source_target_pairs={{0,1},{1,0},{2,3},{3,2},{4,5},{5,4},{6,7},{7,6},{8,9},{9,8},{10,11... | collective-permute-start | bytes 1572872 | tf_op jit(solution)/shard_map/ppermute | solution.py:1041
  52.4 14.2 %collective-permute-start.4 = (bf16[784,128]{1,0:T(8,128)(2,1)}, bf16[784,128]{1,0:T(8,128)(2,1)S(1)}, u32[]{:S(2)}, u32[]{:S(2)}) collective-permute-start(bf16[784,128]{1,0:T(8,128)(2,1)} %collective-permute-done.3.refs_5_), channel_id=1, source_target_pairs={{0,1},{1,0},{2,3},{3,2},{4,5},{5,4},{6,7},{7,6},{8,9},{9,8},{10,11... | collective-permute-start | bytes 602120 | tf_op jit(solution)/shard_map/ppermute | solution.py:1041
  52.9 18.1 %collective-permute-start.6 = (bf16[784,128]{1,0:T(8,128)(2,1)S(1)}, bf16[784,128]{1,0:T(8,128)(2,1)}, u32[]{:S(2)}, u32[]{:S(2)}) collective-permute-start(bf16[784,128]{1,0:T(8,128)(2,1)S(1)} %collective-permute-done.5.refs_7_), channel_id=1, source_target_pairs={{0,1},{1,0},{2,3},{3,2},{4,5},{5,4},{6,7},{7,6},{8,9},{9,8},{10,11... | collective-permute-start | bytes 602120 | tf_op jit(solution)/shard_map/ppermute | solution.py:1041
  54.5 32.2 %collective-permute-start.11 = (bf16[2048,128]{1,0:T(8,128)(2,1)S(1)}, bf16[2048,128]{1,0:T(8,128)(2,1)S(1)}, u32[]{:S(2)}, u32[]{:S(2)}) collective-permute-start(bf16[2048,128]{1,0:T(8,128)(2,1)S(1)} %pad_maximum_fusion.1), channel_id=1, source_target_pairs={{0,1},{1,0},{2,3},{3,2},{4,5},{5,4},{6,7},{7,6},{8,9},{9,8},{10,11... | collective-permute-start | bytes 1572872 | tf_op jit(solution)/shard_map/ppermute | solution.py:1041
  116.3 137.1 %reduce-scatter.5.cloned.1.call-start = ((), (), s32[]{:S(2)}) async-start(), calls=%async_computation.3 | async-start | bytes 2621440 | tf_op jit(solution)/shard_map/reduce_scatter | solution.py:1253
  117.6 37.3 %collective-permute-start.18 = (bf16[2048,128]{1,0:T(8,128)(2,1)}, bf16[2048,128]{1,0:T(8,128)(2,1)S(1)}, u32[]{:S(2)}, u32[]{:S(2)}) collective-permute-start(bf16[2048,128]{1,0:T(8,128)(2,1)} %get-tuple-element.91), channel_id=1, source_target_pairs={{0,1},{1,0},{2,3},{3,2},{4,5},{5,4},{6,7},{7,6},{8,9},{9,8},{10,11... | collective-permute-start | bytes 1572872 | tf_op jit(solution)/shard_map/ppermute | solution.py:1041
  119.1 35.7 %collective-permute-start.15 = (bf16[512,256]{1,0:T(8,128)(2,1)}, bf16[512,256]{1,0:T(8,128)(2,1)S(1)}, u32[]{:S(2)}, u32[]{:S(2)}) collective-permute-start(bf16[512,256]{1,0:T(8,128)(2,1)} %get-tuple-element.87), channel_id=1, source_target_pairs={{0,2},{1,3},{2,0},{3,1},{4,6},{5,7},{6,4},{7,5},{8,10},{9,11},{10,... | collective-permute-start | bytes 786440 | tf_op jit(solution)/shard_map/ppermute | solution.py:1041
  119.1 35.7 %collective-permute-start.16 = (bf16[512,256]{1,0:T(8,128)(2,1)}, bf16[512,256]{1,0:T(8,128)(2,1)S(1)}, u32[]{:S(2)}, u32[]{:S(2)}) collective-permute-start(bf16[512,256]{1,0:T(8,128)(2,1)} %get-tuple-element.88), channel_id=1, source_target_pairs={{0,4},{1,5},{2,6},{3,7},{4,0},{5,1},{6,2},{7,3},{8,12},{9,13},{10,... | collective-permute-start | bytes 786440 | tf_op jit(solution)/shard_map/ppermute | solution.py:1041
  123.4 31.4 %collective-permute-start.17 = (bf16[512,256]{1,0:T(8,128)(2,1)}, bf16[512,256]{1,0:T(8,128)(2,1)S(1)}, u32[]{:S(2)}, u32[]{:S(2)}) collective-permute-start(bf16[512,256]{1,0:T(8,128)(2,1)} %get-tuple-element.89), channel_id=1, source_target_pairs={{0,6},{1,7},{2,4},{3,5},{4,2},{5,3},{6,0},{7,1},{8,14},{9,15},{10,... | collective-permute-start | bytes 786440 | tf_op jit(solution)/shard_map/ppermute | solution.py:1041
  166.9 36.0 %collective-permute-start.19 = (bf16[3136,128]{1,0:T(8,128)(2,1)S(1)}, bf16[3136,128]{1,0:T(8,128)(2,1)S(1)}, u32[]{:S(2)}, u32[]{:S(2)}) collective-permute-start(bf16[3136,128]{1,0:T(8,128)(2,1)S(1)} %copy-done.6), channel_id=1, source_target_pairs={{0,1},{1,0},{2,3},{3,2},{4,5},{5,4},{6,7},{7,6},{8,9},{9,8},{10,11... | collective-permute-start | bytes 2408456 | tf_op jit(solution)/shard_map/ppermute | solution.py:1041
  168.2 20.8 %collective-permute-start.20 = (bf16[512,128]{1,0:T(8,128)(2,1)S(1)}, bf16[512,128]{1,0:T(8,128)(2,1)S(1)}, u32[]{:S(2)}, u32[]{:S(2)}) collective-permute-start(bf16[512,128]{1,0:T(8,128)(2,1)S(1)} %copy-done.47), channel_id=1, source_target_pairs={{0,1},{1,0},{2,3},{3,2},{4,5},{5,4},{6,7},{7,6},{8,9},{9,8},{10,11... | collective-permute-start | bytes 393224 | tf_op jit(solution)/shard_map/ppermute | solution.py:1041
  169.7 19.4 %collective-permute-start.21 = (bf16[512,128]{1,0:T(8,128)(2,1)S(1)}, bf16[512,128]{1,0:T(8,128)(2,1)S(1)}, u32[]{:S(2)}, u32[]{:S(2)}) collective-permute-start(bf16[512,128]{1,0:T(8,128)(2,1)S(1)} %copy-done.46), channel_id=1, source_target_pairs={{0,2},{1,3},{2,0},{3,1},{4,6},{5,7},{6,4},{7,5},{8,10},{9,11},{10,... | collective-permute-start | bytes 393224 | tf_op jit(solution)/shard_map/ppermute | solution.py:1041
  170.3 18.7 %collective-permute-start.22 = (bf16[512,128]{1,0:T(8,128)(2,1)S(1)}, bf16[512,128]{1,0:T(8,128)(2,1)S(1)}, u32[]{:S(2)}, u32[]{:S(2)}) collective-permute-start(bf16[512,128]{1,0:T(8,128)(2,1)S(1)} %copy-done.45), channel_id=1, source_target_pairs={{0,4},{1,5},{2,6},{3,7},{4,0},{5,1},{6,2},{7,3},{8,12},{9,13},{10,... | collective-permute-start | bytes 393224 | tf_op jit(solution)/shard_map/ppermute | solution.py:1041
  174.0 15.1 %collective-permute-start.23 = (bf16[512,128]{1,0:T(8,128)(2,1)S(1)}, bf16[512,128]{1,0:T(8,128)(2,1)S(1)}, u32[]{:S(2)}, u32[]{:S(2)}) collective-permute-start(bf16[512,128]{1,0:T(8,128)(2,1)S(1)} %copy-done.44), channel_id=1, source_target_pairs={{0,6},{1,7},{2,4},{3,5},{4,2},{5,3},{6,0},{7,1},{8,14},{9,15},{10,... | collective-permute-start | bytes 393224 | tf_op jit(solution)/shard_map/ppermute | solution.py:1041
  191.8 11.1 %collective-permute-start.24 = (bf16[1024,128]{1,0:T(8,128)(2,1)}, bf16[1024,128]{1,0:T(8,128)(2,1)S(1)}, u32[]{:S(2)}, u32[]{:S(2)}) collective-permute-start(bf16[1024,128]{1,0:T(8,128)(2,1)} %join.1.refs_1_), channel_id=1, source_target_pairs={{0,16},{8,24},{16,0},{24,8},{1,17},{9,25},{17,1},{25,9},{2,18},{10... | collective-permute-start | bytes 786440 | tf_op jit(solution)/shard_map/ppermute | solution.py:1041
  192.3 10.6 %collective-permute-start.25 = (bf16[1024,128]{1,0:T(8,128)(2,1)}, bf16[1024,128]{1,0:T(8,128)(2,1)S(1)}, u32[]{:S(2)}, u32[]{:S(2)}) collective-permute-start(bf16[1024,128]{1,0:T(8,128)(2,1)} %join.1.refs_1_), channel_id=1, source_target_pairs={{0,8},{8,0},{16,24},{24,16},{1,9},{9,1},{17,25},{25,17},{2,10},{10... | collective-permute-start | bytes 786440 | tf_op jit(solution)/shard_map/ppermute | solution.py:1041
  193.9 17.5 %collective-permute-start.29 = (f32[1,5400]{1,0:T(1,128)S(1)}, f32[1,5400]{1,0:T(1,128)S(1)}, u32[]{:S(2)}, u32[]{:S(2)}) collective-permute-start(f32[1,5400]{1,0:T(1,128)S(1)} %broadcast_in_dim.31), channel_id=1, source_target_pairs={{0,1},{1,0},{2,3},{3,2},{4,5},{5,4},{6,7},{7,6},{8,9},{9,8},{10,11... | collective-permute-start | bytes 64808 | tf_op jit(solution)/shard_map/ppermute | solution.py:1041
  202.9 9.1 %collective-permute-start.30 = (bf16[1024,128]{1,0:T(8,128)(2,1)S(1)}, bf16[1024,128]{1,0:T(8,128)(2,1)S(1)}, u32[]{:S(2)}, u32[]{:S(2)}) collective-permute-start(bf16[1024,128]{1,0:T(8,128)(2,1)S(1)} %collective-permute-done.24.refs_3_), channel_id=1, source_target_pairs={{0,8},{8,0},{16,24},{24,16},{1,9},{9,1},{17,25},{25,17},{2,10},{10... | collective-permute-start | bytes 786440 | tf_op jit(solution)/shard_map/ppermute | solution.py:1041
  207.0 13.2 %collective-permute-start.26 = (bf16[784,128]{1,0:T(8,128)(2,1)}, bf16[784,128]{1,0:T(8,128)(2,1)S(1)}, u32[]{:S(2)}, u32[]{:S(2)}) collective-permute-start(bf16[784,128]{1,0:T(8,128)(2,1)} %get-tuple-element.104), channel_id=1, source_target_pairs={{0,2},{1,3},{2,0},{3,1},{4,6},{5,7},{6,4},{7,5},{8,10},{9,11},{10,... | collective-permute-start | bytes 602120 | tf_op jit(solution)/shard_map/ppermute | solution.py:1041
  208.5 17.6 %collective-permute-start.27 = (bf16[784,128]{1,0:T(8,128)(2,1)}, bf16[784,128]{1,0:T(8,128)(2,1)S(1)}, u32[]{:S(2)}, u32[]{:S(2)}) collective-permute-start(bf16[784,128]{1,0:T(8,128)(2,1)} %get-tuple-element.105), channel_id=1, source_target_pairs={{0,4},{1,5},{2,6},{3,7},{4,0},{5,1},{6,2},{7,3},{8,12},{9,13},{10,... | collective-permute-start | bytes 602120 | tf_op jit(solution)/shard_map/ppermute | solution.py:1041
  210.9 15.2 %collective-permute-start.28 = (bf16[784,128]{1,0:T(8,128)(2,1)}, bf16[784,128]{1,0:T(8,128)(2,1)S(1)}, u32[]{:S(2)}, u32[]{:S(2)}) collective-permute-start(bf16[784,128]{1,0:T(8,128)(2,1)} %get-tuple-element.106), channel_id=1, source_target_pairs={{0,6},{1,7},{2,4},{3,5},{4,2},{5,3},{6,0},{7,1},{8,14},{9,15},{10,... | collective-permute-start | bytes 602120 | tf_op jit(solution)/shard_map/ppermute | solution.py:1041
  246.3 11.3 %collective-permute-start.31 = (bf16[784,128]{1,0:T(8,128)(2,1)}, bf16[784,128]{1,0:T(8,128)(2,1)S(1)}, u32[]{:S(2)}, u32[]{:S(2)}) collective-permute-start(bf16[784,128]{1,0:T(8,128)(2,1)} %get-tuple-element.113.refs_1_), channel_id=1, source_target_pairs={{0,8},{8,0},{16,24},{24,16},{1,9},{9,1},{17,25},{25,17},{2,10},{10... | collective-permute-start | bytes 602120 | tf_op jit(solution)/shard_map/ppermute | solution.py:1041
  (66 other events, 714.7 us)
Sparse Core Ops, SparseCore 0:
  9.6 25.2 all-gather.4
  36.5 22.6 all-gather.6
  116.4 32.2 reduce-scatter.2
  167.0 34.8 reduce-scatter.4

commit v9 on v8

--- a/solution.py
+++ b/solution.py
@@ -108,6 +108,7 @@
         skip_ref,
         expand_ref,
         rest_ref,
+        unit_ref,
         normed_ref,
         conv_in_ref,
         conv_pre_ref,
@@ -131,7 +132,9 @@
             place_columns(rest_ref, places_ref[number], block[...])
 
     hidden = hidden_ref[...].astype(jnp.float32)
-    normed = low(rms_scale(hidden) * gain_one_ref[...])
+    unit = rms_scale(hidden)
+    unit_ref[...] = low(unit)
+    normed = low(unit * gain_one_ref[...])
     normed_ref[...] = normed
     conv_in = dot_nt(normed, rest_ref[:channels, :])
     conv_in_ref[...] = conv_in
@@ -227,27 +230,29 @@
     )
 
 
-def middle_kernel(gate_count, out_count, places_ref, *refs):
+def middle_kernel(count, places_ref, *refs):
     (
         scanned_ref,
         gating_ref,
         d_gnorm_ref,
         cot_ref,
-        normed_ref,
+        unit_ref,
         sums_one_ref,
         sums_two_ref,
         sums_three_ref,
         sums_four_ref,
         out_ref,
         gain_two_ref,
+        gain_one_ref,
+        gate_weight_ref,
         block_ref,
         d_gating_ref,
         d_scanned_ref,
         d_gain_two_ref,
-    ) = refs[:15]
-    gate_refs = refs[15 : 15 + gate_count]
-    out_refs = refs[15 + gate_count : 15 + gate_count + out_count]
-    out_sum, gate_sum = refs[15 + gate_count + out_count :]
+        d_gain_one_ref,
+    ) = refs[:18]
+    grad_refs = refs[18 : 18 + count]
+    out_sum, gate_sum = refs[18 + count :]
     chunk = pl.program_id(0)
 
     @pl.when(chunk == 0)
@@ -275,23 +280,29 @@
     d_gating = low(d_gated * scanned * (open_part * (1.0 + gating * (1.0 - open_part))))
     d_gating_ref[...] = d_gating
     d_scanned_ref[...] = low(d_gated * gate)
-    gate_sum[...] += dot_tn(d_gating, normed_ref[...])
+    gate_sum[...] += dot_tn(d_gating, unit_ref[...])
 
     @pl.when(chunk == pl.num_programs(0) - 1)
     def _():
-        for number, gate_ref in enumerate(gate_refs):
-            columns = gate_ref.shape[1]
-            start = pl.multiple_of(places_ref[number] * columns, columns)
-            gate_ref[...] = low(gate_sum[:, pl.ds(start, columns)])
-        for number, grad_ref in enumerate(out_refs):
+        weights = gate_weight_ref[...].astype(jnp.float32)
+        d_gain_one_ref[...] = jnp.sum(gate_sum[...] * weights, axis=0, keepdims=True)
+        gate_sum[...] = gate_sum[...] * gain_one_ref[...]
+        local_di = gate_sum.shape[0]
+        if grad_refs[0].shape == gate_sum.shape:
+            grad_refs[0][...] = low(gate_sum[...])
+            grad_refs[1][...] = low(out_sum[...])
+            return
+        for number, grad_ref in enumerate(grad_refs):
             columns = grad_ref.shape[1]
-            first = places_ref[gate_count + number]
-            for step in range(out_sum.shape[0] // HEADDIM // out_count):
-                head = first + step * out_count
-                rows = pl.ds(pl.multiple_of(head * HEADDIM, HEADDIM), HEADDIM)
+            for step in range(D // columns // count):
+                place = places_ref[number] + step * count
+                start = pl.multiple_of(place * columns, columns)
+                base = step * 2 * local_di
+                grad_ref[base : base + local_di, :] = low(gate_sum[:, pl.ds(start, columns)])
+                rows = pl.ds(pl.multiple_of(place * HEADDIM, HEADDIM), HEADDIM)
                 for tile in range(D // columns):
-                    base = (step * (D // columns) + tile) * HEADDIM
-                    grad_ref[base : base + HEADDIM, :] = low(
+                    first = base + local_di + tile * HEADDIM
+                    grad_ref[first : first + HEADDIM, :] = low(
                         out_sum[rows, tile * columns : (tile + 1) * columns]
                     )
 
@@ -299,7 +310,7 @@
 def backward_kernel(
     grad_count,
     places_ref,
-    normed_ref,
+    unit_ref,
     conv_in_ref,
     conv_pre_ref,
     dt_ref,
@@ -311,11 +322,14 @@
     dt_bias_ref,
     skip_ref,
     expand_ref,
+    gain_one_ref,
+    rest_weight_ref,
     d_rest_ref,
     d_kernel_ref,
     d_conv_bias_ref,
     d_skip_ref,
     d_head_ref,
+    d_gain_one_ref,
     *refs,
 ):
     grad_refs = refs[:grad_count]
@@ -414,10 +428,13 @@
     ext[BLOCK : BLOCK + 8, :] = ext[0:8, :]
     d_rest = jnp.concatenate([low(d_conv_in), low(d_dt)], 1)
     d_rest_ref[...] = d_rest
-    rest_sum[...] += dot_tn(d_rest, normed_ref[...])
+    rest_sum[...] += dot_tn(d_rest, unit_ref[...])
 
     @pl.when(chunk == pl.num_programs(0) - 1)
     def _():
+        weights = rest_weight_ref[...].astype(jnp.float32)
+        d_gain_one_ref[...] = jnp.sum(rest_sum[...] * weights, axis=0, keepdims=True)
+        rest_sum[...] = rest_sum[...] * gain_one_ref[...]
         for number, grad_ref in enumerate(grad_refs):
             columns = grad_ref.shape[1]
             blocks = rest_sum.shape[1] // columns // grad_count
@@ -437,66 +454,39 @@
     return total
 
 
-def pair_kernel(places_ref, *refs):
-    gate, out = refs[:4], refs[4:6]
-    gate_keep_ref, gate_send_ref = refs[7:9]
-    out_refs = refs[9:-1]
-    paired = sum_of(*gate)
-    columns = gate_keep_ref.shape[1]
-    even = places_ref[0] == 0
-    first, second = low(paired[:, :columns]), low(paired[:, columns:])
-    gate_keep_ref[...] = jnp.where(even, first, second)
-    gate_send_ref[...] = jnp.where(even, second, first)
-    for number, ref in enumerate(out_refs):
-        rows = ref.shape[0]
-        start = pl.multiple_of(places_ref[1 + number] * rows, rows)
-        here = pl.ds(start, rows)
-        ref[...] = low(sum_of(out[0].at[here, :], out[1].at[here, :]))
-
-
-def rest_pair_kernel(places_ref, mine_ref, arrived_ref, *rest_refs):
-    for number, ref in enumerate(rest_refs):
+def pair_kernel(count, places_ref, mine_ref, arrived_ref, *refs):
+    for number, ref in enumerate(refs[count : len(refs) - count]):
         rows = ref.shape[0]
         here = pl.ds(pl.multiple_of(places_ref[number] * rows, rows), rows)
         ref[...] = low(sum_of(mine_ref.at[here, :], arrived_ref.at[here, :]))
 
 
-def join_kernel(places_ref, *refs):
-    joined_ref = refs[-1]
+def hold_kernel(places_ref, *refs):
     rows = refs[0].shape[0]
-    joined_ref[:rows, :] = low(sum_of(*refs[:2]))
-    joined_ref[rows:, :] = low(sum_of(*refs[2:6]))
+    for number, ref in enumerate(refs[:-1]):
+        refs[-1][number * rows : (number + 1) * rows, :] = ref[...]
 
 
 def final_kernel(places_ref, *refs):
-    refs[-2][...] = low(sum_of(*refs[:4]))
-
-
-def vec_kernel(places_ref, *refs):
-    refs[-1][...] = (refs[0][...] + refs[1][...]) + (refs[2][...] + refs[3][...])
+    refs[-1][...] = low(sum_of(*refs[:-1]))
 
 
 def normed_kernel(
-    places_ref,
-    hidden_ref,
-    d_gating_ref,
-    d_rest_ref,
-    gate_weight_ref,
-    rest_weight_ref,
-    d_normed_ref,
-    d_gain_one_ref,
+    places_ref, d_gating_ref, d_rest_ref, gate_weight_ref, rest_weight_ref, mine_ref, send_ref
 ):
     chunk = pl.program_id(0)
-
-    @pl.when(chunk == 0)
+    d_normed = dot_nn(d_gating_ref[...], gate_weight_ref[...])
+    d_normed = low(d_normed + dot_nn(d_rest_ref[...], rest_weight_ref[...]))
+    here = chunk % 2 == places_ref[0]
+    rows = pl.ds(pl.multiple_of(chunk // 2 * BLOCK, BLOCK), BLOCK)
+
+    @pl.when(here)
     def _():
-        d_gain_one_ref[...] = jnp.zeros_like(d_gain_one_ref)
-
-    d_normed = dot_nn(d_gating_ref[...], gate_weight_ref[...])
-    d_normed = d_normed + dot_nn(d_rest_ref[...], rest_weight_ref[...])
-    d_normed_ref[...] = low(d_normed)
-    unit = rms_scale(hidden_ref[...].astype(jnp.float32))
-    d_gain_one_ref[...] += jnp.sum(d_normed * unit, axis=0, keepdims=True)
+        mine_ref[rows, :] = d_normed
+
+    @pl.when(jnp.logical_not(here))
+    def _():
+        send_ref[rows, :] = d_normed
 
 
 def prepare_kernel(places_ref, in_ref, out_ref, rest_ref, gate_out_ref):
@@ -689,6 +679,7 @@
         [
             struct((channels + lanes, D), jnp.bfloat16),
             struct((length, D), jnp.bfloat16),
+            struct((length, D), jnp.bfloat16),
             struct((length, channels)),
             struct((length, channels)),
             struct((length, lanes)),
@@ -698,6 +689,7 @@
         ],
         [
             fixed((channels + lanes, D)),
+            rows_of(D),
             rows_of(D),
             rows_of(channels),
             rows_of(channels),
@@ -748,15 +740,17 @@
     )
 
 
-def run_middle(gate_places, out_places, scanned, gating, d_gnorm, cot, normed, sums, out, gain):
+def run_middle(
+    places, scanned, gating, d_gnorm, cot, unit, sums, out, gain_two, gain_one, gate_weight
+):
     length, local_di = scanned.shape
-    gate_shape = (local_di, D // len(gate_places))
-    out_shape = (local_di, D) if len(out_places) == 1 else (local_di * D // 256, 128)
-    shapes = [gate_shape] * len(gate_places) + [out_shape] * len(out_places)
+    shapes = [(local_di, D)] * 2
+    if len(places) > 1:
+        shapes = [(2 * local_di * D // 256, 128)] * 2
     return call(
-        lambda *refs: middle_kernel(len(gate_places), len(out_places), *refs),
-        gate_places + out_places,
-        [scanned, gating, d_gnorm, cot, normed, *sums, out, gain],
+        lambda *refs: middle_kernel(2, *refs),
+        places,
+        [scanned, gating, d_gnorm, cot, unit, *sums, out, gain_two, gain_one, gate_weight],
         [
             rows_of(local_di),
             rows_of(local_di),
@@ -765,12 +759,13 @@
             rows_of(D),
         ]
         + [pl.BlockSpec((8, BLOCK), lambda q, *_: (0, q))] * 4
-        + [fixed((local_di, D)), fixed((1, local_di))],
+        + [fixed((local_di, D)), fixed((1, local_di)), fixed((1, D)), fixed((local_di, D))],
         [
             struct((length, D), jnp.bfloat16),
             struct((length, local_di), jnp.bfloat16),
             struct((length, local_di), jnp.bfloat16),
             struct((1, local_di)),
+            struct((1, D)),
         ]
         + [struct(shape, jnp.bfloat16) for shape in shapes],
         [
@@ -778,6 +773,7 @@
             rows_of(local_di),
             rows_of(local_di),
             fixed((1, local_di)),
+            fixed((1, D)),
         ]
         + [fixed(shape) for shape in shapes],
         [pltpu.VMEM((local_di, D), jnp.float32), pltpu.VMEM((local_di, D), jnp.float32)],
@@ -789,7 +785,19 @@
 
 
 def run_backward(
-    places, normed, conv_in, conv_pre, dt_raw, y, states, d_scanned, kernel, heads_vectors, expand
+    places,
+    unit,
+    conv_in,
+    conv_pre,
+    dt_raw,
+    y,
+    states,
+    d_scanned,
+    kernel,
+    heads_vectors,
+    expand,
+    gain_one,
+    rest_weight,
 ):
     length, local_di = y.shape
     chunks = length // BLOCK
@@ -803,7 +811,10 @@
     return call(
         lambda *refs: backward_kernel(len(places), *refs),
         places,
-        [normed, conv_in, conv_pre, dt_raw, y, states, d_scanned, kernel, *heads_vectors, expand],
+        [
+            *[unit, conv_in, conv_pre, dt_raw, y, states, d_scanned, kernel],
+            *[*heads_vectors, expand, gain_one, rest_weight],
+        ],
         [
             back(D),
             back(channels),
@@ -817,6 +828,8 @@
             fixed((1, lanes)),
             fixed((1, local_di)),
             fixed((lanes, local_di)),
+            fixed((1, D)),
+            fixed((channels + lanes, D)),
         ],
         [
             struct((length, channels + lanes), jnp.bfloat16),
@@ -824,6 +837,7 @@
             struct((1, channels)),
             struct((1, local_di)),
             struct((2, lanes)),
+            struct((1, D)),
         ]
         + [struct(grad, jnp.bfloat16)] * len(places),
         [
@@ -832,6 +846,7 @@
             fixed((1, channels)),
             fixed((1, local_di)),
             fixed((2, lanes)),
+            fixed((1, D)),
         ]
         + [fixed(grad)] * len(places),
         [
@@ -847,49 +862,16 @@
     )
 
 
-def run_pair(y, out_places, gate, out, through):
-    columns = gate[0].shape[1] // 2
-    shapes = [
-        (gate[0].shape[0], columns),
-        (gate[0].shape[0], columns),
-    ] + [(out[0].shape[0] // len(out_places), out[0].shape[1])] * len(out_places)
-    inputs = [*gate, *out]
-    untouched = pl.BlockSpec(memory_space=pl.ANY)
-    return call(
-        pair_kernel,
-        [y] + out_places,
-        [*inputs, through],
-        [fixed(array.shape) for array in inputs] + [untouched],
-        [struct(shape, jnp.bfloat16) for shape in shapes] + [struct(through.shape, through.dtype)],
-        [fixed(shape) for shape in shapes] + [untouched],
-        [],
-        1,
-        [],
-        (3_000_000, 7_000_000, 0),
-        "pair",
-        [(1 + len(inputs), len(shapes))],
-    )
-
-
-def run_normed(hidden, d_gating, d_rest, gate_weight, rest_weight, arrived):
+def run_normed(parity, d_gating, d_rest, gate_weight, rest_weight, arrived):
     length, local_di = d_gating.shape
     rest = d_rest.shape[1]
     return call(
         normed_kernel,
-        [jnp.int32(0)],
-        [hidden, d_gating, d_rest, gate_weight, rest_weight],
-        [
-            rows_of(D),
-            rows_of(local_di),
-            rows_of(rest),
-            fixed((local_di, D)),
-            fixed((rest, D)),
-        ],
-        [
-            struct((length, D), jnp.bfloat16),
-            struct((1, D)),
-        ],
-        [rows_of(D), fixed((1, D))],
+        [parity],
+        [d_gating, d_rest, gate_weight, rest_weight],
+        [rows_of(local_di), rows_of(rest), fixed((local_di, D)), fixed((rest, D))],
+        [struct((length // 2, D), jnp.bfloat16)] * 2,
+        [fixed((length // 2, D))] * 2,
         [],
         length // BLOCK,
         arrived,
@@ -898,74 +880,57 @@
     )
 
 
-def run_rest_pair(places, mine, arrived, there):
-    rest = (mine.shape[0] // len(places), mine.shape[1])
-    shapes = [struct(rest, jnp.bfloat16)] * len(places)
-    inputs = [mine, arrived]
+def run_pair(places, mine, arrived, through, there):
+    block = (mine.shape[0] // len(places), mine.shape[1])
+    untouched = [pl.BlockSpec(memory_space=pl.ANY)] * len(through)
     return call(
-        rest_pair_kernel,
+        lambda *refs: pair_kernel(len(through), *refs),
         places,
-        inputs,
-        [fixed(array.shape) for array in inputs],
-        shapes,
-        [fixed(shape.shape) for shape in shapes],
+        [mine, arrived, *through],
+        [fixed(mine.shape), fixed(arrived.shape)] + untouched,
+        [struct(block, jnp.bfloat16)] * len(places)
+        + [struct(array.shape, array.dtype) for array in through],
+        [fixed(block)] * len(places) + untouched,
         [],
         1,
         there,
         (2_000_000, 3_000_000, 0),
-        "rest_pair",
-    )
-
-
-def run_join(gate, out, there):
-    inputs = [*gate, *out]
-    shape = (gate[0].shape[0] + out[0].shape[0], gate[0].shape[1])
+        "pair",
+        [(3 + number, len(places) + number) for number in range(len(through))],
+    )
+
+
+def run_hold(blocks, there):
+    rows, columns = blocks[0].shape
+    shape = (rows * len(blocks), columns)
     return call(
-        join_kernel,
+        hold_kernel,
         [jnp.int32(0)],
-        inputs,
-        [fixed(array.shape) for array in inputs],
-        struct(shape, jnp.bfloat16),
+        blocks,
+        [fixed(block.shape) for block in blocks],
+        struct(shape, blocks[0].dtype),
         fixed(shape),
         [],
         1,
         there,
-        (500_000, 1_000_000, 0),
-        "join",
-    )
-
-
-def run_final(rest, through, there):
-    untouched = pl.BlockSpec(memory_space=pl.ANY)
+        (0, 2_000_000, 0),
+        "hold",
+    )
+
+
+def run_final(terms, there):
     return call(
         final_kernel,
         [jnp.int32(0)],
-        [*rest, through],
-        [fixed(array.shape) for array in rest] + [untouched],
-        [struct(rest[0].shape, jnp.bfloat16), struct(through.shape, through.dtype)],
-        [fixed(rest[0].shape), untouched],
+        terms,
+        [fixed(array.shape) for array in terms],
+        struct(terms[0].shape, jnp.bfloat16),
+        fixed(terms[0].shape),
         [],
         1,
         there,
         (500_000, 1_000_000, 0),
         "final",
-        [(1 + len(rest), 1)],
-    )
-
-
-def run_vec(terms):
-    return call(
-        vec_kernel,
-        [jnp.int32(0)],
-        terms,
-        [fixed(array.shape) for array in terms],
-        struct(terms[0].shape),
-        fixed(terms[0].shape),
-        [],
-        1,
-        [],
-        (20_000, 100_000, 0),
-        "vec",
     )
 
 
@@ -1066,18 +1031,15 @@
     return places, blocks
 
 
-def ring_pairs(rows):
+def ring_late(rows, arrived):
     count = lax.axis_size("wshard")
     index = lax.axis_index("wshard")
     places = [(index + count - 2 * step) % count for step in range(count // 2)]
     blocks = [rows]
     for _ in range(count // 2 - 1):
         blocks = blocks + [ring_step(blocks[-1])]
-    swapped = [
-        swap(jnp.concatenate(blocks[first : first + 2], 0), "wshard", 1)
-        for first in range(0, count // 2, 2)
-    ]
-    return places + [place ^ 1 for place in places], blocks + swapped
+    swapped = swap(run_hold(blocks, arrived), "wshard", 1)
+    return places + [place ^ 1 for place in places], blocks + [swapped]
 
 
 def take_block(values, index, rows):
@@ -1148,7 +1110,7 @@
         y, z = shard_index % 2, shard_index // 2
         rest_mine, gate_out_mine = run_prepare(seq_index, in_weight.T, out_weight)
         rest = ring_blocks(rest_mine)
-        gate_out = ring_pairs(gate_out_mine)
+        gate_out = ring_late(gate_out_mine, rest[1][1::2])
         gate_places = [z ^ mask for mask in range(4)]
         out_places = [y, 1 - y]
     else:
@@ -1167,7 +1129,7 @@
         rest = (origin, [lax.all_gather(rest_mine, "wshard", axis=0, tiled=True).T])
         gate_mine = lax.all_gather(gate_mine, "wshard", axis=0, tiled=True).T
         gate_out = (origin, [gate_mine, gather_out(low(out_weight), seq_index, groups)])
-        gate_places, out_places = origin, origin
+        out_places = origin
     hidden_low = lax.all_gather(hidden_rows, "seq", axis=0, tiled=True)
     cot_low = lax.all_gather(cot_rows, "seq", axis=0, tiled=True)
     my_gain_two = heads_of(gain_two, 0, HEADDIM)[None, :]
@@ -1187,6 +1149,7 @@
     ).astype(jnp.float32)
     (
         rest_weight,
+        unit_low,
         normed_low,
         conv_in,
         conv_pre,
@@ -1201,27 +1164,25 @@
         gate_out, cot_low, normed_low, scanned, my_gain_two
     )
     middle = run_middle(
-        gate_places,
         out_places,
         scanned,
         gating,
         d_gnorm,
         cot_low,
-        normed_low,
+        unit_low,
         [sums] + [swap(sums, "seq", mask) for mask in range(1, 4)],
         out_low,
         my_gain_two,
-    )
-    block_part, d_gating, d_scanned, d_gain_two = middle[:4]
-    gate_grads = middle[4 : 4 + len(gate_places)]
-    out_grads = middle[4 + len(gate_places) :]
+        gain_one[None, :],
+        gate_weight,
+    )
+    block_part, d_gating, d_scanned, d_gain_two, d_gain_gate, *gate_out_grads = middle
     block_rows = lax.psum_scatter(block_part, "seq", scatter_dimension=0, tiled=True)
     if rings:
-        gate_pieces = [swap(gate_grads[mask], "wshard", 2 * mask) for mask in range(1, 4)]
-        out_arrived = swap(out_grads[1], "wshard", 1)
-    backward = run_backward(
+        gate_out_arrived = swap(gate_out_grads[1], "wshard", 1)
+    d_rest, d_kernel, d_conv_bias, d_skip_wide, d_head, d_gain_rest, *rest_grads = run_backward(
         out_places,
-        normed_low,
+        unit_low,
         conv_in,
         conv_pre,
         dt_raw,
@@ -1231,28 +1192,12 @@
         my_kernel,
         heads_vectors,
         expand,
-    )
-    d_rest, d_kernel, d_conv_bias, d_skip_wide, d_head = backward[:5]
-    rest_grads = backward[5:]
-    before_normed = []
-    if rings:
-        gate_keep, gate_send, *out_sums, rest_send = run_pair(
-            y,
-            gate_places,
-            [gate_grads[0]] + gate_pieces,
-            [out_grads[0], out_arrived],
-            rest_grads[1],
-        )
-        rest_arrived = swap(rest_send, "wshard", 1)
-        gate_arrived = swap(gate_send, "wshard", 1)
-        out_pieces = [swap(out_sums[mask], "wshard", 2 * mask) for mask in range(1, 4)]
-        before_normed = [gate_keep]
-    d_normed_part, d_gain_one = run_normed(
-        hidden_low, d_gating, d_rest, gate_weight, rest_weight, before_normed
-    )
-    d_normed = lax.psum_scatter(d_normed_part, "seq", scatter_dimension=0, tiled=True)
+        gain_one[None, :],
+        rest_weight,
+    )
+    d_gain_one = d_gain_gate[0] + d_gain_rest[0]
     shared = jnp.concatenate(
-        [d_gain_one[0], d_kernel[:, local_di:].reshape(-1), d_conv_bias[0, local_di:]]
+        [d_gain_one, d_kernel[:, local_di:].reshape(-1), d_conv_bias[0, local_di:]]
     )
     d_skip_part = jnp.sum(d_skip_wide.reshape(local_heads, HEADDIM), axis=1)
     apart = jnp.concatenate(
@@ -1265,43 +1210,59 @@
         ]
     )
     vec_part = jnp.concatenate([shared, apart])[None]
+    near, far = seq_index % 2, seq_index // 2
     if rings:
-        gate_out_part = run_join(
-            [gate_keep, gate_arrived], [out_sums[0]] + out_pieces, [d_gain_one]
+        *gate_out_sums, rest_send, vec_part = run_pair(
+            gate_places,
+            gate_out_grads[0],
+            gate_out_arrived,
+            [rest_grads[1], vec_part],
+            [block_rows],
         )
-        gate_out_far = swap(gate_out_part, "seq", 2)
+        rest_arrived = swap(rest_send, "wshard", 1)
+        gate_out_pieces = [
+            swap(gate_out_sums[mask], "wshard", 2 * mask) for mask in range(1, 4)
+        ]
+        normed_mine, normed_send = run_normed(
+            near, d_gating, d_rest, gate_weight, rest_weight, [gate_out_sums[0]]
+        )
+        vec_parts = lax.all_gather(vec_part, "wshard", axis=0, tiled=True)
+        gate_out_part = run_final(
+            [gate_out_sums[0]] + gate_out_pieces, [normed_mine, vec_parts]
+        )
+        vec_part = jnp.sum(vec_parts, axis=0, keepdims=True)
+        every = lax.all_gather(vec_part, "seq", axis=0, tiled=True)
         gate_out_near = swap(gate_out_part, "seq", 1)
-        rest_sums = run_rest_pair(
-            gate_places,
-            rest_grads[0],
-            rest_arrived,
-            [gate_out_far, gate_out_near, block_rows],
+        rest_sums = run_pair(
+            gate_places, rest_grads[0], rest_arrived, [], [gate_out_near]
         )
         rest_pieces = [swap(rest_sums[mask], "wshard", 2 * mask) for mask in range(1, 4)]
-        spots = [seq_index ^ mask for mask in range(4)]
-        gate_out_blocks = [
-            gate_out_part, gate_out_near, gate_out_far, swap(gate_out_far, "seq", 1)
-        ]
-        in_arrays = (in_weight.T, in_first.T, in_second.T)
-        updated = run_update_gate(
-            spots, gate_out_blocks, in_arrays, (out_weight, out_first, out_second), []
-        )
-        out_first_new, out_second_new, out_weight_new = updated[3:]
-        vec_part = vec_part + swap(vec_part, "wshard", 1)
-        rest_part, vec_part = run_final(
-            [rest_sums[0]] + rest_pieces, vec_part, [out_first_new]
-        )
-        vec_pieces = [swap(vec_part, "wshard", 2 * mask) for mask in range(1, 4)]
-        vec_part = run_vec([vec_part] + vec_pieces)
-        vec_places, vec_blocks = seq_blocks(vec_part)
-        every = jnp.zeros((groups, vec_part.shape[1]), jnp.float32)
-        for spot, block in zip(vec_places, vec_blocks):
-            every = lax.dynamic_update_slice_in_dim(every, block, spot, 0)
+        gate_out_far = swap(gate_out_part, "seq", 2)
     else:
         vec_part = lax.psum(vec_part, "wshard")
         every = lax.all_gather(vec_part, "seq", axis=0, tiled=True)
+        normed_mine, normed_send = run_normed(
+            near, d_gating, d_rest, gate_weight, rest_weight, []
+        )
+    normed_arrived = swap(normed_send, "seq", 1)
+    normed_sum = normed_mine.astype(jnp.float32) + normed_arrived.astype(jnp.float32)
+    normed_far = swap(low(take_block(normed_sum, 1 - far, rows_here)), "seq", 2)
+    if rings:
+        spots = [seq_index ^ mask for mask in range(4)]
+        gate_out_blocks = [gate_out_part, gate_out_near, gate_out_far]
+        gate_out_blocks = gate_out_blocks + [swap(gate_out_far, "seq", 1)]
+        in_arrays = (in_weight.T, in_first.T, in_second.T)
+        updated = run_update_gate(
+            spots,
+            gate_out_blocks,
+            in_arrays,
+            (out_weight, out_first, out_second),
+            [rest_sums[0]],
+        )
+        out_first_new, out_second_new, out_weight_new = updated[3:]
+        rest_part = run_final([rest_sums[0]] + rest_pieces, [out_first_new, every])
     block_out = hidden_rows.astype(jnp.float32) + block_rows.astype(jnp.float32)
-    d_normed = d_normed.astype(jnp.float32)
+    d_normed = take_block(normed_sum, far, rows_here) + normed_far.astype(jnp.float32)
     own_hidden = hidden_rows.astype(jnp.float32)
     own_scale = lax.rsqrt(jnp.mean(own_hidden * own_hidden, axis=-1, keepdims=True) + norm_eps)
     own_unit = own_hidden * own_scale
@@ -1346,10 +1307,10 @@
         in_first_new, in_second_new, in_weight_new = [array.T for array in updated]
     else:
         rest_part = lax.psum_scatter(rest_grads[0].T, "wshard", scatter_dimension=0, tiled=True)
-        gate_part = lax.psum_scatter(gate_grads[0].T, "wshard", scatter_dimension=0, tiled=True)
+        gate_part = lax.psum_scatter(gate_out_grads[0].T, "wshard", scatter_dimension=0, tiled=True)
         gate_every = lax.all_gather(gate_part, "seq", axis=0, tiled=False).astype(jnp.float32)
         rest_every = lax.all_gather(rest_part, "seq", axis=0, tiled=False).astype(jnp.float32)
-        out_total = sum_out_grad(out_grads[0], out_weight.shape[0], seq_index, groups)
+        out_total = sum_out_grad(gate_out_grads[1], out_weight.shape[0], seq_index, groups)
         in_total = jnp.concatenate(
             [
                 merge_heads(gate_every, 1, HEADDIM),

time: 273 us -> 304 us (1.11)
  blocking collectives: 0 us -> 34.5 us
  starting transfers between devices: 40 us -> 28.9 us
  local copies, waits for them, and re-layouts: 20.1 us -> 25.6 us
  waiting for transfers between devices: 80.2 us -> 75.9 us
  Pallas kernels: 106 us -> 110 us
    all_gather x0 -> x1, blocking collectives: none -> 34.5 us  [shards(): vec_parts = lax.all_gather(vec_part, 'wshard', axis=0, tiled=True)]
    ppermute x34 -> x24, waiting for transfers between devices: 55.9 us -> 21.7 us  [swap(): return lax.ppermute(values, axis, route)]
    unnamed x4 -> x5, waiting for transfers between devices: 1.41 us -> 29.4 us
    ppermute x34 -> x24, starting transfers between devices: 34 us -> 22.3 us  [swap(): return lax.ppermute(values, axis, route)]
    pallas_call x13, Pallas kernels: 106 us -> 110 us  [call(): pl.pallas_call(after(kernel, 1 + len(inputs), len(arrived)), grid_spec=pl...]
    unnamed x108 -> x90, local copies, waits for them, and re-layouts: 8.54 us -> 12 us
  transfers between devices with their start and end apart: 44 -> 34, of which waited for: 14 -> 14; matrix products, arithmetic and copies ran while one was open for 8% -> 9% of each run, Pallas kernels for 28% -> 28%
where the time goes in v9:
time: 304 us; the launch traced here: 301 us
  Pallas kernels  110 us (36%)
  waiting for transfers between devices  75.9 us (25%)
  blocking collectives  34.5 us (11%)
  starting transfers between devices  28.9 us (10%)
  local copies, waits for them, and re-layouts  25.6 us (8%)
  between operations  15 us (5%)
  other arithmetic  11.1 us (4%)
    pallas_call x13, Pallas kernels, call(): pl.pallas_call(after(kernel, 1 + len(inputs), len(arrived)), grid_spec=pl...  110 us
    all_gather x1, blocking collectives, shards(): vec_parts = lax.all_gather(vec_part, 'wshard', axis=0, tiled=True)  34.5 us
    unnamed x5, waiting for transfers between devices  29.4 us
    ppermute x6, waiting for transfers between devices, ring_step(): lax.ppermute(held, 'wshard', [(i, (i + 2) % count) for i in range(count)])  24.8 us
    ppermute x24, starting transfers between devices, swap(): return lax.ppermute(values, axis, route)  22.3 us
    ppermute x24, waiting for transfers between devices, swap(): return lax.ppermute(values, axis, route)  21.7 us
    unnamed x90, local copies, waits for them, and re-layouts  12 us
    ppermute x6, starting transfers between devices, ring_step(): lax.ppermute(held, 'wshard', [(i, (i + 2) % count) for i in range(count)])  6.24 us
  transfers between devices with their start and end apart: 34, of which 14 were waited for; matrix products, arithmetic and copies ran while one was open for 9% of the time, Pallas kernels for 28%

profile of v9, /device:TPU:0, one launch (start us, length us, event | category | flops | bytes accessed | tf_op | source)
XLA Modules:
  0.0 301.0 jit_solution(13505416645485770166)
XLA Ops:
  8.7 2.7 prepare.1
  11.5 3.0 %collective-permute-start.7 = (bf16[1024,128]{1,0:T(8,128)(2,1)}, bf16[1024,128]{1,0:T(8,128)(2,1)S(1)}, u32[]{:S(2)}, u32[]{:S(2)}) collective-permute-start(bf16[1024,128]{1,0:T(8,128)(2,1)} %get-tuple-element.65.refs_1_), channel_id=1, source_target_pairs={{0,2},{1,3},{2,4},{3,5},{4,6},{5,7},{6,0},{7,1},{8,10},{9,11},{10,... | collective-permute-start | bytes 786440 | tf_op jit(solution)/shard_map/ppermute | solution.py:1018
  14.5 1.6 collective-permute-start.1
  16.1 7.8 %collective-permute-done.7.refs_2_ = bf16[1024,128]{1,0:T(8,128)(2,1)S(1)} collective-permute-done((bf16[1024,128]{1,0:T(8,128)(2,1)}, bf16[1024,128]{1,0:T(8,128)(2,1)S(1)}, u32[]{:S(2)}, u32[]{:S(2)}) %collective-permute-start.7) | collective-permute-done | bytes 262176 | tf_op jit(solution)/shard_map/ppermute | solution.py:1018
  23.9 1.7 collective-permute-start
  25.6 2.3 collective-permute-done.1.refs_3_
  28.2 9.0 %collective-permute-done.3.refs_5_ = bf16[784,128]{1,0:T(8,128)(2,1)S(1)} collective-permute-done((bf16[784,128]{1,0:T(8,128)(2,1)S(1)}, bf16[784,128]{1,0:T(8,128)(2,1)S(1)}, u32[]{:S(2)}, u32[]{:S(2)}) %collective-permute-start.3) | collective-permute-done | bytes 200736 | tf_op jit(solution)/shard_map/ppermute | solution.py:1018
  41.3 5.7 %collective-permute-done.5.refs_7_ = bf16[784,128]{1,0:T(8,128)(2,1)S(1)} collective-permute-done((bf16[784,128]{1,0:T(8,128)(2,1)S(1)}, bf16[784,128]{1,0:T(8,128)(2,1)S(1)}, u32[]{:S(2)}, u32[]{:S(2)}) %collective-permute-start.5) | collective-permute-done | bytes 200736 | tf_op jit(solution)/shard_map/ppermute | solution.py:1018
  48.9 2.1 collective-permute-done.4.refs_6_.refs_7_
  51.0 2.1 collective-permute-done.6.refs_8_
  53.9 2.3 hold.1
  64.1 15.7 %forward.1 = (bf16[896,1024]{1,0:T(8,128)(2,1)}, bf16[1024,1024]{1,0:T(8,128)(2,1)}, bf16[1024,1024]{1,0:T(8,128)(2,1)}, f32[1024,768]{1,0:T(8,128)}, f32[1024,7...) custom-call(s32[8]{0:T(128)} %stack.105.refs_0_, ...), custom_call_target="tpu_custom_call" | custom-call | flops 6000000000 | bytes 30000000 | tf_op jit(solution)/shard_map/forward/pallas_call | solution.py:625
  80.8 11.2 %gate.1 = (bf16[512,1024]{1,0:T(8,128)(2,1)}, bf16[512,1024]{1,0:T(8,128)(2,1)}, f32[1024,512]{1,0:T(8,128)}, f32[1024,512]{1,0:T(8,128)}, f32[8,1024]{1,0:T(8,128)}) custom-call(s32[8]{0:T(128)} %stack.107.refs_0_, bf16[1024,128]{1,0:T(8,128)(2,1)} %get-tuple-element.65.refs_1_, bf16[1024,128]{1,0:T(8,128)(2,1)} %copy-done.10, ...), custom_call_target="tpu_custom_call" | custom-call | flops 2500000000 | bytes 12000000 | tf_op jit(solution)/shard_map/gate/pallas_call | solution.py:625
  94.5 1.7 collective-permute-done.12.refs_8_
  97.7 12.6 %middle.1 = (bf16[1024,1024]{1,0:T(8,128)(2,1)}, bf16[1024,512]{1,0:T(8,128)(2,1)}, bf16[1024,512]{1,0:T(8,128)(2,1)}, f32[1,512]{1,0:T(1,128)}, f32[1,1024]{1,0...) custom-call(s32[2]{0:T(128)} %pad_add_fusion.refs_0_, ...), custom_call_target="tpu_custom_call" | custom-call | flops 4000000000 | bytes 15000000 | tf_op jit(solution)/shard_map/middle/pallas_call | solution.py:625
  113.8 33.0 %backward.1 = (bf16[1024,896]{1,0:T(8,128)(2,1)}, f32[4,768]{1,0:T(4,128)}, f32[1,768]{1,0:T(1,128)}, f32[1,512]{1,0:T(1,128)}, f32[2,128]{1,0:T(2,128)}, /*inde...) custom-call(s32[2]{0:T(128)} %pad_add_fusion.refs_0_, ...), custom_call_target="tpu_custom_call" | custom-call | flops 14000000000 | bytes 40000000 | tf_op jit(solution)/shard_map/backward/pallas_call | solution.py:625
  154.7 3.3 %pair.2 = (bf16[1024,128]{1,0:T(8,128)(2,1)}, bf16[1024,128]{1,0:T(8,128)(2,1)}, bf16[1024,128]{1,0:T(8,128)(2,1)}, bf16[1024,128]{1,0:T(8,128)(2,1)}, bf16[3136,128]{1,0:T(8,128)(2,1)}, /*index=5*/f32[1,5400]{1,0:T(1,128)}) custom-call(s32[4]{0:T(128)} %pad_add_fusion.1.refs_0_, ...), custom_call_target="tpu_custom_call", output_to_operand_aliasing={{4}: (3, {}), {5}: (4, {})} | custom-call | flops 2000000 | bytes 3000000 | tf_op jit(solution)/shard_map/pair/pallas_call | solution.py:625
  160.7 1.8 collective-permute-start.20
  163.8 7.6 %normed.1 = (bf16[512,1024]{1,0:T(8,128)(2,1)}, bf16[512,1024]{1,0:T(8,128)(2,1)}) custom-call(s32[1]{0:T(128)} %bitcast.21.refs_0_, bf16[1024,512]{1,0:T(8,128)(2,1)} %get-tuple-element.74.refs_1_, bf16[1024,896]{1,0:T(8,128)(2,1)} %get-tuple-element.82.refs_2_, bf16[512,1024]{1,0:T(8,128)(2,1)} %get-tuple-element.72.refs_13_.refs_3_, ...), custom_call_target="tpu_custom_call" | custom-call | flops 3000000000 | bytes 9000000 | tf_op jit(solution)/shard_map/normed/pallas_call | solution.py:625
  171.4 34.5 %all-gather.3 = f32[8,1,5400]{2,1,0:T(1,128)S(1)} all-gather(f32[1,1,5400]{2,1,0:T(1,128)S(1)} %bitcast.100), channel_id=1, replica_groups=mesh['seq'=4,'wshard'=8] {'wshard'}, dimensions={0}, use_global_device_ids=true | all-gather | bytes 194400 | tf_op jit(solution)/shard_map/all_gather | solution.py:1229
  208.6 28.0 %all-reduce.5.cloned.1.call-done = f32[21600]{0:T(1024)} async-done(((f32[21600]{0:T(1024)}), f32[21600]{0:T(1024)}) %all-reduce.5.cloned.1.call-update) | async-done | bytes 86416
  238.5 2.0 final.2.refs_1_
  241.8 6.3 %collective-permute-done.25.refs_3_ = bf16[1024,128]{1,0:T(8,128)(2,1)S(1)} collective-permute-done((bf16[1024,128]{1,0:T(8,128)(2,1)}, bf16[1024,128]{1,0:T(8,128)(2,1)S(1)}, u32[]{:S(2)}, u32[]{:S(2)}) %collective-permute-start.25) | collective-permute-done | bytes 262176 | tf_op jit(solution)/shard_map/ppermute | solution.py:1006
  249.2 3.1 %pair.3 = (bf16[784,128]{1,0:T(8,128)(2,1)}, bf16[784,128]{1,0:T(8,128)(2,1)}, bf16[784,128]{1,0:T(8,128)(2,1)}, bf16[784,128]{1,0:T(8,128)(2,1)}) custom-call(s32[4]{0:T(128)} %pad_add_fusion.1.refs_0_, bf16[3136,128]{1,0:T(8,128)(2,1)} %get-tuple-element.96.refs_1_, bf16[3136,128]{1,0:T(8,128)(2,1)} %copy-done.8, bf16[1024,128]{1,0:T(8,128)(2,1)} %copy-done.5), custom_call_target="tpu_custom_call" | custom-call | flops 2000000 | bytes 3000000 | tf_op jit(solution)/shard_map/pair/pallas_call | solution.py:625
  252.3 1.9 collective-permute-start.22
  254.1 2.4 collective-permute-start.23
  257.4 7.5 %update_gate.1 = (f32[4384,128]{1,0:T(8,128)}, f32[4384,128]{1,0:T(8,128)}, f32[4384,128]{1,0:T(8,128)}, f32[256,1024]{1,0:T(8,128)}, f32[256,1024]{1,0:T(8,128)}, /*index=5*/f32[256,1024]{1,0:T(8,128)}) custom-call(s32[4]{0:T(128)} %pad_add_fusion.2.refs_0_, bf16[1024,128]{1,0:T(8,128)(2,1)} %final.2.refs_1_, bf16[1024,128]{1,0:T(8,128)(2,1)} %copy-done.5, ...), custom_call_target="tpu_custom_call" | custom-call | flops 10000000 | bytes 13000000 | tf_op jit(solution)/shard_map/update_gate/pallas_call | solution.py:625
  264.9 6.8 %collective-permute-done.23.refs_3_ = bf16[784,128]{1,0:T(8,128)(2,1)S(1)} collective-permute-done((bf16[784,128]{1,0:T(8,128)(2,1)}, bf16[784,128]{1,0:T(8,128)(2,1)S(1)}, u32[]{:S(2)}, u32[]{:S(2)}) %collective-permute-start.23) | collective-permute-done | bytes 200736 | tf_op jit(solution)/shard_map/ppermute | solution.py:1006
  272.5 2.0 final.3.refs_1_
  275.2 1.6 convert_add_fusion
  284.5 6.9 %update_rest.1 = (f32[4384,128]{1,0:T(8,128)}, f32[4384,128]{1,0:T(8,128)}, f32[4384,128]{1,0:T(8,128)}) custom-call(s32[4]{0:T(128)} %pad_add_fusion.2.refs_0_, bf16[784,128]{1,0:T(8,128)(2,1)} %final.3.refs_1_, bf16[784,128]{1,0:T(8,128)(2,1)} %copy-done.19, ...), custom_call_target="tpu_custom_call", output_to_operand_aliasing={{0}: (8, {}), {1}: (9, {}), {2}: (10, {})} | custom-call | flops 10000000 | bytes 8000000 | tf_op jit(solution)/shard_map/update_rest/pallas_call | solution.py:625
  292.7 1.8 fusion.6
  (227 shorter events, 53.9 us)
Async XLA Ops:
  7.2 56.9 %all-gather.7.cloned.1.call-start = ((), (), s32[]{:S(2)}) async-start(), calls=%async_computation.2 | async-start | bytes 2621440 | tf_op jit(solution)/shard_map/all_gather | solution.py:1133
  7.9 71.9 %all-gather.9.cloned.1.call-start = ((), (), s32[]{:S(2)}) async-start(), calls=%async_computation.3 | async-start | bytes 2621440 | tf_op jit(solution)/shard_map/all_gather | solution.py:1134
  8.7 145.1 %reduce-scatter.2.cloned.1.call-start = ((), (), s32[]{:S(2)}) async-start(), calls=%async_computation.1 | async-start | bytes 2621440 | tf_op jit(solution)/shard_map/reduce_scatter | solution.py:1180
  11.5 12.4 %collective-permute-start.7 = (bf16[1024,128]{1,0:T(8,128)(2,1)}, bf16[1024,128]{1,0:T(8,128)(2,1)S(1)}, u32[]{:S(2)}, u32[]{:S(2)}) collective-permute-start(bf16[1024,128]{1,0:T(8,128)(2,1)} %get-tuple-element.65.refs_1_), channel_id=1, source_target_pairs={{0,2},{1,3},{2,4},{3,5},{4,6},{5,7},{6,0},{7,1},{8,10},{9,11},{10,... | collective-permute-start | bytes 786440 | tf_op jit(solution)/shard_map/ppermute | solution.py:1018
  14.5 13.4 %collective-permute-start.1 = (bf16[784,128]{1,0:T(8,128)(2,1)}, bf16[784,128]{1,0:T(8,128)(2,1)S(1)}, u32[]{:S(2)}, u32[]{:S(2)}) collective-permute-start(bf16[784,128]{1,0:T(8,128)(2,1)} %get-tuple-element.63.refs_1_), channel_id=1, source_target_pairs={{0,2},{1,3},{2,4},{3,5},{4,6},{5,7},{6,0},{7,1},{8,10},{9,11},{10,... | collective-permute-start | bytes 602120 | tf_op jit(solution)/shard_map/ppermute | solution.py:1018
  23.9 13.4 %collective-permute-start.8 = (bf16[1024,128]{1,0:T(8,128)(2,1)S(1)}, bf16[1024,128]{1,0:T(8,128)(2,1)S(1)}, u32[]{:S(2)}, u32[]{:S(2)}) collective-permute-start(bf16[1024,128]{1,0:T(8,128)(2,1)S(1)} %collective-permute-done.7.refs_2_), channel_id=1, source_target_pairs={{0,2},{1,3},{2,4},{3,5},{4,6},{5,7},{6,0},{7,1},{8,10},{9,11},{10,... | collective-permute-start | bytes 786440 | tf_op jit(solution)/shard_map/ppermute | solution.py:1018
  23.9 24.9 %collective-permute-start = (bf16[784,128]{1,0:T(8,128)(2,1)}, bf16[784,128]{1,0:T(8,128)(2,1)S(1)}, u32[]{:S(2)}, u32[]{:S(2)}) collective-permute-start(bf16[784,128]{1,0:T(8,128)(2,1)} %get-tuple-element.63.refs_1_), channel_id=1, source_target_pairs={{0,1},{1,0},{2,3},{3,2},{4,5},{5,4},{6,7},{7,6},{8,9},{9,8},{10,11... | collective-permute-start | bytes 602120 | tf_op jit(solution)/shard_map/ppermute | solution.py:1006
  27.9 9.4 %collective-permute-start.3 = (bf16[784,128]{1,0:T(8,128)(2,1)S(1)}, bf16[784,128]{1,0:T(8,128)(2,1)S(1)}, u32[]{:S(2)}, u32[]{:S(2)}) collective-permute-start(bf16[784,128]{1,0:T(8,128)(2,1)S(1)} %collective-permute-done.1.refs_3_), channel_id=1, source_target_pairs={{0,2},{1,3},{2,4},{3,5},{4,6},{5,7},{6,0},{7,1},{8,10},{9,11},{10,... | collective-permute-start | bytes 602120 | tf_op jit(solution)/shard_map/ppermute | solution.py:1018
  37.2 9.7 %collective-permute-start.5 = (bf16[784,128]{1,0:T(8,128)(2,1)S(1)}, bf16[784,128]{1,0:T(8,128)(2,1)S(1)}, u32[]{:S(2)}, u32[]{:S(2)}) collective-permute-start(bf16[784,128]{1,0:T(8,128)(2,1)S(1)} %collective-permute-done.3.refs_5_), channel_id=1, source_target_pairs={{0,2},{1,3},{2,4},{3,5},{4,6},{5,7},{6,0},{7,1},{8,10},{9,11},{10,... | collective-permute-start | bytes 602120 | tf_op jit(solution)/shard_map/ppermute | solution.py:1018
  37.3 13.7 %collective-permute-start.9 = (bf16[1024,128]{1,0:T(8,128)(2,1)S(1)}, bf16[1024,128]{1,0:T(8,128)(2,1)S(1)}, u32[]{:S(2)}, u32[]{:S(2)}) collective-permute-start(bf16[1024,128]{1,0:T(8,128)(2,1)S(1)} %collective-permute-done.8.refs_3_), channel_id=1, source_target_pairs={{0,2},{1,3},{2,4},{3,5},{4,6},{5,7},{6,0},{7,1},{8,10},{9,11},{10,... | collective-permute-start | bytes 786440 | tf_op jit(solution)/shard_map/ppermute | solution.py:1018
  39.2 9.7 %collective-permute-start.2 = (bf16[784,128]{1,0:T(8,128)(2,1)S(1)}, bf16[784,128]{1,0:T(8,128)(2,1)S(1)}, u32[]{:S(2)}, u32[]{:S(2)}) collective-permute-start(bf16[784,128]{1,0:T(8,128)(2,1)S(1)} %collective-permute-done.1.refs_3_), channel_id=1, source_target_pairs={{0,1},{1,0},{2,3},{3,2},{4,5},{5,4},{6,7},{7,6},{8,9},{9,8},{10,11... | collective-permute-start | bytes 602120 | tf_op jit(solution)/shard_map/ppermute | solution.py:1006
  40.8 10.2 %collective-permute-start.4 = (bf16[784,128]{1,0:T(8,128)(2,1)S(1)}, bf16[784,128]{1,0:T(8,128)(2,1)S(1)}, u32[]{:S(2)}, u32[]{:S(2)}) collective-permute-start(bf16[784,128]{1,0:T(8,128)(2,1)S(1)} %collective-permute-done.3.refs_5_), channel_id=1, source_target_pairs={{0,1},{1,0},{2,3},{3,2},{4,5},{5,4},{6,7},{7,6},{8,9},{9,8},{10,11... | collective-permute-start | bytes 602120 | tf_op jit(solution)/shard_map/ppermute | solution.py:1006
  47.0 6.2 %collective-permute-start.6 = (bf16[784,128]{1,0:T(8,128)(2,1)S(1)}, bf16[784,128]{1,0:T(8,128)(2,1)S(1)}, u32[]{:S(2)}, u32[]{:S(2)}) collective-permute-start(bf16[784,128]{1,0:T(8,128)(2,1)S(1)} %collective-permute-done.5.refs_7_), channel_id=1, source_target_pairs={{0,1},{1,0},{2,3},{3,2},{4,5},{5,4},{6,7},{7,6},{8,9},{9,8},{10,11... | collective-permute-start | bytes 602120 | tf_op jit(solution)/shard_map/ppermute | solution.py:1006
  56.1 23.7 %collective-permute-start.10 = (bf16[4096,128]{1,0:T(8,128)(2,1)}, bf16[4096,128]{1,0:T(8,128)(2,1)S(1)}, u32[]{:S(2)}, u32[]{:S(2)}) collective-permute-start(bf16[4096,128]{1,0:T(8,128)(2,1)} %hold.1), channel_id=1, source_target_pairs={{0,1},{1,0},{2,3},{3,2},{4,5},{5,4},{6,7},{7,6},{8,9},{9,8},{10,11... | collective-permute-start | bytes 3145736 | tf_op jit(solution)/shard_map/ppermute | solution.py:1006
  92.0 4.2 %collective-permute-start.12 = (f32[8,1024]{1,0:T(8,128)}, f32[8,1024]{1,0:T(8,128)S(1)}, u32[]{:S(2)}, u32[]{:S(2)}) collective-permute-start(f32[8,1024]{1,0:T(8,128)} %get-tuple-element.70.refs_6_), channel_id=1, source_target_pairs={{0,16},{8,24},{16,0},{24,8},{1,17},{9,25},{17,1},{25,9},{2,18},{10... | collective-permute-start | bytes 98312 | tf_op jit(solution)/shard_map/ppermute | solution.py:1006
  93.5 3.6 %collective-permute-start.13 = (f32[8,1024]{1,0:T(8,128)}, f32[8,1024]{1,0:T(8,128)S(1)}, u32[]{:S(2)}, u32[]{:S(2)}) collective-permute-start(f32[8,1024]{1,0:T(8,128)} %get-tuple-element.70.refs_6_), channel_id=1, source_target_pairs={{0,24},{8,16},{16,8},{24,0},{1,25},{9,17},{17,9},{25,1},{2,26},{10... | collective-permute-start | bytes 98312 | tf_op jit(solution)/shard_map/ppermute | solution.py:1006
  110.4 126.2 %all-reduce.5.cloned.1.call-start = ((), (), s32[]{:S(2)}) async-start(), calls=%async_computation.4 | async-start | bytes 180224
  113.1 40.7 %collective-permute-start.14 = (bf16[4096,128]{1,0:T(8,128)(2,1)S(1)}, bf16[4096,128]{1,0:T(8,128)(2,1)S(1)}, u32[]{:S(2)}, u32[]{:S(2)}) collective-permute-start(bf16[4096,128]{1,0:T(8,128)(2,1)S(1)} %copy-done.33), channel_id=1, source_target_pairs={{0,1},{1,0},{2,3},{3,2},{4,5},{5,4},{6,7},{7,6},{8,9},{9,8},{10,11... | collective-permute-start | bytes 3145736 | tf_op jit(solution)/shard_map/ppermute | solution.py:1006
  158.1 79.6 %collective-permute-start.18 = (bf16[1024,128]{1,0:T(8,128)(2,1)}, bf16[1024,128]{1,0:T(8,128)(2,1)S(1)}, u32[]{:S(2)}, u32[]{:S(2)}) collective-permute-start(bf16[1024,128]{1,0:T(8,128)(2,1)} %get-tuple-element.98), channel_id=1, source_target_pairs={{0,2},{1,3},{2,0},{3,1},{4,6},{5,7},{6,4},{7,5},{8,10},{9,11},{10,... | collective-permute-start | bytes 786440 | tf_op jit(solution)/shard_map/ppermute | solution.py:1006
  159.6 78.0 %collective-permute-start.19 = (bf16[1024,128]{1,0:T(8,128)(2,1)}, bf16[1024,128]{1,0:T(8,128)(2,1)S(1)}, u32[]{:S(2)}, u32[]{:S(2)}) collective-permute-start(bf16[1024,128]{1,0:T(8,128)(2,1)} %get-tuple-element.99), channel_id=1, source_target_pairs={{0,4},{1,5},{2,6},{3,7},{4,0},{5,1},{6,2},{7,3},{8,12},{9,13},{10,... | collective-permute-start | bytes 786440 | tf_op jit(solution)/shard_map/ppermute | solution.py:1006
  160.7 77.0 %collective-permute-start.20 = (bf16[1024,128]{1,0:T(8,128)(2,1)}, bf16[1024,128]{1,0:T(8,128)(2,1)S(1)}, u32[]{:S(2)}, u32[]{:S(2)}) collective-permute-start(bf16[1024,128]{1,0:T(8,128)(2,1)} %get-tuple-element.100), channel_id=1, source_target_pairs={{0,6},{1,7},{2,4},{3,5},{4,2},{5,3},{6,0},{7,1},{8,14},{9,15},{10,... | collective-permute-start | bytes 786440 | tf_op jit(solution)/shard_map/ppermute | solution.py:1006
  162.4 85.8 %collective-permute-start.17 = (bf16[3136,128]{1,0:T(8,128)(2,1)}, bf16[3136,128]{1,0:T(8,128)(2,1)S(1)}, u32[]{:S(2)}, u32[]{:S(2)}) collective-permute-start(bf16[3136,128]{1,0:T(8,128)(2,1)} %get-tuple-element.97), channel_id=1, source_target_pairs={{0,1},{1,0},{2,3},{3,2},{4,5},{5,4},{6,7},{7,6},{8,9},{9,8},{10,11... | collective-permute-start | bytes 2408456 | tf_op jit(solution)/shard_map/ppermute | solution.py:1006
  171.4 103.8 %collective-permute-start.15 = (bf16[512,1024]{1,0:T(8,128)(2,1)}, bf16[512,1024]{1,0:T(8,128)(2,1)}, u32[]{:S(2)}, u32[]{:S(2)}) collective-permute-start(bf16[512,1024]{1,0:T(8,128)(2,1)} %get-tuple-element.95), channel_id=1, source_target_pairs={{0,8},{8,0},{16,24},{24,16},{1,9},{9,1},{17,25},{25,17},{2,10},{10... | collective-permute-start | bytes 3145736 | tf_op jit(solution)/shard_map/ppermute | solution.py:1006
  240.6 7.6 %collective-permute-start.25 = (bf16[1024,128]{1,0:T(8,128)(2,1)}, bf16[1024,128]{1,0:T(8,128)(2,1)S(1)}, u32[]{:S(2)}, u32[]{:S(2)}) collective-permute-start(bf16[1024,128]{1,0:T(8,128)(2,1)} %final.2.refs_1_), channel_id=1, source_target_pairs={{0,16},{8,24},{16,0},{24,8},{1,17},{9,25},{17,1},{25,9},{2,18},{10... | collective-permute-start | bytes 786440 | tf_op jit(solution)/shard_map/ppermute | solution.py:1006
  241.8 6.4 %collective-permute-start.21 = (bf16[1024,128]{1,0:T(8,128)(2,1)}, bf16[1024,128]{1,0:T(8,128)(2,1)S(1)}, u32[]{:S(2)}, u32[]{:S(2)}) collective-permute-start(bf16[1024,128]{1,0:T(8,128)(2,1)} %final.2.refs_1_), channel_id=1, source_target_pairs={{0,8},{8,0},{16,24},{24,16},{1,9},{9,1},{17,25},{25,17},{2,10},{10... | collective-permute-start | bytes 786440 | tf_op jit(solution)/shard_map/ppermute | solution.py:1006
  248.2 8.5 %collective-permute-start.26 = (bf16[1024,128]{1,0:T(8,128)(2,1)S(1)}, bf16[1024,128]{1,0:T(8,128)(2,1)S(1)}, u32[]{:S(2)}, u32[]{:S(2)}) collective-permute-start(bf16[1024,128]{1,0:T(8,128)(2,1)S(1)} %collective-permute-done.25.refs_3_), channel_id=1, source_target_pairs={{0,8},{8,0},{16,24},{24,16},{1,9},{9,1},{17,25},{25,17},{2,10},{10... | collective-permute-start | bytes 786440 | tf_op jit(solution)/shard_map/ppermute | solution.py:1006
  252.3 12.6 %collective-permute-start.22 = (bf16[784,128]{1,0:T(8,128)(2,1)}, bf16[784,128]{1,0:T(8,128)(2,1)S(1)}, u32[]{:S(2)}, u32[]{:S(2)}) collective-permute-start(bf16[784,128]{1,0:T(8,128)(2,1)} %get-tuple-element.103), channel_id=1, source_target_pairs={{0,2},{1,3},{2,0},{3,1},{4,6},{5,7},{6,4},{7,5},{8,10},{9,11},{10,... | collective-permute-start | bytes 602120 | tf_op jit(solution)/shard_map/ppermute | solution.py:1006
  254.1 17.6 %collective-permute-start.23 = (bf16[784,128]{1,0:T(8,128)(2,1)}, bf16[784,128]{1,0:T(8,128)(2,1)S(1)}, u32[]{:S(2)}, u32[]{:S(2)}) collective-permute-start(bf16[784,128]{1,0:T(8,128)(2,1)} %get-tuple-element.104), channel_id=1, source_target_pairs={{0,4},{1,5},{2,6},{3,7},{4,0},{5,1},{6,2},{7,3},{8,12},{9,13},{10,... | collective-permute-start | bytes 602120 | tf_op jit(solution)/shard_map/ppermute | solution.py:1006
  256.5 15.2 %collective-permute-start.24 = (bf16[784,128]{1,0:T(8,128)(2,1)}, bf16[784,128]{1,0:T(8,128)(2,1)S(1)}, u32[]{:S(2)}, u32[]{:S(2)}) collective-permute-start(bf16[784,128]{1,0:T(8,128)(2,1)} %get-tuple-element.105), channel_id=1, source_target_pairs={{0,6},{1,7},{2,4},{3,5},{4,2},{5,3},{6,0},{7,1},{8,14},{9,15},{10,... | collective-permute-start | bytes 602120 | tf_op jit(solution)/shard_map/ppermute | solution.py:1006
  274.5 7.7 %collective-permute-start.28 = (bf16[784,128]{1,0:T(8,128)(2,1)}, bf16[784,128]{1,0:T(8,128)(2,1)}, u32[]{:S(2)}, u32[]{:S(2)}) collective-permute-start(bf16[784,128]{1,0:T(8,128)(2,1)} %final.3.refs_1_), channel_id=1, source_target_pairs={{0,16},{8,24},{16,0},{24,8},{1,17},{9,25},{17,1},{25,9},{2,18},{10... | collective-permute-start | bytes 602120 | tf_op jit(solution)/shard_map/ppermute | solution.py:1006
  277.7 14.0 %collective-permute-start.16 = (bf16[256,1024]{1,0:T(8,128)(2,1)}, bf16[256,1024]{1,0:T(8,128)(2,1)S(1)}, u32[]{:S(2)}, u32[]{:S(2)}) collective-permute-start(bf16[256,1024]{1,0:T(8,128)(2,1)} %dynamic-slice_convert_fusion), channel_id=1, source_target_pairs={{0,16},{8,24},{16,0},{24,8},{1,17},{9,25},{17,1},{25,9},{2,18},{10... | collective-permute-start | bytes 1572872 | tf_op jit(solution)/shard_map/ppermute | solution.py:1006
  280.8 2.9 collective-permute-start.27
  (45 other events, 417.8 us)
Sparse Core Ops, SparseCore 0:
  9.6 25.2 all-gather.6
  36.5 22.5 all-gather.8
  110.5 29.7 reduce-scatter.1
  207.4 29.1 all-reduce.4

commit v10 on v9

--- a/solution.py
+++ b/solution.py
@@ -14,6 +14,7 @@
 STEP = 10
 DI = 2048
 CONVCH = 2304
+VEC_ROWS = 48
 
 
 precise = lax.Precision.HIGHEST
@@ -324,16 +325,15 @@
     expand_ref,
     gain_one_ref,
     rest_weight_ref,
+    d_gain_gate_ref,
+    d_gain_two_ref,
     d_rest_ref,
-    d_kernel_ref,
-    d_conv_bias_ref,
-    d_skip_ref,
-    d_head_ref,
-    d_gain_one_ref,
+    vec_ref,
     *refs,
 ):
     grad_refs = refs[:grad_count]
-    ext, d_state, later_state, rest_sum = refs[grad_count:]
+    ext, d_state, later_state, rest_sum = refs[grad_count : grad_count + 4]
+    d_kernel_ref, d_conv_bias_ref, d_skip_ref, d_head_ref = refs[grad_count + 4 :]
     local_di = y_ref.shape[1]
     heads = local_di // HEADDIM
     chunk = pl.program_id(0)
@@ -433,7 +433,16 @@
     @pl.when(chunk == pl.num_programs(0) - 1)
     def _():
         weights = rest_weight_ref[...].astype(jnp.float32)
-        d_gain_one_ref[...] = jnp.sum(rest_sum[...] * weights, axis=0, keepdims=True)
+        d_gain_one = jnp.sum(rest_sum[...] * weights, axis=0, keepdims=True)
+        pieces = [d_gain_one + d_gain_gate_ref[...]]
+        pieces = pieces + [d_kernel_ref[tap : tap + 1, :] for tap in range(WIDTH)]
+        pieces = pieces + [d_conv_bias_ref[...], d_gain_two_ref[...], d_skip_ref[...]]
+        pieces = pieces + [d_head_ref[0:1, :], d_head_ref[1:2, :]]
+        row = 0
+        for piece in pieces:
+            for first in range(0, piece.shape[1], 128):
+                vec_ref[row : row + 1, :] = piece[:, first : first + 128]
+                row = row + 1
         rest_sum[...] = rest_sum[...] * gain_one_ref[...]
         for number, grad_ref in enumerate(grad_refs):
             columns = grad_ref.shape[1]
@@ -454,11 +463,14 @@
     return total
 
 
-def pair_kernel(count, places_ref, mine_ref, arrived_ref, *refs):
-    for number, ref in enumerate(refs[count : len(refs) - count]):
-        rows = ref.shape[0]
+def pair_kernel(count, extra, places_ref, mine_ref, arrived_ref, *refs):
+    for ref in refs[extra + count : len(refs) - count]:
+        if extra:
+            ref[ref.shape[0] - VEC_ROWS :, :] = low(refs[0][...])
+    for number, ref in enumerate(refs[extra + count : len(refs) - count]):
+        rows = ref.shape[0] - extra * VEC_ROWS
         here = pl.ds(pl.multiple_of(places_ref[number] * rows, rows), rows)
-        ref[...] = low(sum_of(mine_ref.at[here, :], arrived_ref.at[here, :]))
+        ref[:rows, :] = low(sum_of(mine_ref.at[here, :], arrived_ref.at[here, :]))
 
 
 def hold_kernel(places_ref, *refs):
@@ -467,8 +479,8 @@
         refs[-1][number * rows : (number + 1) * rows, :] = ref[...]
 
 
-def final_kernel(places_ref, *refs):
-    refs[-1][...] = low(sum_of(*refs[:-1]))
+def final_kernel(count, places_ref, one_ref, two_ref, three_ref, four_ref, *refs):
+    refs[count][...] = low(sum_of(one_ref, two_ref) + sum_of(three_ref, four_ref))
 
 
 def normed_kernel(
@@ -535,7 +547,7 @@
 def update_gate_kernel(groups, places_ref, *refs):
     blocks, in_refs, out_refs = refs[:groups], refs[groups : groups + 3], refs[groups + 3 : groups + 6]
     in_new_refs, out_new_refs = refs[groups + 6 : groups + 9], refs[groups + 9 : groups + 12]
-    (gate_out,) = refs[groups + 12 :]
+    every_ref, gate_out = refs[groups + 12 :]
     chunk = pl.program_id(0)
 
     @pl.when(chunk == 0)
@@ -543,8 +555,9 @@
         for number in range(groups):
             gate_out[places_ref[number]] = blocks[number][...]
 
+    local_di = (gate_out.shape[1] - VEC_ROWS) // 2
+    every_ref[...] = gate_out[:, 2 * local_di :, :]
     update_heads(in_refs, in_new_refs, gate_out, chunk)
-    local_di = gate_out.shape[1] // 2
     columns = gate_out.shape[2]
     for tile in range(D // columns):
         first = local_di + tile * HEADDIM
@@ -798,6 +811,8 @@
     expand,
     gain_one,
     rest_weight,
+    d_gain_gate,
+    d_gain_two,
 ):
     length, local_di = y.shape
     chunks = length // BLOCK
@@ -813,7 +828,7 @@
         places,
         [
             *[unit, conv_in, conv_pre, dt_raw, y, states, d_scanned, kernel],
-            *[*heads_vectors, expand, gain_one, rest_weight],
+            *[*heads_vectors, expand, gain_one, rest_weight, d_gain_gate, d_gain_two],
         ],
         [
             back(D),
@@ -830,23 +845,17 @@
             fixed((lanes, local_di)),
             fixed((1, D)),
             fixed((channels + lanes, D)),
+            fixed((1, D)),
+            fixed((1, local_di)),
         ],
         [
             struct((length, channels + lanes), jnp.bfloat16),
-            struct((WIDTH, channels)),
-            struct((1, channels)),
-            struct((1, local_di)),
-            struct((2, lanes)),
-            struct((1, D)),
+            struct((VEC_ROWS, 128)),
         ]
         + [struct(grad, jnp.bfloat16)] * len(places),
         [
             back(channels + lanes),
-            fixed((WIDTH, channels)),
-            fixed((1, channels)),
-            fixed((1, local_di)),
-            fixed((2, lanes)),
-            fixed((1, D)),
+            fixed((VEC_ROWS, 128)),
         ]
         + [fixed(grad)] * len(places),
         [
@@ -854,6 +863,10 @@
             pltpu.VMEM((STATE, local_di), jnp.float32),
             pltpu.VMEM((STATE, local_di), jnp.float32),
             pltpu.VMEM((channels + lanes, D), jnp.float32),
+            pltpu.VMEM((WIDTH, channels), jnp.float32),
+            pltpu.VMEM((1, channels), jnp.float32),
+            pltpu.VMEM((1, local_di), jnp.float32),
+            pltpu.VMEM((2, lanes), jnp.float32),
         ],
         chunks,
         [],
@@ -880,14 +893,16 @@
     )
 
 
-def run_pair(places, mine, arrived, through, there):
-    block = (mine.shape[0] // len(places), mine.shape[1])
+def run_pair(places, mine, arrived, extra, through, there):
+    rows = mine.shape[0] // len(places) + len(extra) * VEC_ROWS
+    block = (rows, mine.shape[1])
+    inputs = [mine, arrived, *extra]
     untouched = [pl.BlockSpec(memory_space=pl.ANY)] * len(through)
     return call(
-        lambda *refs: pair_kernel(len(through), *refs),
+        lambda *refs: pair_kernel(len(through), len(extra), *refs),
         places,
-        [mine, arrived, *through],
-        [fixed(mine.shape), fixed(arrived.shape)] + untouched,
+        [*inputs, *through],
+        [fixed(array.shape) for array in inputs] + untouched,
         [struct(block, jnp.bfloat16)] * len(places)
         + [struct(array.shape, array.dtype) for array in through],
         [fixed(block)] * len(places) + untouched,
@@ -896,7 +911,7 @@
         there,
         (2_000_000, 3_000_000, 0),
         "pair",
-        [(3 + number, len(places) + number) for number in range(len(through))],
+        [(1 + len(inputs) + number, len(places) + number) for number in range(len(through))],
     )
 
 
@@ -918,19 +933,22 @@
     )
 
 
-def run_final(terms, there):
+def run_final(terms, through, there):
+    untouched = [pl.BlockSpec(memory_space=pl.ANY)] * len(through)
     return call(
-        final_kernel,
+        lambda *refs: final_kernel(len(through), *refs),
         [jnp.int32(0)],
-        terms,
-        [fixed(array.shape) for array in terms],
-        struct(terms[0].shape, jnp.bfloat16),
-        fixed(terms[0].shape),
+        [*terms, *through],
+        [fixed(array.shape) for array in terms] + untouched,
+        [struct(terms[0].shape, jnp.bfloat16)]
+        + [struct(array.shape, array.dtype) for array in through],
+        [fixed(terms[0].shape)] + untouched,
         [],
         1,
         there,
         (500_000, 1_000_000, 0),
         "final",
+        [(1 + len(terms) + number, 1 + number) for number in range(len(through))],
     )
 
 
@@ -946,8 +964,9 @@
         places,
         [*blocks, *arrays],
         [fixed(array.shape) for array in blocks] + specs,
-        [struct(array.shape) for array in arrays],
-        specs,
+        [struct(array.shape) for array in arrays]
+        + [struct((groups, VEC_ROWS, 128), jnp.bfloat16)],
+        specs + [fixed((groups, VEC_ROWS, 128))],
         [pltpu.VMEM((groups,) + blocks[0].shape, jnp.bfloat16)],
         groups,
         there,
@@ -1110,7 +1129,7 @@
         y, z = shard_index % 2, shard_index // 2
         rest_mine, gate_out_mine = run_prepare(seq_index, in_weight.T, out_weight)
         rest = ring_blocks(rest_mine)
-        gate_out = ring_late(gate_out_mine, rest[1][1::2])
+        gate_out_late = gate_out_mine
         gate_places = [z ^ mask for mask in range(4)]
         out_places = [y, 1 - y]
     else:
@@ -1147,6 +1166,11 @@
     expand = (
         jnp.arange(lanes)[:, None] == jnp.arange(local_di)[None, :] // HEADDIM
     ).astype(jnp.float32)
+    if rings:
+        gate_out = ring_late(
+            gate_out_late,
+            rest[1][1::2] + [my_kernel, my_bias[None, :], *heads_vectors, expand],
+        )
     (
         rest_weight,
         unit_low,
@@ -1180,7 +1204,7 @@
     block_rows = lax.psum_scatter(block_part, "seq", scatter_dimension=0, tiled=True)
     if rings:
         gate_out_arrived = swap(gate_out_grads[1], "wshard", 1)
-    d_rest, d_kernel, d_conv_bias, d_skip_wide, d_head, d_gain_rest, *rest_grads = run_backward(
+    d_rest, vec_rows, *rest_grads = run_backward(
         out_places,
         unit_low,
         conv_in,
@@ -1194,29 +1218,17 @@
         expand,
         gain_one[None, :],
         rest_weight,
-    )
-    d_gain_one = d_gain_gate[0] + d_gain_rest[0]
-    shared = jnp.concatenate(
-        [d_gain_one, d_kernel[:, local_di:].reshape(-1), d_conv_bias[0, local_di:]]
-    )
-    d_skip_part = jnp.sum(d_skip_wide.reshape(local_heads, HEADDIM), axis=1)
-    apart = jnp.concatenate(
-        [
-            d_gain_two[0],
-            d_kernel[:, :local_di].reshape(-1),
-            d_conv_bias[0, :local_di],
-            d_head[:, :local_heads].reshape(-1),
-            d_skip_part,
-        ]
-    )
-    vec_part = jnp.concatenate([shared, apart])[None]
+        d_gain_gate,
+        d_gain_two,
+    )
     near, far = seq_index % 2, seq_index // 2
     if rings:
-        *gate_out_sums, rest_send, vec_part = run_pair(
+        *gate_out_sums, rest_send = run_pair(
             gate_places,
             gate_out_grads[0],
             gate_out_arrived,
-            [rest_grads[1], vec_part],
+            [vec_rows],
+            [rest_grads[1]],
             [block_rows],
         )
         rest_arrived = swap(rest_send, "wshard", 1)
@@ -1226,21 +1238,17 @@
         normed_mine, normed_send = run_normed(
             near, d_gating, d_rest, gate_weight, rest_weight, [gate_out_sums[0]]
         )
-        vec_parts = lax.all_gather(vec_part, "wshard", axis=0, tiled=True)
-        gate_out_part = run_final(
-            [gate_out_sums[0]] + gate_out_pieces, [normed_mine, vec_parts]
+        gate_out_part, normed_send = run_final(
+            [gate_out_sums[0]] + gate_out_pieces, [normed_send], []
         )
-        vec_part = jnp.sum(vec_parts, axis=0, keepdims=True)
-        every = lax.all_gather(vec_part, "seq", axis=0, tiled=True)
         gate_out_near = swap(gate_out_part, "seq", 1)
         rest_sums = run_pair(
-            gate_places, rest_grads[0], rest_arrived, [], [gate_out_near]
+            gate_places, rest_grads[0], rest_arrived, [], [], [gate_out_near]
         )
         rest_pieces = [swap(rest_sums[mask], "wshard", 2 * mask) for mask in range(1, 4)]
         gate_out_far = swap(gate_out_part, "seq", 2)
     else:
-        vec_part = lax.psum(vec_part, "wshard")
-        every = lax.all_gather(vec_part, "seq", axis=0, tiled=True)
+        every = lax.all_gather(lax.psum(vec_rows, "wshard"), "seq", axis=0, tiled=False)
         normed_mine, normed_send = run_normed(
             near, d_gating, d_rest, gate_weight, rest_weight, []
         )
@@ -1259,8 +1267,10 @@
             (out_weight, out_first, out_second),
             [rest_sums[0]],
         )
-        out_first_new, out_second_new, out_weight_new = updated[3:]
-        rest_part = run_final([rest_sums[0]] + rest_pieces, [out_first_new, every])
+        out_first_new, out_second_new, out_weight_new, every = updated[3:]
+        rest_part, every = run_final([rest_sums[0]] + rest_pieces, [every], [])
+        every_there = swap(every, "wshard", 1)
+        every = every.astype(jnp.float32) + every_there.astype(jnp.float32)
     block_out = hidden_rows.astype(jnp.float32) + block_rows.astype(jnp.float32)
     d_normed = take_block(normed_sum, far, rows_here) + normed_far.astype(jnp.float32)
     own_hidden = hidden_rows.astype(jnp.float32)
@@ -1271,36 +1281,6 @@
         d_own - own_unit * jnp.mean(d_own * own_unit, axis=-1, keepdims=True)
     )
     block_grad = cot_rows.astype(jnp.float32) + d_hidden
-    shared, every = (
-        jnp.sum(every[:, : shared.shape[0]], axis=0),
-        every[:, shared.shape[0] :],
-    )
-    kernel_end = local_di * (1 + WIDTH)
-    heads_at = kernel_end + local_di
-    both_kernel = D + 2 * STATE * WIDTH
-    vec_total = jnp.concatenate(
-        [
-            shared[:D],
-            merge_heads(every[:, :local_di], 0, HEADDIM),
-            jnp.concatenate(
-                [
-                    merge_heads(
-                        every[:, local_di:kernel_end].reshape(groups, WIDTH, local_di), 1, HEADDIM
-                    ),
-                    shared[D:both_kernel].reshape(WIDTH, 2 * STATE),
-                ],
-                1,
-            ).reshape(-1),
-            merge_heads(every[:, kernel_end:heads_at], 0, HEADDIM),
-            shared[both_kernel:],
-            merge_heads(every[:, heads_at : heads_at + local_heads], 0, 1),
-            merge_heads(every[:, heads_at + local_heads : heads_at + 2 * local_heads], 0, 1),
-            merge_heads(every[:, heads_at + 2 * local_heads :], 0, 1),
-        ]
-    )
-    vec_first_new, vec_second_new, vec_weight_new = adamw_step(
-        vec_weight, vec_first, vec_second, vec_total, vector_rate, 0.0
-    )
     if rings:
         spots, rest_blocks = seq_blocks(rest_part)
         updated = run_update_rest(spots, rest_blocks, in_arrays, updated[:3])
@@ -1326,6 +1306,35 @@
         out_first_new, out_second_new, out_weight_new = adamw_step(
             out_weight, out_first, out_second, out_total, matrix_rate, matrix_decay
         )
+    every = every.reshape(groups, VEC_ROWS * 128)
+    cuts = [0, D]
+    for extent in (WIDTH * channels, channels, local_di, local_di, lanes, lanes):
+        cuts.append(cuts[-1] + extent)
+    parts = [every[:, cuts[number] : cuts[number + 1]] for number in range(7)]
+    kernel_every = parts[1].reshape(groups, WIDTH, channels)
+    kernel_total = jnp.concatenate(
+        [
+            merge_heads(kernel_every[:, :, :local_di], 1, HEADDIM),
+            jnp.sum(kernel_every[:, :, local_di:], axis=0),
+        ],
+        1,
+    )
+    skip_every = jnp.sum(parts[4].reshape(groups, local_heads, HEADDIM), axis=2)
+    vec_total = jnp.concatenate(
+        [
+            jnp.sum(parts[0], axis=0),
+            merge_heads(parts[3], 0, HEADDIM),
+            kernel_total.reshape(-1),
+            merge_heads(parts[2][:, :local_di], 0, HEADDIM),
+            jnp.sum(parts[2][:, local_di:], axis=0),
+            merge_heads(parts[5][:, :local_heads], 0, 1),
+            merge_heads(parts[6][:, :local_heads], 0, 1),
+            merge_heads(skip_every, 0, 1),
+        ]
+    )
+    vec_first_new, vec_second_new, vec_weight_new = adamw_step(
+        vec_weight, vec_first, vec_second, vec_total, vector_rate, 0.0
+    )
     return (
         block_out.reshape(1, rows_here, D),
         block_grad.reshape(1, rows_here, D),

time: 304 us -> 248 us (0.82)
  blocking collectives: 34.5 us -> 0 us
  waiting for transfers between devices: 75.9 us -> 61.3 us
  local copies, waits for them, and re-layouts: 25.6 us -> 20.4 us
    all_gather x1 -> x0, blocking collectives: 34.5 us -> none  [shards(): vec_parts = lax.all_gather(vec_part, 'wshard', axis=0, tiled=True)]
    unnamed x5 -> x3, waiting for transfers between devices: 29.4 us -> 1.39 us
    ppermute x24 -> x25, waiting for transfers between devices: 21.7 us -> 38.9 us  [swap(): return lax.ppermute(values, axis, route)]
    ppermute x6, waiting for transfers between devices: 24.8 us -> 21 us  [ring_step(): lax.ppermute(held, 'wshard', [(i, (i + 2) % count) for i in range(count)])]
    ppermute x24 -> x25, starting transfers between devices: 22.3 us -> 25.4 us  [swap(): return lax.ppermute(values, axis, route)]
    unnamed x90 -> x73, local copies, waits for them, and re-layouts: 12 us -> 9.13 us
  transfers between devices with their start and end apart: 34 -> 34, of which waited for: 14 -> 18; matrix products, arithmetic and copies ran while one was open for 9% -> 8% of each run, Pallas kernels for 28% -> 33%
where the time goes in v10:
time: 248 us; the launch traced here: 246 us
  Pallas kernels  110 us (44%)
  waiting for transfers between devices  61.3 us (25%)
  starting transfers between devices  28.8 us (12%)
  local copies, waits for them, and re-layouts  20.4 us (8%)
  between operations  14.2 us (6%)
  other arithmetic  10.9 us (4%)
    pallas_call x13, Pallas kernels, call(): pl.pallas_call(after(kernel, 1 + len(inputs), len(arrived)), grid_spec=pl...  110 us
    ppermute x25, waiting for transfers between devices, swap(): return lax.ppermute(values, axis, route)  38.9 us
    ppermute x25, starting transfers between devices, swap(): return lax.ppermute(values, axis, route)  25.4 us
    ppermute x6, waiting for transfers between devices, ring_step(): lax.ppermute(held, 'wshard', [(i, (i + 2) % count) for i in range(count)])  21 us
    unnamed x73, local copies, waits for them, and re-layouts  9.13 us
  transfers between devices with their start and end apart: 34, of which 18 were waited for; matrix products, arithmetic and copies ran while one was open for 8% of the time, Pallas kernels for 33%

profile of v10, /device:TPU:0, one launch (start us, length us, event | category | flops | bytes accessed | tf_op | source)
XLA Modules:
  0.0 245.6 jit_solution(352530547468811498)
XLA Ops:
  8.7 2.7 %prepare.1 = (bf16[784,128]{1,0:T(8,128)(2,1)}, bf16[1024,128]{1,0:T(8,128)(2,1)}) custom-call(s32[1]{0:T(128)} %bitcast.11.refs_0_, f32[4384,128]{1,0:T(8,128)} %bitcast.74, f32[256,1024]{1,0:T(8,128)} %refs_8_.1), custom_call_target="tpu_custom_call" | custom-call | flops 100000000 | bytes 4000000 | tf_op jit(solution)/shard_map/prepare/pallas_call | solution.py:638
  11.5 3.0 %collective-permute-start = (bf16[784,128]{1,0:T(8,128)(2,1)}, bf16[784,128]{1,0:T(8,128)(2,1)S(1)}, u32[]{:S(2)}, u32[]{:S(2)}) collective-permute-start(bf16[784,128]{1,0:T(8,128)(2,1)} %get-tuple-element.63.refs_1_), channel_id=1, source_target_pairs={{0,1},{1,0},{2,3},{3,2},{4,5},{5,4},{6,7},{7,6},{8,9},{9,8},{10,11... | collective-permute-start | bytes 602120 | tf_op jit(solution)/shard_map/ppermute | solution.py:1025
  14.4 1.6 collective-permute-start.1
  17.9 6.5 %collective-permute-done.1.refs_3_ = bf16[784,128]{1,0:T(8,128)(2,1)S(1)} collective-permute-done((bf16[784,128]{1,0:T(8,128)(2,1)}, bf16[784,128]{1,0:T(8,128)(2,1)S(1)}, u32[]{:S(2)}, u32[]{:S(2)}) %collective-permute-start.1) | collective-permute-done | bytes 200736 | tf_op jit(solution)/shard_map/ppermute | solution.py:1037
  24.3 5.6 %collective-permute-done.7.refs_2_ = bf16[1024,128]{1,0:T(8,128)(2,1)S(1)} collective-permute-done((bf16[1024,128]{1,0:T(8,128)(2,1)}, bf16[1024,128]{1,0:T(8,128)(2,1)S(1)}, u32[]{:S(2)}, u32[]{:S(2)}) %collective-permute-start.7) | collective-permute-done | bytes 262176 | tf_op jit(solution)/shard_map/ppermute | solution.py:1037
  31.3 2.7 %collective-permute-done.3.refs_5_ = bf16[784,128]{1,0:T(8,128)(2,1)S(1)} collective-permute-done((bf16[784,128]{1,0:T(8,128)(2,1)S(1)}, bf16[784,128]{1,0:T(8,128)(2,1)S(1)}, u32[]{:S(2)}, u32[]{:S(2)}) %collective-permute-start.3) | collective-permute-done | bytes 200736 | tf_op jit(solution)/shard_map/ppermute | solution.py:1037
  34.6 6.1 %collective-permute-done.8.refs_3_ = bf16[1024,128]{1,0:T(8,128)(2,1)S(1)} collective-permute-done((bf16[1024,128]{1,0:T(8,128)(2,1)S(1)}, bf16[1024,128]{1,0:T(8,128)(2,1)S(1)}, u32[]{:S(2)}, u32[]{:S(2)}) %collective-permute-start.8) | collective-permute-done | bytes 262176 | tf_op jit(solution)/shard_map/ppermute | solution.py:1037
  43.4 1.6 collective-permute-start.4
  46.1 3.8 %collective-permute-done.2.refs_4_.refs_6_ = bf16[784,128]{1,0:T(8,128)(2,1)S(1)} collective-permute-done((bf16[784,128]{1,0:T(8,128)(2,1)S(1)}, bf16[784,128]{1,0:T(8,128)(2,1)S(1)}, u32[]{:S(2)}, u32[]{:S(2)}) %collective-permute-start.2) | collective-permute-done | bytes 200736 | tf_op jit(solution)/shard_map/ppermute | solution.py:1025
  49.9 2.1 collective-permute-done.4.refs_6_.refs_7_
  52.1 2.1 collective-permute-done.6.refs_8_
  55.0 2.3 hold.1
  60.4 15.7 %forward.1 = (bf16[896,1024]{1,0:T(8,128)(2,1)}, bf16[1024,1024]{1,0:T(8,128)(2,1)}, bf16[1024,1024]{1,0:T(8,128)(2,1)}, f32[1024,768]{1,0:T(8,128)}, f32[1024,7...) custom-call(s32[8]{0:T(128)} %stack.105.refs_0_, ...), custom_call_target="tpu_custom_call" | custom-call | flops 6000000000 | bytes 30000000 | tf_op jit(solution)/shard_map/forward/pallas_call | solution.py:638
  78.5 11.2 %gate.1 = (bf16[512,1024]{1,0:T(8,128)(2,1)}, bf16[512,1024]{1,0:T(8,128)(2,1)}, f32[1024,512]{1,0:T(8,128)}, f32[1024,512]{1,0:T(8,128)}, f32[8,1024]{1,0:T(8,128)}) custom-call(s32[8]{0:T(128)} %stack.107.refs_0_, bf16[1024,128]{1,0:T(8,128)(2,1)} %get-tuple-element.65.refs_1_, bf16[1024,128]{1,0:T(8,128)(2,1)} %copy-done.13, ...), custom_call_target="tpu_custom_call" | custom-call | flops 2500000000 | bytes 12000000 | tf_op jit(solution)/shard_map/gate/pallas_call | solution.py:638
  92.1 1.8 collective-permute-done.12.refs_8_
  95.4 12.6 %middle.1 = (bf16[1024,1024]{1,0:T(8,128)(2,1)}, bf16[1024,512]{1,0:T(8,128)(2,1)}, bf16[1024,512]{1,0:T(8,128)(2,1)}, f32[1,512]{1,0:T(1,128)}, f32[1,1024]{1,0...) custom-call(s32[2]{0:T(128)} %pad_add_fusion.refs_0_, ...), custom_call_target="tpu_custom_call" | custom-call | flops 4000000000 | bytes 15000000 | tf_op jit(solution)/shard_map/middle/pallas_call | solution.py:638
  109.7 32.6 %backward.1 = (bf16[1024,896]{1,0:T(8,128)(2,1)}, f32[48,128]{1,0:T(8,128)}, bf16[3136,128]{1,0:T(8,128)(2,1)}, bf16[3136,128]{1,0:T(8,128)(2,1)}) custom-call(s32[2]{0:T(128)} %pad_add_fusion.refs_0_, bf16[1024,1024]{1,0:T(8,128)(2,1)} %get-tuple-element.69.refs_5_.refs_1_, f32[1024,768]{1,0:T(8,128)} %get-tuple-element.75.refs_2_, ...), custom_call_target="tpu_custom_call" | custom-call | flops 14000000000 | bytes 40000000 | tf_op jit(solution)/shard_map/backward/pallas_call | solution.py:638
  143.3 3.4 %pair.2 = (bf16[1072,128]{1,0:T(8,128)(2,1)}, bf16[1072,128]{1,0:T(8,128)(2,1)}, bf16[1072,128]{1,0:T(8,128)(2,1)}, bf16[1072,128]{1,0:T(8,128)(2,1)}, bf16[3136,128]{1,0:T(8,128)(2,1)}) custom-call(s32[4]{0:T(128)} %pad_add_fusion.1.refs_0_, bf16[4096,128]{1,0:T(8,128)(2,1)} %get-tuple-element.85.refs_1_, ...), custom_call_target="tpu_custom_call", output_to_operand_aliasing={{4}: (4, {})} | custom-call | flops 2000000 | bytes 3000000 | tf_op jit(solution)/shard_map/pair/pallas_call | solution.py:638
  148.0 3.0 %collective-permute-start.15 = (bf16[1072,128]{1,0:T(8,128)(2,1)}, bf16[1072,128]{1,0:T(8,128)(2,1)S(1)}, u32[]{:S(2)}, u32[]{:S(2)}) collective-permute-start(bf16[1072,128]{1,0:T(8,128)(2,1)} %get-tuple-element.91), channel_id=1, source_target_pairs={{0,2},{1,3},{2,0},{3,1},{4,6},{5,7},{6,4},{7,5},{8,10},{9,11},{10,... | collective-permute-start | bytes 823304 | tf_op jit(solution)/shard_map/ppermute | solution.py:1025
  153.5 7.6 %normed.1 = (bf16[512,1024]{1,0:T(8,128)(2,1)}, bf16[512,1024]{1,0:T(8,128)(2,1)}) custom-call(s32[1]{0:T(128)} %bitcast.21.refs_0_, bf16[1024,512]{1,0:T(8,128)(2,1)} %get-tuple-element.74.refs_1_, bf16[1024,896]{1,0:T(8,128)(2,1)} %get-tuple-element.84.refs_2_, bf16[512,1024]{1,0:T(8,128)(2,1)} %get-tuple-element.72.refs_13_.refs_3_, ...), custom_call_target="tpu_custom_call" | custom-call | flops 3000000000 | bytes 9000000 | tf_op jit(solution)/shard_map/normed/pallas_call | solution.py:638
  162.5 10.9 %collective-permute-done.16.refs_3_ = bf16[1072,128]{1,0:T(8,128)(2,1)S(1)} collective-permute-done((bf16[1072,128]{1,0:T(8,128)(2,1)}, bf16[1072,128]{1,0:T(8,128)(2,1)S(1)}, u32[]{:S(2)}, u32[]{:S(2)}) %collective-permute-start.16) | collective-permute-done | bytes 274464 | tf_op jit(solution)/shard_map/ppermute | solution.py:1025
  174.2 2.1 final.2
  177.1 5.9 %collective-permute-done.25.refs_3_ = bf16[1072,128]{1,0:T(8,128)(2,1)S(1)} collective-permute-done((bf16[1072,128]{1,0:T(8,128)(2,1)}, bf16[1072,128]{1,0:T(8,128)(2,1)S(1)}, u32[]{:S(2)}, u32[]{:S(2)}) %collective-permute-start.25) | collective-permute-done | bytes 274464 | tf_op jit(solution)/shard_map/ppermute | solution.py:1025
  184.0 3.1 %pair.3 = (bf16[784,128]{1,0:T(8,128)(2,1)}, bf16[784,128]{1,0:T(8,128)(2,1)}, bf16[784,128]{1,0:T(8,128)(2,1)}, bf16[784,128]{1,0:T(8,128)(2,1)}) custom-call(s32[4]{0:T(128)} %pad_add_fusion.1.refs_0_, bf16[3136,128]{1,0:T(8,128)(2,1)} %get-tuple-element.96.refs_1_, bf16[3136,128]{1,0:T(8,128)(2,1)} %copy-done.7, bf16[1072,128]{1,0:T(8,128)(2,1)} %copy-done.3), custom_call_target="tpu_custom_call" | custom-call | flops 2000000 | bytes 3000000 | tf_op jit(solution)/shard_map/pair/pallas_call | solution.py:638
  187.1 5.1 %collective-permute-start.22 = (bf16[784,128]{1,0:T(8,128)(2,1)}, bf16[784,128]{1,0:T(8,128)(2,1)S(1)}, u32[]{:S(2)}, u32[]{:S(2)}) collective-permute-start(bf16[784,128]{1,0:T(8,128)(2,1)} %get-tuple-element.100), channel_id=1, source_target_pairs={{0,2},{1,3},{2,0},{3,1},{4,6},{5,7},{6,4},{7,5},{8,10},{9,11},{10,... | collective-permute-start | bytes 602120 | tf_op jit(solution)/shard_map/ppermute | solution.py:1025
  196.1 7.9 %update_gate.1 = (f32[4384,128]{1,0:T(8,128)}, f32[4384,128]{1,0:T(8,128)}, f32[4384,128]{1,0:T(8,128)}, f32[256,1024]{1,0:T(8,128)}, f32[256,1024]{1,0:T(8,128)...) custom-call(s32[4]{0:T(128)} %pad_add_fusion.2.refs_0_, bf16[1072,128]{1,0:T(8,128)(2,1)} %get-tuple-element.98.refs_1_, ...), custom_call_target="tpu_custom_call" | custom-call | flops 10000000 | bytes 13000000 | tf_op jit(solution)/shard_map/update_gate/pallas_call | solution.py:638
  204.0 5.7 %collective-permute-done.23.refs_3_ = bf16[784,128]{1,0:T(8,128)(2,1)S(1)} collective-permute-done((bf16[784,128]{1,0:T(8,128)(2,1)}, bf16[784,128]{1,0:T(8,128)(2,1)S(1)}, u32[]{:S(2)}, u32[]{:S(2)}) %collective-permute-start.23) | collective-permute-done | bytes 200736 | tf_op jit(solution)/shard_map/ppermute | solution.py:1025
  210.5 2.0 final.3
  214.5 2.3 collective-permute-done.30
  222.2 1.9 convert_add_fusion
  229.2 6.9 %update_rest.1 = (f32[4384,128]{1,0:T(8,128)}, f32[4384,128]{1,0:T(8,128)}, f32[4384,128]{1,0:T(8,128)}) custom-call(s32[4]{0:T(128)} %pad_add_fusion.2.refs_0_, bf16[784,128]{1,0:T(8,128)(2,1)} %get-tuple-element.104.refs_1_, bf16[784,128]{1,0:T(8,128)(2,1)} %copy-done.17, ...), custom_call_target="tpu_custom_call", output_to_operand_aliasing={{0}: (8, {}), {1}: (9, {}), {2}: (10, {})} | custom-call | flops 10000000 | bytes 8000000 | tf_op jit(solution)/shard_map/update_rest/pallas_call | solution.py:638
  237.3 1.8 fusion.6
  (200 shorter events, 47.9 us)
Async XLA Ops:
  7.2 53.2 %all-gather.5.cloned.1.call-start = ((), (), s32[]{:S(2)}) async-start(), calls=%async_computation.2 | async-start | bytes 2621440 | tf_op jit(solution)/shard_map/all_gather | solution.py:1152
  7.9 69.6 %all-gather.7.cloned.1.call-start = ((), (), s32[]{:S(2)}) async-start(), calls=%async_computation.3 | async-start | bytes 2621440 | tf_op jit(solution)/shard_map/all_gather | solution.py:1153
  8.7 133.7 %reduce-scatter.2.cloned.1.call-start = ((), (), s32[]{:S(2)}) async-start(), calls=%async_computation.1 | async-start | bytes 2621440 | tf_op jit(solution)/shard_map/reduce_scatter | solution.py:1204
  11.5 34.6 %collective-permute-start = (bf16[784,128]{1,0:T(8,128)(2,1)}, bf16[784,128]{1,0:T(8,128)(2,1)S(1)}, u32[]{:S(2)}, u32[]{:S(2)}) collective-permute-start(bf16[784,128]{1,0:T(8,128)(2,1)} %get-tuple-element.63.refs_1_), channel_id=1, source_target_pairs={{0,1},{1,0},{2,3},{3,2},{4,5},{5,4},{6,7},{7,6},{8,9},{9,8},{10,11... | collective-permute-start | bytes 602120 | tf_op jit(solution)/shard_map/ppermute | solution.py:1025
  14.4 9.9 %collective-permute-start.1 = (bf16[784,128]{1,0:T(8,128)(2,1)}, bf16[784,128]{1,0:T(8,128)(2,1)S(1)}, u32[]{:S(2)}, u32[]{:S(2)}) collective-permute-start(bf16[784,128]{1,0:T(8,128)(2,1)} %get-tuple-element.63.refs_1_), channel_id=1, source_target_pairs={{0,2},{1,3},{2,4},{3,5},{4,6},{5,7},{6,0},{7,1},{8,10},{9,11},{10,... | collective-permute-start | bytes 602120 | tf_op jit(solution)/shard_map/ppermute | solution.py:1037
  16.0 14.0 %collective-permute-start.7 = (bf16[1024,128]{1,0:T(8,128)(2,1)}, bf16[1024,128]{1,0:T(8,128)(2,1)S(1)}, u32[]{:S(2)}, u32[]{:S(2)}) collective-permute-start(bf16[1024,128]{1,0:T(8,128)(2,1)} %get-tuple-element.65.refs_1_), channel_id=1, source_target_pairs={{0,2},{1,3},{2,4},{3,5},{4,6},{5,7},{6,0},{7,1},{8,10},{9,11},{10,... | collective-permute-start | bytes 786440 | tf_op jit(solution)/shard_map/ppermute | solution.py:1037
  24.3 9.6 %collective-permute-start.3 = (bf16[784,128]{1,0:T(8,128)(2,1)S(1)}, bf16[784,128]{1,0:T(8,128)(2,1)S(1)}, u32[]{:S(2)}, u32[]{:S(2)}) collective-permute-start(bf16[784,128]{1,0:T(8,128)(2,1)S(1)} %collective-permute-done.1.refs_3_), channel_id=1, source_target_pairs={{0,2},{1,3},{2,4},{3,5},{4,6},{5,7},{6,0},{7,1},{8,10},{9,11},{10,... | collective-permute-start | bytes 602120 | tf_op jit(solution)/shard_map/ppermute | solution.py:1037
  30.0 10.8 %collective-permute-start.8 = (bf16[1024,128]{1,0:T(8,128)(2,1)S(1)}, bf16[1024,128]{1,0:T(8,128)(2,1)S(1)}, u32[]{:S(2)}, u32[]{:S(2)}) collective-permute-start(bf16[1024,128]{1,0:T(8,128)(2,1)S(1)} %collective-permute-done.7.refs_2_), channel_id=1, source_target_pairs={{0,2},{1,3},{2,4},{3,5},{4,6},{5,7},{6,0},{7,1},{8,10},{9,11},{10,... | collective-permute-start | bytes 786440 | tf_op jit(solution)/shard_map/ppermute | solution.py:1037
  34.0 11.0 %collective-permute-start.5 = (bf16[784,128]{1,0:T(8,128)(2,1)S(1)}, bf16[784,128]{1,0:T(8,128)(2,1)S(1)}, u32[]{:S(2)}, u32[]{:S(2)}) collective-permute-start(bf16[784,128]{1,0:T(8,128)(2,1)S(1)} %collective-permute-done.3.refs_5_), channel_id=1, source_target_pairs={{0,2},{1,3},{2,4},{3,5},{4,6},{5,7},{6,0},{7,1},{8,10},{9,11},{10,... | collective-permute-start | bytes 602120 | tf_op jit(solution)/shard_map/ppermute | solution.py:1037
  40.7 11.3 %collective-permute-start.9 = (bf16[1024,128]{1,0:T(8,128)(2,1)S(1)}, bf16[1024,128]{1,0:T(8,128)(2,1)S(1)}, u32[]{:S(2)}, u32[]{:S(2)}) collective-permute-start(bf16[1024,128]{1,0:T(8,128)(2,1)S(1)} %collective-permute-done.8.refs_3_), channel_id=1, source_target_pairs={{0,2},{1,3},{2,4},{3,5},{4,6},{5,7},{6,0},{7,1},{8,10},{9,11},{10,... | collective-permute-start | bytes 786440 | tf_op jit(solution)/shard_map/ppermute | solution.py:1037
  42.9 7.0 %collective-permute-start.2 = (bf16[784,128]{1,0:T(8,128)(2,1)S(1)}, bf16[784,128]{1,0:T(8,128)(2,1)S(1)}, u32[]{:S(2)}, u32[]{:S(2)}) collective-permute-start(bf16[784,128]{1,0:T(8,128)(2,1)S(1)} %collective-permute-done.1.refs_3_), channel_id=1, source_target_pairs={{0,1},{1,0},{2,3},{3,2},{4,5},{5,4},{6,7},{7,6},{8,9},{9,8},{10,11... | collective-permute-start | bytes 602120 | tf_op jit(solution)/shard_map/ppermute | solution.py:1025
  43.4 8.7 %collective-permute-start.4 = (bf16[784,128]{1,0:T(8,128)(2,1)S(1)}, bf16[784,128]{1,0:T(8,128)(2,1)S(1)}, u32[]{:S(2)}, u32[]{:S(2)}) collective-permute-start(bf16[784,128]{1,0:T(8,128)(2,1)S(1)} %collective-permute-done.3.refs_5_), channel_id=1, source_target_pairs={{0,1},{1,0},{2,3},{3,2},{4,5},{5,4},{6,7},{7,6},{8,9},{9,8},{10,11... | collective-permute-start | bytes 602120 | tf_op jit(solution)/shard_map/ppermute | solution.py:1025
  45.0 9.2 %collective-permute-start.6 = (bf16[784,128]{1,0:T(8,128)(2,1)S(1)}, bf16[784,128]{1,0:T(8,128)(2,1)S(1)}, u32[]{:S(2)}, u32[]{:S(2)}) collective-permute-start(bf16[784,128]{1,0:T(8,128)(2,1)S(1)} %collective-permute-done.5.refs_7_), channel_id=1, source_target_pairs={{0,1},{1,0},{2,3},{3,2},{4,5},{5,4},{6,7},{7,6},{8,9},{9,8},{10,11... | collective-permute-start | bytes 602120 | tf_op jit(solution)/shard_map/ppermute | solution.py:1025
  57.2 20.3 %collective-permute-start.10 = (bf16[4096,128]{1,0:T(8,128)(2,1)}, bf16[4096,128]{1,0:T(8,128)(2,1)S(1)}, u32[]{:S(2)}, u32[]{:S(2)}) collective-permute-start(bf16[4096,128]{1,0:T(8,128)(2,1)} %hold.1), channel_id=1, source_target_pairs={{0,1},{1,0},{2,3},{3,2},{4,5},{5,4},{6,7},{7,6},{8,9},{9,8},{10,11... | collective-permute-start | bytes 3145736 | tf_op jit(solution)/shard_map/ppermute | solution.py:1025
  89.7 4.2 %collective-permute-start.12 = (f32[8,1024]{1,0:T(8,128)}, f32[8,1024]{1,0:T(8,128)S(1)}, u32[]{:S(2)}, u32[]{:S(2)}) collective-permute-start(f32[8,1024]{1,0:T(8,128)} %get-tuple-element.70.refs_6_), channel_id=1, source_target_pairs={{0,16},{8,24},{16,0},{24,8},{1,17},{9,25},{17,1},{25,9},{2,18},{10... | collective-permute-start | bytes 98312 | tf_op jit(solution)/shard_map/ppermute | solution.py:1025
  91.2 3.6 %collective-permute-start.13 = (f32[8,1024]{1,0:T(8,128)}, f32[8,1024]{1,0:T(8,128)S(1)}, u32[]{:S(2)}, u32[]{:S(2)}) collective-permute-start(f32[8,1024]{1,0:T(8,128)} %get-tuple-element.70.refs_6_), channel_id=1, source_target_pairs={{0,24},{8,16},{16,8},{24,0},{1,25},{9,17},{17,9},{25,1},{2,26},{10... | collective-permute-start | bytes 98312 | tf_op jit(solution)/shard_map/ppermute | solution.py:1025
  109.2 33.2 %collective-permute-start.14 = (bf16[4096,128]{1,0:T(8,128)(2,1)S(1)}, bf16[4096,128]{1,0:T(8,128)(2,1)S(1)}, u32[]{:S(2)}, u32[]{:S(2)}) collective-permute-start(bf16[4096,128]{1,0:T(8,128)(2,1)S(1)} %copy-done.29), channel_id=1, source_target_pairs={{0,1},{1,0},{2,3},{3,2},{4,5},{5,4},{6,7},{7,6},{8,9},{9,8},{10,11... | collective-permute-start | bytes 3145736 | tf_op jit(solution)/shard_map/ppermute | solution.py:1025
  146.7 36.3 %collective-permute-start.20 = (bf16[3136,128]{1,0:T(8,128)(2,1)}, bf16[3136,128]{1,0:T(8,128)(2,1)S(1)}, u32[]{:S(2)}, u32[]{:S(2)}) collective-permute-start(bf16[3136,128]{1,0:T(8,128)(2,1)} %get-tuple-element.97), channel_id=1, source_target_pairs={{0,1},{1,0},{2,3},{3,2},{4,5},{5,4},{6,7},{7,6},{8,9},{9,8},{10,11... | collective-permute-start | bytes 2408456 | tf_op jit(solution)/shard_map/ppermute | solution.py:1025
  148.0 14.6 %collective-permute-start.15 = (bf16[1072,128]{1,0:T(8,128)(2,1)}, bf16[1072,128]{1,0:T(8,128)(2,1)S(1)}, u32[]{:S(2)}, u32[]{:S(2)}) collective-permute-start(bf16[1072,128]{1,0:T(8,128)(2,1)} %get-tuple-element.91), channel_id=1, source_target_pairs={{0,2},{1,3},{2,0},{3,1},{4,6},{5,7},{6,4},{7,5},{8,10},{9,11},{10,... | collective-permute-start | bytes 823304 | tf_op jit(solution)/shard_map/ppermute | solution.py:1025
  151.0 22.4 %collective-permute-start.16 = (bf16[1072,128]{1,0:T(8,128)(2,1)}, bf16[1072,128]{1,0:T(8,128)(2,1)S(1)}, u32[]{:S(2)}, u32[]{:S(2)}) collective-permute-start(bf16[1072,128]{1,0:T(8,128)(2,1)} %get-tuple-element.92), channel_id=1, source_target_pairs={{0,4},{1,5},{2,6},{3,7},{4,0},{5,1},{6,2},{7,3},{8,12},{9,13},{10,... | collective-permute-start | bytes 823304 | tf_op jit(solution)/shard_map/ppermute | solution.py:1025
  152.0 21.4 %collective-permute-start.17 = (bf16[1072,128]{1,0:T(8,128)(2,1)}, bf16[1072,128]{1,0:T(8,128)(2,1)S(1)}, u32[]{:S(2)}, u32[]{:S(2)}) collective-permute-start(bf16[1072,128]{1,0:T(8,128)(2,1)} %get-tuple-element.93), channel_id=1, source_target_pairs={{0,6},{1,7},{2,4},{3,5},{4,2},{5,3},{6,0},{7,1},{8,14},{9,15},{10,... | collective-permute-start | bytes 823304 | tf_op jit(solution)/shard_map/ppermute | solution.py:1025
  176.3 6.7 %collective-permute-start.25 = (bf16[1072,128]{1,0:T(8,128)(2,1)}, bf16[1072,128]{1,0:T(8,128)(2,1)S(1)}, u32[]{:S(2)}, u32[]{:S(2)}) collective-permute-start(bf16[1072,128]{1,0:T(8,128)(2,1)} %get-tuple-element.98.refs_1_), channel_id=1, source_target_pairs={{0,16},{8,24},{16,0},{24,8},{1,17},{9,25},{17,1},{25,9},{2,18},{10... | collective-permute-start | bytes 823304 | tf_op jit(solution)/shard_map/ppermute | solution.py:1025
  177.1 5.9 %collective-permute-start.21 = (bf16[1072,128]{1,0:T(8,128)(2,1)}, bf16[1072,128]{1,0:T(8,128)(2,1)S(1)}, u32[]{:S(2)}, u32[]{:S(2)}) collective-permute-start(bf16[1072,128]{1,0:T(8,128)(2,1)} %get-tuple-element.98.refs_1_), channel_id=1, source_target_pairs={{0,8},{8,0},{16,24},{24,16},{1,9},{9,1},{17,25},{25,17},{2,10},{10... | collective-permute-start | bytes 823304 | tf_op jit(solution)/shard_map/ppermute | solution.py:1025
  183.0 12.4 %collective-permute-start.26 = (bf16[1072,128]{1,0:T(8,128)(2,1)S(1)}, bf16[1072,128]{1,0:T(8,128)(2,1)S(1)}, u32[]{:S(2)}, u32[]{:S(2)}) collective-permute-start(bf16[1072,128]{1,0:T(8,128)(2,1)S(1)} %collective-permute-done.25.refs_3_), channel_id=1, source_target_pairs={{0,8},{8,0},{16,24},{24,16},{1,9},{9,1},{17,25},{25,17},{2,10},{10... | collective-permute-start | bytes 823304 | tf_op jit(solution)/shard_map/ppermute | solution.py:1025
  187.1 17.0 %collective-permute-start.22 = (bf16[784,128]{1,0:T(8,128)(2,1)}, bf16[784,128]{1,0:T(8,128)(2,1)S(1)}, u32[]{:S(2)}, u32[]{:S(2)}) collective-permute-start(bf16[784,128]{1,0:T(8,128)(2,1)} %get-tuple-element.100), channel_id=1, source_target_pairs={{0,2},{1,3},{2,0},{3,1},{4,6},{5,7},{6,4},{7,5},{8,10},{9,11},{10,... | collective-permute-start | bytes 602120 | tf_op jit(solution)/shard_map/ppermute | solution.py:1025
  192.1 17.6 %collective-permute-start.23 = (bf16[784,128]{1,0:T(8,128)(2,1)}, bf16[784,128]{1,0:T(8,128)(2,1)S(1)}, u32[]{:S(2)}, u32[]{:S(2)}) collective-permute-start(bf16[784,128]{1,0:T(8,128)(2,1)} %get-tuple-element.101), channel_id=1, source_target_pairs={{0,4},{1,5},{2,6},{3,7},{4,0},{5,1},{6,2},{7,3},{8,12},{9,13},{10,... | collective-permute-start | bytes 602120 | tf_op jit(solution)/shard_map/ppermute | solution.py:1025
  193.2 16.6 %collective-permute-start.24 = (bf16[784,128]{1,0:T(8,128)(2,1)}, bf16[784,128]{1,0:T(8,128)(2,1)S(1)}, u32[]{:S(2)}, u32[]{:S(2)}) collective-permute-start(bf16[784,128]{1,0:T(8,128)(2,1)} %get-tuple-element.102), channel_id=1, source_target_pairs={{0,6},{1,7},{2,4},{3,5},{4,2},{5,3},{6,0},{7,1},{8,14},{9,15},{10,... | collective-permute-start | bytes 602120 | tf_op jit(solution)/shard_map/ppermute | solution.py:1025
  212.5 4.3 %collective-permute-start.30 = (bf16[4,48,128]{2,1,0:T(8,128)(2,1)}, bf16[4,48,128]{2,1,0:T(8,128)(2,1)S(1)}, u32[]{:S(2)}, u32[]{:S(2)}) collective-permute-start(bf16[4,48,128]{2,1,0:T(8,128)(2,1)} %get-tuple-element.114), channel_id=1, source_target_pairs={{0,1},{1,0},{2,3},{3,2},{4,5},{5,4},{6,7},{7,6},{8,9},{9,8},{10,11... | collective-permute-start | bytes 147464 | tf_op jit(solution)/shard_map/ppermute | solution.py:1025
  213.6 7.6 %collective-permute-start.18 = (bf16[512,1024]{1,0:T(8,128)(2,1)S(1)}, bf16[512,1024]{1,0:T(8,128)(2,1)S(1)}, u32[]{:S(2)}, u32[]{:S(2)}) collective-permute-start(bf16[512,1024]{1,0:T(8,128)(2,1)S(1)} %copy-done.4), channel_id=1, source_target_pairs={{0,8},{8,0},{16,24},{24,16},{1,9},{9,1},{17,25},{25,17},{2,10},{10... | collective-permute-start | bytes 3145736 | tf_op jit(solution)/shard_map/ppermute | solution.py:1025
  213.6 14.9 %collective-permute-start.27 = (bf16[784,128]{1,0:T(8,128)(2,1)}, bf16[784,128]{1,0:T(8,128)(2,1)S(1)}, u32[]{:S(2)}, u32[]{:S(2)}) collective-permute-start(bf16[784,128]{1,0:T(8,128)(2,1)} %get-tuple-element.104.refs_1_), channel_id=1, source_target_pairs={{0,8},{8,0},{16,24},{24,16},{1,9},{9,1},{17,25},{25,17},{2,10},{10... | collective-permute-start | bytes 602120 | tf_op jit(solution)/shard_map/ppermute | solution.py:1025
  214.1 12.8 %collective-permute-start.28 = (bf16[784,128]{1,0:T(8,128)(2,1)}, bf16[784,128]{1,0:T(8,128)(2,1)}, u32[]{:S(2)}, u32[]{:S(2)}) collective-permute-start(bf16[784,128]{1,0:T(8,128)(2,1)} %get-tuple-element.104.refs_1_), channel_id=1, source_target_pairs={{0,16},{8,24},{16,0},{24,8},{1,17},{9,25},{17,1},{25,9},{2,18},{10... | collective-permute-start | bytes 602120 | tf_op jit(solution)/shard_map/ppermute | solution.py:1025
  225.0 11.6 %collective-permute-start.19 = (bf16[256,1024]{1,0:T(8,128)(2,1)}, bf16[256,1024]{1,0:T(8,128)(2,1)S(1)}, u32[]{:S(2)}, u32[]{:S(2)}) collective-permute-start(bf16[256,1024]{1,0:T(8,128)(2,1)} %dynamic-slice_convert_fusion), channel_id=1, source_target_pairs={{0,16},{8,24},{16,0},{24,8},{1,17},{9,25},{17,1},{25,9},{2,18},{10... | collective-permute-start | bytes 1572872 | tf_op jit(solution)/shard_map/ppermute | solution.py:1025
  (40 other events, 292.9 us)
Sparse Core Ops, SparseCore 0:
  9.6 25.2 all-gather.4
  36.5 22.5 all-gather.6
  108.1 31.1 reduce-scatter.1

commit v11 on v10

--- a/solution.py
+++ b/solution.py
@@ -17,7 +17,6 @@
 VEC_ROWS = 48
 
 
-precise = lax.Precision.HIGHEST
 norm_eps = 1e-05
 beta_one = 0.9
 beta_two = 0.95
@@ -62,6 +61,21 @@
     return jnp.dot(left, right, precision=precision, preferred_element_type=jnp.float32)
 
 
+def terms_of(values, count):
+    terms = []
+    for _ in range(count):
+        terms.append(values.astype(jnp.bfloat16))
+        values = values - terms[-1].astype(jnp.float32)
+    return terms
+
+
+def sum_terms(product, values, count):
+    total = None
+    for term in terms_of(values, count):
+        total = product(term) if total is None else total + product(term)
+    return total
+
+
 def sigmoid(values):
     return 1.0 / (1.0 + jnp.exp(-values))
 
@@ -79,10 +93,10 @@
     shifted = dt_raw + dt_bias
     step = jnp.maximum(shifted, 0.0) + jnp.log1p(jnp.exp(-jnp.abs(shifted)))
     log_decay = -jnp.exp(a_log) * step
-    ones = jnp.where(lower_mask(), 1.0, 0.0)
-    running = dot_nn(ones, log_decay, precise)
-    step_wide = dot_nn(step, expand, precise)
-    running_wide = dot_nn(running, expand, precise)
+    ones = low(jnp.where(lower_mask(), 1.0, 0.0))
+    running = sum_terms(lambda term: dot_nn(ones, term), log_decay, 3)
+    step_wide = sum_terms(lambda term: dot_nn(term, expand), step, 2)
+    running_wide = sum_terms(lambda term: dot_nn(term, expand), running, 3)
     return shifted, step, log_decay, running, step_wide, running_wide
 
 
@@ -223,9 +237,10 @@
     d_gnorm = dot_nt(cot_ref[...], out_ref[...])
     d_gnorm_ref[...] = d_gnorm
     gated = scanned_ref[...].astype(jnp.float32) * (gating * sigmoid(gating))
-    ones = jnp.ones((8, local_di), jnp.float32)
-    squares = dot_nt(ones, gated * gated, precise)
-    products = dot_nt(ones, d_gnorm * gain_two_ref[...] * gated, precise)
+    ones = jnp.ones((8, local_di), jnp.bfloat16)
+    squares = sum_terms(lambda term: dot_nt(ones, term), gated * gated, 2)
+    products = d_gnorm * gain_two_ref[...] * gated
+    products = sum_terms(lambda term: dot_nt(ones, term), products, 2)
     sums_ref[...] = jnp.where(
         lax.broadcasted_iota(jnp.int32, squares.shape, 0) == 0, squares, products
     )
@@ -406,10 +421,13 @@
     d_c = d_c + dot_nn(d_scores_low, b_rows)
     d_b = d_b + dot_nn(low(d_scores.T), c_rows)
     d_inner = step_wide * d_stepped + skip_ref[...] * d_y
-    d_running = dot_nt(d_y * y_ref[...] - d_stepped * stepped, expand, precise)
-    upper = jnp.where(mask_t, 1.0, 0.0)
-    d_log = dot_nn(upper, d_running, precise) + dot_nt(cross, expand, precise)
-    d_step = dot_nt(d_stepped * inner, expand, precise) - jnp.exp(a_log) * d_log
+    d_running = d_y * y_ref[...] - d_stepped * stepped
+    d_running = sum_terms(lambda term: dot_nt(term, expand), d_running, 2)
+    upper = low(jnp.where(mask_t, 1.0, 0.0))
+    d_log = sum_terms(lambda term: dot_nn(upper, term), d_running, 3)
+    d_log = d_log + sum_terms(lambda term: dot_nt(term, expand), cross, 3)
+    d_step = sum_terms(lambda term: dot_nt(term, expand), d_stepped * inner, 2)
+    d_step = d_step - jnp.exp(a_log) * d_log
     d_dt = d_step * sigmoid(shifted)
     d_head_ref[0:1, :] += jnp.sum(d_log * log_decay, axis=0, keepdims=True)
     d_head_ref[1:2, :] += jnp.sum(d_dt, axis=0, keepdims=True)
@@ -915,12 +933,12 @@
     )
 
 
-def run_hold(blocks, there):
+def run_hold(places, blocks, there):
     rows, columns = blocks[0].shape
     shape = (rows * len(blocks), columns)
     return call(
         hold_kernel,
-        [jnp.int32(0)],
+        places,
         blocks,
         [fixed(block.shape) for block in blocks],
         struct(shape, blocks[0].dtype),
@@ -1050,14 +1068,14 @@
     return places, blocks
 
 
-def ring_late(rows, arrived):
+def ring_late(hold_places, rows, arrived):
     count = lax.axis_size("wshard")
     index = lax.axis_index("wshard")
     places = [(index + count - 2 * step) % count for step in range(count // 2)]
     blocks = [rows]
     for _ in range(count // 2 - 1):
         blocks = blocks + [ring_step(blocks[-1])]
-    swapped = swap(run_hold(blocks, arrived), "wshard", 1)
+    swapped = swap(run_hold(hold_places, blocks, arrived), "wshard", 1)
     return places + [place ^ 1 for place in places], blocks + [swapped]
 
 
@@ -1165,9 +1183,10 @@
     )
     expand = (
         jnp.arange(lanes)[:, None] == jnp.arange(local_di)[None, :] // HEADDIM
-    ).astype(jnp.float32)
+    ).astype(jnp.bfloat16)
     if rings:
         gate_out = ring_late(
+            rest[0],
             gate_out_late,
             rest[1][1::2] + [my_kernel, my_bias[None, :], *heads_vectors, expand],
         )

time: 248 us -> 242 us (0.976)
  Pallas kernels: 110 us -> 100 us
  waiting for transfers between devices: 61.3 us -> 66.3 us
    pallas_call x13, Pallas kernels: 110 us -> 100 us  [call(): pl.pallas_call(after(kernel, 1 + len(inputs), len(arrived)), grid_spec=pl...]
    reduce_scatter x1, waiting for transfers between devices: 0.02 us -> 2.96 us  [shards(): lax.psum_scatter(block_part, 'seq', scatter_dimension=0, tiled=True)]
  transfers between devices with their start and end apart: 34 -> 34, of which waited for: 18 -> 18; matrix products, arithmetic and copies ran while one was open for 8% -> 8% of each run, Pallas kernels for 33% -> 31%
where the time goes in v11:
time: 242 us; the launch traced here: 239 us
  Pallas kernels  100 us (41%)
  waiting for transfers between devices  66.3 us (27%)
  starting transfers between devices  27.7 us (11%)
  local copies, waits for them, and re-layouts  19.3 us (8%)
  between operations  14.2 us (6%)
  other arithmetic  11 us (5%)
    pallas_call x13, Pallas kernels, call(): pl.pallas_call(after(kernel, 1 + len(inputs), len(arrived)), grid_spec=pl...  100 us
    ppermute x25, waiting for transfers between devices, swap(): return lax.ppermute(values, axis, route)  41 us
    ppermute x25, starting transfers between devices, swap(): return lax.ppermute(values, axis, route)  24.4 us
    ppermute x6, waiting for transfers between devices, ring_step(): lax.ppermute(held, 'wshard', [(i, (i + 2) % count) for i in range(count)])  20.9 us
    unnamed x73, local copies, waits for them, and re-layouts  8.18 us
  transfers between devices with their start and end apart: 34, of which 18 were waited for; matrix products, arithmetic and copies ran while one was open for 8% of the time, Pallas kernels for 31%

profile of v11, /device:TPU:0, one launch (start us, length us, event | category | flops | bytes accessed | tf_op | source)
XLA Modules:
  0.0 238.9 jit_solution(14886389498256541703)
XLA Ops:
  8.7 2.7 %prepare.1 = (bf16[784,128]{1,0:T(8,128)(2,1)}, bf16[1024,128]{1,0:T(8,128)(2,1)}) custom-call(s32[1]{0:T(128)} %bitcast.11.refs_0_, f32[4384,128]{1,0:T(8,128)} %bitcast.74, f32[256,1024]{1,0:T(8,128)} %refs_8_.1), custom_call_target="tpu_custom_call" | custom-call | flops 100000000 | bytes 4000000 | tf_op jit(solution)/shard_map/prepare/pallas_call | solution.py:656
  11.5 3.0 %collective-permute-start = (bf16[784,128]{1,0:T(8,128)(2,1)}, bf16[784,128]{1,0:T(8,128)(2,1)S(1)}, u32[]{:S(2)}, u32[]{:S(2)}) collective-permute-start(bf16[784,128]{1,0:T(8,128)(2,1)} %get-tuple-element.63.refs_1_), channel_id=1, source_target_pairs={{0,1},{1,0},{2,3},{3,2},{4,5},{5,4},{6,7},{7,6},{8,9},{9,8},{10,11... | collective-permute-start | bytes 602120 | tf_op jit(solution)/shard_map/ppermute | solution.py:1043
  17.9 6.5 %collective-permute-done.1.refs_3_ = bf16[784,128]{1,0:T(8,128)(2,1)S(1)} collective-permute-done((bf16[784,128]{1,0:T(8,128)(2,1)}, bf16[784,128]{1,0:T(8,128)(2,1)S(1)}, u32[]{:S(2)}, u32[]{:S(2)}) %collective-permute-start.1) | collective-permute-done | bytes 200736 | tf_op jit(solution)/shard_map/ppermute | solution.py:1055
  24.3 5.6 %collective-permute-done.7.refs_2_ = bf16[1024,128]{1,0:T(8,128)(2,1)S(1)} collective-permute-done((bf16[1024,128]{1,0:T(8,128)(2,1)}, bf16[1024,128]{1,0:T(8,128)(2,1)S(1)}, u32[]{:S(2)}, u32[]{:S(2)}) %collective-permute-start.7) | collective-permute-done | bytes 262176 | tf_op jit(solution)/shard_map/ppermute | solution.py:1055
  31.3 2.7 %collective-permute-done.3.refs_5_ = bf16[784,128]{1,0:T(8,128)(2,1)S(1)} collective-permute-done((bf16[784,128]{1,0:T(8,128)(2,1)S(1)}, bf16[784,128]{1,0:T(8,128)(2,1)S(1)}, u32[]{:S(2)}, u32[]{:S(2)}) %collective-permute-start.3) | collective-permute-done | bytes 200736 | tf_op jit(solution)/shard_map/ppermute | solution.py:1055
  34.6 6.1 %collective-permute-done.8.refs_3_ = bf16[1024,128]{1,0:T(8,128)(2,1)S(1)} collective-permute-done((bf16[1024,128]{1,0:T(8,128)(2,1)S(1)}, bf16[1024,128]{1,0:T(8,128)(2,1)S(1)}, u32[]{:S(2)}, u32[]{:S(2)}) %collective-permute-start.8) | collective-permute-done | bytes 262176 | tf_op jit(solution)/shard_map/ppermute | solution.py:1055
  46.6 3.8 %collective-permute-done.2.refs_4_.refs_6_ = bf16[784,128]{1,0:T(8,128)(2,1)S(1)} collective-permute-done((bf16[784,128]{1,0:T(8,128)(2,1)S(1)}, bf16[784,128]{1,0:T(8,128)(2,1)S(1)}, u32[]{:S(2)}, u32[]{:S(2)}) %collective-permute-start.2) | collective-permute-done | bytes 200736 | tf_op jit(solution)/shard_map/ppermute | solution.py:1043
  50.4 2.1 collective-permute-done.4.refs_6_.refs_7_
  52.6 2.1 collective-permute-done.6.refs_8_
  55.5 2.9 %hold.1 = bf16[4096,128]{1,0:T(8,128)(2,1)} custom-call(s32[8]{0:T(128)} %stack.114.refs_0_, bf16[1024,128]{1,0:T(8,128)(2,1)} %get-tuple-element.65.refs_1_, bf16[1024,128]{1,0:T(8,128)(2,1)} %copy-done.13, bf16[1024,128]{1,0:T(8,128)(2,1)} %copy-done.14, bf16[1024,128]{1,0:T(8,128)(2,1)} %copy-done.15, bf16[784,128]{1,0:T(8,128)(2,1)} %copy-done.19, ...), custom_call_target="tpu_custom_call" | custom-call | bytes 2000000 | tf_op jit(solution)/shard_map/hold/pallas_call | solution.py:656
  60.9 14.1 %forward.1 = (bf16[896,1024]{1,0:T(8,128)(2,1)}, bf16[1024,1024]{1,0:T(8,128)(2,1)}, bf16[1024,1024]{1,0:T(8,128)(2,1)}, f32[1024,768]{1,0:T(8,128)}, f32[1024,7...) custom-call(s32[8]{0:T(128)} %stack.114.refs_0_, ...), custom_call_target="tpu_custom_call" | custom-call | flops 6000000000 | bytes 30000000 | tf_op jit(solution)/shard_map/forward/pallas_call | solution.py:656
  75.0 3.7 %collective-permute-done.10.refs_5_ = bf16[4096,128]{1,0:T(8,128)(2,1)S(1)} collective-permute-done((bf16[4096,128]{1,0:T(8,128)(2,1)}, bf16[4096,128]{1,0:T(8,128)(2,1)S(1)}, u32[]{:S(2)}, u32[]{:S(2)}) %collective-permute-start.10) | collective-permute-done | bytes 1048608 | tf_op jit(solution)/shard_map/ppermute | solution.py:1043
  79.6 8.6 %gate.1 = (bf16[512,1024]{1,0:T(8,128)(2,1)}, bf16[512,1024]{1,0:T(8,128)(2,1)}, f32[1024,512]{1,0:T(8,128)}, f32[1024,512]{1,0:T(8,128)}, f32[8,1024]{1,0:T(8,128)}) custom-call(s32[8]{0:T(128)} %stack.116.refs_0_, bf16[1024,128]{1,0:T(8,128)(2,1)} %get-tuple-element.65.refs_1_, bf16[1024,128]{1,0:T(8,128)(2,1)} %copy-done.13, ...), custom_call_target="tpu_custom_call" | custom-call | flops 2500000000 | bytes 12000000 | tf_op jit(solution)/shard_map/gate/pallas_call | solution.py:656
  90.8 1.7 collective-permute-done.12.refs_8_
  94.0 12.6 %middle.1 = (bf16[1024,1024]{1,0:T(8,128)(2,1)}, bf16[1024,512]{1,0:T(8,128)(2,1)}, bf16[1024,512]{1,0:T(8,128)(2,1)}, f32[1,512]{1,0:T(1,128)}, f32[1,1024]{1,0...) custom-call(s32[2]{0:T(128)} %pad_add_fusion.refs_0_, ...), custom_call_target="tpu_custom_call" | custom-call | flops 4000000000 | bytes 15000000 | tf_op jit(solution)/shard_map/middle/pallas_call | solution.py:656
  108.3 26.7 %backward.1 = (bf16[1024,896]{1,0:T(8,128)(2,1)}, f32[48,128]{1,0:T(8,128)}, bf16[3136,128]{1,0:T(8,128)(2,1)}, bf16[3136,128]{1,0:T(8,128)(2,1)}) custom-call(s32[2]{0:T(128)} %pad_add_fusion.refs_0_, bf16[1024,1024]{1,0:T(8,128)(2,1)} %get-tuple-element.69.refs_5_.refs_1_, f32[1024,768]{1,0:T(8,128)} %get-tuple-element.75.refs_2_, ...), custom_call_target="tpu_custom_call" | custom-call | flops 14000000000 | bytes 40000000 | tf_op jit(solution)/shard_map/backward/pallas_call | solution.py:656
  135.0 3.0 %reduce-scatter.2.cloned.1.call-done.refs_5_ = bf16[256,1024]{1,0:T(8,128)(2,1)} async-done(((bf16[1024,1024]{1,0:T(8,128)(2,1)}), bf16[256,1024]{1,0:T(8,128)(2,1)}) %reduce-scatter.2.cloned.1.call-update) | async-done | bytes 524304 | tf_op jit(solution)/shard_map/reduce_scatter | solution.py:1223
  138.0 3.4 %pair.2 = (bf16[1072,128]{1,0:T(8,128)(2,1)}, bf16[1072,128]{1,0:T(8,128)(2,1)}, bf16[1072,128]{1,0:T(8,128)(2,1)}, bf16[1072,128]{1,0:T(8,128)(2,1)}, bf16[3136,128]{1,0:T(8,128)(2,1)}) custom-call(s32[4]{0:T(128)} %pad_add_fusion.1.refs_0_, bf16[4096,128]{1,0:T(8,128)(2,1)} %get-tuple-element.85.refs_1_, ...), custom_call_target="tpu_custom_call", output_to_operand_aliasing={{4}: (4, {})} | custom-call | flops 2000000 | bytes 3000000 | tf_op jit(solution)/shard_map/pair/pallas_call | solution.py:656
  144.3 2.4 %collective-permute-start.16 = (bf16[1072,128]{1,0:T(8,128)(2,1)}, bf16[1072,128]{1,0:T(8,128)(2,1)S(1)}, u32[]{:S(2)}, u32[]{:S(2)}) collective-permute-start(bf16[1072,128]{1,0:T(8,128)(2,1)} %get-tuple-element.92), channel_id=1, source_target_pairs={{0,4},{1,5},{2,6},{3,7},{4,0},{5,1},{6,2},{7,3},{8,12},{9,13},{10,... | collective-permute-start | bytes 823304 | tf_op jit(solution)/shard_map/ppermute | solution.py:1043
  147.2 7.6 %normed.1 = (bf16[512,1024]{1,0:T(8,128)(2,1)}, bf16[512,1024]{1,0:T(8,128)(2,1)}) custom-call(s32[1]{0:T(128)} %bitcast.21.refs_0_, bf16[1024,512]{1,0:T(8,128)(2,1)} %get-tuple-element.74.refs_1_, bf16[1024,896]{1,0:T(8,128)(2,1)} %get-tuple-element.84.refs_2_, bf16[512,1024]{1,0:T(8,128)(2,1)} %get-tuple-element.72.refs_13_.refs_3_, ...), custom_call_target="tpu_custom_call" | custom-call | flops 3000000000 | bytes 9000000 | tf_op jit(solution)/shard_map/normed/pallas_call | solution.py:656
  156.0 10.7 %collective-permute-done.16.refs_3_ = bf16[1072,128]{1,0:T(8,128)(2,1)S(1)} collective-permute-done((bf16[1072,128]{1,0:T(8,128)(2,1)}, bf16[1072,128]{1,0:T(8,128)(2,1)S(1)}, u32[]{:S(2)}, u32[]{:S(2)}) %collective-permute-start.16) | collective-permute-done | bytes 274464 | tf_op jit(solution)/shard_map/ppermute | solution.py:1043
  167.5 2.1 final.2
  170.1 6.1 %collective-permute-done.25.refs_3_ = bf16[1072,128]{1,0:T(8,128)(2,1)S(1)} collective-permute-done((bf16[1072,128]{1,0:T(8,128)(2,1)}, bf16[1072,128]{1,0:T(8,128)(2,1)S(1)}, u32[]{:S(2)}, u32[]{:S(2)}) %collective-permute-start.25) | collective-permute-done | bytes 274464 | tf_op jit(solution)/shard_map/ppermute | solution.py:1043
  177.3 3.1 %pair.3 = (bf16[784,128]{1,0:T(8,128)(2,1)}, bf16[784,128]{1,0:T(8,128)(2,1)}, bf16[784,128]{1,0:T(8,128)(2,1)}, bf16[784,128]{1,0:T(8,128)(2,1)}) custom-call(s32[4]{0:T(128)} %pad_add_fusion.1.refs_0_, bf16[3136,128]{1,0:T(8,128)(2,1)} %get-tuple-element.96.refs_1_, bf16[3136,128]{1,0:T(8,128)(2,1)} %copy-done.7, bf16[1072,128]{1,0:T(8,128)(2,1)} %copy-done.3), custom_call_target="tpu_custom_call" | custom-call | flops 2000000 | bytes 3000000 | tf_op jit(solution)/shard_map/pair/pallas_call | solution.py:656
  180.3 5.0 %collective-permute-start.22 = (bf16[784,128]{1,0:T(8,128)(2,1)}, bf16[784,128]{1,0:T(8,128)(2,1)S(1)}, u32[]{:S(2)}, u32[]{:S(2)}) collective-permute-start(bf16[784,128]{1,0:T(8,128)(2,1)} %get-tuple-element.100), channel_id=1, source_target_pairs={{0,2},{1,3},{2,0},{3,1},{4,6},{5,7},{6,4},{7,5},{8,10},{9,11},{10,... | collective-permute-start | bytes 602120 | tf_op jit(solution)/shard_map/ppermute | solution.py:1043
  189.3 7.7 %update_gate.1 = (f32[4384,128]{1,0:T(8,128)}, f32[4384,128]{1,0:T(8,128)}, f32[4384,128]{1,0:T(8,128)}, f32[256,1024]{1,0:T(8,128)}, f32[256,1024]{1,0:T(8,128)...) custom-call(s32[4]{0:T(128)} %pad_add_fusion.2.refs_0_, bf16[1072,128]{1,0:T(8,128)(2,1)} %get-tuple-element.98.refs_1_, ...), custom_call_target="tpu_custom_call" | custom-call | flops 10000000 | bytes 13000000 | tf_op jit(solution)/shard_map/update_gate/pallas_call | solution.py:656
  197.0 5.9 %collective-permute-done.23.refs_3_ = bf16[784,128]{1,0:T(8,128)(2,1)S(1)} collective-permute-done((bf16[784,128]{1,0:T(8,128)(2,1)}, bf16[784,128]{1,0:T(8,128)(2,1)S(1)}, u32[]{:S(2)}, u32[]{:S(2)}) %collective-permute-start.23) | collective-permute-done | bytes 200736 | tf_op jit(solution)/shard_map/ppermute | solution.py:1043
  203.7 2.0 final.3
  207.9 2.1 collective-permute-done.30
  215.4 1.9 convert_add_fusion
  222.4 6.9 %update_rest.1 = (f32[4384,128]{1,0:T(8,128)}, f32[4384,128]{1,0:T(8,128)}, f32[4384,128]{1,0:T(8,128)}) custom-call(s32[4]{0:T(128)} %pad_add_fusion.2.refs_0_, bf16[784,128]{1,0:T(8,128)(2,1)} %get-tuple-element.104.refs_1_, bf16[784,128]{1,0:T(8,128)(2,1)} %copy-done.17, ...), custom_call_target="tpu_custom_call", output_to_operand_aliasing={{0}: (8, {}), {1}: (9, {}), {2}: (10, {})} | custom-call | flops 10000000 | bytes 8000000 | tf_op jit(solution)/shard_map/update_rest/pallas_call | solution.py:656
  230.6 1.8 fusion.6
  (200 shorter events, 48.1 us)
Async XLA Ops:
  7.2 53.7 %all-gather.5.cloned.1.call-start = ((), (), s32[]{:S(2)}) async-start(), calls=%async_computation.2 | async-start | bytes 2621440 | tf_op jit(solution)/shard_map/all_gather | solution.py:1170
  7.9 70.7 %all-gather.7.cloned.1.call-start = ((), (), s32[]{:S(2)}) async-start(), calls=%async_computation.3 | async-start | bytes 2621440 | tf_op jit(solution)/shard_map/all_gather | solution.py:1171
  8.7 129.3 %reduce-scatter.2.cloned.1.call-start = ((), (), s32[]{:S(2)}) async-start(), calls=%async_computation.1 | async-start | bytes 2621440 | tf_op jit(solution)/shard_map/reduce_scatter | solution.py:1223
  11.5 35.1 %collective-permute-start = (bf16[784,128]{1,0:T(8,128)(2,1)}, bf16[784,128]{1,0:T(8,128)(2,1)S(1)}, u32[]{:S(2)}, u32[]{:S(2)}) collective-permute-start(bf16[784,128]{1,0:T(8,128)(2,1)} %get-tuple-element.63.refs_1_), channel_id=1, source_target_pairs={{0,1},{1,0},{2,3},{3,2},{4,5},{5,4},{6,7},{7,6},{8,9},{9,8},{10,11... | collective-permute-start | bytes 602120 | tf_op jit(solution)/shard_map/ppermute | solution.py:1043
  14.4 9.9 %collective-permute-start.1 = (bf16[784,128]{1,0:T(8,128)(2,1)}, bf16[784,128]{1,0:T(8,128)(2,1)S(1)}, u32[]{:S(2)}, u32[]{:S(2)}) collective-permute-start(bf16[784,128]{1,0:T(8,128)(2,1)} %get-tuple-element.63.refs_1_), channel_id=1, source_target_pairs={{0,2},{1,3},{2,4},{3,5},{4,6},{5,7},{6,0},{7,1},{8,10},{9,11},{10,... | collective-permute-start | bytes 602120 | tf_op jit(solution)/shard_map/ppermute | solution.py:1055
  16.0 14.0 %collective-permute-start.7 = (bf16[1024,128]{1,0:T(8,128)(2,1)}, bf16[1024,128]{1,0:T(8,128)(2,1)S(1)}, u32[]{:S(2)}, u32[]{:S(2)}) collective-permute-start(bf16[1024,128]{1,0:T(8,128)(2,1)} %get-tuple-element.65.refs_1_), channel_id=1, source_target_pairs={{0,2},{1,3},{2,4},{3,5},{4,6},{5,7},{6,0},{7,1},{8,10},{9,11},{10,... | collective-permute-start | bytes 786440 | tf_op jit(solution)/shard_map/ppermute | solution.py:1055
  24.3 9.6 %collective-permute-start.3 = (bf16[784,128]{1,0:T(8,128)(2,1)S(1)}, bf16[784,128]{1,0:T(8,128)(2,1)S(1)}, u32[]{:S(2)}, u32[]{:S(2)}) collective-permute-start(bf16[784,128]{1,0:T(8,128)(2,1)S(1)} %collective-permute-done.1.refs_3_), channel_id=1, source_target_pairs={{0,2},{1,3},{2,4},{3,5},{4,6},{5,7},{6,0},{7,1},{8,10},{9,11},{10,... | collective-permute-start | bytes 602120 | tf_op jit(solution)/shard_map/ppermute | solution.py:1055
  30.0 10.8 %collective-permute-start.8 = (bf16[1024,128]{1,0:T(8,128)(2,1)S(1)}, bf16[1024,128]{1,0:T(8,128)(2,1)S(1)}, u32[]{:S(2)}, u32[]{:S(2)}) collective-permute-start(bf16[1024,128]{1,0:T(8,128)(2,1)S(1)} %collective-permute-done.7.refs_2_), channel_id=1, source_target_pairs={{0,2},{1,3},{2,4},{3,5},{4,6},{5,7},{6,0},{7,1},{8,10},{9,11},{10,... | collective-permute-start | bytes 786440 | tf_op jit(solution)/shard_map/ppermute | solution.py:1055
  34.0 11.5 %collective-permute-start.5 = (bf16[784,128]{1,0:T(8,128)(2,1)S(1)}, bf16[784,128]{1,0:T(8,128)(2,1)S(1)}, u32[]{:S(2)}, u32[]{:S(2)}) collective-permute-start(bf16[784,128]{1,0:T(8,128)(2,1)S(1)} %collective-permute-done.3.refs_5_), channel_id=1, source_target_pairs={{0,2},{1,3},{2,4},{3,5},{4,6},{5,7},{6,0},{7,1},{8,10},{9,11},{10,... | collective-permute-start | bytes 602120 | tf_op jit(solution)/shard_map/ppermute | solution.py:1055
  40.7 11.9 %collective-permute-start.9 = (bf16[1024,128]{1,0:T(8,128)(2,1)S(1)}, bf16[1024,128]{1,0:T(8,128)(2,1)S(1)}, u32[]{:S(2)}, u32[]{:S(2)}) collective-permute-start(bf16[1024,128]{1,0:T(8,128)(2,1)S(1)} %collective-permute-done.8.refs_3_), channel_id=1, source_target_pairs={{0,2},{1,3},{2,4},{3,5},{4,6},{5,7},{6,0},{7,1},{8,10},{9,11},{10,... | collective-permute-start | bytes 786440 | tf_op jit(solution)/shard_map/ppermute | solution.py:1055
  43.4 7.0 %collective-permute-start.2 = (bf16[784,128]{1,0:T(8,128)(2,1)S(1)}, bf16[784,128]{1,0:T(8,128)(2,1)S(1)}, u32[]{:S(2)}, u32[]{:S(2)}) collective-permute-start(bf16[784,128]{1,0:T(8,128)(2,1)S(1)} %collective-permute-done.1.refs_3_), channel_id=1, source_target_pairs={{0,1},{1,0},{2,3},{3,2},{4,5},{5,4},{6,7},{7,6},{8,9},{9,8},{10,11... | collective-permute-start | bytes 602120 | tf_op jit(solution)/shard_map/ppermute | solution.py:1043
  43.9 8.7 %collective-permute-start.4 = (bf16[784,128]{1,0:T(8,128)(2,1)S(1)}, bf16[784,128]{1,0:T(8,128)(2,1)S(1)}, u32[]{:S(2)}, u32[]{:S(2)}) collective-permute-start(bf16[784,128]{1,0:T(8,128)(2,1)S(1)} %collective-permute-done.3.refs_5_), channel_id=1, source_target_pairs={{0,1},{1,0},{2,3},{3,2},{4,5},{5,4},{6,7},{7,6},{8,9},{9,8},{10,11... | collective-permute-start | bytes 602120 | tf_op jit(solution)/shard_map/ppermute | solution.py:1043
  45.5 9.3 %collective-permute-start.6 = (bf16[784,128]{1,0:T(8,128)(2,1)S(1)}, bf16[784,128]{1,0:T(8,128)(2,1)S(1)}, u32[]{:S(2)}, u32[]{:S(2)}) collective-permute-start(bf16[784,128]{1,0:T(8,128)(2,1)S(1)} %collective-permute-done.5.refs_7_), channel_id=1, source_target_pairs={{0,1},{1,0},{2,3},{3,2},{4,5},{5,4},{6,7},{7,6},{8,9},{9,8},{10,11... | collective-permute-start | bytes 602120 | tf_op jit(solution)/shard_map/ppermute | solution.py:1043
  58.4 20.3 %collective-permute-start.10 = (bf16[4096,128]{1,0:T(8,128)(2,1)}, bf16[4096,128]{1,0:T(8,128)(2,1)S(1)}, u32[]{:S(2)}, u32[]{:S(2)}) collective-permute-start(bf16[4096,128]{1,0:T(8,128)(2,1)} %hold.1), channel_id=1, source_target_pairs={{0,1},{1,0},{2,3},{3,2},{4,5},{5,4},{6,7},{7,6},{8,9},{9,8},{10,11... | collective-permute-start | bytes 3145736 | tf_op jit(solution)/shard_map/ppermute | solution.py:1043
  88.3 4.2 %collective-permute-start.12 = (f32[8,1024]{1,0:T(8,128)}, f32[8,1024]{1,0:T(8,128)S(1)}, u32[]{:S(2)}, u32[]{:S(2)}) collective-permute-start(f32[8,1024]{1,0:T(8,128)} %get-tuple-element.70.refs_6_), channel_id=1, source_target_pairs={{0,16},{8,24},{16,0},{24,8},{1,17},{9,25},{17,1},{25,9},{2,18},{10... | collective-permute-start | bytes 98312 | tf_op jit(solution)/shard_map/ppermute | solution.py:1043
  89.9 3.6 %collective-permute-start.13 = (f32[8,1024]{1,0:T(8,128)}, f32[8,1024]{1,0:T(8,128)S(1)}, u32[]{:S(2)}, u32[]{:S(2)}) collective-permute-start(f32[8,1024]{1,0:T(8,128)} %get-tuple-element.70.refs_6_), channel_id=1, source_target_pairs={{0,24},{8,16},{16,8},{24,0},{1,25},{9,17},{17,9},{25,1},{2,26},{10... | collective-permute-start | bytes 98312 | tf_op jit(solution)/shard_map/ppermute | solution.py:1043
  107.8 27.2 %collective-permute-start.14 = (bf16[4096,128]{1,0:T(8,128)(2,1)S(1)}, bf16[4096,128]{1,0:T(8,128)(2,1)S(1)}, u32[]{:S(2)}, u32[]{:S(2)}) collective-permute-start(bf16[4096,128]{1,0:T(8,128)(2,1)S(1)} %copy-done.29), channel_id=1, source_target_pairs={{0,1},{1,0},{2,3},{3,2},{4,5},{5,4},{6,7},{7,6},{8,9},{9,8},{10,11... | collective-permute-start | bytes 3145736 | tf_op jit(solution)/shard_map/ppermute | solution.py:1043
  141.4 34.9 %collective-permute-start.20 = (bf16[3136,128]{1,0:T(8,128)(2,1)}, bf16[3136,128]{1,0:T(8,128)(2,1)S(1)}, u32[]{:S(2)}, u32[]{:S(2)}) collective-permute-start(bf16[3136,128]{1,0:T(8,128)(2,1)} %get-tuple-element.97), channel_id=1, source_target_pairs={{0,1},{1,0},{2,3},{3,2},{4,5},{5,4},{6,7},{7,6},{8,9},{9,8},{10,11... | collective-permute-start | bytes 2408456 | tf_op jit(solution)/shard_map/ppermute | solution.py:1043
  142.8 13.2 %collective-permute-start.15 = (bf16[1072,128]{1,0:T(8,128)(2,1)}, bf16[1072,128]{1,0:T(8,128)(2,1)S(1)}, u32[]{:S(2)}, u32[]{:S(2)}) collective-permute-start(bf16[1072,128]{1,0:T(8,128)(2,1)} %get-tuple-element.91), channel_id=1, source_target_pairs={{0,2},{1,3},{2,0},{3,1},{4,6},{5,7},{6,4},{7,5},{8,10},{9,11},{10,... | collective-permute-start | bytes 823304 | tf_op jit(solution)/shard_map/ppermute | solution.py:1043
  144.3 22.4 %collective-permute-start.16 = (bf16[1072,128]{1,0:T(8,128)(2,1)}, bf16[1072,128]{1,0:T(8,128)(2,1)S(1)}, u32[]{:S(2)}, u32[]{:S(2)}) collective-permute-start(bf16[1072,128]{1,0:T(8,128)(2,1)} %get-tuple-element.92), channel_id=1, source_target_pairs={{0,4},{1,5},{2,6},{3,7},{4,0},{5,1},{6,2},{7,3},{8,12},{9,13},{10,... | collective-permute-start | bytes 823304 | tf_op jit(solution)/shard_map/ppermute | solution.py:1043
  146.7 20.0 %collective-permute-start.17 = (bf16[1072,128]{1,0:T(8,128)(2,1)}, bf16[1072,128]{1,0:T(8,128)(2,1)S(1)}, u32[]{:S(2)}, u32[]{:S(2)}) collective-permute-start(bf16[1072,128]{1,0:T(8,128)(2,1)} %get-tuple-element.93), channel_id=1, source_target_pairs={{0,6},{1,7},{2,4},{3,5},{4,2},{5,3},{6,0},{7,1},{8,14},{9,15},{10,... | collective-permute-start | bytes 823304 | tf_op jit(solution)/shard_map/ppermute | solution.py:1043
  169.5 6.7 %collective-permute-start.25 = (bf16[1072,128]{1,0:T(8,128)(2,1)}, bf16[1072,128]{1,0:T(8,128)(2,1)S(1)}, u32[]{:S(2)}, u32[]{:S(2)}) collective-permute-start(bf16[1072,128]{1,0:T(8,128)(2,1)} %get-tuple-element.98.refs_1_), channel_id=1, source_target_pairs={{0,16},{8,24},{16,0},{24,8},{1,17},{9,25},{17,1},{25,9},{2,18},{10... | collective-permute-start | bytes 823304 | tf_op jit(solution)/shard_map/ppermute | solution.py:1043
  170.1 6.2 %collective-permute-start.21 = (bf16[1072,128]{1,0:T(8,128)(2,1)}, bf16[1072,128]{1,0:T(8,128)(2,1)S(1)}, u32[]{:S(2)}, u32[]{:S(2)}) collective-permute-start(bf16[1072,128]{1,0:T(8,128)(2,1)} %get-tuple-element.98.refs_1_), channel_id=1, source_target_pairs={{0,8},{8,0},{16,24},{24,16},{1,9},{9,1},{17,25},{25,17},{2,10},{10... | collective-permute-start | bytes 823304 | tf_op jit(solution)/shard_map/ppermute | solution.py:1043
  176.3 12.3 %collective-permute-start.26 = (bf16[1072,128]{1,0:T(8,128)(2,1)S(1)}, bf16[1072,128]{1,0:T(8,128)(2,1)S(1)}, u32[]{:S(2)}, u32[]{:S(2)}) collective-permute-start(bf16[1072,128]{1,0:T(8,128)(2,1)S(1)} %collective-permute-done.25.refs_3_), channel_id=1, source_target_pairs={{0,8},{8,0},{16,24},{24,16},{1,9},{9,1},{17,25},{25,17},{2,10},{10... | collective-permute-start | bytes 823304 | tf_op jit(solution)/shard_map/ppermute | solution.py:1043
  180.3 16.6 %collective-permute-start.22 = (bf16[784,128]{1,0:T(8,128)(2,1)}, bf16[784,128]{1,0:T(8,128)(2,1)S(1)}, u32[]{:S(2)}, u32[]{:S(2)}) collective-permute-start(bf16[784,128]{1,0:T(8,128)(2,1)} %get-tuple-element.100), channel_id=1, source_target_pairs={{0,2},{1,3},{2,0},{3,1},{4,6},{5,7},{6,4},{7,5},{8,10},{9,11},{10,... | collective-permute-start | bytes 602120 | tf_op jit(solution)/shard_map/ppermute | solution.py:1043
  185.4 17.6 %collective-permute-start.23 = (bf16[784,128]{1,0:T(8,128)(2,1)}, bf16[784,128]{1,0:T(8,128)(2,1)S(1)}, u32[]{:S(2)}, u32[]{:S(2)}) collective-permute-start(bf16[784,128]{1,0:T(8,128)(2,1)} %get-tuple-element.101), channel_id=1, source_target_pairs={{0,4},{1,5},{2,6},{3,7},{4,0},{5,1},{6,2},{7,3},{8,12},{9,13},{10,... | collective-permute-start | bytes 602120 | tf_op jit(solution)/shard_map/ppermute | solution.py:1043
  186.3 16.7 %collective-permute-start.24 = (bf16[784,128]{1,0:T(8,128)(2,1)}, bf16[784,128]{1,0:T(8,128)(2,1)S(1)}, u32[]{:S(2)}, u32[]{:S(2)}) collective-permute-start(bf16[784,128]{1,0:T(8,128)(2,1)} %get-tuple-element.102), channel_id=1, source_target_pairs={{0,6},{1,7},{2,4},{3,5},{4,2},{5,3},{6,0},{7,1},{8,14},{9,15},{10,... | collective-permute-start | bytes 602120 | tf_op jit(solution)/shard_map/ppermute | solution.py:1043
  205.7 4.3 %collective-permute-start.30 = (bf16[4,48,128]{2,1,0:T(8,128)(2,1)}, bf16[4,48,128]{2,1,0:T(8,128)(2,1)S(1)}, u32[]{:S(2)}, u32[]{:S(2)}) collective-permute-start(bf16[4,48,128]{2,1,0:T(8,128)(2,1)} %get-tuple-element.114), channel_id=1, source_target_pairs={{0,1},{1,0},{2,3},{3,2},{4,5},{5,4},{6,7},{7,6},{8,9},{9,8},{10,11... | collective-permute-start | bytes 147464 | tf_op jit(solution)/shard_map/ppermute | solution.py:1043
  206.8 7.6 %collective-permute-start.18 = (bf16[512,1024]{1,0:T(8,128)(2,1)S(1)}, bf16[512,1024]{1,0:T(8,128)(2,1)S(1)}, u32[]{:S(2)}, u32[]{:S(2)}) collective-permute-start(bf16[512,1024]{1,0:T(8,128)(2,1)S(1)} %copy-done.4), channel_id=1, source_target_pairs={{0,8},{8,0},{16,24},{24,16},{1,9},{9,1},{17,25},{25,17},{2,10},{10... | collective-permute-start | bytes 3145736 | tf_op jit(solution)/shard_map/ppermute | solution.py:1043
  206.8 14.9 %collective-permute-start.27 = (bf16[784,128]{1,0:T(8,128)(2,1)}, bf16[784,128]{1,0:T(8,128)(2,1)S(1)}, u32[]{:S(2)}, u32[]{:S(2)}) collective-permute-start(bf16[784,128]{1,0:T(8,128)(2,1)} %get-tuple-element.104.refs_1_), channel_id=1, source_target_pairs={{0,8},{8,0},{16,24},{24,16},{1,9},{9,1},{17,25},{25,17},{2,10},{10... | collective-permute-start | bytes 602120 | tf_op jit(solution)/shard_map/ppermute | solution.py:1043
  207.3 12.8 %collective-permute-start.28 = (bf16[784,128]{1,0:T(8,128)(2,1)}, bf16[784,128]{1,0:T(8,128)(2,1)}, u32[]{:S(2)}, u32[]{:S(2)}) collective-permute-start(bf16[784,128]{1,0:T(8,128)(2,1)} %get-tuple-element.104.refs_1_), channel_id=1, source_target_pairs={{0,16},{8,24},{16,0},{24,8},{1,17},{9,25},{17,1},{25,9},{2,18},{10... | collective-permute-start | bytes 602120 | tf_op jit(solution)/shard_map/ppermute | solution.py:1043
  218.2 11.6 %collective-permute-start.19 = (bf16[256,1024]{1,0:T(8,128)(2,1)}, bf16[256,1024]{1,0:T(8,128)(2,1)S(1)}, u32[]{:S(2)}, u32[]{:S(2)}) collective-permute-start(bf16[256,1024]{1,0:T(8,128)(2,1)} %dynamic-slice_convert_fusion), channel_id=1, source_target_pairs={{0,16},{8,24},{16,0},{24,8},{1,17},{9,25},{17,1},{25,9},{2,18},{10... | collective-permute-start | bytes 1572872 | tf_op jit(solution)/shard_map/ppermute | solution.py:1043
  (40 other events, 296.7 us)
Sparse Core Ops, SparseCore 0:
  9.6 25.2 all-gather.4
  36.5 22.5 all-gather.6
  106.8 31.1 reduce-scatter.1

commit v12 on v11

--- a/solution.py
+++ b/solution.py
@@ -502,21 +502,10 @@
 
 
 def normed_kernel(
-    places_ref, d_gating_ref, d_rest_ref, gate_weight_ref, rest_weight_ref, mine_ref, send_ref
+    places_ref, d_gating_ref, d_rest_ref, gate_weight_ref, rest_weight_ref, d_normed_ref
 ):
-    chunk = pl.program_id(0)
     d_normed = dot_nn(d_gating_ref[...], gate_weight_ref[...])
-    d_normed = low(d_normed + dot_nn(d_rest_ref[...], rest_weight_ref[...]))
-    here = chunk % 2 == places_ref[0]
-    rows = pl.ds(pl.multiple_of(chunk // 2 * BLOCK, BLOCK), BLOCK)
-
-    @pl.when(here)
-    def _():
-        mine_ref[rows, :] = d_normed
-
-    @pl.when(jnp.logical_not(here))
-    def _():
-        send_ref[rows, :] = d_normed
+    d_normed_ref[...] = low(d_normed + dot_nn(d_rest_ref[...], rest_weight_ref[...]))
 
 
 def prepare_kernel(places_ref, in_ref, out_ref, rest_ref, gate_out_ref):
@@ -893,16 +882,16 @@
     )
 
 
-def run_normed(parity, d_gating, d_rest, gate_weight, rest_weight, arrived):
+def run_normed(d_gating, d_rest, gate_weight, rest_weight, arrived):
     length, local_di = d_gating.shape
     rest = d_rest.shape[1]
     return call(
         normed_kernel,
-        [parity],
+        [jnp.int32(0)],
         [d_gating, d_rest, gate_weight, rest_weight],
         [rows_of(local_di), rows_of(rest), fixed((local_di, D)), fixed((rest, D))],
-        [struct((length // 2, D), jnp.bfloat16)] * 2,
-        [fixed((length // 2, D))] * 2,
+        struct((length, D), jnp.bfloat16),
+        rows_of(D),
         [],
         length // BLOCK,
         arrived,
@@ -1240,7 +1229,6 @@
         d_gain_gate,
         d_gain_two,
     )
-    near, far = seq_index % 2, seq_index // 2
     if rings:
         *gate_out_sums, rest_send = run_pair(
             gate_places,
@@ -1248,50 +1236,45 @@
             gate_out_arrived,
             [vec_rows],
             [rest_grads[1]],
-            [block_rows],
+            [],
         )
         rest_arrived = swap(rest_send, "wshard", 1)
         gate_out_pieces = [
             swap(gate_out_sums[mask], "wshard", 2 * mask) for mask in range(1, 4)
         ]
-        normed_mine, normed_send = run_normed(
-            near, d_gating, d_rest, gate_weight, rest_weight, [gate_out_sums[0]]
+        d_normed_part = run_normed(
+            d_gating, d_rest, gate_weight, rest_weight, [gate_out_sums[0], block_rows]
         )
-        gate_out_part, normed_send = run_final(
-            [gate_out_sums[0]] + gate_out_pieces, [normed_send], []
-        )
-        gate_out_near = swap(gate_out_part, "seq", 1)
         rest_sums = run_pair(
-            gate_places, rest_grads[0], rest_arrived, [], [], [gate_out_near]
+            gate_places, rest_grads[0], rest_arrived, [], [], [d_normed_part]
         )
         rest_pieces = [swap(rest_sums[mask], "wshard", 2 * mask) for mask in range(1, 4)]
-        gate_out_far = swap(gate_out_part, "seq", 2)
+        gate_out_part, d_normed_part = run_final(
+            [gate_out_sums[0]] + gate_out_pieces, [d_normed_part], [rest_sums[0]]
+        )
+        d_normed = lax.psum_scatter(d_normed_part, "seq", scatter_dimension=0, tiled=True)
+        rest_part, gate_out_part = run_final(
+            [rest_sums[0]] + rest_pieces, [gate_out_part], []
+        )
     else:
         every = lax.all_gather(lax.psum(vec_rows, "wshard"), "seq", axis=0, tiled=False)
-        normed_mine, normed_send = run_normed(
-            near, d_gating, d_rest, gate_weight, rest_weight, []
-        )
-    normed_arrived = swap(normed_send, "seq", 1)
-    normed_sum = normed_mine.astype(jnp.float32) + normed_arrived.astype(jnp.float32)
-    normed_far = swap(low(take_block(normed_sum, 1 - far, rows_here)), "seq", 2)
+        d_normed_part = run_normed(d_gating, d_rest, gate_weight, rest_weight, [])
+        d_normed = lax.psum_scatter(d_normed_part, "seq", scatter_dimension=0, tiled=True)
     if rings:
-        spots = [seq_index ^ mask for mask in range(4)]
-        gate_out_blocks = [gate_out_part, gate_out_near, gate_out_far]
-        gate_out_blocks = gate_out_blocks + [swap(gate_out_far, "seq", 1)]
+        spots, gate_out_blocks = seq_blocks(gate_out_part)
         in_arrays = (in_weight.T, in_first.T, in_second.T)
         updated = run_update_gate(
             spots,
             gate_out_blocks,
             in_arrays,
             (out_weight, out_first, out_second),
-            [rest_sums[0]],
+            [],
         )
         out_first_new, out_second_new, out_weight_new, every = updated[3:]
-        rest_part, every = run_final([rest_sums[0]] + rest_pieces, [every], [])
         every_there = swap(every, "wshard", 1)
         every = every.astype(jnp.float32) + every_there.astype(jnp.float32)
     block_out = hidden_rows.astype(jnp.float32) + block_rows.astype(jnp.float32)
-    d_normed = take_block(normed_sum, far, rows_here) + normed_far.astype(jnp.float32)
+    d_normed = d_normed.astype(jnp.float32)
     own_hidden = hidden_rows.astype(jnp.float32)
     own_scale = lax.rsqrt(jnp.mean(own_hidden * own_hidden, axis=-1, keepdims=True) + norm_eps)
     own_unit = own_hidden * own_scale

time: 242 us -> 245 us (1.012)
  waiting for transfers between devices: 66.3 us -> 79.1 us
  local copies, waits for them, and re-layouts: 19.3 us -> 15.1 us
  other arithmetic: 11 us -> 8.29 us
    ppermute x25 -> x23, waiting for transfers between devices: 41 us -> 56.8 us  [swap(): return lax.ppermute(values, axis, route)]
    reduce_scatter x1, waiting for transfers between devices: 2.96 us -> 0.01 us  [shards(): lax.psum_scatter(block_part, 'seq', scatter_dimension=0, tiled=True)]
    unnamed x73 -> x81, local copies, waits for them, and re-layouts: 8.18 us -> 7.64 us
    ppermute x25 -> x23, starting transfers between devices: 24.4 us -> 24.2 us  [swap(): return lax.ppermute(values, axis, route)]
  transfers between devices with their start and end apart: 34 -> 33, of which waited for: 18 -> 16; matrix products, arithmetic and copies ran while one was open for 8% -> 5% of each run, Pallas kernels for 31% -> 31%
where the time goes in v12:
time: 245 us; the launch traced here: 244 us
  Pallas kernels  99.4 us (41%)
  waiting for transfers between devices  79.1 us (32%)
  starting transfers between devices  27.8 us (11%)
  local copies, waits for them, and re-layouts  15.1 us (6%)
  between operations  14.2 us (6%)
  other arithmetic  8.29 us (3%)
    pallas_call x13, Pallas kernels, call(): pl.pallas_call(after(kernel, 1 + len(inputs), len(arrived)), grid_spec=pl...  99.4 us
    ppermute x23, waiting for transfers between devices, swap(): return lax.ppermute(values, axis, route)  56.8 us
    ppermute x23, starting transfers between devices, swap(): return lax.ppermute(values, axis, route)  24.2 us
    ppermute x6, waiting for transfers between devices, ring_step(): lax.ppermute(held, 'wshard', [(i, (i + 2) % count) for i in range(count)])  20.9 us
    unnamed x81, local copies, waits for them, and re-layouts  7.64 us
  transfers between devices with their start and end apart: 33, of which 16 were waited for; matrix products, arithmetic and copies ran while one was open for 5% of the time, Pallas kernels for 31%

profile of v12, /device:TPU:0, one launch (start us, length us, event | category | flops | bytes accessed | tf_op | source)
XLA Modules:
  0.0 244.0 jit_solution(1393140695005304322)
XLA Ops:
  8.7 2.7 %prepare.1 = (bf16[784,128]{1,0:T(8,128)(2,1)}, bf16[1024,128]{1,0:T(8,128)(2,1)}) custom-call(s32[1]{0:T(128)} %bitcast.11.refs_0_, f32[4384,128]{1,0:T(8,128)} %bitcast.73, f32[256,1024]{1,0:T(8,128)} %refs_8_.1), custom_call_target="tpu_custom_call" | custom-call | flops 100000000 | bytes 4000000 | tf_op jit(solution)/shard_map/prepare/pallas_call | solution.py:645
  11.5 3.0 %collective-permute-start = (bf16[784,128]{1,0:T(8,128)(2,1)}, bf16[784,128]{1,0:T(8,128)(2,1)S(1)}, u32[]{:S(2)}, u32[]{:S(2)}) collective-permute-start(bf16[784,128]{1,0:T(8,128)(2,1)} %get-tuple-element.61.refs_1_), channel_id=1, source_target_pairs={{0,1},{1,0},{2,3},{3,2},{4,5},{5,4},{6,7},{7,6},{8,9},{9,8},{10,11... | collective-permute-start | bytes 602120 | tf_op jit(solution)/shard_map/ppermute | solution.py:1032
  17.9 6.5 %collective-permute-done.1.refs_3_ = bf16[784,128]{1,0:T(8,128)(2,1)S(1)} collective-permute-done((bf16[784,128]{1,0:T(8,128)(2,1)}, bf16[784,128]{1,0:T(8,128)(2,1)S(1)}, u32[]{:S(2)}, u32[]{:S(2)}) %collective-permute-start.1) | collective-permute-done | bytes 200736 | tf_op jit(solution)/shard_map/ppermute | solution.py:1044
  24.3 5.6 %collective-permute-done.7.refs_2_ = bf16[1024,128]{1,0:T(8,128)(2,1)S(1)} collective-permute-done((bf16[1024,128]{1,0:T(8,128)(2,1)}, bf16[1024,128]{1,0:T(8,128)(2,1)S(1)}, u32[]{:S(2)}, u32[]{:S(2)}) %collective-permute-start.7) | collective-permute-done | bytes 262176 | tf_op jit(solution)/shard_map/ppermute | solution.py:1044
  31.3 2.7 %collective-permute-done.3.refs_5_ = bf16[784,128]{1,0:T(8,128)(2,1)S(1)} collective-permute-done((bf16[784,128]{1,0:T(8,128)(2,1)S(1)}, bf16[784,128]{1,0:T(8,128)(2,1)S(1)}, u32[]{:S(2)}, u32[]{:S(2)}) %collective-permute-start.3) | collective-permute-done | bytes 200736 | tf_op jit(solution)/shard_map/ppermute | solution.py:1044
  34.6 6.1 %collective-permute-done.8.refs_3_ = bf16[1024,128]{1,0:T(8,128)(2,1)S(1)} collective-permute-done((bf16[1024,128]{1,0:T(8,128)(2,1)S(1)}, bf16[1024,128]{1,0:T(8,128)(2,1)S(1)}, u32[]{:S(2)}, u32[]{:S(2)}) %collective-permute-start.8) | collective-permute-done | bytes 262176 | tf_op jit(solution)/shard_map/ppermute | solution.py:1044
  46.7 3.9 %collective-permute-done.2.refs_4_.refs_6_ = bf16[784,128]{1,0:T(8,128)(2,1)S(1)} collective-permute-done((bf16[784,128]{1,0:T(8,128)(2,1)S(1)}, bf16[784,128]{1,0:T(8,128)(2,1)S(1)}, u32[]{:S(2)}, u32[]{:S(2)}) %collective-permute-start.2) | collective-permute-done | bytes 200736 | tf_op jit(solution)/shard_map/ppermute | solution.py:1032
  50.5 2.1 collective-permute-done.4.refs_6_.refs_7_
  52.7 2.1 collective-permute-done.6.refs_8_
  55.6 2.9 %hold.1 = bf16[4096,128]{1,0:T(8,128)(2,1)} custom-call(s32[8]{0:T(128)} %stack.111.refs_0_, bf16[1024,128]{1,0:T(8,128)(2,1)} %get-tuple-element.63.refs_1_, bf16[1024,128]{1,0:T(8,128)(2,1)} %copy-done.11, bf16[1024,128]{1,0:T(8,128)(2,1)} %copy-done.12, bf16[1024,128]{1,0:T(8,128)(2,1)} %copy-done.13, bf16[784,128]{1,0:T(8,128)(2,1)} %copy-done.18, ...), custom_call_target="tpu_custom_call" | custom-call | bytes 2000000 | tf_op jit(solution)/shard_map/hold/pallas_call | solution.py:645
  61.0 14.1 %forward.1 = (bf16[896,1024]{1,0:T(8,128)(2,1)}, bf16[1024,1024]{1,0:T(8,128)(2,1)}, bf16[1024,1024]{1,0:T(8,128)(2,1)}, f32[1024,768]{1,0:T(8,128)}, f32[1024,7...) custom-call(s32[8]{0:T(128)} %stack.111.refs_0_, ...), custom_call_target="tpu_custom_call" | custom-call | flops 6000000000 | bytes 30000000 | tf_op jit(solution)/shard_map/forward/pallas_call | solution.py:645
  75.1 3.7 %collective-permute-done.10.refs_5_ = bf16[4096,128]{1,0:T(8,128)(2,1)S(1)} collective-permute-done((bf16[4096,128]{1,0:T(8,128)(2,1)}, bf16[4096,128]{1,0:T(8,128)(2,1)S(1)}, u32[]{:S(2)}, u32[]{:S(2)}) %collective-permute-start.10) | collective-permute-done | bytes 1048608 | tf_op jit(solution)/shard_map/ppermute | solution.py:1032
  79.7 8.6 %gate.1 = (bf16[512,1024]{1,0:T(8,128)(2,1)}, bf16[512,1024]{1,0:T(8,128)(2,1)}, f32[1024,512]{1,0:T(8,128)}, f32[1024,512]{1,0:T(8,128)}, f32[8,1024]{1,0:T(8,128)}) custom-call(s32[8]{0:T(128)} %stack.113.refs_0_, bf16[1024,128]{1,0:T(8,128)(2,1)} %get-tuple-element.63.refs_1_, bf16[1024,128]{1,0:T(8,128)(2,1)} %copy-done.11, ...), custom_call_target="tpu_custom_call" | custom-call | flops 2500000000 | bytes 12000000 | tf_op jit(solution)/shard_map/gate/pallas_call | solution.py:645
  90.9 1.7 collective-permute-done.12.refs_8_
  94.1 12.6 %middle.1 = (bf16[1024,1024]{1,0:T(8,128)(2,1)}, bf16[1024,512]{1,0:T(8,128)(2,1)}, bf16[1024,512]{1,0:T(8,128)(2,1)}, f32[1,512]{1,0:T(1,128)}, f32[1,1024]{1,0...) custom-call(s32[2]{0:T(128)} %pad_add_fusion.refs_0_, ...), custom_call_target="tpu_custom_call" | custom-call | flops 4000000000 | bytes 15000000 | tf_op jit(solution)/shard_map/middle/pallas_call | solution.py:645
  108.4 26.4 %backward.1 = (bf16[1024,896]{1,0:T(8,128)(2,1)}, f32[48,128]{1,0:T(8,128)}, bf16[3136,128]{1,0:T(8,128)(2,1)}, bf16[3136,128]{1,0:T(8,128)(2,1)}) custom-call(s32[2]{0:T(128)} %pad_add_fusion.refs_0_, bf16[1024,1024]{1,0:T(8,128)(2,1)} %get-tuple-element.67.refs_5_.refs_1_, f32[1024,768]{1,0:T(8,128)} %get-tuple-element.74.refs_2_, ...), custom_call_target="tpu_custom_call" | custom-call | flops 14000000000 | bytes 40000000 | tf_op jit(solution)/shard_map/backward/pallas_call | solution.py:645
  135.8 3.4 %pair.2 = (bf16[1072,128]{1,0:T(8,128)(2,1)}, bf16[1072,128]{1,0:T(8,128)(2,1)}, bf16[1072,128]{1,0:T(8,128)(2,1)}, bf16[1072,128]{1,0:T(8,128)(2,1)}, bf16[3136,128]{1,0:T(8,128)(2,1)}) custom-call(s32[4]{0:T(128)} %pad_add_fusion.1.refs_0_, bf16[4096,128]{1,0:T(8,128)(2,1)} %get-tuple-element.72.refs_1_, ...), custom_call_target="tpu_custom_call", output_to_operand_aliasing={{4}: (4, {})} | custom-call | flops 2000000 | bytes 3000000 | tf_op jit(solution)/shard_map/pair/pallas_call | solution.py:645
  140.7 3.0 %collective-permute-start.15 = (bf16[1072,128]{1,0:T(8,128)(2,1)}, bf16[1072,128]{1,0:T(8,128)(2,1)S(1)}, u32[]{:S(2)}, u32[]{:S(2)}) collective-permute-start(bf16[1072,128]{1,0:T(8,128)(2,1)} %get-tuple-element.86), channel_id=1, source_target_pairs={{0,2},{1,3},{2,0},{3,1},{4,6},{5,7},{6,4},{7,5},{8,10},{9,11},{10,... | collective-permute-start | bytes 823304 | tf_op jit(solution)/shard_map/ppermute | solution.py:1032
  146.2 7.2 %normed.1.refs_3_.refs_5_ = bf16[1024,1024]{1,0:T(8,128)(2,1)} custom-call(s32[1]{0:T(128)} %constant.128.clone.1.refs_0_, bf16[1024,512]{1,0:T(8,128)(2,1)} %get-tuple-element.89.refs_1_, bf16[1024,896]{1,0:T(8,128)(2,1)} %get-tuple-element.90.refs_2_, bf16[512,1024]{1,0:T(8,128)(2,1)} %get-tuple-element.70.refs_13_.refs_3_, ...), custom_call_target="tpu_custom_call" | custom-call | flops 3000000000 | bytes 9000000 | tf_op jit(solution)/shard_map/normed/pallas_call | solution.py:645
  153.4 5.7 %collective-permute-done.18.refs_2_ = bf16[3136,128]{1,0:T(8,128)(2,1)S(1)} collective-permute-done((bf16[3136,128]{1,0:T(8,128)(2,1)}, bf16[3136,128]{1,0:T(8,128)(2,1)S(1)}, u32[]{:S(2)}, u32[]{:S(2)}) %collective-permute-start.18) | collective-permute-done | bytes 802848 | tf_op jit(solution)/shard_map/ppermute | solution.py:1032
  160.0 3.0 %pair.3 = (bf16[784,128]{1,0:T(8,128)(2,1)}, bf16[784,128]{1,0:T(8,128)(2,1)}, bf16[784,128]{1,0:T(8,128)(2,1)}, bf16[784,128]{1,0:T(8,128)(2,1)}) custom-call(s32[4]{0:T(128)} %pad_add_fusion.1.refs_0_, bf16[3136,128]{1,0:T(8,128)(2,1)} %get-tuple-element.91.refs_1_, bf16[3136,128]{1,0:T(8,128)(2,1)} %copy-done.3, bf16[1024,1024]{1,0:T(8,128)(2,1)} %normed.1.refs_3_.refs_5_), custom_call_target="tpu_custom_call" | custom-call | flops 2000000 | bytes 3000000 | tf_op jit(solution)/shard_map/pair/pallas_call | solution.py:645
  163.0 3.1 %collective-permute-done.16.refs_3_ = bf16[1072,128]{1,0:T(8,128)(2,1)S(1)} collective-permute-done((bf16[1072,128]{1,0:T(8,128)(2,1)}, bf16[1072,128]{1,0:T(8,128)(2,1)S(1)}, u32[]{:S(2)}, u32[]{:S(2)}) %collective-permute-start.16) | collective-permute-done | bytes 274464 | tf_op jit(solution)/shard_map/ppermute | solution.py:1032
  166.9 2.1 final.2
  169.1 4.8 %collective-permute-start.19 = (bf16[784,128]{1,0:T(8,128)(2,1)S(1)}, bf16[784,128]{1,0:T(8,128)(2,1)S(1)}, u32[]{:S(2)}, u32[]{:S(2)}) collective-permute-start(bf16[784,128]{1,0:T(8,128)(2,1)S(1)} %copy-done.36), channel_id=1, source_target_pairs={{0,2},{1,3},{2,0},{3,1},{4,6},{5,7},{6,4},{7,5},{8,10},{9,11},{10,... | collective-permute-start | bytes 602120 | tf_op jit(solution)/shard_map/ppermute | solution.py:1032
  176.4 3.7 %collective-permute-done.19.refs_2_ = bf16[784,128]{1,0:T(8,128)(2,1)S(1)} collective-permute-done((bf16[784,128]{1,0:T(8,128)(2,1)S(1)}, bf16[784,128]{1,0:T(8,128)(2,1)S(1)}, u32[]{:S(2)}, u32[]{:S(2)}) %collective-permute-start.19) | collective-permute-done | bytes 200736 | tf_op jit(solution)/shard_map/ppermute | solution.py:1032
  180.1 10.5 %collective-permute-done.20.refs_3_ = bf16[784,128]{1,0:T(8,128)(2,1)S(1)} collective-permute-done((bf16[784,128]{1,0:T(8,128)(2,1)S(1)}, bf16[784,128]{1,0:T(8,128)(2,1)S(1)}, u32[]{:S(2)}, u32[]{:S(2)}) %collective-permute-start.20) | collective-permute-done | bytes 200736 | tf_op jit(solution)/shard_map/ppermute | solution.py:1032
  191.3 2.0 final.3
  193.6 13.0 %collective-permute-done.26.refs_3_ = bf16[1072,128]{1,0:T(8,128)(2,1)S(1)} collective-permute-done((bf16[1072,128]{1,0:T(8,128)(2,1)}, bf16[1072,128]{1,0:T(8,128)(2,1)S(1)}, u32[]{:S(2)}, u32[]{:S(2)}) %collective-permute-start.26) | collective-permute-done | bytes 274464 | tf_op jit(solution)/shard_map/ppermute | solution.py:1032
  208.1 6.2 %collective-permute-done.23.refs_3_ = bf16[784,128]{1,0:T(8,128)(2,1)S(1)} collective-permute-done((bf16[784,128]{1,0:T(8,128)(2,1)}, bf16[784,128]{1,0:T(8,128)(2,1)S(1)}, u32[]{:S(2)}, u32[]{:S(2)}) %collective-permute-start.23) | collective-permute-done | bytes 200736 | tf_op jit(solution)/shard_map/ppermute | solution.py:1032
  215.1 7.5 %update_gate.1 = (f32[4384,128]{1,0:T(8,128)}, f32[4384,128]{1,0:T(8,128)}, f32[4384,128]{1,0:T(8,128)}, f32[256,1024]{1,0:T(8,128)}, f32[256,1024]{1,0:T(8,128)...) custom-call(s32[4]{0:T(128)} %pad_add_fusion.2.refs_0_, bf16[1072,128]{1,0:T(8,128)(2,1)} %get-tuple-element.100.refs_1_, ...), custom_call_target="tpu_custom_call" | custom-call | flops 10000000 | bytes 13000000 | tf_op jit(solution)/shard_map/update_gate/pallas_call | solution.py:645
  224.0 7.0 %update_rest.1 = (f32[4384,128]{1,0:T(8,128)}, f32[4384,128]{1,0:T(8,128)}, f32[4384,128]{1,0:T(8,128)}) custom-call(s32[4]{0:T(128)} %pad_add_fusion.2.refs_0_, bf16[784,128]{1,0:T(8,128)(2,1)} %get-tuple-element.99.refs_1_, bf16[784,128]{1,0:T(8,128)(2,1)} %copy-done.16, ...), custom_call_target="tpu_custom_call", output_to_operand_aliasing={{0}: (8, {}), {1}: (9, {}), {2}: (10, {})} | custom-call | flops 10000000 | bytes 8000000 | tf_op jit(solution)/shard_map/update_rest/pallas_call | solution.py:645
  234.7 2.8 %fusion.6 = (f32[1,256,1024]{2,1,0:T(8,128)}, f32[1,256,1024]{2,1,0:T(8,128)}) fusion(bf16[256,1024]{1,0:T(8,128)(2,1)} %reduce-scatter.5.cloned.1.call-done, bf16[1,256,1024]{2,1,0:T(8,128)(2,1)S(1)} %copy-done.1, bf16[1,256,1024]{2,1,0:T(8,128)(2,1)S(1)} %copy-done, f32[256]{0:T(256)S(1)} %broadcast_multiply_fusion, f32[1024]{0:T(1024)S(1)} %copy-done.28, ...), kind=kLoop, calls=%fused_computation.9 | loop fusion | flops 2883584 | bytes 4200448 | tf_op jit(solution)/shard_map/reshape | solution.py:1342
  (205 shorter events, 40.1 us)
Async XLA Ops:
  7.2 53.8 %all-gather.5.cloned.1.call-start = ((), (), s32[]{:S(2)}) async-start(), calls=%async_computation.4 | async-start | bytes 2621440 | tf_op jit(solution)/shard_map/all_gather | solution.py:1159
  7.9 70.8 %all-gather.7.cloned.1.call-start = ((), (), s32[]{:S(2)}) async-start(), calls=%async_computation.5 | async-start | bytes 2621440 | tf_op jit(solution)/shard_map/all_gather | solution.py:1160
  8.7 137.5 %reduce-scatter.3.cloned.1.call-start = ((), (), s32[]{:S(2)}) async-start(), calls=%async_computation.2 | async-start | bytes 2621440 | tf_op jit(solution)/shard_map/reduce_scatter | solution.py:1212
  11.5 35.2 %collective-permute-start = (bf16[784,128]{1,0:T(8,128)(2,1)}, bf16[784,128]{1,0:T(8,128)(2,1)S(1)}, u32[]{:S(2)}, u32[]{:S(2)}) collective-permute-start(bf16[784,128]{1,0:T(8,128)(2,1)} %get-tuple-element.61.refs_1_), channel_id=1, source_target_pairs={{0,1},{1,0},{2,3},{3,2},{4,5},{5,4},{6,7},{7,6},{8,9},{9,8},{10,11... | collective-permute-start | bytes 602120 | tf_op jit(solution)/shard_map/ppermute | solution.py:1032
  14.4 9.9 %collective-permute-start.1 = (bf16[784,128]{1,0:T(8,128)(2,1)}, bf16[784,128]{1,0:T(8,128)(2,1)S(1)}, u32[]{:S(2)}, u32[]{:S(2)}) collective-permute-start(bf16[784,128]{1,0:T(8,128)(2,1)} %get-tuple-element.61.refs_1_), channel_id=1, source_target_pairs={{0,2},{1,3},{2,4},{3,5},{4,6},{5,7},{6,0},{7,1},{8,10},{9,11},{10,... | collective-permute-start | bytes 602120 | tf_op jit(solution)/shard_map/ppermute | solution.py:1044
  16.0 14.0 %collective-permute-start.7 = (bf16[1024,128]{1,0:T(8,128)(2,1)}, bf16[1024,128]{1,0:T(8,128)(2,1)S(1)}, u32[]{:S(2)}, u32[]{:S(2)}) collective-permute-start(bf16[1024,128]{1,0:T(8,128)(2,1)} %get-tuple-element.63.refs_1_), channel_id=1, source_target_pairs={{0,2},{1,3},{2,4},{3,5},{4,6},{5,7},{6,0},{7,1},{8,10},{9,11},{10,... | collective-permute-start | bytes 786440 | tf_op jit(solution)/shard_map/ppermute | solution.py:1044
  24.3 9.6 %collective-permute-start.3 = (bf16[784,128]{1,0:T(8,128)(2,1)S(1)}, bf16[784,128]{1,0:T(8,128)(2,1)S(1)}, u32[]{:S(2)}, u32[]{:S(2)}) collective-permute-start(bf16[784,128]{1,0:T(8,128)(2,1)S(1)} %collective-permute-done.1.refs_3_), channel_id=1, source_target_pairs={{0,2},{1,3},{2,4},{3,5},{4,6},{5,7},{6,0},{7,1},{8,10},{9,11},{10,... | collective-permute-start | bytes 602120 | tf_op jit(solution)/shard_map/ppermute | solution.py:1044
  30.0 10.8 %collective-permute-start.8 = (bf16[1024,128]{1,0:T(8,128)(2,1)S(1)}, bf16[1024,128]{1,0:T(8,128)(2,1)S(1)}, u32[]{:S(2)}, u32[]{:S(2)}) collective-permute-start(bf16[1024,128]{1,0:T(8,128)(2,1)S(1)} %collective-permute-done.7.refs_2_), channel_id=1, source_target_pairs={{0,2},{1,3},{2,4},{3,5},{4,6},{5,7},{6,0},{7,1},{8,10},{9,11},{10,... | collective-permute-start | bytes 786440 | tf_op jit(solution)/shard_map/ppermute | solution.py:1044
  34.0 11.6 %collective-permute-start.5 = (bf16[784,128]{1,0:T(8,128)(2,1)S(1)}, bf16[784,128]{1,0:T(8,128)(2,1)S(1)}, u32[]{:S(2)}, u32[]{:S(2)}) collective-permute-start(bf16[784,128]{1,0:T(8,128)(2,1)S(1)} %collective-permute-done.3.refs_5_), channel_id=1, source_target_pairs={{0,2},{1,3},{2,4},{3,5},{4,6},{5,7},{6,0},{7,1},{8,10},{9,11},{10,... | collective-permute-start | bytes 602120 | tf_op jit(solution)/shard_map/ppermute | solution.py:1044
  40.7 11.9 %collective-permute-start.9 = (bf16[1024,128]{1,0:T(8,128)(2,1)S(1)}, bf16[1024,128]{1,0:T(8,128)(2,1)S(1)}, u32[]{:S(2)}, u32[]{:S(2)}) collective-permute-start(bf16[1024,128]{1,0:T(8,128)(2,1)S(1)} %collective-permute-done.8.refs_3_), channel_id=1, source_target_pairs={{0,2},{1,3},{2,4},{3,5},{4,6},{5,7},{6,0},{7,1},{8,10},{9,11},{10,... | collective-permute-start | bytes 786440 | tf_op jit(solution)/shard_map/ppermute | solution.py:1044
  43.5 7.0 %collective-permute-start.2 = (bf16[784,128]{1,0:T(8,128)(2,1)S(1)}, bf16[784,128]{1,0:T(8,128)(2,1)S(1)}, u32[]{:S(2)}, u32[]{:S(2)}) collective-permute-start(bf16[784,128]{1,0:T(8,128)(2,1)S(1)} %collective-permute-done.1.refs_3_), channel_id=1, source_target_pairs={{0,1},{1,0},{2,3},{3,2},{4,5},{5,4},{6,7},{7,6},{8,9},{9,8},{10,11... | collective-permute-start | bytes 602120 | tf_op jit(solution)/shard_map/ppermute | solution.py:1032
  44.0 8.7 %collective-permute-start.4 = (bf16[784,128]{1,0:T(8,128)(2,1)S(1)}, bf16[784,128]{1,0:T(8,128)(2,1)S(1)}, u32[]{:S(2)}, u32[]{:S(2)}) collective-permute-start(bf16[784,128]{1,0:T(8,128)(2,1)S(1)} %collective-permute-done.3.refs_5_), channel_id=1, source_target_pairs={{0,1},{1,0},{2,3},{3,2},{4,5},{5,4},{6,7},{7,6},{8,9},{9,8},{10,11... | collective-permute-start | bytes 602120 | tf_op jit(solution)/shard_map/ppermute | solution.py:1032
  45.5 9.3 %collective-permute-start.6 = (bf16[784,128]{1,0:T(8,128)(2,1)S(1)}, bf16[784,128]{1,0:T(8,128)(2,1)S(1)}, u32[]{:S(2)}, u32[]{:S(2)}) collective-permute-start(bf16[784,128]{1,0:T(8,128)(2,1)S(1)} %collective-permute-done.5.refs_7_), channel_id=1, source_target_pairs={{0,1},{1,0},{2,3},{3,2},{4,5},{5,4},{6,7},{7,6},{8,9},{9,8},{10,11... | collective-permute-start | bytes 602120 | tf_op jit(solution)/shard_map/ppermute | solution.py:1032
  58.5 20.3 %collective-permute-start.10 = (bf16[4096,128]{1,0:T(8,128)(2,1)}, bf16[4096,128]{1,0:T(8,128)(2,1)S(1)}, u32[]{:S(2)}, u32[]{:S(2)}) collective-permute-start(bf16[4096,128]{1,0:T(8,128)(2,1)} %hold.1), channel_id=1, source_target_pairs={{0,1},{1,0},{2,3},{3,2},{4,5},{5,4},{6,7},{7,6},{8,9},{9,8},{10,11... | collective-permute-start | bytes 3145736 | tf_op jit(solution)/shard_map/ppermute | solution.py:1032
  88.4 4.2 %collective-permute-start.12 = (f32[8,1024]{1,0:T(8,128)}, f32[8,1024]{1,0:T(8,128)S(1)}, u32[]{:S(2)}, u32[]{:S(2)}) collective-permute-start(f32[8,1024]{1,0:T(8,128)} %get-tuple-element.68.refs_6_), channel_id=1, source_target_pairs={{0,16},{8,24},{16,0},{24,8},{1,17},{9,25},{17,1},{25,9},{2,18},{10... | collective-permute-start | bytes 98312 | tf_op jit(solution)/shard_map/ppermute | solution.py:1032
  90.0 3.6 %collective-permute-start.13 = (f32[8,1024]{1,0:T(8,128)}, f32[8,1024]{1,0:T(8,128)S(1)}, u32[]{:S(2)}, u32[]{:S(2)}) collective-permute-start(f32[8,1024]{1,0:T(8,128)} %get-tuple-element.68.refs_6_), channel_id=1, source_target_pairs={{0,24},{8,16},{16,8},{24,0},{1,25},{9,17},{17,9},{25,1},{2,26},{10... | collective-permute-start | bytes 98312 | tf_op jit(solution)/shard_map/ppermute | solution.py:1032
  106.7 126.5 %reduce-scatter.5.cloned.1.call-start = ((), (), s32[]{:S(2)}) async-start(), calls=%async_computation.3 | async-start | bytes 2621440 | tf_op jit(solution)/shard_map/reduce_scatter | solution.py:1255
  107.9 26.9 %collective-permute-start.14 = (bf16[4096,128]{1,0:T(8,128)(2,1)S(1)}, bf16[4096,128]{1,0:T(8,128)(2,1)S(1)}, u32[]{:S(2)}, u32[]{:S(2)}) collective-permute-start(bf16[4096,128]{1,0:T(8,128)(2,1)S(1)} %copy-done.30), channel_id=1, source_target_pairs={{0,1},{1,0},{2,3},{3,2},{4,5},{5,4},{6,7},{7,6},{8,9},{9,8},{10,11... | collective-permute-start | bytes 3145736 | tf_op jit(solution)/shard_map/ppermute | solution.py:1032
  139.2 19.9 %collective-permute-start.18 = (bf16[3136,128]{1,0:T(8,128)(2,1)}, bf16[3136,128]{1,0:T(8,128)(2,1)S(1)}, u32[]{:S(2)}, u32[]{:S(2)}) collective-permute-start(bf16[3136,128]{1,0:T(8,128)(2,1)} %get-tuple-element.92), channel_id=1, source_target_pairs={{0,1},{1,0},{2,3},{3,2},{4,5},{5,4},{6,7},{7,6},{8,9},{9,8},{10,11... | collective-permute-start | bytes 2408456 | tf_op jit(solution)/shard_map/ppermute | solution.py:1032
  140.7 22.3 %collective-permute-start.15 = (bf16[1072,128]{1,0:T(8,128)(2,1)}, bf16[1072,128]{1,0:T(8,128)(2,1)S(1)}, u32[]{:S(2)}, u32[]{:S(2)}) collective-permute-start(bf16[1072,128]{1,0:T(8,128)(2,1)} %get-tuple-element.86), channel_id=1, source_target_pairs={{0,2},{1,3},{2,0},{3,1},{4,6},{5,7},{6,4},{7,5},{8,10},{9,11},{10,... | collective-permute-start | bytes 823304 | tf_op jit(solution)/shard_map/ppermute | solution.py:1032
  143.7 22.4 %collective-permute-start.16 = (bf16[1072,128]{1,0:T(8,128)(2,1)}, bf16[1072,128]{1,0:T(8,128)(2,1)S(1)}, u32[]{:S(2)}, u32[]{:S(2)}) collective-permute-start(bf16[1072,128]{1,0:T(8,128)(2,1)} %get-tuple-element.87), channel_id=1, source_target_pairs={{0,4},{1,5},{2,6},{3,7},{4,0},{5,1},{6,2},{7,3},{8,12},{9,13},{10,... | collective-permute-start | bytes 823304 | tf_op jit(solution)/shard_map/ppermute | solution.py:1032
  144.8 21.4 %collective-permute-start.17 = (bf16[1072,128]{1,0:T(8,128)(2,1)}, bf16[1072,128]{1,0:T(8,128)(2,1)S(1)}, u32[]{:S(2)}, u32[]{:S(2)}) collective-permute-start(bf16[1072,128]{1,0:T(8,128)(2,1)} %get-tuple-element.88), channel_id=1, source_target_pairs={{0,6},{1,7},{2,4},{3,5},{4,2},{5,3},{6,0},{7,1},{8,14},{9,15},{10,... | collective-permute-start | bytes 823304 | tf_op jit(solution)/shard_map/ppermute | solution.py:1032
  169.1 11.0 %collective-permute-start.19 = (bf16[784,128]{1,0:T(8,128)(2,1)S(1)}, bf16[784,128]{1,0:T(8,128)(2,1)S(1)}, u32[]{:S(2)}, u32[]{:S(2)}) collective-permute-start(bf16[784,128]{1,0:T(8,128)(2,1)S(1)} %copy-done.36), channel_id=1, source_target_pairs={{0,2},{1,3},{2,0},{3,1},{4,6},{5,7},{6,4},{7,5},{8,10},{9,11},{10,... | collective-permute-start | bytes 602120 | tf_op jit(solution)/shard_map/ppermute | solution.py:1032
  173.8 16.8 %collective-permute-start.20 = (bf16[784,128]{1,0:T(8,128)(2,1)S(1)}, bf16[784,128]{1,0:T(8,128)(2,1)S(1)}, u32[]{:S(2)}, u32[]{:S(2)}) collective-permute-start(bf16[784,128]{1,0:T(8,128)(2,1)S(1)} %copy-done.35), channel_id=1, source_target_pairs={{0,4},{1,5},{2,6},{3,7},{4,0},{5,1},{6,2},{7,3},{8,12},{9,13},{10,... | collective-permute-start | bytes 602120 | tf_op jit(solution)/shard_map/ppermute | solution.py:1032
  174.9 15.6 %collective-permute-start.21 = (bf16[784,128]{1,0:T(8,128)(2,1)S(1)}, bf16[784,128]{1,0:T(8,128)(2,1)S(1)}, u32[]{:S(2)}, u32[]{:S(2)}) collective-permute-start(bf16[784,128]{1,0:T(8,128)(2,1)S(1)} %copy-done.34), channel_id=1, source_target_pairs={{0,6},{1,7},{2,4},{3,5},{4,2},{5,3},{6,0},{7,1},{8,14},{9,15},{10,... | collective-permute-start | bytes 602120 | tf_op jit(solution)/shard_map/ppermute | solution.py:1032
  193.3 13.4 %collective-permute-start.26 = (bf16[1072,128]{1,0:T(8,128)(2,1)}, bf16[1072,128]{1,0:T(8,128)(2,1)S(1)}, u32[]{:S(2)}, u32[]{:S(2)}) collective-permute-start(bf16[1072,128]{1,0:T(8,128)(2,1)} %get-tuple-element.100.refs_1_), channel_id=1, source_target_pairs={{0,16},{8,24},{16,0},{24,8},{1,17},{9,25},{17,1},{25,9},{2,18},{10... | collective-permute-start | bytes 823304 | tf_op jit(solution)/shard_map/ppermute | solution.py:1032
  193.6 20.7 %collective-permute-start.25 = (bf16[1072,128]{1,0:T(8,128)(2,1)}, bf16[1072,128]{1,0:T(8,128)(2,1)S(1)}, u32[]{:S(2)}, u32[]{:S(2)}) collective-permute-start(bf16[1072,128]{1,0:T(8,128)(2,1)} %get-tuple-element.100.refs_1_), channel_id=1, source_target_pairs={{0,8},{8,0},{16,24},{24,16},{1,9},{9,1},{17,25},{25,17},{2,10},{10... | collective-permute-start | bytes 823304 | tf_op jit(solution)/shard_map/ppermute | solution.py:1032
  206.7 7.6 %collective-permute-start.27 = (bf16[1072,128]{1,0:T(8,128)(2,1)S(1)}, bf16[1072,128]{1,0:T(8,128)(2,1)S(1)}, u32[]{:S(2)}, u32[]{:S(2)}) collective-permute-start(bf16[1072,128]{1,0:T(8,128)(2,1)S(1)} %collective-permute-done.26.refs_3_), channel_id=1, source_target_pairs={{0,8},{8,0},{16,24},{24,16},{1,9},{9,1},{17,25},{25,17},{2,10},{10... | collective-permute-start | bytes 823304 | tf_op jit(solution)/shard_map/ppermute | solution.py:1032
  206.7 7.6 %collective-permute-start.23 = (bf16[784,128]{1,0:T(8,128)(2,1)}, bf16[784,128]{1,0:T(8,128)(2,1)S(1)}, u32[]{:S(2)}, u32[]{:S(2)}) collective-permute-start(bf16[784,128]{1,0:T(8,128)(2,1)} %get-tuple-element.99.refs_1_), channel_id=1, source_target_pairs={{0,16},{8,24},{16,0},{24,8},{1,17},{9,25},{17,1},{25,9},{2,18},{10... | collective-permute-start | bytes 602120 | tf_op jit(solution)/shard_map/ppermute | solution.py:1032
  207.8 15.5 %collective-permute-start.22 = (bf16[784,128]{1,0:T(8,128)(2,1)}, bf16[784,128]{1,0:T(8,128)(2,1)S(1)}, u32[]{:S(2)}, u32[]{:S(2)}) collective-permute-start(bf16[784,128]{1,0:T(8,128)(2,1)} %get-tuple-element.99.refs_1_), channel_id=1, source_target_pairs={{0,8},{8,0},{16,24},{24,16},{1,9},{9,1},{17,25},{25,17},{2,10},{10... | collective-permute-start | bytes 602120 | tf_op jit(solution)/shard_map/ppermute | solution.py:1032
  214.3 9.0 %collective-permute-start.24 = (bf16[784,128]{1,0:T(8,128)(2,1)S(1)}, bf16[784,128]{1,0:T(8,128)(2,1)S(1)}, u32[]{:S(2)}, u32[]{:S(2)}) collective-permute-start(bf16[784,128]{1,0:T(8,128)(2,1)S(1)} %collective-permute-done.23.refs_3_), channel_id=1, source_target_pairs={{0,8},{8,0},{16,24},{24,16},{1,9},{9,1},{17,25},{25,17},{2,10},{10... | collective-permute-start | bytes 602120 | tf_op jit(solution)/shard_map/ppermute | solution.py:1032
  222.7 8.3 %collective-permute-start.28 = (bf16[4,48,128]{2,1,0:T(8,128)(2,1)}, bf16[4,48,128]{2,1,0:T(8,128)(2,1)S(1)}, u32[]{:S(2)}, u32[]{:S(2)}) collective-permute-start(bf16[4,48,128]{2,1,0:T(8,128)(2,1)} %get-tuple-element.110), channel_id=1, source_target_pairs={{0,1},{1,0},{2,3},{3,2},{4,5},{5,4},{6,7},{7,6},{8,9},{9,8},{10,11... | collective-permute-start | bytes 147464 | tf_op jit(solution)/shard_map/ppermute | solution.py:1032
  (43 other events, 322.1 us)
Sparse Core Ops, SparseCore 0:
  9.6 25.2 all-gather.4
  36.5 22.5 all-gather.6
  106.9 31.2 reduce-scatter.2
  169.2 38.7 reduce-scatter.4

commit v13 on v11

--- a/solution.py
+++ b/solution.py
@@ -348,7 +348,8 @@
 ):
     grad_refs = refs[:grad_count]
     ext, d_state, later_state, rest_sum = refs[grad_count : grad_count + 4]
-    d_kernel_ref, d_conv_bias_ref, d_skip_ref, d_head_ref = refs[grad_count + 4 :]
+    d_kernel_ref, d_conv_bias_ref, d_skip_ref, d_head_ref = refs[grad_count + 4 : grad_count + 8]
+    rest_before, unit_before = refs[grad_count + 8 :]
     local_di = y_ref.shape[1]
     heads = local_di // HEADDIM
     chunk = pl.program_id(0)
@@ -359,11 +360,14 @@
         d_state[...] = jnp.zeros_like(d_state)
         later_state[...] = jnp.zeros_like(later_state)
         rest_sum[...] = jnp.zeros_like(rest_sum)
+        rest_before[...] = jnp.zeros_like(rest_before)
+        unit_before[...] = jnp.zeros_like(unit_before)
         d_kernel_ref[...] = jnp.zeros_like(d_kernel_ref)
         d_conv_bias_ref[...] = jnp.zeros_like(d_conv_bias_ref)
         d_skip_ref[...] = jnp.zeros_like(d_skip_ref)
         d_head_ref[...] = jnp.zeros_like(d_head_ref)
 
+    rest_sum[...] += dot_tn(rest_before[...], unit_before[...])
     expand = expand_ref[...]
     conv_pre = conv_pre_ref[...]
     open_part = sigmoid(conv_pre)
@@ -446,10 +450,12 @@
     ext[BLOCK : BLOCK + 8, :] = ext[0:8, :]
     d_rest = jnp.concatenate([low(d_conv_in), low(d_dt)], 1)
     d_rest_ref[...] = d_rest
-    rest_sum[...] += dot_tn(d_rest, unit_ref[...])
+    rest_before[...] = d_rest
+    unit_before[...] = unit_ref[...]
 
     @pl.when(chunk == pl.num_programs(0) - 1)
     def _():
+        rest_sum[...] += dot_tn(d_rest, unit_ref[...])
         weights = rest_weight_ref[...].astype(jnp.float32)
         d_gain_one = jnp.sum(rest_sum[...] * weights, axis=0, keepdims=True)
         pieces = [d_gain_one + d_gain_gate_ref[...]]
@@ -885,6 +891,8 @@
             pltpu.VMEM((1, channels), jnp.float32),
             pltpu.VMEM((1, local_di), jnp.float32),
             pltpu.VMEM((2, lanes), jnp.float32),
+            pltpu.VMEM((BLOCK, channels + lanes), jnp.bfloat16),
+            pltpu.VMEM((BLOCK, D), jnp.bfloat16),
         ],
         chunks,
         [],
@@ -1248,14 +1256,14 @@
             gate_out_arrived,
             [vec_rows],
             [rest_grads[1]],
-            [block_rows],
+            [],
         )
         rest_arrived = swap(rest_send, "wshard", 1)
         gate_out_pieces = [
             swap(gate_out_sums[mask], "wshard", 2 * mask) for mask in range(1, 4)
         ]
         normed_mine, normed_send = run_normed(
-            near, d_gating, d_rest, gate_weight, rest_weight, [gate_out_sums[0]]
+            near, d_gating, d_rest, gate_weight, rest_weight, [gate_out_sums[0], block_rows]
         )
         gate_out_part, normed_send = run_final(
             [gate_out_sums[0]] + gate_out_pieces, [normed_send], []

time: 242 us -> 241 us (level)
  waiting for transfers between devices: 66.3 us -> 63.6 us
    reduce_scatter x1, waiting for transfers between devices: 2.96 us -> 0.01 us  [shards(): lax.psum_scatter(block_part, 'seq', scatter_dimension=0, tiled=True)]
  transfers between devices with their start and end apart: 34 -> 34, of which waited for: 18 -> 17; matrix products, arithmetic and copies ran while one was open for 8% -> 8% of each run, Pallas kernels for 31% -> 32%
where the time goes in v13:
time: 241 us; the launch traced here: 239 us
  Pallas kernels  100 us (41%)
  waiting for transfers between devices  63.6 us (26%)
  starting transfers between devices  29 us (12%)
  local copies, waits for them, and re-layouts  20.3 us (8%)
  between operations  14.2 us (6%)
  other arithmetic  11 us (5%)
    pallas_call x13, Pallas kernels, call(): pl.pallas_call(after(kernel, 1 + len(inputs), len(arrived)), grid_spec=pl...  100 us
    ppermute x25, waiting for transfers between devices, swap(): return lax.ppermute(values, axis, route)  41.3 us
    ppermute x25, starting transfers between devices, swap(): return lax.ppermute(values, axis, route)  25.6 us
    ppermute x6, waiting for transfers between devices, ring_step(): lax.ppermute(held, 'wshard', [(i, (i + 2) % count) for i in range(count)])  20.9 us
    unnamed x73, local copies, waits for them, and re-layouts  9.17 us
  transfers between devices with their start and end apart: 34, of which 17 were waited for; matrix products, arithmetic and copies ran while one was open for 8% of the time, Pallas kernels for 32%

profile of v13, /device:TPU:0, one launch (start us, length us, event | category | flops | bytes accessed | tf_op | source)
XLA Modules:
  0.0 238.5 jit_solution(1337454995243471750)
XLA Ops:
  8.7 2.7 %prepare.1 = (bf16[784,128]{1,0:T(8,128)(2,1)}, bf16[1024,128]{1,0:T(8,128)(2,1)}) custom-call(s32[1]{0:T(128)} %bitcast.11.refs_0_, f32[4384,128]{1,0:T(8,128)} %bitcast.74, f32[256,1024]{1,0:T(8,128)} %refs_8_.1), custom_call_target="tpu_custom_call" | custom-call | flops 100000000 | bytes 4000000 | tf_op jit(solution)/shard_map/prepare/pallas_call | solution.py:662
  11.5 3.0 %collective-permute-start = (bf16[784,128]{1,0:T(8,128)(2,1)}, bf16[784,128]{1,0:T(8,128)(2,1)S(1)}, u32[]{:S(2)}, u32[]{:S(2)}) collective-permute-start(bf16[784,128]{1,0:T(8,128)(2,1)} %get-tuple-element.63.refs_1_), channel_id=1, source_target_pairs={{0,1},{1,0},{2,3},{3,2},{4,5},{5,4},{6,7},{7,6},{8,9},{9,8},{10,11... | collective-permute-start | bytes 602120 | tf_op jit(solution)/shard_map/ppermute | solution.py:1051
  17.9 6.5 %collective-permute-done.1.refs_3_ = bf16[784,128]{1,0:T(8,128)(2,1)S(1)} collective-permute-done((bf16[784,128]{1,0:T(8,128)(2,1)}, bf16[784,128]{1,0:T(8,128)(2,1)S(1)}, u32[]{:S(2)}, u32[]{:S(2)}) %collective-permute-start.1) | collective-permute-done | bytes 200736 | tf_op jit(solution)/shard_map/ppermute | solution.py:1063
  24.3 5.6 %collective-permute-done.7.refs_2_ = bf16[1024,128]{1,0:T(8,128)(2,1)S(1)} collective-permute-done((bf16[1024,128]{1,0:T(8,128)(2,1)}, bf16[1024,128]{1,0:T(8,128)(2,1)S(1)}, u32[]{:S(2)}, u32[]{:S(2)}) %collective-permute-start.7) | collective-permute-done | bytes 262176 | tf_op jit(solution)/shard_map/ppermute | solution.py:1063
  31.3 2.7 %collective-permute-done.3.refs_5_ = bf16[784,128]{1,0:T(8,128)(2,1)S(1)} collective-permute-done((bf16[784,128]{1,0:T(8,128)(2,1)S(1)}, bf16[784,128]{1,0:T(8,128)(2,1)S(1)}, u32[]{:S(2)}, u32[]{:S(2)}) %collective-permute-start.3) | collective-permute-done | bytes 200736 | tf_op jit(solution)/shard_map/ppermute | solution.py:1063
  34.6 6.1 %collective-permute-done.8.refs_3_ = bf16[1024,128]{1,0:T(8,128)(2,1)S(1)} collective-permute-done((bf16[1024,128]{1,0:T(8,128)(2,1)S(1)}, bf16[1024,128]{1,0:T(8,128)(2,1)S(1)}, u32[]{:S(2)}, u32[]{:S(2)}) %collective-permute-start.8) | collective-permute-done | bytes 262176 | tf_op jit(solution)/shard_map/ppermute | solution.py:1063
  43.9 1.6 collective-permute-start.4
  46.6 3.8 %collective-permute-done.2.refs_4_.refs_6_ = bf16[784,128]{1,0:T(8,128)(2,1)S(1)} collective-permute-done((bf16[784,128]{1,0:T(8,128)(2,1)S(1)}, bf16[784,128]{1,0:T(8,128)(2,1)S(1)}, u32[]{:S(2)}, u32[]{:S(2)}) %collective-permute-start.2) | collective-permute-done | bytes 200736 | tf_op jit(solution)/shard_map/ppermute | solution.py:1051
  50.4 2.1 collective-permute-done.4.refs_6_.refs_7_
  52.6 2.1 collective-permute-done.6.refs_8_
  55.5 2.9 %hold.1 = bf16[4096,128]{1,0:T(8,128)(2,1)} custom-call(s32[8]{0:T(128)} %stack.114.refs_0_, bf16[1024,128]{1,0:T(8,128)(2,1)} %get-tuple-element.65.refs_1_, bf16[1024,128]{1,0:T(8,128)(2,1)} %copy-done.13, bf16[1024,128]{1,0:T(8,128)(2,1)} %copy-done.14, bf16[1024,128]{1,0:T(8,128)(2,1)} %copy-done.15, bf16[784,128]{1,0:T(8,128)(2,1)} %copy-done.19, ...), custom_call_target="tpu_custom_call" | custom-call | bytes 2000000 | tf_op jit(solution)/shard_map/hold/pallas_call | solution.py:662
  60.9 14.1 %forward.1 = (bf16[896,1024]{1,0:T(8,128)(2,1)}, bf16[1024,1024]{1,0:T(8,128)(2,1)}, bf16[1024,1024]{1,0:T(8,128)(2,1)}, f32[1024,768]{1,0:T(8,128)}, f32[1024,7...) custom-call(s32[8]{0:T(128)} %stack.114.refs_0_, ...), custom_call_target="tpu_custom_call" | custom-call | flops 6000000000 | bytes 30000000 | tf_op jit(solution)/shard_map/forward/pallas_call | solution.py:662
  75.0 3.7 %collective-permute-done.10.refs_5_ = bf16[4096,128]{1,0:T(8,128)(2,1)S(1)} collective-permute-done((bf16[4096,128]{1,0:T(8,128)(2,1)}, bf16[4096,128]{1,0:T(8,128)(2,1)S(1)}, u32[]{:S(2)}, u32[]{:S(2)}) %collective-permute-start.10) | collective-permute-done | bytes 1048608 | tf_op jit(solution)/shard_map/ppermute | solution.py:1051
  79.6 8.6 %gate.1 = (bf16[512,1024]{1,0:T(8,128)(2,1)}, bf16[512,1024]{1,0:T(8,128)(2,1)}, f32[1024,512]{1,0:T(8,128)}, f32[1024,512]{1,0:T(8,128)}, f32[8,1024]{1,0:T(8,128)}) custom-call(s32[8]{0:T(128)} %stack.116.refs_0_, bf16[1024,128]{1,0:T(8,128)(2,1)} %get-tuple-element.65.refs_1_, bf16[1024,128]{1,0:T(8,128)(2,1)} %copy-done.13, ...), custom_call_target="tpu_custom_call" | custom-call | flops 2500000000 | bytes 12000000 | tf_op jit(solution)/shard_map/gate/pallas_call | solution.py:662
  90.8 1.7 collective-permute-done.12.refs_8_
  94.0 12.6 %middle.1 = (bf16[1024,1024]{1,0:T(8,128)(2,1)}, bf16[1024,512]{1,0:T(8,128)(2,1)}, bf16[1024,512]{1,0:T(8,128)(2,1)}, f32[1,512]{1,0:T(1,128)}, f32[1,1024]{1,0...) custom-call(s32[2]{0:T(128)} %pad_add_fusion.refs_0_, ...), custom_call_target="tpu_custom_call" | custom-call | flops 4000000000 | bytes 15000000 | tf_op jit(solution)/shard_map/middle/pallas_call | solution.py:662
  108.3 26.8 %backward.1 = (bf16[1024,896]{1,0:T(8,128)(2,1)}, f32[48,128]{1,0:T(8,128)}, bf16[3136,128]{1,0:T(8,128)(2,1)}, bf16[3136,128]{1,0:T(8,128)(2,1)}) custom-call(s32[2]{0:T(128)} %pad_add_fusion.refs_0_, bf16[1024,1024]{1,0:T(8,128)(2,1)} %get-tuple-element.69.refs_5_.refs_1_, f32[1024,768]{1,0:T(8,128)} %get-tuple-element.75.refs_2_, ...), custom_call_target="tpu_custom_call" | custom-call | flops 14000000000 | bytes 40000000 | tf_op jit(solution)/shard_map/backward/pallas_call | solution.py:662
  136.1 3.4 %pair.2 = (bf16[1072,128]{1,0:T(8,128)(2,1)}, bf16[1072,128]{1,0:T(8,128)(2,1)}, bf16[1072,128]{1,0:T(8,128)(2,1)}, bf16[1072,128]{1,0:T(8,128)(2,1)}, bf16[3136,128]{1,0:T(8,128)(2,1)}) custom-call(s32[4]{0:T(128)} %pad_add_fusion.1.refs_0_, bf16[4096,128]{1,0:T(8,128)(2,1)} %get-tuple-element.85.refs_1_, ...), custom_call_target="tpu_custom_call", output_to_operand_aliasing={{4}: (4, {})} | custom-call | flops 2000000 | bytes 3000000 | tf_op jit(solution)/shard_map/pair/pallas_call | solution.py:662
  140.9 3.0 %collective-permute-start.15 = (bf16[1072,128]{1,0:T(8,128)(2,1)}, bf16[1072,128]{1,0:T(8,128)(2,1)S(1)}, u32[]{:S(2)}, u32[]{:S(2)}) collective-permute-start(bf16[1072,128]{1,0:T(8,128)(2,1)} %get-tuple-element.91), channel_id=1, source_target_pairs={{0,2},{1,3},{2,0},{3,1},{4,6},{5,7},{6,4},{7,5},{8,10},{9,11},{10,... | collective-permute-start | bytes 823304 | tf_op jit(solution)/shard_map/ppermute | solution.py:1051
  146.4 7.6 %normed.1 = (bf16[512,1024]{1,0:T(8,128)(2,1)}, bf16[512,1024]{1,0:T(8,128)(2,1)}) custom-call(s32[1]{0:T(128)} %bitcast.21.refs_0_, bf16[1024,512]{1,0:T(8,128)(2,1)} %get-tuple-element.74.refs_1_, bf16[1024,896]{1,0:T(8,128)(2,1)} %get-tuple-element.84.refs_2_, bf16[512,1024]{1,0:T(8,128)(2,1)} %get-tuple-element.72.refs_13_.refs_3_, ...), custom_call_target="tpu_custom_call" | custom-call | flops 3000000000 | bytes 9000000 | tf_op jit(solution)/shard_map/normed/pallas_call | solution.py:662
  155.5 10.8 %collective-permute-done.16.refs_3_ = bf16[1072,128]{1,0:T(8,128)(2,1)S(1)} collective-permute-done((bf16[1072,128]{1,0:T(8,128)(2,1)}, bf16[1072,128]{1,0:T(8,128)(2,1)S(1)}, u32[]{:S(2)}, u32[]{:S(2)}) %collective-permute-start.16) | collective-permute-done | bytes 274464 | tf_op jit(solution)/shard_map/ppermute | solution.py:1051
  167.1 2.1 final.2
  170.0 5.8 %collective-permute-done.25.refs_3_ = bf16[1072,128]{1,0:T(8,128)(2,1)S(1)} collective-permute-done((bf16[1072,128]{1,0:T(8,128)(2,1)}, bf16[1072,128]{1,0:T(8,128)(2,1)S(1)}, u32[]{:S(2)}, u32[]{:S(2)}) %collective-permute-start.25) | collective-permute-done | bytes 274464 | tf_op jit(solution)/shard_map/ppermute | solution.py:1051
  176.9 3.1 %pair.3 = (bf16[784,128]{1,0:T(8,128)(2,1)}, bf16[784,128]{1,0:T(8,128)(2,1)}, bf16[784,128]{1,0:T(8,128)(2,1)}, bf16[784,128]{1,0:T(8,128)(2,1)}) custom-call(s32[4]{0:T(128)} %pad_add_fusion.1.refs_0_, bf16[3136,128]{1,0:T(8,128)(2,1)} %get-tuple-element.96.refs_1_, bf16[3136,128]{1,0:T(8,128)(2,1)} %copy-done.6, bf16[1072,128]{1,0:T(8,128)(2,1)} %copy-done.2), custom_call_target="tpu_custom_call" | custom-call | flops 2000000 | bytes 3000000 | tf_op jit(solution)/shard_map/pair/pallas_call | solution.py:662
  180.0 5.1 %collective-permute-start.22 = (bf16[784,128]{1,0:T(8,128)(2,1)}, bf16[784,128]{1,0:T(8,128)(2,1)S(1)}, u32[]{:S(2)}, u32[]{:S(2)}) collective-permute-start(bf16[784,128]{1,0:T(8,128)(2,1)} %get-tuple-element.100), channel_id=1, source_target_pairs={{0,2},{1,3},{2,0},{3,1},{4,6},{5,7},{6,4},{7,5},{8,10},{9,11},{10,... | collective-permute-start | bytes 602120 | tf_op jit(solution)/shard_map/ppermute | solution.py:1051
  189.2 7.7 %update_gate.1 = (f32[4384,128]{1,0:T(8,128)}, f32[4384,128]{1,0:T(8,128)}, f32[4384,128]{1,0:T(8,128)}, f32[256,1024]{1,0:T(8,128)}, f32[256,1024]{1,0:T(8,128)...) custom-call(s32[4]{0:T(128)} %pad_add_fusion.2.refs_0_, bf16[1072,128]{1,0:T(8,128)(2,1)} %get-tuple-element.98.refs_1_, ...), custom_call_target="tpu_custom_call" | custom-call | flops 10000000 | bytes 13000000 | tf_op jit(solution)/shard_map/update_gate/pallas_call | solution.py:662
  196.9 5.8 %collective-permute-done.23.refs_3_ = bf16[784,128]{1,0:T(8,128)(2,1)S(1)} collective-permute-done((bf16[784,128]{1,0:T(8,128)(2,1)}, bf16[784,128]{1,0:T(8,128)(2,1)S(1)}, u32[]{:S(2)}, u32[]{:S(2)}) %collective-permute-start.23) | collective-permute-done | bytes 200736 | tf_op jit(solution)/shard_map/ppermute | solution.py:1051
  203.5 2.0 final.3
  207.4 2.4 collective-permute-done.30
  215.1 1.9 convert_add_fusion
  222.1 6.9 %update_rest.1 = (f32[4384,128]{1,0:T(8,128)}, f32[4384,128]{1,0:T(8,128)}, f32[4384,128]{1,0:T(8,128)}) custom-call(s32[4]{0:T(128)} %pad_add_fusion.2.refs_0_, bf16[784,128]{1,0:T(8,128)(2,1)} %get-tuple-element.104.refs_1_, bf16[784,128]{1,0:T(8,128)(2,1)} %copy-done.17, ...), custom_call_target="tpu_custom_call", output_to_operand_aliasing={{0}: (8, {}), {1}: (9, {}), {2}: (10, {})} | custom-call | flops 10000000 | bytes 8000000 | tf_op jit(solution)/shard_map/update_rest/pallas_call | solution.py:662
  230.2 1.8 fusion.6
  (200 shorter events, 48.3 us)
Async XLA Ops:
  7.2 53.7 %all-gather.5.cloned.1.call-start = ((), (), s32[]{:S(2)}) async-start(), calls=%async_computation.2 | async-start | bytes 2621440 | tf_op jit(solution)/shard_map/all_gather | solution.py:1178
  7.9 70.7 %all-gather.7.cloned.1.call-start = ((), (), s32[]{:S(2)}) async-start(), calls=%async_computation.3 | async-start | bytes 2621440 | tf_op jit(solution)/shard_map/all_gather | solution.py:1179
  8.7 137.7 %reduce-scatter.2.cloned.1.call-start = ((), (), s32[]{:S(2)}) async-start(), calls=%async_computation.1 | async-start | bytes 2621440 | tf_op jit(solution)/shard_map/reduce_scatter | solution.py:1231
  11.5 35.1 %collective-permute-start = (bf16[784,128]{1,0:T(8,128)(2,1)}, bf16[784,128]{1,0:T(8,128)(2,1)S(1)}, u32[]{:S(2)}, u32[]{:S(2)}) collective-permute-start(bf16[784,128]{1,0:T(8,128)(2,1)} %get-tuple-element.63.refs_1_), channel_id=1, source_target_pairs={{0,1},{1,0},{2,3},{3,2},{4,5},{5,4},{6,7},{7,6},{8,9},{9,8},{10,11... | collective-permute-start | bytes 602120 | tf_op jit(solution)/shard_map/ppermute | solution.py:1051
  14.4 9.9 %collective-permute-start.1 = (bf16[784,128]{1,0:T(8,128)(2,1)}, bf16[784,128]{1,0:T(8,128)(2,1)S(1)}, u32[]{:S(2)}, u32[]{:S(2)}) collective-permute-start(bf16[784,128]{1,0:T(8,128)(2,1)} %get-tuple-element.63.refs_1_), channel_id=1, source_target_pairs={{0,2},{1,3},{2,4},{3,5},{4,6},{5,7},{6,0},{7,1},{8,10},{9,11},{10,... | collective-permute-start | bytes 602120 | tf_op jit(solution)/shard_map/ppermute | solution.py:1063
  16.0 14.0 %collective-permute-start.7 = (bf16[1024,128]{1,0:T(8,128)(2,1)}, bf16[1024,128]{1,0:T(8,128)(2,1)S(1)}, u32[]{:S(2)}, u32[]{:S(2)}) collective-permute-start(bf16[1024,128]{1,0:T(8,128)(2,1)} %get-tuple-element.65.refs_1_), channel_id=1, source_target_pairs={{0,2},{1,3},{2,4},{3,5},{4,6},{5,7},{6,0},{7,1},{8,10},{9,11},{10,... | collective-permute-start | bytes 786440 | tf_op jit(solution)/shard_map/ppermute | solution.py:1063
  24.3 9.6 %collective-permute-start.3 = (bf16[784,128]{1,0:T(8,128)(2,1)S(1)}, bf16[784,128]{1,0:T(8,128)(2,1)S(1)}, u32[]{:S(2)}, u32[]{:S(2)}) collective-permute-start(bf16[784,128]{1,0:T(8,128)(2,1)S(1)} %collective-permute-done.1.refs_3_), channel_id=1, source_target_pairs={{0,2},{1,3},{2,4},{3,5},{4,6},{5,7},{6,0},{7,1},{8,10},{9,11},{10,... | collective-permute-start | bytes 602120 | tf_op jit(solution)/shard_map/ppermute | solution.py:1063
  30.0 10.8 %collective-permute-start.8 = (bf16[1024,128]{1,0:T(8,128)(2,1)S(1)}, bf16[1024,128]{1,0:T(8,128)(2,1)S(1)}, u32[]{:S(2)}, u32[]{:S(2)}) collective-permute-start(bf16[1024,128]{1,0:T(8,128)(2,1)S(1)} %collective-permute-done.7.refs_2_), channel_id=1, source_target_pairs={{0,2},{1,3},{2,4},{3,5},{4,6},{5,7},{6,0},{7,1},{8,10},{9,11},{10,... | collective-permute-start | bytes 786440 | tf_op jit(solution)/shard_map/ppermute | solution.py:1063
  34.0 11.5 %collective-permute-start.5 = (bf16[784,128]{1,0:T(8,128)(2,1)S(1)}, bf16[784,128]{1,0:T(8,128)(2,1)S(1)}, u32[]{:S(2)}, u32[]{:S(2)}) collective-permute-start(bf16[784,128]{1,0:T(8,128)(2,1)S(1)} %collective-permute-done.3.refs_5_), channel_id=1, source_target_pairs={{0,2},{1,3},{2,4},{3,5},{4,6},{5,7},{6,0},{7,1},{8,10},{9,11},{10,... | collective-permute-start | bytes 602120 | tf_op jit(solution)/shard_map/ppermute | solution.py:1063
  40.7 11.9 %collective-permute-start.9 = (bf16[1024,128]{1,0:T(8,128)(2,1)S(1)}, bf16[1024,128]{1,0:T(8,128)(2,1)S(1)}, u32[]{:S(2)}, u32[]{:S(2)}) collective-permute-start(bf16[1024,128]{1,0:T(8,128)(2,1)S(1)} %collective-permute-done.8.refs_3_), channel_id=1, source_target_pairs={{0,2},{1,3},{2,4},{3,5},{4,6},{5,7},{6,0},{7,1},{8,10},{9,11},{10,... | collective-permute-start | bytes 786440 | tf_op jit(solution)/shard_map/ppermute | solution.py:1063
  43.4 7.0 %collective-permute-start.2 = (bf16[784,128]{1,0:T(8,128)(2,1)S(1)}, bf16[784,128]{1,0:T(8,128)(2,1)S(1)}, u32[]{:S(2)}, u32[]{:S(2)}) collective-permute-start(bf16[784,128]{1,0:T(8,128)(2,1)S(1)} %collective-permute-done.1.refs_3_), channel_id=1, source_target_pairs={{0,1},{1,0},{2,3},{3,2},{4,5},{5,4},{6,7},{7,6},{8,9},{9,8},{10,11... | collective-permute-start | bytes 602120 | tf_op jit(solution)/shard_map/ppermute | solution.py:1051
  43.9 8.7 %collective-permute-start.4 = (bf16[784,128]{1,0:T(8,128)(2,1)S(1)}, bf16[784,128]{1,0:T(8,128)(2,1)S(1)}, u32[]{:S(2)}, u32[]{:S(2)}) collective-permute-start(bf16[784,128]{1,0:T(8,128)(2,1)S(1)} %collective-permute-done.3.refs_5_), channel_id=1, source_target_pairs={{0,1},{1,0},{2,3},{3,2},{4,5},{5,4},{6,7},{7,6},{8,9},{9,8},{10,11... | collective-permute-start | bytes 602120 | tf_op jit(solution)/shard_map/ppermute | solution.py:1051
  45.5 9.3 %collective-permute-start.6 = (bf16[784,128]{1,0:T(8,128)(2,1)S(1)}, bf16[784,128]{1,0:T(8,128)(2,1)S(1)}, u32[]{:S(2)}, u32[]{:S(2)}) collective-permute-start(bf16[784,128]{1,0:T(8,128)(2,1)S(1)} %collective-permute-done.5.refs_7_), channel_id=1, source_target_pairs={{0,1},{1,0},{2,3},{3,2},{4,5},{5,4},{6,7},{7,6},{8,9},{9,8},{10,11... | collective-permute-start | bytes 602120 | tf_op jit(solution)/shard_map/ppermute | solution.py:1051
  58.4 20.3 %collective-permute-start.10 = (bf16[4096,128]{1,0:T(8,128)(2,1)}, bf16[4096,128]{1,0:T(8,128)(2,1)S(1)}, u32[]{:S(2)}, u32[]{:S(2)}) collective-permute-start(bf16[4096,128]{1,0:T(8,128)(2,1)} %hold.1), channel_id=1, source_target_pairs={{0,1},{1,0},{2,3},{3,2},{4,5},{5,4},{6,7},{7,6},{8,9},{9,8},{10,11... | collective-permute-start | bytes 3145736 | tf_op jit(solution)/shard_map/ppermute | solution.py:1051
  88.3 4.2 %collective-permute-start.12 = (f32[8,1024]{1,0:T(8,128)}, f32[8,1024]{1,0:T(8,128)S(1)}, u32[]{:S(2)}, u32[]{:S(2)}) collective-permute-start(f32[8,1024]{1,0:T(8,128)} %get-tuple-element.70.refs_6_), channel_id=1, source_target_pairs={{0,16},{8,24},{16,0},{24,8},{1,17},{9,25},{17,1},{25,9},{2,18},{10... | collective-permute-start | bytes 98312 | tf_op jit(solution)/shard_map/ppermute | solution.py:1051
  89.9 3.6 %collective-permute-start.13 = (f32[8,1024]{1,0:T(8,128)}, f32[8,1024]{1,0:T(8,128)S(1)}, u32[]{:S(2)}, u32[]{:S(2)}) collective-permute-start(f32[8,1024]{1,0:T(8,128)} %get-tuple-element.70.refs_6_), channel_id=1, source_target_pairs={{0,24},{8,16},{16,8},{24,0},{1,25},{9,17},{17,9},{25,1},{2,26},{10... | collective-permute-start | bytes 98312 | tf_op jit(solution)/shard_map/ppermute | solution.py:1051
  107.8 27.3 %collective-permute-start.14 = (bf16[4096,128]{1,0:T(8,128)(2,1)S(1)}, bf16[4096,128]{1,0:T(8,128)(2,1)S(1)}, u32[]{:S(2)}, u32[]{:S(2)}) collective-permute-start(bf16[4096,128]{1,0:T(8,128)(2,1)S(1)} %copy-done.29), channel_id=1, source_target_pairs={{0,1},{1,0},{2,3},{3,2},{4,5},{5,4},{6,7},{7,6},{8,9},{9,8},{10,11... | collective-permute-start | bytes 3145736 | tf_op jit(solution)/shard_map/ppermute | solution.py:1051
  139.5 36.4 %collective-permute-start.20 = (bf16[3136,128]{1,0:T(8,128)(2,1)}, bf16[3136,128]{1,0:T(8,128)(2,1)S(1)}, u32[]{:S(2)}, u32[]{:S(2)}) collective-permute-start(bf16[3136,128]{1,0:T(8,128)(2,1)} %get-tuple-element.97), channel_id=1, source_target_pairs={{0,1},{1,0},{2,3},{3,2},{4,5},{5,4},{6,7},{7,6},{8,9},{9,8},{10,11... | collective-permute-start | bytes 2408456 | tf_op jit(solution)/shard_map/ppermute | solution.py:1051
  140.9 14.6 %collective-permute-start.15 = (bf16[1072,128]{1,0:T(8,128)(2,1)}, bf16[1072,128]{1,0:T(8,128)(2,1)S(1)}, u32[]{:S(2)}, u32[]{:S(2)}) collective-permute-start(bf16[1072,128]{1,0:T(8,128)(2,1)} %get-tuple-element.91), channel_id=1, source_target_pairs={{0,2},{1,3},{2,0},{3,1},{4,6},{5,7},{6,4},{7,5},{8,10},{9,11},{10,... | collective-permute-start | bytes 823304 | tf_op jit(solution)/shard_map/ppermute | solution.py:1051
  143.9 22.4 %collective-permute-start.16 = (bf16[1072,128]{1,0:T(8,128)(2,1)}, bf16[1072,128]{1,0:T(8,128)(2,1)S(1)}, u32[]{:S(2)}, u32[]{:S(2)}) collective-permute-start(bf16[1072,128]{1,0:T(8,128)(2,1)} %get-tuple-element.92), channel_id=1, source_target_pairs={{0,4},{1,5},{2,6},{3,7},{4,0},{5,1},{6,2},{7,3},{8,12},{9,13},{10,... | collective-permute-start | bytes 823304 | tf_op jit(solution)/shard_map/ppermute | solution.py:1051
  145.0 21.3 %collective-permute-start.17 = (bf16[1072,128]{1,0:T(8,128)(2,1)}, bf16[1072,128]{1,0:T(8,128)(2,1)S(1)}, u32[]{:S(2)}, u32[]{:S(2)}) collective-permute-start(bf16[1072,128]{1,0:T(8,128)(2,1)} %get-tuple-element.93), channel_id=1, source_target_pairs={{0,6},{1,7},{2,4},{3,5},{4,2},{5,3},{6,0},{7,1},{8,14},{9,15},{10,... | collective-permute-start | bytes 823304 | tf_op jit(solution)/shard_map/ppermute | solution.py:1051
  169.1 6.7 %collective-permute-start.25 = (bf16[1072,128]{1,0:T(8,128)(2,1)}, bf16[1072,128]{1,0:T(8,128)(2,1)S(1)}, u32[]{:S(2)}, u32[]{:S(2)}) collective-permute-start(bf16[1072,128]{1,0:T(8,128)(2,1)} %get-tuple-element.98.refs_1_), channel_id=1, source_target_pairs={{0,16},{8,24},{16,0},{24,8},{1,17},{9,25},{17,1},{25,9},{2,18},{10... | collective-permute-start | bytes 823304 | tf_op jit(solution)/shard_map/ppermute | solution.py:1051
  170.0 5.9 %collective-permute-start.21 = (bf16[1072,128]{1,0:T(8,128)(2,1)}, bf16[1072,128]{1,0:T(8,128)(2,1)S(1)}, u32[]{:S(2)}, u32[]{:S(2)}) collective-permute-start(bf16[1072,128]{1,0:T(8,128)(2,1)} %get-tuple-element.98.refs_1_), channel_id=1, source_target_pairs={{0,8},{8,0},{16,24},{24,16},{1,9},{9,1},{17,25},{25,17},{2,10},{10... | collective-permute-start | bytes 823304 | tf_op jit(solution)/shard_map/ppermute | solution.py:1051
  175.9 12.6 %collective-permute-start.26 = (bf16[1072,128]{1,0:T(8,128)(2,1)S(1)}, bf16[1072,128]{1,0:T(8,128)(2,1)S(1)}, u32[]{:S(2)}, u32[]{:S(2)}) collective-permute-start(bf16[1072,128]{1,0:T(8,128)(2,1)S(1)} %collective-permute-done.25.refs_3_), channel_id=1, source_target_pairs={{0,8},{8,0},{16,24},{24,16},{1,9},{9,1},{17,25},{25,17},{2,10},{10... | collective-permute-start | bytes 823304 | tf_op jit(solution)/shard_map/ppermute | solution.py:1051
  180.0 16.8 %collective-permute-start.22 = (bf16[784,128]{1,0:T(8,128)(2,1)}, bf16[784,128]{1,0:T(8,128)(2,1)S(1)}, u32[]{:S(2)}, u32[]{:S(2)}) collective-permute-start(bf16[784,128]{1,0:T(8,128)(2,1)} %get-tuple-element.100), channel_id=1, source_target_pairs={{0,2},{1,3},{2,0},{3,1},{4,6},{5,7},{6,4},{7,5},{8,10},{9,11},{10,... | collective-permute-start | bytes 602120 | tf_op jit(solution)/shard_map/ppermute | solution.py:1051
  185.1 17.6 %collective-permute-start.23 = (bf16[784,128]{1,0:T(8,128)(2,1)}, bf16[784,128]{1,0:T(8,128)(2,1)S(1)}, u32[]{:S(2)}, u32[]{:S(2)}) collective-permute-start(bf16[784,128]{1,0:T(8,128)(2,1)} %get-tuple-element.101), channel_id=1, source_target_pairs={{0,4},{1,5},{2,6},{3,7},{4,0},{5,1},{6,2},{7,3},{8,12},{9,13},{10,... | collective-permute-start | bytes 602120 | tf_op jit(solution)/shard_map/ppermute | solution.py:1051
  186.1 16.6 %collective-permute-start.24 = (bf16[784,128]{1,0:T(8,128)(2,1)}, bf16[784,128]{1,0:T(8,128)(2,1)S(1)}, u32[]{:S(2)}, u32[]{:S(2)}) collective-permute-start(bf16[784,128]{1,0:T(8,128)(2,1)} %get-tuple-element.102), channel_id=1, source_target_pairs={{0,6},{1,7},{2,4},{3,5},{4,2},{5,3},{6,0},{7,1},{8,14},{9,15},{10,... | collective-permute-start | bytes 602120 | tf_op jit(solution)/shard_map/ppermute | solution.py:1051
  205.5 4.3 %collective-permute-start.30 = (bf16[4,48,128]{2,1,0:T(8,128)(2,1)}, bf16[4,48,128]{2,1,0:T(8,128)(2,1)S(1)}, u32[]{:S(2)}, u32[]{:S(2)}) collective-permute-start(bf16[4,48,128]{2,1,0:T(8,128)(2,1)} %get-tuple-element.114), channel_id=1, source_target_pairs={{0,1},{1,0},{2,3},{3,2},{4,5},{5,4},{6,7},{7,6},{8,9},{9,8},{10,11... | collective-permute-start | bytes 147464 | tf_op jit(solution)/shard_map/ppermute | solution.py:1051
  206.5 7.6 %collective-permute-start.18 = (bf16[512,1024]{1,0:T(8,128)(2,1)S(1)}, bf16[512,1024]{1,0:T(8,128)(2,1)S(1)}, u32[]{:S(2)}, u32[]{:S(2)}) collective-permute-start(bf16[512,1024]{1,0:T(8,128)(2,1)S(1)} %copy-done.4), channel_id=1, source_target_pairs={{0,8},{8,0},{16,24},{24,16},{1,9},{9,1},{17,25},{25,17},{2,10},{10... | collective-permute-start | bytes 3145736 | tf_op jit(solution)/shard_map/ppermute | solution.py:1051
  206.5 14.8 %collective-permute-start.27 = (bf16[784,128]{1,0:T(8,128)(2,1)}, bf16[784,128]{1,0:T(8,128)(2,1)S(1)}, u32[]{:S(2)}, u32[]{:S(2)}) collective-permute-start(bf16[784,128]{1,0:T(8,128)(2,1)} %get-tuple-element.104.refs_1_), channel_id=1, source_target_pairs={{0,8},{8,0},{16,24},{24,16},{1,9},{9,1},{17,25},{25,17},{2,10},{10... | collective-permute-start | bytes 602120 | tf_op jit(solution)/shard_map/ppermute | solution.py:1051
  207.0 12.7 %collective-permute-start.28 = (bf16[784,128]{1,0:T(8,128)(2,1)}, bf16[784,128]{1,0:T(8,128)(2,1)}, u32[]{:S(2)}, u32[]{:S(2)}) collective-permute-start(bf16[784,128]{1,0:T(8,128)(2,1)} %get-tuple-element.104.refs_1_), channel_id=1, source_target_pairs={{0,16},{8,24},{16,0},{24,8},{1,17},{9,25},{17,1},{25,9},{2,18},{10... | collective-permute-start | bytes 602120 | tf_op jit(solution)/shard_map/ppermute | solution.py:1051
  218.0 11.5 %collective-permute-start.19 = (bf16[256,1024]{1,0:T(8,128)(2,1)}, bf16[256,1024]{1,0:T(8,128)(2,1)S(1)}, u32[]{:S(2)}, u32[]{:S(2)}) collective-permute-start(bf16[256,1024]{1,0:T(8,128)(2,1)} %dynamic-slice_convert_fusion), channel_id=1, source_target_pairs={{0,16},{8,24},{16,0},{24,8},{1,17},{9,25},{17,1},{25,9},{2,18},{10... | collective-permute-start | bytes 1572872 | tf_op jit(solution)/shard_map/ppermute | solution.py:1051
  (40 other events, 295.8 us)
Sparse Core Ops, SparseCore 0:
  9.6 25.2 all-gather.4
  36.5 22.5 all-gather.6
  106.8 31.1 reduce-scatter.1
